TPU v7x, 32 devices: a whole 2x2x4 slice. The times are simulated.
32 devices in a mesh: dp: 8 (over y, x, core), tensor: 4 (over z).
Axes of the slice: x: 2, y: 2, z: 4, core: 2. Of those that a mesh axis runs over, the one named last changes fastest.
Arguments:
- tokens: bfloat16 [4096, 2048], P(('dp', 'tensor')), may hold values from -6 to 6
- picture_ids: int32 [4096], P('dp'), may hold values from 0 to 1, as said below
- routes: int32 [4096, 4], P('dp'), may hold values from 0 to 7, as said below
- slot_order: int32 [4096, 4], P('dp'), may hold values from 0 to 319, as said below
- norm_gains: bfloat16 [2, 2048], P(None, ('dp', 'tensor')), may hold values from 0.5 to 1.5
- w_query: bfloat16 [2048, 2048], P('dp', 'tensor'), may hold values from -0.125 to 0.125
- w_key: bfloat16 [2048, 2048], P('dp', 'tensor'), may hold values from -0.125 to 0.125
- w_value: bfloat16 [2048, 2048], P('dp', 'tensor'), may hold values from -0.125 to 0.125
- w_out: bfloat16 [2048, 2048], P('tensor', 'dp'), may hold values from -0.75 to 0.75
- qkv_bias: bfloat16 [3, 16, 128], P(None, 'tensor', 'dp'), may hold values from -3 to 3
- router: bfloat16 [2048, 9], P('dp'), may hold values from -0.06591797 to 0.06591797
- shared_gate: bfloat16 [2048, 5632], P('dp', 'tensor'), may hold values from -0.125 to 0.125
- shared_up: bfloat16 [2048, 5632], P('dp', 'tensor'), may hold values from -0.125 to 0.125
- shared_down: bfloat16 [5632, 2048], P('tensor', 'dp'), may hold values from -0.21875 to 0.21875
- expert_gate: bfloat16 [8, 2048, 1408], P(None, 'dp', 'tensor'), may hold values from -0.125 to 0.125
- expert_up: bfloat16 [8, 2048, 1408], P(None, 'dp', 'tensor'), may hold values from -0.125 to 0.125
- expert_down: bfloat16 [8, 1408, 2048], P(None, 'tensor', 'dp'), may hold values from -0.625 to 0.625
- out_grad: bfloat16 [4096, 2048], P(('dp', 'tensor')), may hold values from -6 to 6
Outputs:
- output: bfloat16 [4096, 2048], P(('dp', 'tensor'))
- input_grad: bfloat16 [4096, 2048], P(('dp', 'tensor'))
- gains_grad: float32 [2, 2048], P(None, ('dp', 'tensor'))
- query_grad: float32 [2048, 2048], P('dp', 'tensor')
- key_grad: float32 [2048, 2048], P('dp', 'tensor')
- value_grad: float32 [2048, 2048], P('dp', 'tensor')
- out_proj_grad: float32 [2048, 2048], P('tensor', 'dp')
- bias_grad: float32 [3, 16, 128], P(None, 'tensor', 'dp')
- router_grad: float32 [2048, 9], P('dp')
- shared_gate_grad: float32 [2048, 5632], P('dp', 'tensor')
- shared_up_grad: float32 [2048, 5632], P('dp', 'tensor')
- shared_down_grad: float32 [5632, 2048], P('tensor', 'dp')
- expert_gate_grad: float32 [8, 2048, 1408], P(None, 'dp', 'tensor')
- expert_up_grad: float32 [8, 2048, 1408], P(None, 'dp', 'tensor')
- expert_down_grad: float32 [8, 1408, 2048], P(None, 'tensor', 'dp')
Inputs may be any that keep to these rules, and one draw needn't show every extreme that they name: `picture_ids`: each sequence of 512 tokens holds exactly one run of 256 consecutive tokens numbered 1; all its other tokens are 0. `routes`: each token names 4 different experts. Within one sequence no expert is named by more than 320 tokens, and one expert by exactly 320. Within one sequence, the tokens that name an expert hold its slots 0 to one less than their number, each once; slot_order[t, k] belongs to the expert routes[t, k].
All inputs are finite; a program needn't handle non-finite values.
Results may differ from a plain program's by a relative error of at most 0.029.
Values may be sent and summed in bfloat16 or wider, within the bound.
A program may use at most 320 MiB of HBM per device.

v0:
```python
import jax
import jax.numpy as jnp
from jax import lax
from jax.sharding import PartitionSpec as P

EPS = 1e-06
THETA = 1000000.0
BLOCK_ROWS = 512


def rope_tables(length, width):
    half_width = width // 2
    inverse = THETA ** (-(2.0 * jnp.arange(half_width, dtype=jnp.float32)) / width)
    angles = jnp.arange(length, dtype=jnp.float32)[:, None] * inverse[None, :]
    return (jnp.cos(angles), jnp.sin(angles))


def rotate(field_in, cos_part, sin_part):
    half_width = field_in.shape[-1] // 2
    lower_half = field_in[..., :half_width]
    upper_half = field_in[..., half_width:]
    cos_rows = cos_part[:, None, :]
    sin_rows = sin_part[:, None, :]
    return jnp.concatenate(
        [
            lower_half * cos_rows - upper_half * sin_rows,
            upper_half * cos_rows + lower_half * sin_rows,
        ],
        axis=-1,
    )


def rotate_back(grad_in, cos_part, sin_part):
    half_width = grad_in.shape[-1] // 2
    lower_half = grad_in[..., :half_width]
    upper_half = grad_in[..., half_width:]
    cos_rows = cos_part[:, None, :]
    sin_rows = sin_part[:, None, :]
    return jnp.concatenate(
        [
            lower_half * cos_rows + upper_half * sin_rows,
            upper_half * cos_rows - lower_half * sin_rows,
        ],
        axis=-1,
    )


def silu_parts(gate_in):
    gate_sig = jax.nn.sigmoid(gate_in)
    return (gate_in * gate_sig, gate_sig * (1.0 + gate_in * (1.0 - gate_sig)))


def reduce_feed(factors):
    (
        rows_two,
        slot_placed_rows,
        egate_grad,
        expert_up_gradient,
        expert_grad_out,
        expert_act,
        sgate_grad,
        sup_grad,
        shared_grad_out,
        shared_act,
        grad_router,
    ) = factors
    grad_sdown = jnp.dot(shared_act.T, shared_grad_out, preferred_element_type=jnp.float32)
    grad_sgate = jnp.dot(rows_two.T, sgate_grad, preferred_element_type=jnp.float32)
    grad_sup = jnp.dot(rows_two.T, sup_grad, preferred_element_type=jnp.float32)
    grad_edown = jnp.einsum(
        "ecf,ecd->efd", expert_act, expert_grad_out, preferred_element_type=jnp.float32
    )
    grad_egate = jnp.einsum(
        "woi,woy->wiy", slot_placed_rows, egate_grad, preferred_element_type=jnp.float32
    )
    gradient_expert_up = jnp.einsum(
        "woi,woy->wiy", slot_placed_rows, expert_up_gradient, preferred_element_type=jnp.float32
    )
    return (
        lax.psum_scatter(
            grad_router.astype(jnp.bfloat16), "dp", scatter_dimension=0, tiled=True
        ).astype(jnp.float32),
        lax.psum_scatter(
            grad_sgate.astype(jnp.bfloat16), "dp", scatter_dimension=0, tiled=True
        ).astype(jnp.float32),
        lax.psum_scatter(
            grad_sup.astype(jnp.bfloat16), "dp", scatter_dimension=0, tiled=True
        ).astype(jnp.float32),
        lax.psum_scatter(
            grad_sdown.astype(jnp.bfloat16), "dp", scatter_dimension=1, tiled=True
        ).astype(jnp.float32),
        lax.psum_scatter(
            grad_egate.astype(jnp.bfloat16), "dp", scatter_dimension=1, tiled=True
        ).astype(jnp.float32),
        lax.psum_scatter(
            gradient_expert_up.astype(jnp.bfloat16), "dp", scatter_dimension=1, tiled=True
        ).astype(jnp.float32),
        lax.psum_scatter(
            grad_edown.astype(jnp.bfloat16), "dp", scatter_dimension=2, tiled=True
        ).astype(jnp.float32),
    )


def local(
    tokens,
    picture_ids,
    routes,
    slot_order,
    norm_gains,
    w_query,
    w_key,
    w_value,
    w_out,
    qkv_bias,
    router,
    shared_gate,
    shared_up,
    shared_down,
    expert_gate,
    expert_up,
    expert_down,
    out_grad,
):
    seq_len = picture_ids.shape[0]
    local_rows = tokens.shape[0]
    experts = expert_gate.shape[0]
    top_count = routes.shape[1]
    capacity = 5 * seq_len * top_count // (4 * experts)
    gain_rows = lax.all_gather(norm_gains, ("dp", "tensor"), axis=1, tiled=True).astype(jnp.float32)
    full_query, full_key, full_value, full_out, full_bias = (
        lax.all_gather(w_query, "dp", axis=0, tiled=True),
        lax.all_gather(w_key, "dp", axis=0, tiled=True),
        lax.all_gather(w_value, "dp", axis=0, tiled=True),
        lax.all_gather(w_out, "dp", axis=1, tiled=True),
        lax.all_gather(qkv_bias, "dp", axis=2, tiled=True),
    )
    heads_local = full_bias.shape[1]
    head_width = full_bias.shape[2]
    inputs = tokens.astype(jnp.float32)
    first_scale = lax.rsqrt(jnp.mean(inputs * inputs, axis=-1, keepdims=True) + EPS)
    first_unit = inputs * first_scale
    first_norm = (first_unit * gain_rows[0]).astype(jnp.bfloat16)
    rows_one = lax.all_gather(first_norm, "tensor", axis=0, tiled=True)
    bias_flat = full_bias.astype(jnp.float32).reshape(3, heads_local * head_width)
    query_pre = jnp.dot(rows_one, full_query, preferred_element_type=jnp.float32) + bias_flat[0]
    key_pre = jnp.dot(rows_one, full_key, preferred_element_type=jnp.float32) + bias_flat[1]
    value_pre = jnp.dot(rows_one, full_value, preferred_element_type=jnp.float32) + bias_flat[2]
    cos_part, sin_part = rope_tables(seq_len, head_width)
    queries = rotate(
        query_pre.reshape(seq_len, heads_local, head_width), cos_part, sin_part
    ).astype(jnp.bfloat16)
    keys_in = rotate(key_pre.reshape(seq_len, heads_local, head_width), cos_part, sin_part).astype(
        jnp.bfloat16
    )
    values_in = value_pre.astype(jnp.bfloat16).reshape(seq_len, heads_local, head_width)
    positions = jnp.arange(seq_len, dtype=jnp.int32)
    block_rows = min(seq_len, BLOCK_ROWS)
    blocks = seq_len // block_rows
    score_scale = head_width ** (-0.5)

    def scores_of(block_start):
        raw_scores = (
            jnp.einsum("qhd,khd->hqk", queries, keys_in, preferred_element_type=jnp.float32)
            * score_scale
        )
        row_ids = block_start + jnp.arange(block_rows, dtype=jnp.int32)
        allowed = jnp.logical_or(
            positions[None, :] <= row_ids[:, None], picture_ids[:, None] * picture_ids[None, :] > 0
        )
        return (jnp.where(allowed[None], raw_scores, -1e30), queries)

    def forward_block(block_index):
        masked, query_block = scores_of(block_index * block_rows)
        row_max = jnp.max(masked, axis=-1, keepdims=True)
        weights = jnp.exp(masked - row_max)
        row_total = jnp.sum(weights, axis=-1, keepdims=True)
        softmax_probs = weights / row_total
        mixed = jnp.einsum(
            "hqk,khd->qhd",
            softmax_probs.astype(jnp.bfloat16),
            values_in,
            preferred_element_type=jnp.float32,
        )
        return (mixed.astype(jnp.bfloat16), row_max[..., 0] + jnp.log(row_total[..., 0]))

    head_mix, log_totals = lax.map(forward_block, jnp.arange(blocks))
    heads_out = head_mix.reshape(seq_len, heads_local * head_width)
    attn_part = jnp.dot(heads_out, full_out, preferred_element_type=jnp.float32)
    attention = lax.psum_scatter(
        attn_part.astype(jnp.bfloat16), "tensor", scatter_dimension=0, tiled=True
    ).astype(jnp.float32)
    hidden = inputs + attention
    second_scale = lax.rsqrt(jnp.mean(hidden * hidden, axis=-1, keepdims=True) + EPS)
    second_unit = hidden * second_scale
    second_norm = (second_unit * gain_rows[1]).astype(jnp.bfloat16)
    rows_two = lax.all_gather(second_norm, "tensor", axis=0, tiled=True)
    (
        complete_router_weight,
        complete_shared_gate,
        complete_shared_up,
        complete_shared_down,
        complete_expert_gate,
        complete_expert_up,
        complete_expert_down,
    ) = (
        lax.all_gather(router, "dp", axis=0, tiled=True),
        lax.all_gather(shared_gate, "dp", axis=0, tiled=True),
        lax.all_gather(shared_up, "dp", axis=0, tiled=True),
        lax.all_gather(shared_down, "dp", axis=1, tiled=True),
        lax.all_gather(expert_gate, "dp", axis=1, tiled=True),
        lax.all_gather(expert_up, "dp", axis=1, tiled=True),
        lax.all_gather(expert_down, "dp", axis=2, tiled=True),
    )
    logits = jnp.dot(rows_two, complete_router_weight, preferred_element_type=jnp.float32)
    expert_probs = jax.nn.softmax(logits[:, :experts], axis=-1)
    shared_weight = jax.nn.sigmoid(logits[:, experts])
    gate_probs = jnp.take_along_axis(expert_probs, routes, axis=1)
    matches = routes[None] == jnp.arange(experts, dtype=jnp.int32)[:, None, None]
    present = jnp.any(matches, axis=-1)
    slot_table = jnp.sum(jnp.where(matches, slot_order[None], 0), axis=-1)
    gate_table = jnp.sum(jnp.where(matches, gate_probs[None], 0.0), axis=-1)
    onehot_mask = jnp.logical_and(
        jnp.arange(capacity, dtype=jnp.int32)[None, :, None] == slot_table[:, None, :],
        present[:, None, :],
    )
    onehot = onehot_mask.astype(jnp.bfloat16)
    slot_placed_rows = jnp.einsum(
        "ect,td->ecd", onehot, rows_two, preferred_element_type=jnp.float32
    ).astype(jnp.bfloat16)
    gate_in = jnp.einsum(
        "tuk,tkb->tub", slot_placed_rows, complete_expert_gate, preferred_element_type=jnp.float32
    )
    up_projection_input = jnp.einsum(
        "tuk,tkb->tub", slot_placed_rows, complete_expert_up, preferred_element_type=jnp.float32
    )
    gate_activation, gate_slope = silu_parts(gate_in)
    expert_act = (gate_activation * up_projection_input).astype(jnp.bfloat16)
    expert_out = jnp.einsum(
        "ecf,efd->ecd", expert_act, complete_expert_down, preferred_element_type=jnp.float32
    )
    slot_index = routes * capacity + slot_order
    picked = jnp.take(expert_out.reshape(experts * capacity, -1), slot_index, axis=0)
    expert_mix = jnp.sum(gate_probs[:, :, None] * picked, axis=1)
    sgate_in = jnp.dot(rows_two, complete_shared_gate, preferred_element_type=jnp.float32)
    sup_in = jnp.dot(rows_two, complete_shared_up, preferred_element_type=jnp.float32)
    sgate_silu, sgate_slope = silu_parts(sgate_in)
    shared_act = (sgate_silu * sup_in).astype(jnp.bfloat16)
    shared_out = jnp.dot(shared_act, complete_shared_down, preferred_element_type=jnp.float32)
    mlp_part = expert_mix + shared_weight[:, None] * shared_out
    feed_out = lax.psum_scatter(
        mlp_part.astype(jnp.bfloat16), "tensor", scatter_dimension=0, tiled=True
    ).astype(jnp.float32)
    output = (hidden + feed_out).astype(jnp.bfloat16)
    grad_rows = lax.all_gather(out_grad, "tensor", axis=0, tiled=True)
    grad_float = grad_rows.astype(jnp.float32)
    shared_grad_out = (shared_weight[:, None] * grad_float).astype(jnp.bfloat16)
    shared_dot = jnp.sum(grad_float * shared_out, axis=-1)
    shared_act_grad = jnp.dot(
        shared_grad_out, complete_shared_down.T, preferred_element_type=jnp.float32
    )
    sgate_grad = (shared_act_grad * sup_in * sgate_slope).astype(jnp.bfloat16)
    sup_grad = (shared_act_grad * sgate_silu).astype(jnp.bfloat16)
    second_part = jnp.dot(
        sgate_grad, complete_shared_gate.T, preferred_element_type=jnp.float32
    ) + jnp.dot(sup_grad, complete_shared_up.T, preferred_element_type=jnp.float32)
    routed_grad = jnp.einsum("ect,td->ecd", onehot, grad_rows, preferred_element_type=jnp.float32)
    gate_slot = jnp.sum(jnp.where(onehot_mask, gate_table[:, None, :], 0.0), axis=-1)
    expert_grad_out = (gate_slot[:, :, None] * routed_grad).astype(jnp.bfloat16)
    gate_dot = jnp.sum(picked * grad_float[:, None, :], axis=-1)
    activation_gradient = jnp.einsum(
        "ecd,efd->ecf", expert_grad_out, complete_expert_down, preferred_element_type=jnp.float32
    )
    egate_grad = (activation_gradient * up_projection_input * gate_slope).astype(jnp.bfloat16)
    expert_up_gradient = (activation_gradient * gate_activation).astype(jnp.bfloat16)
    slotted_grad = jnp.einsum(
        "xqs,xhs->xqh", egate_grad, complete_expert_gate, preferred_element_type=jnp.float32
    ) + jnp.einsum(
        "xqs,xhs->xqh", expert_up_gradient, complete_expert_up, preferred_element_type=jnp.float32
    )
    second_part = second_part + jnp.sum(
        jnp.take(slotted_grad.reshape(experts * capacity, -1), slot_index, axis=0), axis=1
    )
    gate_terms = jnp.concatenate([gate_dot, shared_dot[:, None]], axis=1)
    second_grad, gate_sums = (
        lax.psum_scatter(
            second_part.astype(jnp.bfloat16), "tensor", scatter_dimension=0, tiled=True
        ).astype(jnp.float32),
        lax.psum_scatter(
            gate_terms.astype(jnp.bfloat16), "tensor", scatter_dimension=0, tiled=True
        ).astype(jnp.float32),
    )
    row_start = lax.axis_index("tensor") * local_rows
    probs_mine = lax.dynamic_slice_in_dim(expert_probs, row_start, local_rows, 0)
    routes_mine = lax.dynamic_slice_in_dim(routes, row_start, local_rows, 0)
    weight_mine = lax.dynamic_slice_in_dim(shared_weight, row_start, local_rows, 0)
    route_grad = jnp.sum(
        jnp.where(
            routes_mine[:, :, None] == jnp.arange(experts, dtype=jnp.int32)[None, None, :],
            gate_sums[:, :top_count, None],
            0.0,
        ),
        axis=1,
    )
    expert_logit_grad = probs_mine * (
        route_grad - jnp.sum(probs_mine * route_grad, axis=-1, keepdims=True)
    )
    weight_logit_grad = gate_sums[:, top_count] * weight_mine * (1.0 - weight_mine)
    logits_grad = jnp.concatenate([expert_logit_grad, weight_logit_grad[:, None]], axis=1).astype(
        jnp.bfloat16
    )
    second_grad = second_grad + jnp.dot(
        logits_grad, complete_router_weight.T, preferred_element_type=jnp.float32
    )
    gain_two_grad = jnp.sum(second_grad * second_unit, axis=0)
    unit_two = second_grad * gain_rows[1]
    hidden_grad = out_grad.astype(jnp.float32) + second_scale * (
        unit_two - second_unit * jnp.mean(unit_two * second_unit, axis=-1, keepdims=True)
    )
    attention_grad = hidden_grad.astype(jnp.bfloat16)
    attn_grad_rows, logits_rows = (
        lax.all_gather(attention_grad, "tensor", axis=0, tiled=True),
        lax.all_gather(logits_grad, "tensor", axis=0, tiled=True),
    )
    grad_router = jnp.dot(rows_two.T, logits_rows, preferred_element_type=jnp.float32)
    factors = (
        rows_two,
        slot_placed_rows,
        egate_grad,
        expert_up_gradient,
        expert_grad_out,
        expert_act,
        sgate_grad,
        sup_grad,
        shared_grad_out,
        shared_act,
        grad_router,
    )
    grad_wout = jnp.dot(heads_out.T, attn_grad_rows, preferred_element_type=jnp.float32)
    mix_grad = (
        jnp.dot(attn_grad_rows, full_out.T, preferred_element_type=jnp.float32)
        .astype(jnp.bfloat16)
        .reshape(seq_len, heads_local, head_width)
    )

    def backward_block(carry, block_index):
        key_sums, value_sums = carry
        block_start = block_index * block_rows
        masked, query_block = scores_of(block_start)
        softmax_probs = jnp.exp(masked - log_totals[block_index][:, :, None])
        prob_grad = jnp.einsum(
            "qhd,khd->hqk", mix_grad, values_in, preferred_element_type=jnp.float32
        )
        row_delta = jnp.sum(softmax_probs * prob_grad, axis=-1, keepdims=True)
        score_grad = (softmax_probs * (prob_grad - row_delta)).astype(jnp.bfloat16)
        query_block_grad = (
            jnp.einsum("hqk,khd->qhd", score_grad, keys_in, preferred_element_type=jnp.float32)
            * score_scale
        )
        key_sums = (
            key_sums
            + jnp.einsum(
                "hqk,qhd->khd", score_grad, query_block, preferred_element_type=jnp.float32
            )
            * score_scale
        )
        value_sums = value_sums + jnp.einsum(
            "hqk,qhd->khd",
            softmax_probs.astype(jnp.bfloat16),
            mix_grad,
            preferred_element_type=jnp.float32,
        )
        return ((key_sums, value_sums), query_block_grad)

    empty_keys = jnp.zeros((seq_len, heads_local, head_width), jnp.float32)
    (key_rot_grad, value_out_grad), query_rot_grad = lax.scan(
        backward_block, (empty_keys, empty_keys), jnp.arange(blocks)
    )
    query_rot_grad = query_rot_grad.reshape(seq_len, heads_local, head_width)
    query_pre_grad = (
        rotate_back(query_rot_grad, cos_part, sin_part).reshape(seq_len, -1).astype(jnp.bfloat16)
    )
    key_pre_grad = (
        rotate_back(key_rot_grad, cos_part, sin_part).reshape(seq_len, -1).astype(jnp.bfloat16)
    )
    value_pre_grad = value_out_grad.reshape(seq_len, -1).astype(jnp.bfloat16)
    grad_wquery = jnp.dot(rows_one.T, query_pre_grad, preferred_element_type=jnp.float32)
    grad_wkey = jnp.dot(rows_one.T, key_pre_grad, preferred_element_type=jnp.float32)
    grad_wvalue = jnp.dot(rows_one.T, value_pre_grad, preferred_element_type=jnp.float32)
    grad_bias = jnp.stack(
        [
            jnp.sum(query_pre_grad.astype(jnp.float32), axis=0),
            jnp.sum(key_pre_grad.astype(jnp.float32), axis=0),
            jnp.sum(value_pre_grad.astype(jnp.float32), axis=0),
        ]
    ).reshape(3, heads_local, head_width)
    first_part = (
        jnp.dot(query_pre_grad, full_query.T, preferred_element_type=jnp.float32)
        + jnp.dot(key_pre_grad, full_key.T, preferred_element_type=jnp.float32)
        + jnp.dot(value_pre_grad, full_value.T, preferred_element_type=jnp.float32)
    )
    first_grad = lax.psum_scatter(
        first_part.astype(jnp.bfloat16), "tensor", scatter_dimension=0, tiled=True
    ).astype(jnp.float32)
    gain_one_grad = jnp.sum(first_grad * first_unit, axis=0)
    unit_one = first_grad * gain_rows[0]
    input_grad = hidden_grad + first_scale * (
        unit_one - first_unit * jnp.mean(unit_one * first_unit, axis=-1, keepdims=True)
    )
    feed_sums = reduce_feed(factors)
    attn_sums = (
        lax.psum_scatter(
            grad_wquery.astype(jnp.bfloat16), "dp", scatter_dimension=0, tiled=True
        ).astype(jnp.float32),
        lax.psum_scatter(
            grad_wkey.astype(jnp.bfloat16), "dp", scatter_dimension=0, tiled=True
        ).astype(jnp.float32),
        lax.psum_scatter(
            grad_wvalue.astype(jnp.bfloat16), "dp", scatter_dimension=0, tiled=True
        ).astype(jnp.float32),
        lax.psum_scatter(
            grad_wout.astype(jnp.bfloat16), "dp", scatter_dimension=1, tiled=True
        ).astype(jnp.float32),
        lax.psum_scatter(
            grad_bias.astype(jnp.bfloat16), "dp", scatter_dimension=2, tiled=True
        ).astype(jnp.float32),
    )
    router_sum = feed_sums[0]
    gain_sums = lax.psum_scatter(
        jnp.stack([gain_one_grad, gain_two_grad]), ("dp", "tensor"), scatter_dimension=1, tiled=True
    )
    return (
        output,
        input_grad.astype(jnp.bfloat16),
        gain_sums,
        attn_sums[0],
        attn_sums[1],
        attn_sums[2],
        attn_sums[3],
        attn_sums[4],
        router_sum,
        feed_sums[1],
        feed_sums[2],
        feed_sums[3],
        feed_sums[4],
        feed_sums[5],
        feed_sums[6],
    )


def solution(mesh):
    return jax.shard_map(
        local,
        mesh=mesh,
        in_specs=(
            P(("dp", "tensor"), None),
            P("dp"),
            P("dp", None),
            P("dp", None),
            P(None, ("dp", "tensor")),
            P("dp", "tensor"),
            P("dp", "tensor"),
            P("dp", "tensor"),
            P("tensor", "dp"),
            P(None, "tensor", "dp"),
            P("dp", None),
            P("dp", "tensor"),
            P("dp", "tensor"),
            P("tensor", "dp"),
            P(None, "dp", "tensor"),
            P(None, "dp", "tensor"),
            P(None, "tensor", "dp"),
            P(("dp", "tensor"), None),
        ),
        out_specs=(
            P(("dp", "tensor"), None),
            P(("dp", "tensor"), None),
            P(None, ("dp", "tensor")),
            P("dp", "tensor"),
            P("dp", "tensor"),
            P("dp", "tensor"),
            P("tensor", "dp"),
            P(None, "tensor", "dp"),
            P("dp", None),
            P("dp", "tensor"),
            P("dp", "tensor"),
            P("tensor", "dp"),
            P(None, "dp", "tensor"),
            P(None, "dp", "tensor"),
            P(None, "tensor", "dp"),
        ),
        check_vma=False,
    )
```

profile of v0, /device:TPU:0, one launch (start us, length us, event | category | flops | bytes accessed | tf_op | source)
XLA Modules:
  0.0 2001.6 jit_solution(6844482497256799862)
XLA Ops:
  7.2 69.5 %all-gather = bf16[32,64,2]{1,2,0:T(2,128)(2,1)S(1)} all-gather(bf16[1,64,2]{1,2,0:T(2,128)(2,1)} %bitcast.156), channel_id=1, replica_groups=mesh['dp'=8,'tensor'=4] {'dp','tensor'}, dimensions={0}, use_global_device_ids=true | all-gather | bytes 8448 | tf_op jit(solution)/shard_map/all_gather | solution.py:129
  94.9 27.6 %all-gather.16.cloned.1.call-done = bf16[512,2048]{1,0:T(8,128)(2,1)} async-done(((bf16[128,2048]{1,0:T(8,128)(2,1)}), bf16[512,2048]{1,0:T(8,128)(2,1)}) %all-gather.16.cloned.1.call-update) | async-done | bytes 2097168 | tf_op jit(solution)/shard_map/all_gather | solution.py:143
  122.5 28.6 %all-gather.20.cloned.1.call-done = bf16[2048,512]{1,0:T(8,128)(2,1)} async-done(((bf16[256,512]{1,0:T(8,128)(2,1)}), bf16[2048,512]{1,0:T(8,128)(2,1)}) %all-gather.20.cloned.1.call-update) | async-done | bytes 2097168 | tf_op jit(solution)/shard_map/all_gather | solution.py:131
  155.4 25.5 %all-gather.22.cloned.1.call-done = bf16[2048,512]{1,0:T(8,128)(2,1)} async-done(((bf16[256,512]{1,0:T(8,128)(2,1)}), bf16[2048,512]{1,0:T(8,128)(2,1)}) %all-gather.22.cloned.1.call-update) | async-done | bytes 2097168 | tf_op jit(solution)/shard_map/all_gather | solution.py:132
  195.9 14.7 all-gather.18.cloned.1.call-done
  215.3 25.2 %all-gather.24.cloned.1.call-done = bf16[512,2048]{1,0:T(8,128)(2,1)} async-done(((bf16[512,256]{1,0:T(8,128)(2,1)}), bf16[512,2048]{1,0:T(8,128)(2,1)}) %all-gather.24.cloned.1.call-update) | async-done | bytes 2097168 | tf_op jit(solution)/shard_map/all_gather | solution.py:134
  246.0 42.7 %reduce-scatter.25.cloned.1.call-done = bf16[128,2048]{1,0:T(8,128)(2,1)} async-done(((bf16[512,2048]{1,0:T(8,128)(2,1)}), bf16[128,2048]{1,0:T(8,128)(2,1)}) %reduce-scatter.25.cloned.1.call-update) | async-done | bytes 524304 | tf_op jit(solution)/shard_map/reduce_scatter | solution.py:189
  307.4 28.4 %all-gather.40.cloned.1.call-done = bf16[512,2048]{1,0:T(8,128)(2,1)} async-done(((bf16[128,2048]{1,0:T(8,128)(2,1)}), bf16[512,2048]{1,0:T(8,128)(2,1)}) %all-gather.40.cloned.1.call-update) | async-done | bytes 2097168 | tf_op jit(solution)/shard_map/all_gather | solution.py:254
  339.8 42.8 %all-gather.26.cloned.1.call-done = bf16[512,2048]{1,0:T(8,128)(2,1)} async-done(((bf16[128,2048]{1,0:T(8,128)(2,1)}), bf16[512,2048]{1,0:T(8,128)(2,1)}) %all-gather.26.cloned.1.call-update) | async-done | bytes 2097168 | tf_op jit(solution)/shard_map/all_gather | solution.py:196
  385.0 12.5 gather_fusion
  400.1 26.7 %all-gather.34.cloned.1.call-done = bf16[2048,1408]{1,0:T(8,128)(2,1)} async-done(((bf16[256,1408]{1,0:T(8,128)(2,1)}), bf16[2048,1408]{1,0:T(8,128)(2,1)}) %all-gather.34.cloned.1.call-update) | async-done | bytes 5767184 | tf_op jit(solution)/shard_map/all_gather | solution.py:207
  434.4 37.6 %all-gather.36.cloned.1.call-done = bf16[2048,1408]{1,0:T(8,128)(2,1)} async-done(((bf16[256,1408]{1,0:T(8,128)(2,1)}), bf16[2048,1408]{1,0:T(8,128)(2,1)}) %all-gather.36.cloned.1.call-update) | async-done | bytes 5767184 | tf_op jit(solution)/shard_map/all_gather | solution.py:208
  479.6 38.8 %all-gather.38.cloned.1.call-done = bf16[1408,2048]{1,0:T(8,128)(2,1)} async-done(((bf16[1408,256]{1,0:T(8,128)(2,1)}), bf16[1408,2048]{1,0:T(8,128)(2,1)}) %all-gather.38.cloned.1.call-update) | async-done | bytes 5767184 | tf_op jit(solution)/shard_map/all_gather | solution.py:209
  518.4 10.9 multiply_convert_fusion.6
  554.9 35.3 %all-gather.28.cloned.1.call-done = bf16[8,2048,352]{1,2,0:T(8,128)(2,1)} async-done(((bf16[8,256,352]{1,2,0:T(8,128)(2,1)}), bf16[8,2048,352]{1,2,0:T(8,128)(2,1)}) %all-gather.28.cloned.1.call-update) | async-done | bytes 11534352 | tf_op jit(solution)/shard_map/all_gather | solution.py:210
  590.2 15.0 fusion.60
  605.2 57.0 %all-gather.30.cloned.1.call-done = bf16[8,2048,352]{1,2,0:T(8,128)(2,1)} async-done(((bf16[8,256,352]{1,2,0:T(8,128)(2,1)}), bf16[8,2048,352]{1,2,0:T(8,128)(2,1)}) %all-gather.30.cloned.1.call-update) | async-done | bytes 11534352 | tf_op jit(solution)/shard_map/all_gather | solution.py:211
  662.2 14.9 fusion.61
  677.1 56.9 %all-gather.32.cloned.1.call-done = bf16[8,352,2048]{2,1,0:T(8,128)(2,1)} async-done(((bf16[8,352,256]{2,1,0:T(8,128)(2,1)}), bf16[8,352,2048]{2,1,0:T(8,128)(2,1)}) %all-gather.32.cloned.1.call-update) | async-done | bytes 11534352 | tf_op jit(solution)/shard_map/all_gather | solution.py:212
  734.0 16.7 multiply_convert_fusion.3
  750.7 15.2 fusion.66
  765.9 17.4 convolution_add_fusion
  783.3 23.4 %gather_fusion.2 = f32[2048,2048]{1,0:T(8,128)} fusion(f32[2560,2048]{1,0:T(8,128)} %bitcast.119, s32[2048]{0:T(1024)S(1)} %copy-done.5), kind=kCustom, calls=%fused_computation.1.clone | custom fusion | bytes 33562624 | tf_op jit(solution)/shard_map/jit(_take)/gather | solution.py:281
  806.7 19.1 reshape.295
  825.9 14.7 fusion.62
  840.6 23.4 %gather_fusion.1 = f32[2048,2048]{1,0:T(8,128)} fusion(f32[2560,2048]{1,0:T(8,128)} %bitcast.120, s32[2048]{0:T(1024)S(1)} %copy-done.5), kind=kCustom, calls=%fused_computation.clone | custom fusion | bytes 33562624 | tf_op jit(solution)/shard_map/jit(_take)/gather | solution.py:242
  864.0 19.0 reshape.291
  883.0 35.7 %multiply_reduce_fusion = (bf16[512,4]{1,0:T(8,128)(2,1)S(1)}, f32[512,2048]{1,0:T(8,128)S(1)}, f32[512,2048]{1,0:T(8,128)}) fusion(f32[512,4,2048]{2,1,0:T(4,128)} %reshape.291, f32[512,2048]{1,0:T(8,128)} %convert_element_type.240, pred[512,4]{1,0:T(8,128)(4,1)S(1)} %copy-done.42, f32[512,4]{1,0:T(8,128)S(1)} %copy-done.35, f32[512,4,2048]{2,1,0:T(4,128)} %reshape.295), kind=kLoop, calls=%fused_computation.5 | loop fusion | flops 27260928 | bytes 46151680 | tf_op jit(solution)/shard_map/reduce_sum | solution.py:269
  927.6 10.3 add_convert_fusion.1
  947.8 43.8 %reduce-scatter.29.cloned.1.call-done = bf16[128,2048]{1,0:T(8,128)(2,1)} async-done(((bf16[512,2048]{1,0:T(8,128)(2,1)}), bf16[128,2048]{1,0:T(8,128)(2,1)}) %reduce-scatter.29.cloned.1.call-update) | async-done | bytes 524304 | tf_op jit(solution)/shard_map/reduce_scatter | solution.py:285
  995.4 45.2 %all-gather.42.cloned.1.call-done = bf16[512,2048]{1,0:T(8,128)(2,1)} async-done(((bf16[128,2048]{1,0:T(8,128)(2,1)}), bf16[512,2048]{1,0:T(8,128)(2,1)}) %all-gather.42.cloned.1.call-update) | async-done | bytes 2097168 | tf_op jit(solution)/shard_map/all_gather | solution.py:321
  1083.7 13.3 all_gather.71
  1124.7 11.3 convolution_convert_fusion.3
  1137.6 11.4 convolution_convert_fusion.5
  1150.5 11.3 convolution_convert_fusion.4
  1166.7 60.4 %reduce-scatter.43.cloned.1.call-done = bf16[256,1408]{1,0:T(8,128)(2,1)} async-done(((bf16[2048,1408]{1,0:T(8,128)(2,1)}), bf16[256,1408]{1,0:T(8,128)(2,1)}) %reduce-scatter.43.cloned.1.call-update) | async-done | bytes 720912 | tf_op jit(solution)/shard_map/reduce_scatter | solution.py:83
  1229.4 60.2 %reduce-scatter.45.cloned.1.call-done = bf16[256,1408]{1,0:T(8,128)(2,1)} async-done(((bf16[2048,1408]{1,0:T(8,128)(2,1)}), bf16[256,1408]{1,0:T(8,128)(2,1)}) %reduce-scatter.45.cloned.1.call-update) | async-done | bytes 720912 | tf_op jit(solution)/shard_map/reduce_scatter | solution.py:86
  1292.0 33.0 %reduce-scatter.41.cloned.1.call-done = bf16[256,9]{0,1:T(8,128)(2,1)} async-done(((bf16[2048,9]{0,1:T(8,128)(2,1)}), bf16[256,9]{0,1:T(8,128)(2,1)}) %reduce-scatter.41.cloned.1.call-update) | async-done | bytes 4624 | tf_op jit(solution)/shard_map/reduce_scatter | solution.py:80
  1326.3 33.5 %reduce-scatter.59.cloned.1.call-done = bf16[16,12]{1,0:T(8,128)(2,1)} async-done(((bf16[128,12]{1,0:T(8,128)(2,1)}), bf16[16,12]{1,0:T(8,128)(2,1)}) %reduce-scatter.59.cloned.1.call-update) | async-done | bytes 400
  1361.3 43.3 %reduce-scatter.37.cloned.1.call-done = bf16[256,512]{1,0:T(8,128)(2,1)} async-done(((bf16[2048,512]{1,0:T(8,128)(2,1)}), bf16[256,512]{1,0:T(8,128)(2,1)}) %reduce-scatter.37.cloned.1.call-update) | async-done | bytes 262160 | tf_op jit(solution)/shard_map/reduce_scatter | solution.py:417
  1406.4 42.7 %reduce-scatter.39.cloned.1.call-done = bf16[512,256]{1,0:T(8,128)(2,1)} async-done(((bf16[512,2048]{1,0:T(8,128)(2,1)}), bf16[512,256]{1,0:T(8,128)(2,1)}) %reduce-scatter.39.cloned.1.call-update) | async-done | bytes 262160 | tf_op jit(solution)/shard_map/reduce_scatter | solution.py:420
  1450.9 43.5 %reduce-scatter.33.cloned.1.call-done = bf16[256,512]{1,0:T(8,128)(2,1)} async-done(((bf16[2048,512]{1,0:T(8,128)(2,1)}), bf16[256,512]{1,0:T(8,128)(2,1)}) %reduce-scatter.33.cloned.1.call-update) | async-done | bytes 262160 | tf_op jit(solution)/shard_map/reduce_scatter | solution.py:411
  1496.2 42.6 %reduce-scatter.35.cloned.1.call-done = bf16[256,512]{1,0:T(8,128)(2,1)} async-done(((bf16[2048,512]{1,0:T(8,128)(2,1)}), bf16[256,512]{1,0:T(8,128)(2,1)}) %reduce-scatter.35.cloned.1.call-update) | async-done | bytes 262160 | tf_op jit(solution)/shard_map/reduce_scatter | solution.py:414
  1540.6 45.1 %reduce-scatter.27.cloned.1.call-done = bf16[128,2048]{1,0:T(8,128)(2,1)} async-done(((bf16[512,2048]{1,0:T(8,128)(2,1)}), bf16[128,2048]{1,0:T(8,128)(2,1)}) %reduce-scatter.27.cloned.1.call-update) | async-done | bytes 524304 | tf_op jit(solution)/shard_map/reduce_scatter | solution.py:250
  1588.5 134.6 %reduce-scatter.57.cloned.1.call-done = f32[64,2]{1,0:T(8,128)} async-done(((f32[2048,2]{1,0:T(8,128)}), f32[64,2]{1,0:T(8,128)}) %reduce-scatter.57.cloned.1.call-update) | async-done | bytes 528
  1724.5 85.8 %reduce-scatter.53.cloned.1.call-done = bf16[8,352,256]{2,1,0:T(8,128)(2,1)} async-done(((bf16[8,352,2048]{2,1,0:T(8,128)(2,1)}), bf16[8,352,256]{2,1,0:T(8,128)(2,1)}) %reduce-scatter.53.cloned.1.call-update) | async-done | bytes 1441808 | tf_op jit(solution)/shard_map/reduce_scatter | solution.py:98
  1813.5 87.5 %reduce-scatter.49.cloned.1.call-done = bf16[8,256,352]{1,2,0:T(8,128)(2,1)} async-done(((bf16[8,2048,352]{1,2,0:T(8,128)(2,1)}), bf16[8,256,352]{1,2,0:T(8,128)(2,1)}) %reduce-scatter.49.cloned.1.call-update) | async-done | bytes 1441808 | tf_op jit(solution)/shard_map/reduce_scatter | solution.py:92
  1904.2 87.5 %reduce-scatter.51.cloned.1.call-done = bf16[8,256,352]{1,2,0:T(8,128)(2,1)} async-done(((bf16[8,2048,352]{1,2,0:T(8,128)(2,1)}), bf16[8,256,352]{1,2,0:T(8,128)(2,1)}) %reduce-scatter.51.cloned.1.call-update) | async-done | bytes 1441808 | tf_op jit(solution)/shard_map/reduce_scatter | solution.py:95
  (329 shorter events, 244.7 us)
Async XLA Ops:
  7.2 86.7 %copy-start.54 = (s32[512]{0:T(512)S(1)}, s32[512]{0:T(512)}, u32[]{:S(2)}) copy-start(s32[512]{0:T(512)} %param.21) | copy-start | bytes 6148
  7.2 115.3 %all-gather.16.cloned.1.call-start = ((), (), s32[]{:S(2)}) async-start(), calls=%async_computation.18 | async-start | bytes 2621440 | tf_op jit(solution)/shard_map/all_gather | solution.py:143
  76.8 213.3 %copy-start.43 = (f32[1,2048]{1,0:T(1,128)}, f32[1,2048]{1,0:T(1,128)S(1)}, u32[]{:S(2)}) copy-start(f32[1,2048]{1,0:T(1,128)S(1)} %get-tuple-element.115) | copy-start | bytes 24580
  78.1 76.5 %copy-start.59 = (f32[128]{0:T(128)}, f32[128]{0:T(128)S(1)}, u32[]{:S(2)}) copy-start(f32[128]{0:T(128)S(1)} %add_rsqrt_fusion.1) | copy-start | bytes 1540
  80.2 70.9 %all-gather.20.cloned.1.call-start = ((), (), s32[]{:S(2)}) async-start(), calls=%async_computation.20 | async-start | bytes 2359296 | tf_op jit(solution)/shard_map/all_gather | solution.py:131
  80.9 100.0 %all-gather.22.cloned.1.call-start = ((), (), s32[]{:S(2)}) async-start(), calls=%async_computation.21 | async-start | bytes 2359296 | tf_op jit(solution)/shard_map/all_gather | solution.py:132
  81.6 128.9 %all-gather.18.cloned.1.call-start = ((), (), s32[]{:S(2)}) async-start(), calls=%async_computation.19 | async-start | bytes 2359296 | tf_op jit(solution)/shard_map/all_gather | solution.py:133
  82.2 158.3 %all-gather.24.cloned.1.call-start = ((), (), s32[]{:S(2)}) async-start(), calls=%async_computation.22 | async-start | bytes 2359296 | tf_op jit(solution)/shard_map/all_gather | solution.py:134
  82.8 206.0 %reduce-scatter.25.cloned.1.call-start = ((), (), s32[]{:S(2)}) async-start(), calls=%async_computation.23 | async-start | bytes 2621440 | tf_op jit(solution)/shard_map/reduce_scatter | solution.py:189
  93.8 95.4 %copy-start.26 = (f32[512,64]{1,0:T(8,128)}, f32[512,64]{1,0:T(8,128)S(1)}, u32[]{:S(2)}) copy-start(f32[512,64]{1,0:T(8,128)S(1)} %get-tuple-element.117) | copy-start | bytes 393220
  244.8 91.0 %all-gather.40.cloned.1.call-start = ((), (), s32[]{:S(2)}) async-start(), calls=%async_computation.32 | async-start | bytes 2621440 | tf_op jit(solution)/shard_map/all_gather | solution.py:254
  245.5 137.1 %all-gather.26.cloned.1.call-start = ((), (), s32[]{:S(2)}) async-start(), calls=%async_computation.24 | async-start | bytes 2621440 | tf_op jit(solution)/shard_map/all_gather | solution.py:196
  292.2 134.6 %all-gather.34.cloned.1.call-start = ((), (), s32[]{:S(2)}) async-start(), calls=%async_computation.28 | async-start | bytes 6488064 | tf_op jit(solution)/shard_map/all_gather | solution.py:207
  292.9 179.1 %all-gather.36.cloned.1.call-start = ((), (), s32[]{:S(2)}) async-start(), calls=%async_computation.29 | async-start | bytes 6488064 | tf_op jit(solution)/shard_map/all_gather | solution.py:208
  293.5 224.9 %all-gather.38.cloned.1.call-start = ((), (), s32[]{:S(2)}) async-start(), calls=%async_computation.30 | async-start | bytes 6488064 | tf_op jit(solution)/shard_map/all_gather | solution.py:209
  294.3 296.0 %all-gather.28.cloned.1.call-start = ((), (), s32[]{:S(2)}) async-start(), calls=%async_computation.25 | async-start | bytes 12976128 | tf_op jit(solution)/shard_map/all_gather | solution.py:210
  294.8 367.4 %all-gather.30.cloned.1.call-start = ((), (), s32[]{:S(2)}) async-start(), calls=%async_computation.26 | async-start | bytes 12976128 | tf_op jit(solution)/shard_map/all_gather | solution.py:211
  295.6 438.4 %all-gather.32.cloned.1.call-start = ((), (), s32[]{:S(2)}) async-start(), calls=%async_computation.27 | async-start | bytes 12976128 | tf_op jit(solution)/shard_map/all_gather | solution.py:212
  296.2 650.7 %reduce-scatter.55.cloned.1.call-start = ((), (), s32[]{:S(2)}) async-start(), calls=%async_computation.47 | async-start | bytes 163840
  306.7 78.1 %copy-start.37 = (bf16[2048,9]{0,1:T(8,128)(2,1)}, bf16[2048,9]{0,1:T(8,128)(2,1)S(1)}, u32[]{:S(2)}) copy-start(bf16[2048,9]{0,1:T(8,128)(2,1)S(1)} %all_gather.62) | copy-start | bytes 110596
  398.8 119.6 %copy-start.61 = (f32[512,1]{0,1:T(1,128)}, f32[512,1]{0,1:T(1,128)S(1)}, u32[]{:S(2)}) copy-start(f32[512,1]{0,1:T(1,128)S(1)} %fusion.46) | copy-start | bytes 6148
  927.5 64.1 %reduce-scatter.29.cloned.1.call-start = ((), (), s32[]{:S(2)}) async-start(), calls=%async_computation.33 | async-start | bytes 2621440 | tf_op jit(solution)/shard_map/reduce_scatter | solution.py:285
  927.5 64.1 %copy-start.7 = (bf16[128,2048]{1,0:T(8,128)(2,1)S(1)}, bf16[128,2048]{1,0:T(8,128)(2,1)}, u32[]{:S(2)}) copy-start(bf16[128,2048]{1,0:T(8,128)(2,1)} %param.20) | copy-start | bytes 1572868
  927.6 64.0 %copy-start.10 = (bf16[128,2048]{1,0:T(8,128)(2,1)S(1)}, bf16[128,2048]{1,0:T(8,128)(2,1)}, u32[]{:S(2)}) copy-start(bf16[128,2048]{1,0:T(8,128)(2,1)} %reduce-scatter.25.cloned.1.call-done) | copy-start | bytes 1572868
  927.6 64.0 %copy-start.38 = (bf16[2048,9]{0,1:T(8,128)(2,1)S(1)}, bf16[2048,9]{0,1:T(8,128)(2,1)}, u32[]{:S(2)}) copy-start(bf16[2048,9]{0,1:T(8,128)(2,1)} %copy-done.37) | copy-start | bytes 110596
  938.0 102.6 %all-gather.42.cloned.1.call-start = ((), (), s32[]{:S(2)}) async-start(), calls=%async_computation.34 | async-start | bytes 2621440 | tf_op jit(solution)/shard_map/all_gather | solution.py:321
  995.2 124.7 %reduce-scatter.31.cloned.1.call-start = ((), (), s32[]{:S(2)}) async-start(), calls=%async_computation.35 | async-start | bytes 2621440 | tf_op jit(solution)/shard_map/reduce_scatter | solution.py:401
  1059.6 104.8 %reduce-scatter.47.cloned.1.call-start = ((), (), s32[]{:S(2)}) async-start(), calls=%async_computation.43 | async-start | bytes 6488064 | tf_op jit(solution)/shard_map/reduce_scatter | solution.py:89
  1067.6 159.5 %reduce-scatter.43.cloned.1.call-start = ((), (), s32[]{:S(2)}) async-start(), calls=%async_computation.41 | async-start | bytes 6488064 | tf_op jit(solution)/shard_map/reduce_scatter | solution.py:83
  1075.6 214.0 %reduce-scatter.45.cloned.1.call-start = ((), (), s32[]{:S(2)}) async-start(), calls=%async_computation.42 | async-start | bytes 6488064 | tf_op jit(solution)/shard_map/reduce_scatter | solution.py:86
  1083.6 241.3 %reduce-scatter.41.cloned.1.call-start = ((), (), s32[]{:S(2)}) async-start(), calls=%async_computation.40 | async-start | bytes 73728 | tf_op jit(solution)/shard_map/reduce_scatter | solution.py:80
  1099.6 260.2 %reduce-scatter.59.cloned.1.call-start = ((), (), s32[]{:S(2)}) async-start(), calls=%async_computation.49 | async-start | bytes 36864
  1100.6 304.0 %reduce-scatter.37.cloned.1.call-start = ((), (), s32[]{:S(2)}) async-start(), calls=%async_computation.38 | async-start | bytes 2359296 | tf_op jit(solution)/shard_map/reduce_scatter | solution.py:417
  1105.0 344.2 %reduce-scatter.39.cloned.1.call-start = ((), (), s32[]{:S(2)}) async-start(), calls=%async_computation.39 | async-start | bytes 2359296 | tf_op jit(solution)/shard_map/reduce_scatter | solution.py:420
  1109.8 384.7 %reduce-scatter.33.cloned.1.call-start = ((), (), s32[]{:S(2)}) async-start(), calls=%async_computation.36 | async-start | bytes 2359296 | tf_op jit(solution)/shard_map/reduce_scatter | solution.py:411
  1114.5 424.3 %reduce-scatter.35.cloned.1.call-start = ((), (), s32[]{:S(2)}) async-start(), calls=%async_computation.37 | async-start | bytes 2359296 | tf_op jit(solution)/shard_map/reduce_scatter | solution.py:414
  1119.1 466.6 %reduce-scatter.27.cloned.1.call-start = ((), (), s32[]{:S(2)}) async-start(), calls=%async_computation.31 | async-start | bytes 2621440 | tf_op jit(solution)/shard_map/reduce_scatter | solution.py:250
  1119.8 603.3 %reduce-scatter.57.cloned.1.call-start = ((), (), s32[]{:S(2)}) async-start(), calls=%async_computation.48 | async-start | bytes 1081344
  1124.6 685.7 %reduce-scatter.53.cloned.1.call-start = ((), (), s32[]{:S(2)}) async-start(), calls=%async_computation.46 | async-start | bytes 12976128 | tf_op jit(solution)/shard_map/reduce_scatter | solution.py:98
  1136.1 764.9 %reduce-scatter.49.cloned.1.call-start = ((), (), s32[]{:S(2)}) async-start(), calls=%async_computation.44 | async-start | bytes 12976128 | tf_op jit(solution)/shard_map/reduce_scatter | solution.py:92
  1149.0 842.6 %reduce-scatter.51.cloned.1.call-start = ((), (), s32[]{:S(2)}) async-start(), calls=%async_computation.45 | async-start | bytes 12976128 | tf_op jit(solution)/shard_map/reduce_scatter | solution.py:95
  1166.7 373.9 %copy-start.65 = (f32[128]{0:T(128)S(1)}, f32[128]{0:T(128)}, u32[]{:S(2)}) copy-start(f32[128]{0:T(128)} %get-tuple-element.78) | copy-start | bytes 1540
  1166.7 419.0 %copy-start.13 = (f32[128,2048]{1,0:T(8,128)S(1)}, f32[128,2048]{1,0:T(8,128)}, u32[]{:S(2)}) copy-start(f32[128,2048]{1,0:T(8,128)} %copy-done.12) | copy-start | bytes 3145732
  1166.7 419.0 %copy-start.32 = (bf16[128,2048]{1,0:T(8,128)(2,1)S(1)}, bf16[128,2048]{1,0:T(8,128)(2,1)}, u32[]{:S(2)}) copy-start(bf16[128,2048]{1,0:T(8,128)(2,1)} %reduce-scatter.31.cloned.1.call-done) | copy-start | bytes 1572868
  1166.7 419.0 %copy-start.45 = (f32[1,2048]{1,0:T(1,128)S(1)}, f32[1,2048]{1,0:T(1,128)}, u32[]{:S(2)}) copy-start(f32[1,2048]{1,0:T(1,128)} %copy-done.43) | copy-start | bytes 24580
  1166.7 419.0 %copy-start.57 = (f32[128]{0:T(128)S(1)}, f32[128]{0:T(128)}, u32[]{:S(2)}) copy-start(f32[128]{0:T(128)} %copy-done.55) | copy-start | bytes 1540
  1166.7 419.0 %copy-start.60 = (f32[128]{0:T(128)S(1)}, f32[128]{0:T(128)}, u32[]{:S(2)}) copy-start(f32[128]{0:T(128)} %copy-done.59) | copy-start | bytes 1540
  1166.7 419.0 %copy-start.64 = (f32[128]{0:T(128)S(1)}, f32[128]{0:T(128)}, u32[]{:S(2)}) copy-start(f32[128]{0:T(128)} %copy-done.63) | copy-start | bytes 1540
  (54 other events, 846.0 us)
Sparse Core Ops, SparseCore 0:
  80.3 42.1 all-gather.15
  124.4 26.6 all-gather.19
  152.9 27.8 all-gather.21
  182.6 27.8 all-gather.17
  212.3 28.1 all-gather.23
  244.9 43.8 reduce-scatter.24
  290.4 45.2 all-gather.39
  338.0 44.6 all-gather.25
  384.7 42.0 all-gather.33
  428.7 43.3 all-gather.35
  474.0 44.3 all-gather.37
  520.3 69.8 all-gather.27
  592.3 69.8 all-gather.29
  664.1 69.8 all-gather.31
  927.6 19.1 reduce-scatter.54
  949.6 41.9 reduce-scatter.28
  995.3 45.2 all-gather.41
  1059.7 42.7 reduce-scatter.30
  1106.0 58.3 reduce-scatter.46
  1168.0 59.0 reduce-scatter.42
  1230.6 59.0 reduce-scatter.44
  1293.5 31.4 reduce-scatter.40
  1328.5 31.2 reduce-scatter.58
  1363.3 41.2 reduce-scatter.36
  1407.9 41.2 reduce-scatter.38
  1453.2 41.2 reduce-scatter.32
  1497.6 41.1 reduce-scatter.34
  1541.8 43.8 reduce-scatter.26
  1588.5 134.5 reduce-scatter.56
  1726.9 83.3 reduce-scatter.52
  1814.2 86.7 reduce-scatter.48
  1904.9 86.7 reduce-scatter.50
where the time goes:
time: 2010 us; the launch traced here: 2000 us
  waiting for transfers between devices  1390 us (69%)
  matrix products  278 us (14%)
  local copies, waits for them, and re-layouts  122 us (6%)
  blocking collectives  100 us (5%)
  other arithmetic  88.6 us (4%)
    unnamed x35, waiting for transfers between devices  184 us
    reduce_scatter x1, waiting for transfers between devices, reduce_feed(): lax.psum_scatter(grad_egate.astype(jnp.bfloat16), 'dp', scatter_dimension...  87.5 us
    reduce_scatter x1, waiting for transfers between devices, reduce_feed(): lax.psum_scatter(gradient_expert_up.astype(jnp.bfloat16), 'dp', scatter_d...  87.5 us
    reduce_scatter x1, waiting for transfers between devices, reduce_feed(): lax.psum_scatter(grad_edown.astype(jnp.bfloat16), 'dp', scatter_dimension...  85.8 us
    all_gather x1, blocking collectives, local(): lax.all_gather(norm_gains, ('dp', 'tensor'), axis=1, tiled=True)  69.5 us
    reduce_scatter x1, waiting for transfers between devices, reduce_feed(): lax.psum_scatter(grad_sgate.astype(jnp.bfloat16), 'dp', scatter_dimension...  60.4 us
    reduce_scatter x1, waiting for transfers between devices, reduce_feed(): lax.psum_scatter(grad_sup.astype(jnp.bfloat16), 'dp', scatter_dimension=0...  60.2 us
    all_gather x1, waiting for transfers between devices, local(): lax.all_gather(expert_up, 'dp', axis=1, tiled=True)  57 us
  transfers between devices with their start and end apart: 32, of which 31 were waited for; matrix products, arithmetic and copies ran while one was open for 13% of the time, Pallas kernels for 0%

commit v1 on v0

v1 whole, which is shorter than its diff:
```python
import functools

import jax
import jax.numpy as jnp
from jax import lax
from jax.experimental import pallas as pl
from jax.experimental.pallas import tpu as pltpu
from jax.sharding import PartitionSpec as P

EPS = 1e-06
THETA = 1000000.0
BF = jnp.bfloat16
F32 = jnp.float32


def rope_tables(length, width):
    half_width = width // 2
    inverse = THETA ** (-(2.0 * jnp.arange(half_width, dtype=F32)) / width)
    angles = jnp.arange(length, dtype=F32)[:, None] * inverse[None, :]
    return jnp.cos(angles), jnp.sin(angles)


def rotate(field_in, cos_part, sin_part):
    half_width = field_in.shape[-1] // 2
    low, high = field_in[..., :half_width], field_in[..., half_width:]
    cos_rows, sin_rows = cos_part[:, None, :], sin_part[:, None, :]
    return jnp.concatenate(
        [low * cos_rows - high * sin_rows, high * cos_rows + low * sin_rows], axis=-1
    )


def einsum(spec, *args):
    return jnp.einsum(spec, *args, preferred_element_type=F32)


def silu_parts(gate_in):
    gate_sig = jax.nn.sigmoid(gate_in)
    return gate_in * gate_sig, gate_sig * (1.0 + gate_in * (1.0 - gate_sig))


def after(array, *others):
    return lax.optimization_barrier((array,) + others)[0]


def pick(array, index, axis):
    return lax.dynamic_index_in_dim(array, index, axis, keepdims=False)


VMEM_LIMIT = 58 * 2**20


def dot(left, right, left_dim=1, right_dim=0):
    return lax.dot_general(
        left, right, (((left_dim,), (right_dim,)), ((), ())), preferred_element_type=F32
    )


def call(body, grid, in_specs, out_specs, out_shape, flops, moved, scratch=()):
    return pl.pallas_call(
        body,
        grid=grid,
        in_specs=in_specs,
        out_specs=out_specs,
        out_shape=out_shape,
        scratch_shapes=scratch,
        cost_estimate=pl.CostEstimate(flops=flops, bytes_accessed=moved, transcendentals=0),
        compiler_params=pltpu.CompilerParams(vmem_limit_bytes=VMEM_LIMIT),
    )


def act_body(
    experts,
    units,
    group_ref,
    slot_ref,
    rows_ref,
    grads_ref,
    router_ref,
    gateup_ref,
    down_ref,
    slotted_ref,
    slotgrad_ref,
    pair_ref,
    act_ref,
    terms_ref,
    pair_s_ref,
    act_s_ref,
    inner_s_ref,
    probs_ref,
):
    unit = pl.program_id(1)
    half = gateup_ref.shape[1] // 2
    seq_len = rows_ref.shape[1]
    capacity = slotted_ref.shape[2]

    @pl.when(unit == 0)
    def _():
        logits = dot(router_ref[...], rows_ref[0], 1, 1)
        row = lax.broadcasted_iota(jnp.int32, logits.shape, 0)
        routed = jnp.where(row < experts, logits, -1e30)
        raised = jnp.exp(routed - jnp.max(routed, axis=0, keepdims=True))
        soft = raised / jnp.sum(raised, axis=0, keepdims=True)
        probs_ref[0] = jnp.where(row < experts, soft, jax.nn.sigmoid(logits))

    def parts(data, cot, weight):
        both = dot(data, gateup_ref[0], 1, 1)
        cot_in = dot(cot, down_ref[0], 1, 1)
        gate_in, up_in = both[:, :half], both[:, half:]
        gate_act, gate_slope = silu_parts(gate_in)
        act = gate_act * up_in
        inner = jnp.sum(act.astype(BF).astype(F32) * cot_in, axis=1, keepdims=True)
        cot_in = cot_in * weight
        return (
            (act * weight).astype(BF),
            (cot_in * up_in * gate_slope).astype(BF),
            (cot_in * gate_act).astype(BF),
            inner,
        )

    @pl.when(unit < units - 1)
    def _():
        slot = slot_ref[0, pl.ds(unit, 1), :]
        mask = lax.broadcasted_iota(jnp.int32, (capacity, seq_len), 0) == slot
        onehot = mask.astype(F32).astype(BF)
        slotted_ref[0, 0] = dot(onehot, rows_ref[0]).astype(BF)
        slotgrad_ref[0, 0] = dot(onehot, grads_ref[0]).astype(BF)
        probs = probs_ref[0]
        row = lax.broadcasted_iota(jnp.int32, probs.shape, 0)
        expert = group_ref[0] * (units - 1) + unit
        gate = jnp.sum(jnp.where(row == expert, probs, 0.0), axis=0, keepdims=True)
        weight = jnp.sum(jnp.where(mask, gate, 0.0), axis=1, keepdims=True)
        act, gate_grad, up_grad, inner = parts(slotted_ref[0, 0], slotgrad_ref[0, 0], weight)
        act_ref[0, 0] = act
        pair_ref[0, 0, :, :half] = gate_grad
        pair_ref[0, 0, :, half:] = up_grad
        terms_ref[0, pl.ds(unit, 1), :] = jnp.sum(
            jnp.where(mask, inner, 0.0), axis=0, keepdims=True
        )

    @pl.when(unit == units - 1)
    def _():
        logits = dot(rows_ref[0], router_ref[...], 1, 1)
        weight = jax.nn.sigmoid(logits[:, experts : experts + 1])
        act, gate_grad, up_grad, inner = parts(rows_ref[0], grads_ref[0], weight)
        act_s_ref[0] = act
        pair_s_ref[0, :, :half] = gate_grad
        pair_s_ref[0, :, half:] = up_grad
        inner_s_ref[0] = inner


def act_call(experts, capacity, group, slots, rows, grads, router, gateup, down):
    count, seq_len, width = rows.shape
    units, wide, _ = gateup.shape
    half = wide // 2
    routed = units - 1

    def seq(s, u):
        return (s, 0, 0)

    def unit(s, u):
        return (u, 0, 0)

    def slot(s, u):
        return (jnp.minimum(u, routed - 1), s, 0, 0)

    work = count * (routed * capacity + seq_len) * width
    return call(
        functools.partial(act_body, experts, units),
        (count, units),
        [
            pl.BlockSpec(memory_space=pltpu.SMEM),
            pl.BlockSpec((1, routed, seq_len), seq),
            pl.BlockSpec((1, seq_len, width), seq),
            pl.BlockSpec((1, seq_len, width), seq),
            pl.BlockSpec(router.shape, lambda s, u: (0, 0)),
            pl.BlockSpec((1, wide, width), unit),
            pl.BlockSpec((1, half, width), unit),
        ],
        [
            pl.BlockSpec((1, 1, capacity, width), slot),
            pl.BlockSpec((1, 1, capacity, width), slot),
            pl.BlockSpec((1, 1, capacity, wide), slot),
            pl.BlockSpec((1, 1, capacity, half), slot),
            pl.BlockSpec((1, routed, seq_len), seq),
            pl.BlockSpec((1, seq_len, wide), seq),
            pl.BlockSpec((1, seq_len, half), seq),
            pl.BlockSpec((1, seq_len, 1), seq),
            pl.BlockSpec((1,) + (router.shape[0], seq_len), seq),
        ],
        [
            jax.ShapeDtypeStruct((routed, count, capacity, width), BF),
            jax.ShapeDtypeStruct((routed, count, capacity, width), BF),
            jax.ShapeDtypeStruct((routed, count, capacity, wide), BF),
            jax.ShapeDtypeStruct((routed, count, capacity, half), BF),
            jax.ShapeDtypeStruct((count, routed, seq_len), F32),
            jax.ShapeDtypeStruct((count, seq_len, wide), BF),
            jax.ShapeDtypeStruct((count, seq_len, half), BF),
            jax.ShapeDtypeStruct((count, seq_len, 1), F32),
            jax.ShapeDtypeStruct((count, router.shape[0], seq_len), F32),
        ],
        2 * work * 3 * half + 4 * count * routed * capacity * seq_len * width,
        8 * count * seq_len * width * 2,
    )(group, slots, rows, grads, router, gateup, down)


def back_body(slot_ref, routed_ref, shared_ref, weight_ref, out_ref):
    routed, _, capacity, _ = routed_ref.shape
    seq_len = shared_ref.shape[1]
    total = dot(shared_ref[0], weight_ref[routed])
    lane = lax.broadcasted_iota(jnp.int32, (seq_len, capacity), 1)
    for e in range(routed):
        slot_rows = dot(routed_ref[e, 0], weight_ref[e]).astype(BF)
        onehot = (lane == slot_ref[0, e]).astype(F32).astype(BF)
        total = total + dot(onehot, slot_rows)
    out_ref[0] = total.astype(BF)


def back_call(slots, routed, shared, weight):
    units, wide, width = weight.shape
    count, seq_len, _ = shared.shape
    capacity = routed.shape[2]
    block = min(width, 512)
    work = count * ((units - 1) * capacity + seq_len) * width
    return call(
        back_body,
        (width // block, count),
        [
            pl.BlockSpec((1, units - 1, seq_len, 1), lambda j, s: (s, 0, 0, 0)),
            pl.BlockSpec((units - 1, 1, capacity, wide), lambda j, s: (0, s, 0, 0)),
            pl.BlockSpec((1, seq_len, wide), lambda j, s: (s, 0, 0)),
            pl.BlockSpec((units, wide, block), lambda j, s: (0, 0, j)),
        ],
        pl.BlockSpec((1, seq_len, block), lambda j, s: (s, 0, j)),
        jax.ShapeDtypeStruct((count, seq_len, width), BF),
        2 * work * wide + 2 * count * (units - 1) * capacity * seq_len * width,
        units * wide * width * 2 + count * seq_len * width * 2,
    )(slots, routed, shared, weight)


def outer_body(keep, pad, left_a, right_a, left_b, right_b, out_ref):
    total = dot(left_a[0], right_a[0], 0, 0) + dot(left_b[0], right_b[0], 0, 0)
    total = total.astype(BF)
    blocks, _, rows, slice_width = out_ref.shape
    for part in range(rows // keep):
        for k in range(blocks):
            out_ref[k, 0, part * keep : (part + 1) * keep] = total[
                part * pad : part * pad + keep, k * slice_width : (k + 1) * slice_width
            ]


def outer_call(keep, pad, dp, pairs):
    (left_a, right_a), (left_b, right_b) = pairs
    units, rows, wide = left_a.shape
    width = right_a.shape[2]
    slice_width = width // dp
    blocks = max(1, 512 // slice_width)
    kept = wide // pad * keep

    def left(n):
        return pl.BlockSpec((1, n, wide), lambda u, j: (u, 0, 0))

    def right(n):
        return pl.BlockSpec((1, n, blocks * slice_width), lambda u, j: (u, 0, j))

    return call(
        functools.partial(outer_body, keep, pad),
        (units, dp // blocks),
        [left(rows), right(rows), left(rows), right(rows)],
        pl.BlockSpec((blocks, 1, kept, slice_width), lambda u, j: (j, u, 0, 0)),
        jax.ShapeDtypeStruct((dp, units, kept, slice_width), BF),
        4 * units * rows * wide * width,
        units * rows * (wide + width) * 4,
    )(left_a, right_a, left_b, right_b)


def local(
    dp,
    tokens,
    picture_ids,
    routes,
    slot_order,
    norm_gains,
    w_query,
    w_key,
    w_value,
    w_out,
    qkv_bias,
    router,
    shared_gate,
    shared_up,
    shared_down,
    expert_gate,
    expert_up,
    expert_down,
    out_grad,
):
    seq_len = picture_ids.shape[0]
    local_rows = tokens.shape[0]
    width = tokens.shape[1]
    experts, slice_width, hidden_units = expert_gate.shape
    top_count = routes.shape[1]
    capacity = 5 * seq_len * top_count // (4 * experts)
    heads_local = qkv_bias.shape[1]
    head_width = w_query.shape[1] // heads_local
    pair_heads = heads_local // 2
    pair_width = pair_heads * head_width
    mine_experts = experts // 4
    hidden_pad = -(-hidden_units // 128) * 128

    me = lax.axis_index("dp")
    zi = lax.axis_index("tensor")
    core, xi = me % 2, (me // 2) % 2
    group = me % 4
    bits = []
    while 2 ** (len(bits) + 1) <= dp:
        bits.append(2 ** len(bits))
    upper = bits[2:]

    def swap(array, bit):
        return lax.ppermute(array, "dp", [(i, i ^ bit) for i in range(dp)])

    def bit_of(bit):
        return (me // bit) % 2

    def join(mine, theirs, bit, axis):
        n = mine.shape[axis]
        shape = list(mine.shape)
        shape[axis] = 2 * n
        out = jnp.zeros(shape, mine.dtype)
        out = lax.dynamic_update_slice_in_dim(out, mine, n * bit_of(bit), axis)
        return lax.dynamic_update_slice_in_dim(out, theirs, n * (1 - bit_of(bit)), axis)

    def half(array, which, axis):
        n = array.shape[axis] // 2
        return lax.dynamic_slice_in_dim(array, which * n, n, axis)

    gains_z = lax.all_gather(norm_gains, "tensor", axis=1, tiled=True)
    misc_rows = 16
    bias_width = 3 * pair_heads * qkv_bias.shape[2]
    bias_cores = qkv_bias.reshape(3, 2, -1).swapaxes(0, 1).reshape(2, bias_width)

    def misc_pack(core_bias):
        wide = jnp.zeros((misc_rows, 2 * pair_width), BF)
        wide = wide.at[: experts + 1, :slice_width].set(router.T)
        wide = wide.at[experts + 1, :bias_width].set(core_bias)
        return wide.at[experts + 2 : experts + 4, :slice_width].set(gains_z)

    qk = jnp.concatenate(
        [w.reshape(slice_width, 2, pair_width) for w in (w_query, w_key)], axis=2
    )
    qk = jnp.concatenate(
        [qk, jnp.stack([misc_pack(bias_cores[0]), misc_pack(bias_cores[1])], axis=1)], axis=0
    )
    vo = jnp.concatenate(
        [w.reshape(slice_width, 2, pair_width) for w in (w_value, w_out.T)], axis=2
    )
    tokens_z = lax.all_gather(tokens, "tensor", axis=0, tiled=True)

    def gather_attention(pack, order):
        dims = (1,) * len(bits[1:])
        both = join(pick(pack, core, 1)[None], swap(pick(pack, 1 - core, 1), 1)[None], 1, 0)
        both = both.reshape(dims + both.shape)
        for bit in order:
            axis = len(bits) - 1 - bits.index(bit)
            both = join(both, swap(both, bit), bit, axis)
        return both.reshape((dp,) + both.shape[-2:])

    qk_all = gather_attention(qk, bits[1:])
    vo_full = gather_attention(vo, bits[:0:-1]).reshape(width, 2 * pair_width)
    qk_full = qk_all[:, :slice_width].reshape(width, 2 * pair_width)
    misc = qk_all[:, slice_width:]
    router_full = misc[:, : experts + 1, :slice_width].swapaxes(1, 2).reshape(width, -1)
    gain_rows = misc[:, experts + 2 : experts + 4, :slice_width].swapaxes(0, 1)
    gain_rows = gain_rows.reshape(2, width).astype(F32)
    bias = misc[:, experts + 1, :bias_width].astype(F32)
    bias = bias.reshape(dp, 3 * pair_heads, -1).swapaxes(0, 1).reshape(3, pair_width)

    tokens_sib = swap(tokens_z, 1)
    grad_z = lax.all_gather(out_grad, "tensor", axis=0, tiled=True)

    codes = jnp.concatenate([routes, slot_order], axis=1).T
    codes_x = swap(codes, 2)
    both_codes = swap(jnp.stack([codes, codes_x]), 1)
    codes_a = jnp.stack([codes, both_codes[0]])
    codes_b = jnp.stack([codes_x, both_codes[1]])
    pictures = jnp.stack([picture_ids, swap(picture_ids, 1)])

    def core_units(routed, shared):
        routed = routed.reshape(2, 2, mine_experts, hidden_units, slice_width)
        shared = shared.reshape(2, 2, 1, hidden_units, slice_width)

        def cut(which):
            return jnp.concatenate([pick(routed, which, 1), pick(shared, which, 1)], axis=1)

        return join(cut(core), swap(cut(1 - core), 1), 1, 3)

    def x_units(held):
        return join(pick(held, xi, 0), swap(pick(held, 1 - xi, 0), 2), 2, 2)

    def upper_units(held):
        for bit in upper[:-1]:
            held = join(held, swap(held, bit), bit, 2)
        return held, swap(held, upper[-1])

    def padded(*pairs):
        n = pairs[0][0].shape[-1]
        out = jnp.zeros((mine_experts + 1, len(pairs) * hidden_pad, 2 * n), BF)
        zero = jnp.int32(0)
        for k, (mine, theirs) in enumerate(pairs):
            row = jnp.int32(k * hidden_pad)
            out = lax.dynamic_update_slice(out, mine, (zero, row, n * bit_of(upper[-1])))
            out = lax.dynamic_update_slice(out, theirs, (zero, row, n * (1 - bit_of(upper[-1]))))
        return out

    down_c = core_units(expert_down, shared_down)
    gate_c = core_units(expert_gate.swapaxes(1, 2), shared_gate.T)
    up_c = core_units(expert_up.swapaxes(1, 2), shared_up.T)
    down_x = x_units(down_c)
    gate_x = x_units(gate_c)
    up_x = x_units(up_c)
    grad_x = swap(after(grad_z, up_x), 2)
    down_y = upper_units(down_x)
    gate_y = upper_units(gate_x)
    up_y = upper_units(up_x)

    rows_f = jnp.stack([tokens_z, tokens_sib]).astype(F32)
    qk_full = after(qk_full, down_c, gate_c, up_c)
    first_scale = lax.rsqrt(jnp.mean(rows_f * rows_f, axis=-1, keepdims=True) + EPS)
    first_norm = (rows_f * first_scale * gain_rows[0]).astype(BF)
    qk_pre = einsum("std,df->stf", first_norm, qk_full) + jnp.concatenate([bias[0], bias[1]])
    values = (einsum("std,df->stf", first_norm, vo_full[:, :pair_width]) + bias[2]).astype(BF)
    cos_part, sin_part = rope_tables(seq_len, head_width)
    qk_rot = rotate(
        qk_pre.reshape(2, seq_len, 2 * pair_heads, head_width), cos_part, sin_part
    ).astype(BF)
    qk_rot = after(qk_rot, down_x)
    queries, keys = qk_rot[:, :, :pair_heads], qk_rot[:, :, pair_heads:]
    values = values.reshape(2, seq_len, pair_heads, head_width)
    positions = jnp.arange(seq_len, dtype=jnp.int32)
    allowed = jnp.logical_or(
        positions[None, None, :] <= positions[None, :, None],
        pictures[:, :, None] * pictures[:, None, :] > 0,
    )
    score_scale = head_width ** (-0.5)
    scores = einsum("sqhd,skhd->shqk", queries, keys) * score_scale
    scores = jnp.where(allowed[:, None], scores, -1e30)
    weights = jnp.exp(scores - jnp.max(scores, axis=-1, keepdims=True))
    probs = weights / jnp.sum(weights, axis=-1, keepdims=True)
    probs_low = probs.astype(BF)
    head_mix = einsum("shqk,skhd->sqhd", probs_low, values).astype(BF)
    heads_out = after(head_mix.reshape(2, seq_len, pair_width), gate_x)
    out_weight = vo_full[:, pair_width:]
    attn_part = einsum("sqf,df->sqd", heads_out, out_weight)

    def core_sum(own, sibling):
        return own + swap(sibling.astype(BF), 1).astype(F32)

    def z_scatter(array):
        return lax.psum_scatter(
            array.astype(BF), "tensor", scatter_dimension=0, tiled=True
        ).astype(F32)

    inputs = tokens.astype(F32)
    hidden = inputs + z_scatter(core_sum(attn_part[0], attn_part[1]))
    hidden = after(hidden, up_x, down_y[1])
    second_scale = lax.rsqrt(jnp.mean(hidden * hidden, axis=-1, keepdims=True) + EPS)
    second_unit = hidden * second_scale
    second_norm = (second_unit * gain_rows[1]).astype(BF)
    norm_z = lax.all_gather(second_norm, "tensor", axis=0, tiled=True)
    norm_z = after(norm_z, gate_y[1], grad_x)
    down_all = padded(down_y)
    gateup_all = padded(gate_y, up_y)

    norm_x = swap(norm_z, 2)
    norm_a = jnp.stack([norm_z, swap(norm_z, 1)])
    norm_b = jnp.stack([norm_x, swap(norm_x, 1)])
    grad_a = jnp.stack([grad_z, swap(grad_z, 1)])
    grad_b = jnp.stack([grad_x, swap(grad_x, 1)])

    expert_ids = group * mine_experts + jnp.arange(mine_experts, dtype=jnp.int32)

    router_rows = jnp.pad(router_full.T, ((0, 16 - experts - 1), (0, 0)))
    group_ids = group.astype(jnp.int32).reshape(1)

    def slots_of(codes_in):
        routes_in, slots_in = codes_in[:, None, :top_count], codes_in[:, None, top_count:]
        matches = routes_in == expert_ids[None, :, None, None]
        return jnp.max(jnp.where(matches, slots_in, -1), axis=2)

    def feed(slots, rows, grads):
        slotted, slot_grad, pair, act, terms, pair_s, act_s, inner_s, probs_out = act_call(
            experts, capacity, group_ids, slots, rows, grads, router_rows, gateup_all, down_all
        )
        terms = jnp.concatenate([terms.swapaxes(1, 2), inner_s], axis=-1)
        flat = [a.reshape(mine_experts, -1, a.shape[-1]) for a in (slotted, slot_grad, pair, act)]
        shared = [a.reshape(1, -1, a.shape[-1]) for a in (rows, grads, pair_s, act_s)]
        return (pair, pair_s), (act, act_s), terms, (flat, shared), probs_out

    slots_a, slots_b = slots_of(codes_a), slots_of(codes_b)
    fed_a = feed(slots_a, norm_a, grad_a)
    fed_b = feed(slots_b, norm_b, grad_b)
    columns_a, columns_b = slots_a[..., None], slots_b[..., None]
    row_grad_b = back_call(columns_b, *fed_b[0], gateup_all)
    row_grad_a = back_call(after(columns_a, row_grad_b), *fed_a[0], gateup_all)
    row_out_b = back_call(after(columns_b, row_grad_a), *fed_b[1], down_all)
    row_out_a = back_call(columns_a, *fed_a[1], down_all)

    def spread(terms):
        wide = jnp.zeros(terms.shape[:-1] + (128,), F32)
        wide = lax.dynamic_update_slice_in_dim(
            wide, terms[..., :mine_experts], group * mine_experts, terms.ndim - 1
        )
        return wide.at[..., experts].set(terms[..., mine_experts])

    def group_sum(a, b):
        across = b[0].astype(F32) + swap(b[1].astype(BF), 1).astype(F32)
        near = a[0].astype(F32) + swap(a[1].astype(BF), 1).astype(F32)
        return near + swap(across.astype(BF), 2).astype(F32)

    grad_sum = group_sum(row_grad_a, row_grad_b)
    term_sum = group_sum(spread(fed_a[2]), spread(fed_b[2]))
    packed = z_scatter(jnp.concatenate([grad_sum, term_sum], axis=-1))
    second_grad, gate_sums = packed[:, :width], packed[:, width:]

    data_a, data_b = fed_a[3], fed_b[3]

    def unit_grads(left, right):
        return jnp.concatenate(
            [
                outer_call(
                    hidden_units,
                    hidden_pad,
                    dp,
                    [(data[k][left], data[k][right]) for data in (data_a, data_b)],
                )
                for k in range(2)
            ],
            axis=1,
        )

    def scatter_units(total):
        total = total.reshape((2,) * len(bits) + total.shape[1:])
        for bit in reversed(upper):
            axis = len(bits) - 1 - bits.index(bit)
            sent = half(total, 1 - bit_of(bit), axis)
            kept = half(total, bit_of(bit), axis)
            total = (kept.astype(F32) + swap(sent, bit).astype(F32)).astype(BF)
        total = total.reshape((2, 2) + total.shape[len(bits) :])
        held = join(pick(total, xi, 0)[None], swap(pick(total, 1 - xi, 0), 2)[None], 2, 0)
        return join(pick(held, core, 1)[:, None], swap(pick(held, 1 - core, 1), 1)[:, None], 1, 1)

    def split_units(held):
        routed = held[:, :, :mine_experts].reshape(experts, -1, slice_width)
        shared = held[:, :, mine_experts]
        return routed.astype(F32), shared.astype(F32)

    gateup_sum = scatter_units(unit_grads(2, 0))
    down_sum = scatter_units(unit_grads(3, 1))
    routed_gu, shared_gu = split_units(gateup_sum)
    routed_down, shared_down_sum = split_units(down_sum)
    shared_gu = shared_gu.reshape(4, 2, hidden_units, slice_width)
    egate_sum = routed_gu[:, :hidden_units].swapaxes(1, 2)
    eup_sum = routed_gu[:, hidden_units:].swapaxes(1, 2)
    sgate_sum = shared_gu[:, 0].reshape(-1, slice_width).T
    sup_sum = shared_gu[:, 1].reshape(-1, slice_width).T
    sdown_sum = shared_down_sum.reshape(-1, slice_width)

    row_start = zi * local_rows
    probs_local = lax.dynamic_slice_in_dim(fed_a[4][0], row_start, local_rows, 1).T
    probs_mine, weight_mine = probs_local[:, :experts], probs_local[:, experts]
    route_grad = gate_sums[:, :experts]
    expert_logit_grad = probs_mine * (
        route_grad - jnp.sum(probs_mine * route_grad, axis=-1, keepdims=True)
    )
    weight_logit_grad = gate_sums[:, experts] * weight_mine * (1.0 - weight_mine)
    logits_grad = jnp.concatenate([expert_logit_grad, weight_logit_grad[:, None]], axis=1).astype(
        BF
    )
    second_grad = second_grad + einsum("tf,df->td", logits_grad, router_full)
    gain_two_grad = jnp.sum(second_grad * second_unit, axis=0)
    unit_two = second_grad * gain_rows[1]
    hidden_grad = out_grad.astype(F32) + second_scale * (
        unit_two - second_unit * jnp.mean(unit_two * second_unit, axis=-1, keepdims=True)
    )
    attention_grad = hidden_grad.astype(BF)
    wide_logits = jnp.pad(logits_grad, ((0, 0), (0, 128 - experts - 1)))
    back_z = lax.all_gather(
        jnp.concatenate([attention_grad, wide_logits], axis=1), "tensor", axis=0, tiled=True
    )
    out_sum = after(group_sum(row_out_a, row_out_b), back_z)
    output = (hidden + z_scatter(out_sum)).astype(BF)
    logits_z = back_z[:, width : width + 16]
    back_own = back_z[:, :width]
    back_rows = jnp.stack([back_own, swap(back_own, 1)])

    router_part = einsum("tf,td->fd", logits_z, norm_z)[: experts + 1]

    out_proj = einsum("std,stf->df", back_rows, heads_out)
    mix_grad = einsum("std,df->stf", back_rows, out_weight).astype(BF)
    mix_grad = mix_grad.reshape(2, seq_len, pair_heads, head_width)
    prob_grad = einsum("sqhd,skhd->shqk", mix_grad, values)
    score_grad = (
        probs * (prob_grad - jnp.sum(probs * prob_grad, axis=-1, keepdims=True))
    ).astype(BF)
    query_rot = einsum("shqk,skhd->sqhd", score_grad, keys) * score_scale
    key_rot = einsum("shqk,sqhd->skhd", score_grad, queries) * score_scale
    value_grad = einsum("shqk,sqhd->skhd", probs_low, mix_grad)
    qk_grad = rotate(jnp.concatenate([query_rot, key_rot], axis=2), cos_part, -sin_part)
    qk_grad = qk_grad.astype(BF).reshape(2, seq_len, 2 * pair_width)
    v_grad = value_grad.astype(BF).reshape(2, seq_len, pair_width)
    first_part = einsum("stf,df->std", qk_grad, qk_full) + einsum(
        "stf,df->std", v_grad, vo_full[:, :pair_width]
    )
    first_grad = z_scatter(core_sum(first_part[0], first_part[1]))

    gain_one_grad = jnp.sum(first_part * (rows_f * first_scale), axis=(0, 1))
    bias_part = jnp.concatenate(
        [jnp.sum(qk_grad.astype(F32), axis=(0, 1)), jnp.sum(v_grad.astype(F32), axis=(0, 1))]
    )
    bias_part = bias_part.reshape(3 * pair_heads, dp, -1).swapaxes(0, 1).reshape(dp, 1, -1)
    gain_part = jnp.stack([gain_one_grad, gain_two_grad]).reshape(2, dp, slice_width)

    def wide_rows(rows):
        return jnp.pad(rows, ((0, 0), (0, 0), (0, 2 * pair_width - rows.shape[2])))

    misc_part = jnp.concatenate(
        [
            wide_rows(router_part.reshape(experts + 1, dp, slice_width).swapaxes(0, 1)),
            wide_rows(bias_part),
            wide_rows(gain_part.swapaxes(0, 1)),
            jnp.zeros((dp, misc_rows - experts - 4, 2 * pair_width), F32),
        ],
        axis=1,
    )
    qk_total = einsum("std,stf->df", first_norm, qk_grad).reshape(dp, slice_width, -1)
    qk_total = jnp.concatenate([qk_total, misc_part], axis=1)
    vo_total = jnp.concatenate([einsum("std,stf->df", first_norm, v_grad), out_proj], axis=1)
    vo_total = vo_total.reshape(dp, slice_width, -1)

    def scatter_attention(total, order):
        total = total.reshape((2,) * len(bits) + total.shape[1:])
        for bit in order:
            axis = len(bits) - 1 - bits.index(bit)
            sent = half(total, 1 - bit_of(bit), axis).astype(BF)
            total = half(total, bit_of(bit), axis) + swap(sent, bit).astype(F32)
        total = total.reshape((2,) + total.shape[-2:]).astype(BF)
        return pick(total, core, 0), swap(pick(total, 1 - core, 0), 1)

    def columns_of(mine, theirs):
        held = join(mine[:slice_width, None], theirs[:slice_width, None], 1, 1)
        first, second = held[..., :pair_width], held[..., pair_width:]
        return (
            first.reshape(slice_width, -1).astype(F32),
            second.reshape(slice_width, -1).astype(F32),
        )

    qk_mine, qk_theirs = scatter_attention(qk_total, bits[:0:-1])
    vo_mine, vo_theirs = scatter_attention(vo_total, bits[1:])
    qk_sums = columns_of(qk_mine, qk_theirs)
    vo_sums = columns_of(vo_mine, vo_theirs)
    misc_mine = qk_mine[slice_width:].astype(F32)
    misc_theirs = qk_theirs[slice_width:].astype(F32)
    misc_sum = misc_mine + misc_theirs
    router_sum = misc_sum[: experts + 1, :slice_width].T
    bias_sums = join(
        misc_mine[experts + 1, :bias_width].reshape(3, 1, pair_heads, -1),
        misc_theirs[experts + 1, :bias_width].reshape(3, 1, pair_heads, -1),
        1,
        1,
    ).reshape(3, heads_local, -1)
    gain_sums = lax.all_gather(
        misc_sum[experts + 2 : experts + 4, :slice_width], "tensor", axis=0, tiled=False
    )
    tensor = gain_sums.shape[0]
    gain_sums = jnp.sum(gain_sums, axis=0).reshape(2, tensor, -1)
    gain_sums = pick(gain_sums, zi, 1)

    unit_mine = inputs * lax.rsqrt(jnp.mean(inputs * inputs, axis=-1, keepdims=True) + EPS)
    scale_mine = lax.rsqrt(jnp.mean(inputs * inputs, axis=-1, keepdims=True) + EPS)
    unit_one = first_grad * gain_rows[0]
    input_grad = hidden_grad + scale_mine * (
        unit_one - unit_mine * jnp.mean(unit_one * unit_mine, axis=-1, keepdims=True)
    )
    return (
        output,
        input_grad.astype(BF),
        gain_sums,
        qk_sums[0],
        qk_sums[1],
        vo_sums[0],
        vo_sums[1].T,
        bias_sums,
        router_sum,
        sgate_sum,
        sup_sum,
        sdown_sum,
        egate_sum,
        eup_sum,
        routed_down,
    )


def solution(mesh):
    return jax.shard_map(
        functools.partial(local, mesh.shape["dp"]),
        mesh=mesh,
        in_specs=(
            P(("dp", "tensor"), None),
            P("dp"),
            P("dp", None),
            P("dp", None),
            P(None, ("dp", "tensor")),
            P("dp", "tensor"),
            P("dp", "tensor"),
            P("dp", "tensor"),
            P("tensor", "dp"),
            P(None, "tensor", "dp"),
            P("dp", None),
            P("dp", "tensor"),
            P("dp", "tensor"),
            P("tensor", "dp"),
            P(None, "dp", "tensor"),
            P(None, "dp", "tensor"),
            P(None, "tensor", "dp"),
            P(("dp", "tensor"), None),
        ),
        out_specs=(
            P(("dp", "tensor"), None),
            P(("dp", "tensor"), None),
            P(None, ("dp", "tensor")),
            P("dp", "tensor"),
            P("dp", "tensor"),
            P("dp", "tensor"),
            P("tensor", "dp"),
            P(None, "tensor", "dp"),
            P("dp", None),
            P("dp", "tensor"),
            P("dp", "tensor"),
            P("tensor", "dp"),
            P(None, "dp", "tensor"),
            P(None, "dp", "tensor"),
            P(None, "tensor", "dp"),
        ),
        check_vma=False,
    )
```

time: 2010 us -> 1060 us (0.53)
  waiting for transfers between devices: 1390 us -> 372 us
  matrix products: 278 us -> 34.4 us
  Pallas kernels: 0 us -> 178 us
  local copies, waits for them, and re-layouts: 122 us -> 273 us
  blocking collectives: 100 us -> 24 us
  starting transfers between devices: 2.71 us -> 35 us
  other arithmetic: 88.6 us -> 119 us
    reduce_scatter x15 -> x4, waiting for transfers between devices: 721 us -> 12.7 us  [z_scatter(): lax.psum_scatter(array.astype(BF), 'tensor', scatter_dimension=0, tiled=T...]
    all_gather x14 -> x4, waiting for transfers between devices: 490 us -> 36 us  [the longest x1 36 us: local(): grad_z = lax.all_gather(out_grad, 'tensor', axis=0, tiled=True)]
    ppermute x0 -> x49, waiting for transfers between devices: none -> 322 us  [swap(): return lax.ppermute(array, 'dp', [(i, i ^ bit) for i in range(dp)])]
    dot_general x41 -> x17, matrix products: 278 us -> 34.4 us  [einsum(): return jnp.einsum(spec, *args, preferred_element_type=F32)]
    unnamed x35 -> x8, waiting for transfers between devices: 184 us -> 0.8 us
    pallas_call x0 -> x10, Pallas kernels: none -> 178 us  [the longest x4 72.7 us: back_call(): call(back_body, (width // block, count), [pl.BlockSpec((1, units - 1, seq...]
    gather x9 -> x0, local copies, waits for them, and re-layouts: 98.2 us -> none  [the longest x2 42.6 us: local(): jnp.take(slotted_grad.reshape(experts * capacity, -1), slot_index, axis=0)]
    dynamic_update_slice x0 -> x41, local copies, waits for them, and re-layouts: none -> 97.6 us  [the longest x19 47.6 us: join(): lax.dynamic_update_slice_in_dim(out, theirs, n * (1 - bit_of(bit)), axis)]
  transfers between devices with their start and end apart: 32 -> 57, of which waited for: 31 -> 19; matrix products, arithmetic and copies ran while one was open for 13% -> 34% of each run, Pallas kernels for 0% -> 12%
where the time goes in v1:
time: 1060 us; the launch traced here: 1050 us
  waiting for transfers between devices  372 us (35%)
  local copies, waits for them, and re-layouts  273 us (26%)
  Pallas kernels  178 us (17%)
  other arithmetic  119 us (11%)
  starting transfers between devices  35 us (3%)
  matrix products  34.4 us (3%)
  blocking collectives  24 us (2%)
  between operations  16.4 us (2%)
    ppermute x49, waiting for transfers between devices, swap(): return lax.ppermute(array, 'dp', [(i, i ^ bit) for i in range(dp)])  322 us
    pallas_call x4, Pallas kernels, back_call(): call(back_body, (width // block, count), [pl.BlockSpec((1, units - 1, seq...  72.7 us
    pallas_call x2, Pallas kernels, act_call(): call(functools.partial(act_body, experts, units), (count, units), [pl.Blo...  59.5 us
    dynamic_update_slice x19, local copies, waits for them, and re-layouts, join(): lax.dynamic_update_slice_in_dim(out, theirs, n * (1 - bit_of(bit)), axis)  47.6 us
    pallas_call x4, Pallas kernels, outer_call(): call(functools.partial(outer_body, keep, pad), (units, dp // blocks), [le...  45.4 us
    all_gather x1, waiting for transfers between devices, local(): grad_z = lax.all_gather(out_grad, 'tensor', axis=0, tiled=True)  36 us
    unnamed x217, local copies, waits for them, and re-layouts  35.7 us
    ppermute x49, starting transfers between devices, swap(): return lax.ppermute(array, 'dp', [(i, i ^ bit) for i in range(dp)])  34.5 us
  transfers between devices with their start and end apart: 57, of which 19 were waited for; matrix products, arithmetic and copies ran while one was open for 34% of the time, Pallas kernels for 12%

profile of v1, /device:TPU:0, one launch (start us, length us, event | category | flops | bytes accessed | tf_op | source)
XLA Modules:
  0.0 1050.8 jit_solution(3715357814392700963)
XLA Ops:
  12.1 12.1 %all-gather.1 = bf16[4,64,2]{1,2,0:T(2,128)(2,1)S(1)} all-gather(bf16[1,64,2]{1,2,0:T(2,128)(2,1)S(1)} %bitcast.476), channel_id=1, replica_groups=mesh['dp'=8,'tensor'=4] {'tensor'}, dimensions={0}, use_global_device_ids=true | all-gather | bytes 1280 | tf_op jit(solution)/shard_map/all_gather | solution.py:337
  48.3 10.6 %dynamic_update_slice.148 = bf16[1,1,2,256,512]{3,2,1,0,4:T(2,128)(2,1)} dynamic-update-slice(bf16[1,1,2,256,512]{3,2,1,0,4:T(2,128)(2,1)} %broadcast_in_dim.128, bf16[1,1,1,256,512]{3,2,1,0,4:T(2,128)(2,1)S(1)} %copy.418, s32[]{:T(128)} %constant.623.clone.1, s32[]{:T(128)} %constant.623.clone.1, s32[]{:T(128)S(6)} %select_n.339, s32[]{:T(128)} %constant.623.clone.1, s32[]{:T(128)} %constant.623.clone.1) | dynamic-update-slice | bytes 524292 | tf_op jit(solution)/shard_map/dynamic_update_slice | solution.py:330
  60.9 10.6 %dynamic_update_slice.149 = bf16[1,1,2,256,512]{3,2,1,0,4:T(2,128)(2,1)} dynamic-update-slice(bf16[1,1,2,256,512]{3,2,1,0,4:T(2,128)(2,1)} %dynamic_update_slice.148, bf16[1,1,1,256,512]{3,2,1,0,4:T(2,128)(2,1)S(1)} %copy.420, s32[]{:T(128)} %constant.623.clone.1, s32[]{:T(128)} %constant.623.clone.1, s32[]{:T(128)S(6)} %select_n.340, s32[]{:T(128)} %constant.623.clone.1, s32[]{:T(128)} %constant.623.clone.1) | dynamic-update-slice | bytes 524292 | tf_op jit(solution)/shard_map/dynamic_update_slice | solution.py:331
  118.3 4.5 reshape_reshape.6
  130.1 6.7 collective-permute-done.11
  139.2 19.5 %collective-permute-done.12 = bf16[3,352,512]{2,1,0:T(8,128)(2,1)} collective-permute-done((bf16[3,352,512]{2,1,0:T(8,128)(2,1)}, bf16[3,352,512]{2,1,0:T(8,128)(2,1)}, u32[]{:S(2)}, u32[]{:S(2)}) %collective-permute-start.12) | collective-permute-done | bytes 1081376 | tf_op jit(solution)/shard_map/ppermute | solution.py:320
  185.2 4.1 collective-permute-done.13
  198.4 22.5 %collective-permute-done.14 = bf16[3,352,512]{2,1,0:T(8,128)(2,1)S(1)} collective-permute-done((bf16[3,352,512]{2,1,0:T(8,128)(2,1)S(1)}, bf16[3,352,512]{2,1,0:T(8,128)(2,1)S(1)}, u32[]{:S(2)}, u32[]{:S(2)}) %collective-permute-start.14) | collective-permute-done | bytes 1081376 | tf_op jit(solution)/shard_map/ppermute | solution.py:320
  221.0 12.7 %reduce-scatter.5.cloned.1.call-done = bf16[128,2048]{1,0:T(8,128)(2,1)} async-done(((bf16[512,2048]{1,0:T(8,128)(2,1)}), bf16[128,2048]{1,0:T(8,128)(2,1)}) %reduce-scatter.5.cloned.1.call-update) | async-done | bytes 524304 | tf_op jit(solution)/shard_map/reduce_scatter | solution.py:459
  235.7 6.1 collective-permute-done.15
  244.7 36.0 %all-gather.12.cloned.1.call-done = bf16[512,2048]{1,0:T(8,128)(2,1)} async-done(((bf16[128,2048]{1,0:T(8,128)(2,1)}), bf16[512,2048]{1,0:T(8,128)(2,1)}) %all-gather.12.cloned.1.call-update) | async-done | bytes 2097168 | tf_op jit(solution)/shard_map/all_gather | solution.py:379
  282.1 9.6 collective-permute-done.18
  291.7 36.6 %collective-permute-done.19 = bf16[512,2048]{1,0:T(8,128)(2,1)} collective-permute-done((bf16[512,2048]{1,0:T(8,128)(2,1)}, bf16[512,2048]{1,0:T(8,128)(2,1)}, u32[]{:S(2)}, u32[]{:S(2)}) %collective-permute-start.19) | collective-permute-done | bytes 2097184 | tf_op jit(solution)/shard_map/ppermute | solution.py:320
  332.0 43.5 %collective-permute-done.16 = s32[8,512]{1,0:T(8,128)S(1)} collective-permute-done((s32[8,512]{1,0:T(8,128)S(1)}, s32[8,512]{1,0:T(8,128)S(1)}, u32[]{:S(2)}, u32[]{:S(2)}) %collective-permute-start.16) | collective-permute-done | bytes 16416 | tf_op jit(solution)/shard_map/ppermute | solution.py:320
  394.4 5.5 pad_maximum_fusion.4.grads_ref
  399.9 4.8 pad_maximum_fusion.6.grads_ref
  404.7 4.0 pad_maximum_fusion.3.rows_ref
  408.8 4.5 pad_maximum_fusion.5.rows_ref
  413.3 29.6 %shard_map.291 = (bf16[2,2,320,2048]{3,2,1,0:T(8,128)(2,1)}, bf16[2,2,320,2048]{3,2,1,0:T(8,128)(2,1)}, bf16[2,2,320,768]{3,2,1,0:T(8,128)(2,1)}, bf16[2,2,320,3...) custom-call(s32[1]{0:T(128)} %bitcast.76.group_ref, ...), custom_call_target="tpu_custom_call" | custom-call | flops 16240345088 | bytes 33554432 | tf_op jit(solution)/shard_map/pallas_call | solution.py:167
  442.9 20.2 %shard_map.292 = bf16[2,512,2048]{2,1,0:T(8,128)(2,1)} custom-call(s32[2,2,512,1]{3,2,1,0:T(8,128)} %copy.434.slot_ref, bf16[2,2,320,768]{3,2,1,0:T(8,128)(2,1)} %get-tuple-element.141.routed_ref, bf16[2,512,768]{2,1,0:T(8,128)(2,1)} %get-tuple-element.142.shared_ref, bf16[3,768,2048]{2,1,0:T(8,128)(2,1)} %copy-done.12), custom_call_target="tpu_custom_call" | custom-call | flops 9932111872 | bytes 13631488 | tf_op jit(solution)/shard_map/pallas_call | solution.py:224
  465.0 30.0 %shard_map.289 = (bf16[2,2,320,2048]{3,2,1,0:T(8,128)(2,1)}, bf16[2,2,320,2048]{3,2,1,0:T(8,128)(2,1)}, bf16[2,2,320,768]{3,2,1,0:T(8,128)(2,1)}, bf16[2,2,320,3...) custom-call(s32[1]{0:T(128)} %bitcast.76.group_ref, ...), custom_call_target="tpu_custom_call" | custom-call | flops 16240345088 | bytes 33554432 | tf_op jit(solution)/shard_map/pallas_call | solution.py:167
  496.3 20.1 %shard_map.293 = bf16[2,512,2048]{2,1,0:T(8,128)(2,1)} custom-call(s32[2,2,512,1]{3,2,1,0:T(8,128)} %copy.435.slot_ref, bf16[2,2,320,768]{3,2,1,0:T(8,128)(2,1)} %get-tuple-element.144.routed_ref, bf16[2,512,768]{2,1,0:T(8,128)(2,1)} %get-tuple-element.145.shared_ref, bf16[3,768,2048]{2,1,0:T(8,128)(2,1)} %copy-done.12), custom_call_target="tpu_custom_call" | custom-call | flops 9932111872 | bytes 13631488 | tf_op jit(solution)/shard_map/pallas_call | solution.py:224
  543.1 30.0 %collective-permute-done.34 = bf16[512,128]{1,0:T(8,128)(2,1)S(1)} collective-permute-done((bf16[512,128]{1,0:T(8,128)(2,1)S(1)}, bf16[512,128]{1,0:T(8,128)(2,1)S(1)}, u32[]{:S(2)}, u32[]{:S(2)}) %collective-permute-start.34) | collective-permute-done | bytes 131104 | tf_op jit(solution)/shard_map/ppermute | solution.py:320
  574.1 4.1 fusion.15
  580.9 11.2 %shard_map.296 = bf16[8,1,704,256]{3,2,1,0:T(8,128)(2,1)} custom-call(bf16[1,1024,768]{2,1,0:T(8,128)(2,1)} %bitcast.486, bf16[1,1024,2048]{2,1,0:T(8,128)(2,1)} %bitcast.411, bf16[1,1024,768]{2,1,0:T(8,128)(2,1)} %bitcast.485, bf16[1,1024,2048]{2,1,0:T(8,128)(2,1)} %bitcast.412), custom_call_target="tpu_custom_call" | custom-call | flops 6442450944 | bytes 11534336 | tf_op jit(solution)/shard_map/pallas_call | solution.py:265
  592.1 15.3 %shard_map.295 = bf16[8,2,704,256]{3,2,1,0:T(8,128)(2,1)} custom-call(bf16[2,640,768]{2,1,0:T(8,128)(2,1)} %bitcast.484, bf16[2,640,2048]{2,1,0:T(8,128)(2,1)} %bitcast.482, bf16[2,640,768]{2,1,0:T(8,128)(2,1)} %bitcast.483, bf16[2,640,2048]{2,1,0:T(8,128)(2,1)} %bitcast.481), custom_call_target="tpu_custom_call" | custom-call | flops 8053063680 | bytes 14417920 | tf_op jit(solution)/shard_map/pallas_call | solution.py:265
  607.3 7.7 pad_maximum_fusion
  615.0 4.6 constant_dynamic-slice_fusion.3
  621.0 7.7 shard_map.298
  628.7 11.3 %shard_map.297 = bf16[8,2,352,256]{3,2,1,0:T(8,128)(2,1)} custom-call(bf16[2,640,384]{2,1,0:T(8,128)(2,1)} %bitcast.435, bf16[2,640,2048]{2,1,0:T(8,128)(2,1)} %bitcast.408, bf16[2,640,384]{2,1,0:T(8,128)(2,1)} %bitcast.434, bf16[2,640,2048]{2,1,0:T(8,128)(2,1)} %bitcast.407), custom_call_target="tpu_custom_call" | custom-call | flops 4026531840 | bytes 12451840 | tf_op jit(solution)/shard_map/pallas_call | solution.py:265
  640.0 4.2 pad_maximum_fusion.1
  657.7 16.1 %shard_map.290 = bf16[2,512,2048]{2,1,0:T(8,128)(2,1)} custom-call(s32[2,2,512,1]{3,2,1,0:T(8,128)} %copy.433.slot_ref, bf16[2,2,320,384]{3,2,1,0:T(8,128)(2,1)} %get-tuple-element.139.routed_ref, bf16[2,512,384]{2,1,0:T(8,128)(2,1)} %get-tuple-element.140.shared_ref, bf16[3,384,2048]{2,1,0:T(8,128)(2,1)} %copy-done.29), custom_call_target="tpu_custom_call" | custom-call | flops 6308233216 | bytes 8912896 | tf_op jit(solution)/shard_map/pallas_call | solution.py:224
  675.2 16.2 %shard_map.294 = bf16[2,512,2048]{2,1,0:T(8,128)(2,1)} custom-call(s32[2,2,512,1]{3,2,1,0:T(8,128)} %copy.436.slot_ref, bf16[2,2,320,384]{3,2,1,0:T(8,128)(2,1)} %get-tuple-element.147.routed_ref, bf16[2,512,384]{2,1,0:T(8,128)(2,1)} %get-tuple-element.148.shared_ref, bf16[3,384,2048]{2,1,0:T(8,128)(2,1)} %copy-done.29), custom_call_target="tpu_custom_call" | custom-call | flops 6308233216 | bytes 8912896 | tf_op jit(solution)/shard_map/pallas_call | solution.py:224
  694.6 66.2 %collective-permute-done.46 = bf16[1,2,2,3,352,256]{5,4,3,2,1,0:T(8,128)(2,1)} collective-permute-done((bf16[1,2,2,3,352,256]{5,4,3,2,1,0:T(8,128)(2,1)}, bf16[1,2,2,3,352,256]{5,4,3,2,1,0:T(8,128)(2,1)}, u32[]{:S(2)}, u32[]{:S(2)}) %collective-permute-start.46) | collective-permute-done | bytes 2162720 | tf_op jit(solution)/shard_map/ppermute | solution.py:320
  766.4 4.7 add_convert_fusion
  786.4 5.5 collective-permute-done.47
  796.5 41.8 %collective-permute-done.44 = bf16[2,3,704,256]{3,2,0,1:T(8,128)(2,1)} collective-permute-done((bf16[2,3,704,256]{3,2,0,1:T(8,128)(2,1)}, bf16[2,3,704,256]{3,2,0,1:T(8,128)(2,1)}, u32[]{:S(2)}, u32[]{:S(2)}) %collective-permute-start.44) | collective-permute-done | bytes 2162720 | tf_op jit(solution)/shard_map/ppermute | solution.py:320
  854.8 4.4 fusion.25
  865.0 4.3 copy-done
  870.9 9.8 collective-permute-done.28
  880.7 4.8 fusion.17
  912.4 5.6 copy.503
  923.6 7.0 fusion.20
  936.1 13.5 %concatenate.103 = f32[8,272,512]{2,1,0:T(8,128)} concatenate(f32[8,256,512]{2,1,0:T(8,128)} %fusion.20, f32[8,9,512]{2,1,0:T(8,128)} %pad.48, f32[8,1,512]{2,1,0:T(1,128)} %pad.49, f32[8,2,512]{2,1,0:T(2,128)} %pad.50, f32[8,4,512]{2,1,0:T(4,128)} %broadcast_in_dim.138), dimensions={1} | concatenate | bytes 8912896 | tf_op jit(solution)/shard_map/concatenate | solution.py:636
  963.5 15.5 %collective-permute-done.37 = bf16[1,2,2,272,512]{4,3,2,1,0:T(8,128)(2,1)S(1)} collective-permute-done((bf16[1,2,2,272,512]{4,3,2,1,0:T(8,128)(2,1)S(1)}, bf16[1,2,2,272,512]{4,3,2,1,0:T(8,128)(2,1)S(1)}, u32[]{:S(2)}, u32[]{:S(2)}) %collective-permute-start.37) | collective-permute-done | bytes 1114144 | tf_op jit(solution)/shard_map/ppermute | solution.py:320
  995.9 9.7 dynamic_update_slice.174
  1012.6 9.7 dynamic_update_slice.175
  1026.2 11.9 %all-gather.2 = f32[4,2,256]{2,1,0:T(2,128)S(1)} all-gather(f32[1,2,256]{2,1,0:T(2,128)S(1)} %slice_bitcast_fusion.25), channel_id=2, replica_groups=mesh['dp'=8,'tensor'=4] {'tensor'}, dimensions={0}, use_global_device_ids=true | all-gather | bytes 10240 | tf_op jit(solution)/shard_map/all_gather | solution.py:671
  (579 shorter events, 337.8 us)
Async XLA Ops:
  7.2 92.8 %all-gather.8.cloned.1.call-start = ((), (), s32[]{:S(2)}) async-start(), calls=%async_computation.4 | async-start | bytes 2621440 | tf_op jit(solution)/shard_map/all_gather | solution.py:357
  11.0 48.6 %collective-permute-start.4 = (bf16[256,512]{1,0:T(8,128)(2,1)}, bf16[256,512]{1,0:T(8,128)(2,1)}, u32[]{:S(2)}, u32[]{:S(2)}) collective-permute-start(bf16[256,512]{1,0:T(8,128)(2,1)} %bitcast.24), channel_id=1, source_target_pairs={{0,4},{4,0},{8,12},{12,8},{16,20},{20,16},{24,28},{28,24},{1,5},{5... | collective-permute-start | bytes 786440 | tf_op jit(solution)/shard_map/ppermute | solution.py:320
  25.8 47.2 %collective-permute-start.1 = (bf16[272,512]{1,0:T(8,128)(2,1)}, bf16[272,512]{1,0:T(8,128)(2,1)}, u32[]{:S(2)}, u32[]{:S(2)}) collective-permute-start(bf16[272,512]{1,0:T(8,128)(2,1)} %bitcast.15), channel_id=1, source_target_pairs={{0,4},{4,0},{8,12},{12,8},{16,20},{20,16},{24,28},{28,24},{1,5},{5... | collective-permute-start | bytes 835592 | tf_op jit(solution)/shard_map/ppermute | solution.py:320
  25.9 207.8 %reduce-scatter.5.cloned.1.call-start = ((), (), s32[]{:S(2)}) async-start(), calls=%async_computation.5 | async-start | bytes 2621440 | tf_op jit(solution)/shard_map/reduce_scatter | solution.py:459
  30.6 81.0 %collective-permute-start.10 = (bf16[2,3,352,256]{3,2,1,0:T(8,128)(2,1)}, bf16[2,3,352,256]{3,2,1,0:T(8,128)(2,1)}, u32[]{:S(2)}, u32[]{:S(2)}) collective-permute-start(bf16[2,3,352,256]{3,2,1,0:T(8,128)(2,1)} %pad_maximum_fusion.17), channel_id=1, source_target_pairs={{0,4},{4,0},{8,12},{12,8},{16,20},{20,16},{24,28},{28,24},{1,5},{5... | collective-permute-start | bytes 3244040 | tf_op jit(solution)/shard_map/ppermute | solution.py:320
  32.2 67.9 %collective-permute-start.9 = (bf16[2,3,352,256]{3,2,1,0:T(8,128)(2,1)}, bf16[2,3,352,256]{3,2,1,0:T(8,128)(2,1)}, u32[]{:S(2)}, u32[]{:S(2)}) collective-permute-start(bf16[2,3,352,256]{3,2,1,0:T(8,128)(2,1)} %pad_maximum_fusion.16), channel_id=1, source_target_pairs={{0,4},{4,0},{8,12},{12,8},{16,20},{20,16},{24,28},{28,24},{1,5},{5... | collective-permute-start | bytes 3244040 | tf_op jit(solution)/shard_map/ppermute | solution.py:320
  32.2 26.7 %collective-permute-start.7 = (s32[512]{0:T(512)}, s32[512]{0:T(512)}, u32[]{:S(2)}, u32[]{:S(2)}) collective-permute-start(s32[512]{0:T(512)} %param.35), channel_id=1, source_target_pairs={{0,4},{4,0},{8,12},{12,8},{16,20},{20,16},{24,28},{28,24},{1,5},{5... | collective-permute-start | bytes 6152 | tf_op jit(solution)/shard_map/ppermute | solution.py:320
  58.9 37.3 %collective-permute-start.8 = (bf16[2,3,352,256]{3,2,1,0:T(8,128)(2,1)}, bf16[2,3,352,256]{3,2,1,0:T(8,128)(2,1)}, u32[]{:S(2)}, u32[]{:S(2)}) collective-permute-start(bf16[2,3,352,256]{3,2,1,0:T(8,128)(2,1)} %pad_maximum_fusion.15), channel_id=1, source_target_pairs={{0,4},{4,0},{8,12},{12,8},{16,20},{20,16},{24,28},{28,24},{1,5},{5... | collective-permute-start | bytes 3244040 | tf_op jit(solution)/shard_map/ppermute | solution.py:320
  87.2 28.1 %collective-permute-start.6 = (bf16[2,1,2,256,512]{3,2,1,0,4:T(2,128)(2,1)}, bf16[2,1,2,256,512]{3,2,1,0,4:T(2,128)(2,1)}, u32[]{:S(2)}, u32[]{:S(2)}) collective-permute-start(bf16[2,1,2,256,512]{3,2,1,0,4:T(2,128)(2,1)} %constant_dynamic-update-slice_fusion.18), channel_id=1, source_target_pairs={{0,8},{4,12},{8,0},{12,4},{16,24},{20,28},{24,16},{28,20},{1,9},{5... | collective-permute-start | bytes 3145736 | tf_op jit(solution)/shard_map/ppermute | solution.py:320
  94.3 28.6 %collective-permute-start.3 = (bf16[1,2,2,272,512]{4,3,2,1,0:T(8,128)(2,1)S(1)}, bf16[1,2,2,272,512]{4,3,2,1,0:T(8,128)(2,1)}, u32[]{:S(2)}, u32[]{:S(2)}) collective-permute-start(bf16[1,2,2,272,512]{4,3,2,1,0:T(8,128)(2,1)S(1)} %constant_dynamic-update-slice_fusion.22), channel_id=1, source_target_pairs={{0,16},{4,20},{8,24},{12,28},{16,0},{20,4},{24,8},{28,12},{1,17},{... | collective-permute-start | bytes 3342344 | tf_op jit(solution)/shard_map/ppermute | solution.py:320
  99.5 37.3 %collective-permute-start.11 = (bf16[3,352,512]{2,1,0:T(8,128)(2,1)}, bf16[3,352,512]{2,1,0:T(8,128)(2,1)}, u32[]{:S(2)}, u32[]{:S(2)}) collective-permute-start(bf16[3,352,512]{2,1,0:T(8,128)(2,1)} %dynamic-slice_bitcast_fusion.5), channel_id=1, source_target_pairs={{0,8},{4,12},{8,0},{12,4},{16,24},{20,28},{24,16},{28,20},{1,9},{5... | collective-permute-start | bytes 3244040 | tf_op jit(solution)/shard_map/ppermute | solution.py:320
  100.0 61.0 %collective-permute-start = (bf16[512,2048]{1,0:T(8,128)(2,1)}, bf16[512,2048]{1,0:T(8,128)(2,1)S(1)}, u32[]{:S(2)}, u32[]{:S(2)}) collective-permute-start(bf16[512,2048]{1,0:T(8,128)(2,1)} %all-gather.8.cloned.1.call-done), channel_id=1, source_target_pairs={{0,4},{4,0},{8,12},{12,8},{16,20},{20,16},{24,28},{28,24},{1,5},{5... | collective-permute-start | bytes 6291464 | tf_op jit(solution)/shard_map/ppermute | solution.py:320
  111.5 47.2 %collective-permute-start.12 = (bf16[3,352,512]{2,1,0:T(8,128)(2,1)}, bf16[3,352,512]{2,1,0:T(8,128)(2,1)}, u32[]{:S(2)}, u32[]{:S(2)}) collective-permute-start(bf16[3,352,512]{2,1,0:T(8,128)(2,1)} %dynamic-slice_bitcast_fusion.4), channel_id=1, source_target_pairs={{0,8},{4,12},{8,0},{12,4},{16,24},{20,28},{24,16},{28,20},{1,9},{5... | collective-permute-start | bytes 3244040 | tf_op jit(solution)/shard_map/ppermute | solution.py:320
  191.5 89.2 %all-gather.12.cloned.1.call-start = ((), (), s32[]{:S(2)}) async-start(), calls=%async_computation.7 | async-start | bytes 2621440 | tf_op jit(solution)/shard_map/all_gather | solution.py:379
  192.2 136.1 %all-gather.10.cloned.1.call-start = ((), (), s32[]{:S(2)}) async-start(), calls=%async_computation.6 | async-start | bytes 2621440 | tf_op jit(solution)/shard_map/all_gather | solution.py:469
  192.3 49.5 %collective-permute-start.15 = (bf16[3,352,1024]{2,1,0:T(8,128)(2,1)}, bf16[3,352,1024]{2,1,0:T(8,128)(2,1)}, u32[]{:S(2)}, u32[]{:S(2)}) collective-permute-start(bf16[3,352,1024]{2,1,0:T(8,128)(2,1)} %constant_dynamic-update-slice_fusion.12), channel_id=1, source_target_pairs={{0,16},{4,20},{8,24},{12,28},{16,0},{20,4},{24,8},{28,12},{1,17},{... | collective-permute-start | bytes 6488072 | tf_op jit(solution)/shard_map/ppermute | solution.py:320
  195.2 25.7 %collective-permute-start.14 = (bf16[3,352,512]{2,1,0:T(8,128)(2,1)S(1)}, bf16[3,352,512]{2,1,0:T(8,128)(2,1)S(1)}, u32[]{:S(2)}, u32[]{:S(2)}) collective-permute-start(bf16[3,352,512]{2,1,0:T(8,128)(2,1)S(1)} %dynamic-slice_bitcast_fusion.3), channel_id=1, source_target_pairs={{0,8},{4,12},{8,0},{12,4},{16,24},{20,28},{24,16},{28,20},{1,9},{5... | collective-permute-start | bytes 3244040 | tf_op jit(solution)/shard_map/ppermute | solution.py:320
  242.9 401.3 %reduce-scatter.7.cloned.1.call-start = ((), (), s32[]{:S(2)}) async-start(), calls=%async_computation.8 | async-start | bytes 2785280 | tf_op jit(solution)/shard_map/reduce_scatter | solution.py:459
  243.1 48.6 %collective-permute-start.18 = (bf16[3,352,1024]{2,1,0:T(8,128)(2,1)}, bf16[3,352,1024]{2,1,0:T(8,128)(2,1)}, u32[]{:S(2)}, u32[]{:S(2)}) collective-permute-start(bf16[3,352,1024]{2,1,0:T(8,128)(2,1)} %constant_dynamic-update-slice_fusion.11), channel_id=1, source_target_pairs={{0,16},{4,20},{8,24},{12,28},{16,0},{20,4},{24,8},{28,12},{1,17},{... | collective-permute-start | bytes 6488072 | tf_op jit(solution)/shard_map/ppermute | solution.py:320
  280.7 47.7 %collective-permute-start.19 = (bf16[512,2048]{1,0:T(8,128)(2,1)}, bf16[512,2048]{1,0:T(8,128)(2,1)}, u32[]{:S(2)}, u32[]{:S(2)}) collective-permute-start(bf16[512,2048]{1,0:T(8,128)(2,1)} %all-gather.12.cloned.1.call-done), channel_id=1, source_target_pairs={{0,8},{4,12},{8,0},{12,4},{16,24},{20,28},{24,16},{28,20},{1,9},{5... | collective-permute-start | bytes 6291464 | tf_op jit(solution)/shard_map/ppermute | solution.py:320
  328.4 50.5 %collective-permute-start.24 = (bf16[512,2048]{1,0:T(8,128)(2,1)}, bf16[512,2048]{1,0:T(8,128)(2,1)}, u32[]{:S(2)}, u32[]{:S(2)}) collective-permute-start(bf16[512,2048]{1,0:T(8,128)(2,1)} %all-gather.10.cloned.1.call-done), channel_id=1, source_target_pairs={{0,8},{4,12},{8,0},{12,4},{16,24},{20,28},{24,16},{28,20},{1,9},{5... | collective-permute-start | bytes 6291464 | tf_op jit(solution)/shard_map/ppermute | solution.py:320
  329.8 60.6 %collective-permute-start.22 = (bf16[3,352,1024]{2,1,0:T(8,128)(2,1)S(1)}, bf16[3,352,1024]{2,1,0:T(8,128)(2,1)}, u32[]{:S(2)}, u32[]{:S(2)}) collective-permute-start(bf16[3,352,1024]{2,1,0:T(8,128)(2,1)S(1)} %constant_dynamic-update-slice_fusion.10), channel_id=1, source_target_pairs={{0,16},{4,20},{8,24},{12,28},{16,0},{20,4},{24,8},{28,12},{1,17},{... | collective-permute-start | bytes 6488072 | tf_op jit(solution)/shard_map/ppermute | solution.py:320
  331.3 62.8 %collective-permute-start.21 = (bf16[512,2048]{1,0:T(8,128)(2,1)}, bf16[512,2048]{1,0:T(8,128)(2,1)}, u32[]{:S(2)}, u32[]{:S(2)}) collective-permute-start(bf16[512,2048]{1,0:T(8,128)(2,1)} %all-gather.12.cloned.1.call-done), channel_id=1, source_target_pairs={{0,4},{4,0},{8,12},{12,8},{16,20},{20,16},{24,28},{28,24},{1,5},{5... | collective-permute-start | bytes 6291464 | tf_op jit(solution)/shard_map/ppermute | solution.py:320
  331.3 44.1 %collective-permute-start.16 = (s32[8,512]{1,0:T(8,128)S(1)}, s32[8,512]{1,0:T(8,128)S(1)}, u32[]{:S(2)}, u32[]{:S(2)}) collective-permute-start(s32[8,512]{1,0:T(8,128)S(1)} %get-tuple-element.314), channel_id=1, source_target_pairs={{0,8},{4,12},{8,0},{12,4},{16,24},{20,28},{24,16},{28,20},{1,9},{5... | collective-permute-start | bytes 49160 | tf_op jit(solution)/shard_map/ppermute | solution.py:320
  375.4 24.4 %collective-permute-start.26 = (bf16[512,2048]{1,0:T(8,128)(2,1)}, bf16[512,2048]{1,0:T(8,128)(2,1)}, u32[]{:S(2)}, u32[]{:S(2)}) collective-permute-start(bf16[512,2048]{1,0:T(8,128)(2,1)} %collective-permute-done.19), channel_id=1, source_target_pairs={{0,4},{4,0},{8,12},{12,8},{16,20},{20,16},{24,28},{28,24},{1,5},{5... | collective-permute-start | bytes 6291464 | tf_op jit(solution)/shard_map/ppermute | solution.py:320
  376.6 28.1 %collective-permute-start.20 = (bf16[512,2048]{1,0:T(8,128)(2,1)}, bf16[512,2048]{1,0:T(8,128)(2,1)}, u32[]{:S(2)}, u32[]{:S(2)}) collective-permute-start(bf16[512,2048]{1,0:T(8,128)(2,1)} %all-gather.10.cloned.1.call-done), channel_id=1, source_target_pairs={{0,4},{4,0},{8,12},{12,8},{16,20},{20,16},{24,28},{28,24},{1,5},{5... | collective-permute-start | bytes 6291464 | tf_op jit(solution)/shard_map/ppermute | solution.py:320
  378.9 29.9 %collective-permute-start.25 = (bf16[512,2048]{1,0:T(8,128)(2,1)}, bf16[512,2048]{1,0:T(8,128)(2,1)}, u32[]{:S(2)}, u32[]{:S(2)}) collective-permute-start(bf16[512,2048]{1,0:T(8,128)(2,1)} %collective-permute-done.24), channel_id=1, source_target_pairs={{0,4},{4,0},{8,12},{12,8},{16,20},{20,16},{24,28},{28,24},{1,5},{5... | collective-permute-start | bytes 6291464 | tf_op jit(solution)/shard_map/ppermute | solution.py:320
  464.8 55.4 %collective-permute-start.30 = (bf16[512,2048]{1,0:T(8,128)(2,1)S(1)}, bf16[512,2048]{1,0:T(8,128)(2,1)}, u32[]{:S(2)}, u32[]{:S(2)}) collective-permute-start(bf16[512,2048]{1,0:T(8,128)(2,1)S(1)} %slice_bitcast_fusion.4), channel_id=1, source_target_pairs={{0,4},{4,0},{8,12},{12,8},{16,20},{20,16},{24,28},{28,24},{1,5},{5... | collective-permute-start | bytes 6291464 | tf_op jit(solution)/shard_map/ppermute | solution.py:320
  519.8 54.3 %collective-permute-start.29 = (bf16[512,2048]{1,0:T(8,128)(2,1)}, bf16[512,2048]{1,0:T(8,128)(2,1)}, u32[]{:S(2)}, u32[]{:S(2)}) collective-permute-start(bf16[512,2048]{1,0:T(8,128)(2,1)} %slice_bitcast_fusion.6), channel_id=1, source_target_pairs={{0,4},{4,0},{8,12},{12,8},{16,20},{20,16},{24,28},{28,24},{1,5},{5... | collective-permute-start | bytes 6291464 | tf_op jit(solution)/shard_map/ppermute | solution.py:320
  522.6 51.5 %collective-permute-start.31 = (bf16[512,2048]{1,0:T(8,128)(2,1)S(1)}, bf16[512,2048]{1,0:T(8,128)(2,1)}, u32[]{:S(2)}, u32[]{:S(2)}) collective-permute-start(bf16[512,2048]{1,0:T(8,128)(2,1)S(1)} %fusion.13), channel_id=1, source_target_pairs={{0,8},{4,12},{8,0},{12,4},{16,24},{20,28},{24,16},{28,20},{1,9},{5... | collective-permute-start | bytes 6291464 | tf_op jit(solution)/shard_map/ppermute | solution.py:320
  541.9 31.3 %collective-permute-start.34 = (bf16[512,128]{1,0:T(8,128)(2,1)S(1)}, bf16[512,128]{1,0:T(8,128)(2,1)S(1)}, u32[]{:S(2)}, u32[]{:S(2)}) collective-permute-start(bf16[512,128]{1,0:T(8,128)(2,1)S(1)} %fusion.60), channel_id=1, source_target_pairs={{0,8},{4,12},{8,0},{12,4},{16,24},{20,28},{24,16},{28,20},{1,9},{5... | collective-permute-start | bytes 393224 | tf_op jit(solution)/shard_map/ppermute | solution.py:320
  579.8 195.0 %all-gather.14.cloned.1.call-start = ((), (), s32[]{:S(2)}) async-start(), calls=%async_computation.9 | async-start | bytes 2785280 | tf_op jit(solution)/shard_map/all_gather | solution.py:587
  619.6 146.9 %collective-permute-start.43 = (bf16[1,2,2,3,704,256]{5,4,3,2,1,0:T(8,128)(2,1)}, bf16[1,2,2,3,704,256]{5,4,3,2,1,0:T(8,128)(2,1)}, u32[]{:S(2)}, u32[]{:S(2)}) collective-permute-start(bf16[1,2,2,3,704,256]{5,4,3,2,1,0:T(8,128)(2,1)} %constant_dynamic-slice_fusion.3), channel_id=1, source_target_pairs={{0,16},{4,20},{8,24},{12,28},{16,0},{20,4},{24,8},{28,12},{1,17},{... | collective-permute-start | bytes 12976136 | tf_op jit(solution)/shard_map/ppermute | solution.py:320
  652.1 387.3 %reduce-scatter.11.cloned.1.call-start = ((), (), s32[]{:S(2)}) async-start(), calls=%async_computation.11 | async-start | bytes 2621440 | tf_op jit(solution)/shard_map/reduce_scatter | solution.py:459
  655.3 105.6 %collective-permute-start.46 = (bf16[1,2,2,3,352,256]{5,4,3,2,1,0:T(8,128)(2,1)}, bf16[1,2,2,3,352,256]{5,4,3,2,1,0:T(8,128)(2,1)}, u32[]{:S(2)}, u32[]{:S(2)}) collective-permute-start(bf16[1,2,2,3,352,256]{5,4,3,2,1,0:T(8,128)(2,1)} %constant_dynamic-slice_fusion), channel_id=1, source_target_pairs={{0,16},{4,20},{8,24},{12,28},{16,0},{20,4},{24,8},{28,12},{1,17},{... | collective-permute-start | bytes 6488072 | tf_op jit(solution)/shard_map/ppermute | solution.py:320
  694.6 84.5 %collective-permute-start.27 = (bf16[512,2048]{1,0:T(8,128)(2,1)}, bf16[512,2048]{1,0:T(8,128)(2,1)}, u32[]{:S(2)}, u32[]{:S(2)}) collective-permute-start(bf16[512,2048]{1,0:T(8,128)(2,1)} %slice_bitcast_fusion.8), channel_id=1, source_target_pairs={{0,4},{4,0},{8,12},{12,8},{16,20},{20,16},{24,28},{28,24},{1,5},{5... | collective-permute-start | bytes 6291464 | tf_op jit(solution)/shard_map/ppermute | solution.py:320
  764.9 27.0 %collective-permute-start.47 = (bf16[2,3,352,256]{3,2,1,0:T(8,128)(2,1)}, bf16[2,3,352,256]{3,2,1,0:T(8,128)(2,1)S(1)}, u32[]{:S(2)}, u32[]{:S(2)}) collective-permute-start(bf16[2,3,352,256]{3,2,1,0:T(8,128)(2,1)} %dynamic-slice_bitcast_fusion.2), channel_id=1, source_target_pairs={{0,8},{4,12},{8,0},{12,4},{16,24},{20,28},{24,16},{28,20},{1,9},{5... | collective-permute-start | bytes 3244040 | tf_op jit(solution)/shard_map/ppermute | solution.py:320
  774.3 64.0 %collective-permute-start.44 = (bf16[2,3,704,256]{3,2,0,1:T(8,128)(2,1)}, bf16[2,3,704,256]{3,2,0,1:T(8,128)(2,1)}, u32[]{:S(2)}, u32[]{:S(2)}) collective-permute-start(bf16[2,3,704,256]{3,2,0,1:T(8,128)(2,1)} %bitcast.375), channel_id=1, source_target_pairs={{0,8},{4,12},{8,0},{12,4},{16,24},{20,28},{24,16},{28,20},{1,9},{5... | collective-permute-start | bytes 6488072 | tf_op jit(solution)/shard_map/ppermute | solution.py:320
  777.1 65.2 %collective-permute-start.35 = (bf16[512,2048]{1,0:T(8,128)(2,1)S(1)}, bf16[512,2048]{1,0:T(8,128)(2,1)S(1)}, u32[]{:S(2)}, u32[]{:S(2)}) collective-permute-start(bf16[512,2048]{1,0:T(8,128)(2,1)S(1)} %get-tuple-element.266), channel_id=1, source_target_pairs={{0,4},{4,0},{8,12},{12,8},{16,20},{20,16},{24,28},{28,24},{1,5},{5... | collective-permute-start | bytes 6291464 | tf_op jit(solution)/shard_map/ppermute | solution.py:320
  779.1 91.8 %collective-permute-start.23 = (bf16[512,2048]{1,0:T(8,128)(2,1)}, bf16[512,2048]{1,0:T(8,128)(2,1)}, u32[]{:S(2)}, u32[]{:S(2)}) collective-permute-start(bf16[512,2048]{1,0:T(8,128)(2,1)} %slice_bitcast_fusion.10), channel_id=1, source_target_pairs={{0,4},{4,0},{8,12},{12,8},{16,20},{20,16},{24,28},{28,24},{1,5},{5... | collective-permute-start | bytes 6291464 | tf_op jit(solution)/shard_map/ppermute | solution.py:320
  784.6 96.0 %collective-permute-start.28 = (bf16[512,2048]{1,0:T(8,128)(2,1)}, bf16[512,2048]{1,0:T(8,128)(2,1)}, u32[]{:S(2)}, u32[]{:S(2)}) collective-permute-start(bf16[512,2048]{1,0:T(8,128)(2,1)} %fusion.16), channel_id=1, source_target_pairs={{0,8},{4,12},{8,0},{12,4},{16,24},{20,28},{24,16},{28,20},{1,9},{5... | collective-permute-start | bytes 6291464 | tf_op jit(solution)/shard_map/ppermute | solution.py:320
  793.3 92.1 %collective-permute-start.48 = (bf16[2,3,352,256]{3,2,1,0:T(8,128)(2,1)}, bf16[2,3,352,256]{3,2,1,0:T(8,128)(2,1)}, u32[]{:S(2)}, u32[]{:S(2)}) collective-permute-start(bf16[2,3,352,256]{3,2,1,0:T(8,128)(2,1)} %get-tuple-element.267), channel_id=1, source_target_pairs={{0,4},{4,0},{8,12},{12,8},{16,20},{20,16},{24,28},{28,24},{1,5},{5... | collective-permute-start | bytes 3244040 | tf_op jit(solution)/shard_map/ppermute | solution.py:320
  842.3 51.2 %collective-permute-start.45 = (bf16[2,3,704,256]{3,2,0,1:T(8,128)(2,1)}, bf16[2,3,704,256]{3,2,0,1:T(8,128)(2,1)}, u32[]{:S(2)}, u32[]{:S(2)}) collective-permute-start(bf16[2,3,704,256]{3,2,0,1:T(8,128)(2,1)} %get-tuple-element.259), channel_id=1, source_target_pairs={{0,4},{4,0},{8,12},{12,8},{16,20},{20,16},{24,28},{28,24},{1,5},{5... | collective-permute-start | bytes 6488072 | tf_op jit(solution)/shard_map/ppermute | solution.py:320
  870.9 30.2 %collective-permute-start.36 = (bf16[512,2048]{1,0:T(8,128)(2,1)}, bf16[512,2048]{1,0:T(8,128)(2,1)}, u32[]{:S(2)}, u32[]{:S(2)}) collective-permute-start(bf16[512,2048]{1,0:T(8,128)(2,1)} %fusion.24), channel_id=1, source_target_pairs={{0,4},{4,0},{8,12},{12,8},{16,20},{20,16},{24,28},{28,24},{1,5},{5... | collective-permute-start | bytes 6291464 | tf_op jit(solution)/shard_map/ppermute | solution.py:320
  904.8 136.0 %reduce-scatter.9.cloned.1.call-start = ((), (), s32[]{:S(2)}) async-start(), calls=%async_computation.10 | async-start | bytes 2621440 | tf_op jit(solution)/shard_map/reduce_scatter | solution.py:459
  920.6 38.6 %collective-permute-start.40 = (bf16[2,1,2,256,512]{4,3,2,1,0:T(8,128)(2,1)}, bf16[2,1,2,256,512]{4,3,2,1,0:T(8,128)(2,1)}, u32[]{:S(2)}, u32[]{:S(2)}) collective-permute-start(bf16[2,1,2,256,512]{4,3,2,1,0:T(8,128)(2,1)} %dynamic-slice_convert_fusion.1), channel_id=1, source_target_pairs={{0,8},{4,12},{8,0},{12,4},{16,24},{20,28},{24,16},{28,20},{1,9},{5... | collective-permute-start | bytes 3145736 | tf_op jit(solution)/shard_map/ppermute | solution.py:320
  951.4 27.6 %collective-permute-start.37 = (bf16[1,2,2,272,512]{4,3,2,1,0:T(8,128)(2,1)S(1)}, bf16[1,2,2,272,512]{4,3,2,1,0:T(8,128)(2,1)S(1)}, u32[]{:S(2)}, u32[]{:S(2)}) collective-permute-start(bf16[1,2,2,272,512]{4,3,2,1,0:T(8,128)(2,1)S(1)} %dynamic-slice_convert_fusion), channel_id=1, source_target_pairs={{0,16},{4,20},{8,24},{12,28},{16,0},{20,4},{24,8},{28,12},{1,17},{... | collective-permute-start | bytes 3342344 | tf_op jit(solution)/shard_map/ppermute | solution.py:320
  962.9 24.3 %collective-permute-start.41 = (bf16[1,1,2,256,512]{4,3,2,1,0:T(8,128)(2,1)}, bf16[1,1,2,256,512]{4,3,2,1,0:T(8,128)(2,1)}, u32[]{:S(2)}, u32[]{:S(2)}) collective-permute-start(bf16[1,1,2,256,512]{4,3,2,1,0:T(8,128)(2,1)} %dynamic-slice_convert_fusion.3), channel_id=1, source_target_pairs={{0,16},{4,20},{8,24},{12,28},{16,0},{20,4},{24,8},{28,12},{1,17},{... | collective-permute-start | bytes 1572872 | tf_op jit(solution)/shard_map/ppermute | solution.py:320
  (108 other events, 1225.0 us)
Sparse Core Ops, SparseCore 0:
  26.0 44.2 all-gather.7
  191.6 42.0 reduce-scatter.4
  235.4 45.2 all-gather.11
  282.8 44.6 all-gather.9
  579.9 45.2 reduce-scatter.6
  652.2 46.7 all-gather.13
  904.9 42.9 reduce-scatter.10
  987.3 43.0 reduce-scatter.8

commit v2 on v1

--- a/solution.py
+++ b/solution.py
@@ -273,7 +273,542 @@
     )(left_a, right_a, left_b, right_b)
 
 
-def local(
+MESH = pl.DeviceIdType.MESH
+
+
+class Copies:
+    def __init__(self, send, recv, here):
+        self.send, self.recv, self.here = send, recv, here
+        self.remote_count = self.local_count = 0
+
+    def remote(self, src, dst, **device):
+        k = self.remote_count
+        self.remote_count += 1
+        return pltpu.make_async_remote_copy(
+            src_ref=src,
+            dst_ref=dst,
+            send_sem=self.send.at[k],
+            recv_sem=self.recv.at[k],
+            device_id=device,
+            device_id_type=MESH,
+        )
+
+    def local(self, src, dst):
+        k = self.local_count
+        self.local_count += 1
+        return pltpu.make_async_copy(src, dst, self.here.at[k])
+
+
+class Line:
+    def __init__(self, copies, buffer, z, depth, rows):
+        self.z, self.depth = z, depth
+
+        def piece(p):
+            return buffer.at[pl.ds(pl.multiple_of(p * rows, rows), rows)]
+
+        def make(k, sign):
+            p = z - sign * k
+            return copies.remote(piece(p), piece(p), tensor=z + sign)
+
+        self.ups = [make(k, 1) for k in range(depth - 1)]
+        self.downs = [make(k, -1) for k in range(depth - 1)]
+
+    def sends(self, k):
+        z, top = self.z, self.depth - 1
+        return (
+            (self.ups[k], jnp.logical_and(z < top, z >= k)),
+            (self.downs[k], jnp.logical_and(z > 0, z + k <= top)),
+        )
+
+    def begin(self):
+        for copy, there in self.sends(0):
+            pl.when(there)(copy.start)
+
+    def step(self, k, each=None):
+        z, top = self.z, self.depth - 1
+        arrivals = (
+            (self.ups[k - 1], z >= k, z - k),
+            (self.downs[k - 1], z + k <= top, z + k),
+        )
+        onward = self.sends(k) if k < top else (None, None)
+        for (copy, there, p), further in zip(arrivals, onward):
+
+            def arrive(copy=copy, p=p):
+                copy.wait_recv()
+                if each is not None:
+                    each(k, p)
+
+            pl.when(there)(arrive)
+            if further is not None:
+                pl.when(further[1])(further[0].start)
+
+    def finish(self):
+        for k in range(self.depth - 1):
+            for copy, there in self.sends(k):
+                pl.when(there)(copy.wait_send)
+
+
+def peer_of(me, r):
+    out, bit = me, 1
+    while bit <= r:
+        if r & bit:
+            out = out + bit - 2 * bit * (me // bit % 2)
+        bit *= 2
+    return out
+
+
+def greet(me, z, dp, depth):
+    barrier = pltpu.get_barrier_semaphore()
+    for r in range(1, dp):
+        pl.semaphore_signal(barrier, inc=1, device_id={"dp": peer_of(me, r)}, device_id_type=MESH)
+    for r in range(1, depth):
+        pl.semaphore_signal(
+            barrier, inc=1, device_id={"tensor": (z + r) % depth}, device_id_type=MESH
+        )
+    pl.semaphore_wait(barrier, dp - 1 + depth - 1)
+
+
+def spin(field, cos_rows, sin_rows):
+    return field * cos_rows + pltpu.roll(field, field.shape[-1] // 2, 1) * sin_rows
+
+
+def forward_body(
+    sizes,
+    codes_ref,
+    misc_ref,
+    gains_ref,
+    cos_ref,
+    sin_ref,
+    tokens_ref,
+    outgrad_ref,
+    wq_ref,
+    wk_ref,
+    wv_ref,
+    wo_ref,
+    eg_ref,
+    eu_ref,
+    ed_ref,
+    sg_ref,
+    su_ref,
+    sd_ref,
+    hidden_ref,
+    norm_ref,
+    grads_ref,
+    gateup_ref,
+    down_ref,
+    codes_all,
+    misc_all,
+    gain_rows,
+    tok,
+    weights,
+    qkv_ref,
+    probs_ref,
+    mix_ref,
+    fnorm,
+    part,
+    part_in,
+    scatter_in,
+    gains_all,
+    zeros,
+    send,
+    recv,
+    here,
+):
+    dp, depth, experts, hidden_units, head = sizes
+    me, z = lax.axis_index("dp"), lax.axis_index("tensor")
+    core, x = me % 2, (me // 2) % 2
+    bits = [2**k for k in range(dp.bit_length() - 1)]
+    upper = bits[2:]
+    rows, width = tokens_ref.shape
+    seq_len = rows * depth
+    slice_width = width // dp
+    routed = experts // 4
+    c = Copies(send, recv, here)
+
+    def bit_of(bit):
+        return (me // bit) % 2
+
+    greet(me, z, dp, depth)
+
+    first = []
+    own_codes = c.local(codes_ref, codes_all.at[0])
+    own_misc = c.local(misc_ref, misc_all.at[me])
+    own_gains = c.local(gains_ref, gains_all.at[z, me])
+    for copy in (own_codes, own_misc, own_gains):
+        copy.start()
+    for r in range(1, 4):
+        first.append(c.remote(codes_ref, codes_all.at[r], dp=peer_of(me, r)))
+    gain_copies = [c.remote(gains_ref, gains_all.at[z, me], dp=peer_of(me, r)) for r in range(1, dp)]
+    misc_copies = [c.remote(misc_ref, misc_all.at[me], dp=peer_of(me, r)) for r in range(1, dp)]
+    for copy in gain_copies + misc_copies + first:
+        copy.start()
+
+    def piece(buffer, p):
+        return buffer.at[pl.ds(pl.multiple_of(p * rows, rows), rows)]
+
+    own_tok = c.local(tokens_ref, piece(tok.at[0], z))
+    own_tok.start()
+    own_grad = c.local(outgrad_ref, piece(grads_ref.at[0], z))
+    own_grad.start()
+
+    def columns(k, n):
+        return pl.ds(pl.multiple_of(k * n, n), n)
+
+    pair = wq_ref.shape[1] // 2
+    own_at = tuple(bit_of(bit) for bit in reversed(bits))
+    core_copies = []
+    for k, w in enumerate((wq_ref, wk_ref, wv_ref, wo_ref)):
+        place = weights.at[own_at + (slice(None), pl.ds(k * pair, pair))]
+        core_copies.append(c.remote(w.at[:, columns(1 - core, pair)], place, dp=peer_of(me, 1)))
+        core_copies.append(c.local(w.at[:, columns(core, pair)], place))
+    for copy in core_copies:
+        copy.start()
+
+    own_tok.wait()
+    tok_line = Line(c, tok.at[0], z, depth, rows)
+    tok_line.begin()
+    tok_pass = [c.remote(tokens_ref, piece(tok.at[1], z), dp=peer_of(me, 1))]
+    tok_pass[0].start()
+
+    zeros[...] = jnp.zeros_like(zeros)
+    pad = zeros.shape[1]
+    pads = [c.local(zeros, down_ref.at[:, 0, pl.ds(hidden_units, pad)])]
+    pads += [c.local(zeros, gateup_ref.at[:, k, pl.ds(hidden_units, pad)]) for k in range(2)]
+    matrices = ((ed_ref, sd_ref, down_ref, 0), (eg_ref, sg_ref, gateup_ref, 0), (eu_ref, su_ref, gateup_ref, 1))
+    slab = columns(me, slice_width)
+
+    def group_copies(routed_src, shared_src, dst, k, r):
+        group = (peer_of(me, r)) % 4
+        many = (
+            routed_src.at[pl.ds(group * routed, routed)],
+            dst.at[pl.ds(0, routed), k, pl.ds(0, hidden_units), slab],
+        )
+        one = (shared_src.at[group], dst.at[routed, k, pl.ds(0, hidden_units), slab])
+        if r == 0:
+            return [c.local(*many), c.local(*one)]
+        return [c.remote(*many, dp=peer_of(me, r)), c.remote(*one, dp=peer_of(me, r))]
+
+    near = [[copy for r in (0, 1) for copy in group_copies(*m, r)] for m in matrices]
+    far = [[copy for r in (2, 3) for copy in group_copies(*m, r)] for m in matrices]
+
+    def upper_copies(dst, k):
+        copies = []
+        for bit in upper:
+            n = bit * slice_width
+            cols = pl.ds(pl.multiple_of(me // bit * n, n), n)
+            place = dst.at[:, k, pl.ds(0, hidden_units), cols]
+            copies.append(c.remote(place, place, dp=peer_of(me, bit)))
+        return copies
+
+    over = [upper_copies(m[2], m[3]) for m in matrices]
+
+    for copy in core_copies:
+        copy.wait()
+
+    def weight_copies(order, half):
+        have, copies = [1], []
+        for bit in order:
+            index = tuple(
+                pl.ds(0, 2) if b in have else pl.ds(bit_of(b), 1) for b in reversed(bits)
+            )
+            place = weights.at[index + (slice(None), pl.ds(half * 2 * pair, 2 * pair))]
+            copies.append(c.remote(place, place, dp=peer_of(me, bit)))
+            have.append(bit)
+        return copies
+
+    qk_copies = weight_copies(bits[1:], 0)
+    vo_copies = weight_copies(bits[:0:-1], 1)
+    qk_copies[0].start()
+    vo_copies[0].start()
+    for copy in pads + [copy for m in near for copy in m]:
+        copy.start()
+
+    own_gains.wait()
+    for copy in gain_copies:
+        copy.wait_recv()
+    gain_spread = [
+        c.remote(gains_all.at[z], gains_all.at[z], tensor=(z + r) % depth) for r in range(1, depth)
+    ]
+    for copy in gain_spread:
+        copy.start()
+
+    def pass_on(buffer_from, buffer_to, passed):
+        ups = [c.remote(piece(buffer_from, z - k), piece(buffer_to, z - k), dp=peer_of(me, 1)) for k in range(1, depth)]
+        downs = [c.remote(piece(buffer_from, z + k), piece(buffer_to, z + k), dp=peer_of(me, 1)) for k in range(1, depth)]
+        for k in range(1, depth):
+            passed.append((ups[k - 1], z >= k))
+            passed.append((downs[k - 1], z + k <= depth - 1))
+
+        def each(k, p, up):
+            (ups if up else downs)[k - 1].start()
+
+        return each
+
+    tok_passed = []
+    pass_tok = pass_on(tok.at[0], tok.at[1], tok_passed)
+
+    def line_step(line, k, each):
+        top = depth - 1
+        onward = line.sends(k) if k < top else (None, None)
+        for up, copy, there, further in (
+            (True, line.ups[k - 1], z >= k, onward[0]),
+            (False, line.downs[k - 1], z + k <= top, onward[1]),
+        ):
+            pl.when(there)(copy.wait_recv)
+            if further is not None:
+                pl.when(further[1])(further[0].start)
+            if each is not None:
+                pl.when(there)(functools.partial(each, k, None, up))
+
+    line_step(tok_line, 1, pass_tok)
+    for k in range(1, len(bits) - 1):
+        qk_copies[k - 1].wait_recv()
+        qk_copies[k].start()
+        vo_copies[k - 1].wait_recv()
+        vo_copies[k].start()
+    for m in far:
+        for copy in m:
+            copy.start()
+    own_grad.wait()
+    grad_line = Line(c, grads_ref.at[0], z, depth, rows)
+    for k in range(2, depth):
+        line_step(tok_line, k, pass_tok)
+    grad_line.begin()
+
+    for copy in gain_spread:
+        copy.wait_recv()
+    for d in range(dp):
+        total = gains_all[0, d]
+        for t in range(1, depth):
+            total = total + gains_all[t, d]
+        gain_rows[:, d * slice_width : (d + 1) * slice_width] = total
+
+    def norm_rows(s):
+        def block(i, carry):
+            at = pl.ds(pl.multiple_of(i * rows, rows), rows)
+            data = tok[s, at, :].astype(F32)
+            scale = lax.rsqrt(jnp.mean(data * data, axis=-1, keepdims=True) + EPS)
+            fnorm[at, :] = (data * scale * gain_rows[0:1, :]).astype(BF)
+            return carry
+
+        lax.fori_loop(0, depth, block, 0)
+
+    own_misc.wait()
+    for copy in misc_copies:
+        copy.wait_recv()
+    bias_in = jnp.zeros(misc_ref.shape, F32)
+    sub = lax.broadcasted_iota(jnp.int32, misc_ref.shape, 0)
+    for d in range(dp):
+        bias_in = jnp.where(sub == d, misc_all[d, pl.ds(experts + 1 + core, 1), :], bias_in)
+    bias_in = bias_in.astype(BF)
+    heads3 = 3 * pair
+    head_slice = head // dp
+    lane = lax.broadcasted_iota(jnp.int32, (bias_in.shape[1], heads3), 1)
+    sub = lax.broadcasted_iota(jnp.int32, (bias_in.shape[1], heads3), 0)
+    place = (lane // head * head_slice + lane % head_slice == sub).astype(F32).astype(BF)
+    spread = dot(bias_in, place)
+    lane = lax.broadcasted_iota(jnp.int32, spread.shape, 1)
+    sub = lax.broadcasted_iota(jnp.int32, spread.shape, 0)
+    bias = jnp.sum(jnp.where(lane % head // head_slice == sub, spread, 0.0), axis=0, keepdims=True)
+
+    qk_copies[-1].wait_recv()
+    vo_copies[-1].wait_recv()
+    pairs = pair // head
+
+    def project(s):
+        def block(i, carry):
+            at = pl.ds(pl.multiple_of(i * 2 * rows, 2 * rows), 2 * rows)
+            full = weights[...].reshape(width, 4 * pair)
+            pre = dot(fnorm[at, :], full[:, : 3 * pair]) + bias
+            cos_rows, sin_rows = cos_ref[at, :], sin_ref[at, :]
+            for kind in range(3):
+                for h in range(pairs):
+                    a = (kind * pairs + h) * head
+                    field = pre[:, a : a + head]
+                    if kind < 2:
+                        field = spin(field, cos_rows, sin_rows)
+                    qkv_ref[kind, s * pairs + h, at, :] = field.astype(BF)
+            return carry
+
+        lax.fori_loop(0, depth // 2, block, 0)
+
+    norm_rows(0)
+    project(0)
+    line_step(grad_line, 1, None)
+    for copy in near[0]:
+        copy.wait()
+    for copy in far[0]:
+        copy.wait_recv()
+    over[0][0].start()
+    tok_pass[0].wait()
+    for copy, there in tok_passed:
+        pl.when(there)(copy.wait)
+    norm_rows(1)
+    project(1)
+
+    own_codes.wait()
+    for copy in first:
+        copy.wait()
+    causal_block = seq_len // 2
+
+    def attend(s):
+        flags = codes_all[s]
+        sub = lax.broadcasted_iota(jnp.int32, flags.shape, 0)
+        flags = jnp.where(sub == 8, flags, 0).astype(F32).astype(BF)
+        for h in range(pairs):
+            for b in range(2):
+                at = slice(b * causal_block, (b + 1) * causal_block)
+                seen = dot(flags[:, at], flags, 0, 0)
+                row = lax.broadcasted_iota(jnp.int32, seen.shape, 0) + b * causal_block
+                col = lax.broadcasted_iota(jnp.int32, seen.shape, 1)
+                scores = dot(qkv_ref[0, s * pairs + h, at, :], qkv_ref[1, s * pairs + h], 1, 1)
+                scores = scores * head ** (-0.5)
+                scores = jnp.where(jnp.logical_or(col <= row, seen > 0.5), scores, -1e30)
+                raised = jnp.exp(scores - jnp.max(scores, axis=1, keepdims=True))
+                probs = raised / jnp.sum(raised, axis=1, keepdims=True)
+                probs = probs.astype(BF)
+                probs_ref[s * pairs + h, at, :] = probs
+                mixed = dot(probs, qkv_ref[2, s * pairs + h])
+                mix_ref[s, at, h * head : (h + 1) * head] = mixed.astype(BF)
+
+    def project_out(s):
+        for d in range(dp):
+            index = tuple(d // bit % 2 for bit in reversed(bits))
+            block = weights[index + (slice(None), slice(3 * pair, 4 * pair))]
+            at = slice(d * slice_width, (d + 1) * slice_width)
+            part[s, :, at] = dot(mix_ref[s], block, 1, 1).astype(BF)
+
+    attend(1)
+    if depth > 2:
+        line_step(grad_line, 2, None)
+    project_out(1)
+    part_pass = c.remote(part.at[1], part_in, dp=peer_of(me, 1))
+    part_pass.start()
+    attend(0)
+    project_out(0)
+    for copy in near[1]:
+        copy.wait()
+    for copy in far[1]:
+        copy.wait_recv()
+    over[1][0].start()
+    part_pass.wait_recv()
+
+    scatter = []
+    for r in list(range(1, depth)) + [0]:
+        at = pl.ds(pl.multiple_of((z + r) % depth * rows, rows), rows)
+        total = part[0, at, :].astype(F32) + part_in[at, :].astype(F32)
+        if r:
+            part[0, at, :] = total.astype(BF)
+            copy = c.remote(part.at[0, at], scatter_in.at[r - 1], tensor=(z + r) % depth)
+            copy.start()
+            scatter.append(copy)
+        else:
+            hidden_ref[...] = total + tok[0, at, :].astype(F32)
+
+    for k in range(3, depth):
+        line_step(grad_line, k, None)
+    x_grad = c.remote(grads_ref.at[0], grads_ref.at[2], dp=peer_of(me, 2))
+    x_grad.start()
+    own_pass = c.remote(grads_ref.at[0], grads_ref.at[1], dp=peer_of(me, 1))
+    own_pass.start()
+    for copy in near[2]:
+        copy.wait()
+    for copy in far[2]:
+        copy.wait_recv()
+    over[2][0].start()
+
+    for copy in scatter:
+        copy.wait_recv()
+    total = hidden_ref[...]
+    for r in range(1, depth):
+        total = total + scatter_in[r - 1].astype(F32)
+    hidden_ref[...] = total
+    scale = lax.rsqrt(jnp.mean(total * total, axis=-1, keepdims=True) + EPS)
+    norm_ref[0, pl.ds(pl.multiple_of(z * rows, rows), rows), :] = (
+        total * scale * gain_rows[1:2, :]
+    ).astype(BF)
+    norm_line = Line(c, norm_ref.at[0], z, depth, rows)
+    norm_line.begin()
+    norm_own = c.remote(piece(norm_ref.at[0], z), piece(norm_ref.at[1], z), dp=peer_of(me, 1))
+    norm_own.start()
+    norm_passed = []
+    pass_norm = pass_on(norm_ref.at[0], norm_ref.at[1], norm_passed)
+    for k in range(1, depth):
+        line_step(norm_line, k, pass_norm)
+
+    x_grad.wait_recv()
+    grad_pass = c.remote(grads_ref.at[2], grads_ref.at[3], dp=peer_of(me, 1))
+    grad_pass.start()
+    for k in range(1, len(upper)):
+        for chain in over:
+            chain[k - 1].wait_recv()
+            chain[k].start()
+    for chain in over:
+        chain[-1].wait_recv()
+    norm_own.wait()
+    for copy, there in norm_passed:
+        pl.when(there)(copy.wait)
+    own_pass.wait()
+    grad_pass.wait()
+    for line in (tok_line, grad_line, norm_line):
+        line.finish()
+    for copy in pads:
+        copy.wait()
+    for copy in gain_copies + misc_copies + gain_spread + qk_copies + vo_copies + scatter:
+        copy.wait_send()
+    for copy in [part_pass, x_grad] + [y for m in far for y in m] + [y for m in over for y in m]:
+        copy.wait_send()
+
+
+def forward_call(dp, depth, experts, head, small, arrays, units):
+    codes, misc, gains, cos_rows, sin_rows = small
+    tokens, pair = arrays[0], arrays[2].shape[1] // 2
+    rows, width = tokens.shape
+    seq_len = rows * depth
+    hidden_units = units[0].shape[1]
+    hidden_pad = -(-hidden_units // 128) * 128
+    routed = experts // 4
+    bits = dp.bit_length() - 1
+    pairs = pair // head
+    vmem, hbm = pl.BlockSpec(memory_space=pltpu.VMEM), pl.BlockSpec(memory_space=pl.ANY)
+    shape = jax.ShapeDtypeStruct
+    return pl.pallas_call(
+        functools.partial(forward_body, (dp, depth, experts, hidden_units, head)),
+        in_specs=[vmem] * 5 + [hbm] * 12,
+        out_specs=[vmem, vmem, hbm, hbm, hbm] + [vmem] * 8,
+        out_shape=[
+            shape((rows, width), F32),
+            shape((2, seq_len, width), BF),
+            shape((4, seq_len, width), BF),
+            shape((routed + 1, 2, hidden_pad, width), BF),
+            shape((routed + 1, 1, hidden_pad, width), BF),
+            shape((4,) + codes.shape, codes.dtype),
+            shape((dp,) + misc.shape, F32),
+            shape((8, width), F32),
+            shape((2, seq_len, width), BF),
+            shape((2,) * bits + (width // dp, 4 * pair), BF),
+            shape((3, 2 * pairs, seq_len, head), BF),
+            shape((2 * pairs, seq_len, seq_len), BF),
+            shape((2, seq_len, pair), BF),
+        ],
+        scratch_shapes=[
+            pltpu.VMEM((seq_len, width), BF),
+            pltpu.VMEM((2, seq_len, width), BF),
+            pltpu.VMEM((seq_len, width), BF),
+            pltpu.VMEM((depth - 1, rows, width), BF),
+            pltpu.VMEM((depth, dp) + gains.shape, F32),
+            pltpu.VMEM((routed + 1, hidden_pad - hidden_units, width), BF),
+            pltpu.SemaphoreType.DMA((160,)),
+            pltpu.SemaphoreType.DMA((160,)),
+            pltpu.SemaphoreType.DMA((32,)),
+        ],
+        compiler_params=pltpu.CompilerParams(
+            collective_id=0, has_side_effects=True, vmem_limit_bytes=VMEM_LIMIT
+        ),
+    )(codes, misc, gains, cos_rows, sin_rows, *arrays, *units)
+
+
+def local_plain(
     dp,
     tokens,
     picture_ids,
@@ -700,9 +1235,388 @@
     )
 
 
+def local_fused(
+    dp,
+    depth,
+    tokens,
+    picture_ids,
+    routes,
+    slot_order,
+    norm_gains,
+    w_query,
+    w_key,
+    w_value,
+    w_out,
+    qkv_bias,
+    router,
+    shared_gate,
+    shared_up,
+    shared_down,
+    expert_gate,
+    expert_up,
+    expert_down,
+    out_grad,
+):
+    seq_len = picture_ids.shape[0]
+    local_rows = tokens.shape[0]
+    width = tokens.shape[1]
+    experts, slice_width, hidden_units = expert_gate.shape
+    top_count = routes.shape[1]
+    capacity = 5 * seq_len * top_count // (4 * experts)
+    heads_local = qkv_bias.shape[1]
+    head_width = w_query.shape[1] // heads_local
+    pair_heads = heads_local // 2
+    pair_width = pair_heads * head_width
+    mine_experts = experts // 4
+    hidden_pad = -(-hidden_units // 128) * 128
+
+    me = lax.axis_index("dp")
+    zi = lax.axis_index("tensor")
+    core, xi = me % 2, (me // 2) % 2
+    group = me % 4
+    bits = []
+    while 2 ** (len(bits) + 1) <= dp:
+        bits.append(2 ** len(bits))
+    upper = bits[2:]
+
+    def swap(array, bit):
+        return lax.ppermute(array, "dp", [(i, i ^ bit) for i in range(dp)])
+
+    def bit_of(bit):
+        return (me // bit) % 2
+
+    def join(mine, theirs, bit, axis):
+        n = mine.shape[axis]
+        shape = list(mine.shape)
+        shape[axis] = 2 * n
+        out = jnp.zeros(shape, mine.dtype)
+        out = lax.dynamic_update_slice_in_dim(out, mine, n * bit_of(bit), axis)
+        return lax.dynamic_update_slice_in_dim(out, theirs, n * (1 - bit_of(bit)), axis)
+
+    def half(array, which, axis):
+        n = array.shape[axis] // 2
+        return lax.dynamic_slice_in_dim(array, which * n, n, axis)
+
+    codes = jnp.concatenate([routes.T, slot_order.T, picture_ids[None]], axis=0)
+    codes = jnp.pad(codes, ((0, 16 - codes.shape[0]), (0, 0)))
+    bias_cores = qkv_bias.reshape(3, 2, -1).swapaxes(0, 1).reshape(2, -1)
+    bias_width = bias_cores.shape[1]
+    misc = jnp.zeros((16, slice_width), F32)
+    misc = misc.at[: experts + 1].set(router.T.astype(F32))
+    misc = misc.at[experts + 1 : experts + 3, :bias_width].set(bias_cores.astype(F32))
+    gains = lax.dynamic_update_slice(
+        jnp.zeros((8, slice_width), F32),
+        norm_gains.astype(F32),
+        (jnp.int32(0), zi * norm_gains.shape[1]),
+    )
+    cos_part, sin_part = rope_tables(seq_len, head_width)
+    cos_rows = jnp.concatenate([cos_part, cos_part], axis=1)
+    sin_rows = jnp.concatenate([-sin_part, sin_part], axis=1)
+    (
+        hidden,
+        norm_own,
+        grads_all,
+        gateup_all,
+        down_all,
+        codes_all,
+        misc_all,
+        gain_rows,
+        tok,
+        attn_weights,
+        qkv,
+        probs_low,
+        heads_out,
+    ) = forward_call(
+        dp,
+        depth,
+        experts,
+        head_width,
+        (codes, misc, gains, cos_rows, sin_rows),
+        (tokens, out_grad, w_query, w_key, w_value, w_out.T),
+        (
+            expert_gate.swapaxes(1, 2),
+            expert_up.swapaxes(1, 2),
+            expert_down,
+            shared_gate.T.reshape(4, hidden_units, slice_width),
+            shared_up.T.reshape(4, hidden_units, slice_width),
+            shared_down.reshape(4, hidden_units, slice_width),
+        ),
+    )
+    gateup_all = gateup_all.reshape(mine_experts + 1, 2 * hidden_pad, width)
+    down_all = down_all.reshape(mine_experts + 1, hidden_pad, width)
+    attn_weights = attn_weights.reshape(width, 4 * pair_width)
+    qk_full, vo_full = attn_weights[:, : 2 * pair_width], attn_weights[:, 2 * pair_width :]
+    out_weight = vo_full[:, pair_width:]
+    router_rows = jnp.concatenate([misc_all[d] for d in range(dp)], axis=1)
+    router_rows = jnp.where(jnp.arange(16)[:, None] <= experts, router_rows, 0.0).astype(BF)
+    router_full = router_rows[: experts + 1].T
+    codes_all = codes_all[:, : 2 * top_count]
+    codes_a, codes_b = codes_all[:2], codes_all[2:]
+    misc_rows = 16
+    rows_f = tok.astype(F32)
+    first_scale = lax.rsqrt(jnp.mean(rows_f * rows_f, axis=-1, keepdims=True) + EPS)
+    score_scale = head_width ** (-0.5)
+    inputs = tokens.astype(F32)
+    second_scale = lax.rsqrt(jnp.mean(hidden * hidden, axis=-1, keepdims=True) + EPS)
+    second_unit = hidden * second_scale
+
+    def core_sum(own, sibling):
+        return own + swap(sibling.astype(BF), 1).astype(F32)
+
+    def z_scatter(array):
+        return lax.psum_scatter(
+            array.astype(BF), "tensor", scatter_dimension=0, tiled=True
+        ).astype(F32)
+
+    norm_z = norm_own[0]
+    norm_a = norm_own
+    norm_x = swap(norm_z, 2)
+    norm_b = jnp.stack([norm_x, swap(norm_x, 1)])
+    grad_a, grad_b = grads_all[:2], grads_all[2:]
+
+    expert_ids = group * mine_experts + jnp.arange(mine_experts, dtype=jnp.int32)
+
+    group_ids = group.astype(jnp.int32).reshape(1)
+
+    def slots_of(codes_in):
+        routes_in, slots_in = codes_in[:, None, :top_count], codes_in[:, None, top_count:]
+        matches = routes_in == expert_ids[None, :, None, None]
+        return jnp.max(jnp.where(matches, slots_in, -1), axis=2)
+
+    def feed(slots, rows, grads):
+        slotted, slot_grad, pair, act, terms, pair_s, act_s, inner_s, probs_out = act_call(
+            experts, capacity, group_ids, slots, rows, grads, router_rows, gateup_all, down_all
+        )
+        terms = jnp.concatenate([terms.swapaxes(1, 2), inner_s], axis=-1)
+        flat = [a.reshape(mine_experts, -1, a.shape[-1]) for a in (slotted, slot_grad, pair, act)]
+        shared = [a.reshape(1, -1, a.shape[-1]) for a in (rows, grads, pair_s, act_s)]
+        return (pair, pair_s), (act, act_s), terms, (flat, shared), probs_out
+
+    slots_a, slots_b = slots_of(codes_a), slots_of(codes_b)
+    fed_a = feed(slots_a, norm_a, grad_a)
+    fed_b = feed(slots_b, norm_b, grad_b)
+    columns_a, columns_b = slots_a[..., None], slots_b[..., None]
+    row_grad_b = back_call(columns_b, *fed_b[0], gateup_all)
+    row_grad_a = back_call(after(columns_a, row_grad_b), *fed_a[0], gateup_all)
+    row_out_b = back_call(after(columns_b, row_grad_a), *fed_b[1], down_all)
+    row_out_a = back_call(columns_a, *fed_a[1], down_all)
+
+    def spread(terms):
+        wide = jnp.zeros(terms.shape[:-1] + (128,), F32)
+        wide = lax.dynamic_update_slice_in_dim(
+            wide, terms[..., :mine_experts], group * mine_experts, terms.ndim - 1
+        )
+        return wide.at[..., experts].set(terms[..., mine_experts])
+
+    def group_sum(a, b):
+        across = b[0].astype(F32) + swap(b[1].astype(BF), 1).astype(F32)
+        near = a[0].astype(F32) + swap(a[1].astype(BF), 1).astype(F32)
+        return near + swap(across.astype(BF), 2).astype(F32)
+
+    grad_sum = group_sum(row_grad_a, row_grad_b)
+    term_sum = group_sum(spread(fed_a[2]), spread(fed_b[2]))
+    packed = z_scatter(jnp.concatenate([grad_sum, term_sum], axis=-1))
+    second_grad, gate_sums = packed[:, :width], packed[:, width:]
+
+    data_a, data_b = fed_a[3], fed_b[3]
+
+    def unit_grads(left, right):
+        return jnp.concatenate(
+            [
+                outer_call(
+                    hidden_units,
+                    hidden_pad,
+                    dp,
+                    [(data[k][left], data[k][right]) for data in (data_a, data_b)],
+                )
+                for k in range(2)
+            ],
+            axis=1,
+        )
+
+    def scatter_units(total):
+        total = total.reshape((2,) * len(bits) + total.shape[1:])
+        for bit in reversed(upper):
+            axis = len(bits) - 1 - bits.index(bit)
+            sent = half(total, 1 - bit_of(bit), axis)
+            kept = half(total, bit_of(bit), axis)
+            total = (kept.astype(F32) + swap(sent, bit).astype(F32)).astype(BF)
+        total = total.reshape((2, 2) + total.shape[len(bits) :])
+        held = join(pick(total, xi, 0)[None], swap(pick(total, 1 - xi, 0), 2)[None], 2, 0)
+        return join(pick(held, core, 1)[:, None], swap(pick(held, 1 - core, 1), 1)[:, None], 1, 1)
+
+    def split_units(held):
+        routed = held[:, :, :mine_experts].reshape(experts, -1, slice_width)
+        shared = held[:, :, mine_experts]
+        return routed.astype(F32), shared.astype(F32)
+
+    gateup_sum = scatter_units(unit_grads(2, 0))
+    down_sum = scatter_units(unit_grads(3, 1))
+    routed_gu, shared_gu = split_units(gateup_sum)
+    routed_down, shared_down_sum = split_units(down_sum)
+    shared_gu = shared_gu.reshape(4, 2, hidden_units, slice_width)
+    egate_sum = routed_gu[:, :hidden_units].swapaxes(1, 2)
+    eup_sum = routed_gu[:, hidden_units:].swapaxes(1, 2)
+    sgate_sum = shared_gu[:, 0].reshape(-1, slice_width).T
+    sup_sum = shared_gu[:, 1].reshape(-1, slice_width).T
+    sdown_sum = shared_down_sum.reshape(-1, slice_width)
+
+    row_start = zi * local_rows
+    probs_local = lax.dynamic_slice_in_dim(fed_a[4][0], row_start, local_rows, 1).T
+    probs_mine, weight_mine = probs_local[:, :experts], probs_local[:, experts]
+    route_grad = gate_sums[:, :experts]
+    expert_logit_grad = probs_mine * (
+        route_grad - jnp.sum(probs_mine * route_grad, axis=-1, keepdims=True)
+    )
+    weight_logit_grad = gate_sums[:, experts] * weight_mine * (1.0 - weight_mine)
+    logits_grad = jnp.concatenate([expert_logit_grad, weight_logit_grad[:, None]], axis=1).astype(
+        BF
+    )
+    second_grad = second_grad + einsum("tf,df->td", logits_grad, router_full)
+    gain_two_grad = jnp.sum(second_grad * second_unit, axis=0)
+    unit_two = second_grad * gain_rows[1]
+    hidden_grad = out_grad.astype(F32) + second_scale * (
+        unit_two - second_unit * jnp.mean(unit_two * second_unit, axis=-1, keepdims=True)
+    )
+    attention_grad = hidden_grad.astype(BF)
+    wide_logits = jnp.pad(logits_grad, ((0, 0), (0, 128 - experts - 1)))
+    back_z = lax.all_gather(
+        jnp.concatenate([attention_grad, wide_logits], axis=1), "tensor", axis=0, tiled=True
+    )
+    out_sum = after(group_sum(row_out_a, row_out_b), back_z)
+    output = (hidden + z_scatter(out_sum)).astype(BF)
+    logits_z = back_z[:, width : width + 16]
+    back_own = back_z[:, :width]
+    back_rows = jnp.stack([back_own, swap(back_own, 1)])
+
+    router_part = einsum("tf,td->fd", logits_z, norm_z)[: experts + 1]
+
+    first_norm = (rows_f * first_scale * gain_rows[0]).astype(BF)
+    out_proj = einsum("std,stf->df", back_rows, heads_out)
+    mix_grad = einsum("std,df->stf", back_rows, out_weight).astype(BF)
+    mix_grad = mix_grad.reshape(2, seq_len, pair_heads, head_width).swapaxes(1, 2)
+    mix_grad = mix_grad.reshape(2 * pair_heads, seq_len, head_width)
+    queries, keys, values = qkv[0], qkv[1], qkv[2]
+    prob_grad = einsum("nqd,nkd->nqk", mix_grad, values)
+    probs = probs_low.astype(F32)
+    score_grad = (
+        probs * (prob_grad - jnp.sum(probs * prob_grad, axis=-1, keepdims=True))
+    ).astype(BF)
+    query_rot = einsum("nqk,nkd->nqd", score_grad, keys) * score_scale
+    key_rot = einsum("nqk,nqd->nkd", score_grad, queries) * score_scale
+    value_grad = einsum("nqk,nqd->nkd", probs_low, mix_grad)
+
+    def unspin(field):
+        return field * cos_rows - jnp.roll(field, head_width // 2, axis=-1) * sin_rows
+
+    def lanes_of(field):
+        field = field.reshape(2, pair_heads, seq_len, head_width).swapaxes(1, 2)
+        return field.astype(BF).reshape(2, seq_len, pair_width)
+
+    qk_grad = jnp.concatenate([lanes_of(unspin(query_rot)), lanes_of(unspin(key_rot))], axis=-1)
+    v_grad = lanes_of(value_grad)
+    first_part = einsum("stf,df->std", qk_grad, qk_full) + einsum(
+        "stf,df->std", v_grad, vo_full[:, :pair_width]
+    )
+    first_grad = z_scatter(core_sum(first_part[0], first_part[1]))
+
+    gain_one_grad = jnp.sum(first_part * (rows_f * first_scale), axis=(0, 1))
+    bias_part = jnp.concatenate(
+        [jnp.sum(qk_grad.astype(F32), axis=(0, 1)), jnp.sum(v_grad.astype(F32), axis=(0, 1))]
+    )
+    bias_part = bias_part.reshape(3 * pair_heads, dp, -1).swapaxes(0, 1).reshape(dp, 1, -1)
+    gain_part = jnp.stack([gain_one_grad, gain_two_grad]).reshape(2, dp, slice_width)
+
+    def wide_rows(rows):
+        return jnp.pad(rows, ((0, 0), (0, 0), (0, 2 * pair_width - rows.shape[2])))
+
+    misc_part = jnp.concatenate(
+        [
+            wide_rows(router_part.reshape(experts + 1, dp, slice_width).swapaxes(0, 1)),
+            wide_rows(bias_part),
+            wide_rows(gain_part.swapaxes(0, 1)),
+            jnp.zeros((dp, misc_rows - experts - 4, 2 * pair_width), F32),
+        ],
+        axis=1,
+    )
+    qk_total = einsum("std,stf->df", first_norm, qk_grad).reshape(dp, slice_width, -1)
+    qk_total = jnp.concatenate([qk_total, misc_part], axis=1)
+    vo_total = jnp.concatenate([einsum("std,stf->df", first_norm, v_grad), out_proj], axis=1)
+    vo_total = vo_total.reshape(dp, slice_width, -1)
+
+    def scatter_attention(total, order):
+        total = total.reshape((2,) * len(bits) + total.shape[1:])
+        for bit in order:
+            axis = len(bits) - 1 - bits.index(bit)
+            sent = half(total, 1 - bit_of(bit), axis).astype(BF)
+            total = half(total, bit_of(bit), axis) + swap(sent, bit).astype(F32)
+        total = total.reshape((2,) + total.shape[-2:]).astype(BF)
+        return pick(total, core, 0), swap(pick(total, 1 - core, 0), 1)
+
+    def columns_of(mine, theirs):
+        held = join(mine[:slice_width, None], theirs[:slice_width, None], 1, 1)
+        first, second = held[..., :pair_width], held[..., pair_width:]
+        return (
+            first.reshape(slice_width, -1).astype(F32),
+            second.reshape(slice_width, -1).astype(F32),
+        )
+
+    qk_mine, qk_theirs = scatter_attention(qk_total, bits[:0:-1])
+    vo_mine, vo_theirs = scatter_attention(vo_total, bits[1:])
+    qk_sums = columns_of(qk_mine, qk_theirs)
+    vo_sums = columns_of(vo_mine, vo_theirs)
+    misc_mine = qk_mine[slice_width:].astype(F32)
+    misc_theirs = qk_theirs[slice_width:].astype(F32)
+    misc_sum = misc_mine + misc_theirs
+    router_sum = misc_sum[: experts + 1, :slice_width].T
+    bias_sums = join(
+        misc_mine[experts + 1, :bias_width].reshape(3, 1, pair_heads, -1),
+        misc_theirs[experts + 1, :bias_width].reshape(3, 1, pair_heads, -1),
+        1,
+        1,
+    ).reshape(3, heads_local, -1)
+    gain_sums = lax.all_gather(
+        misc_sum[experts + 2 : experts + 4, :slice_width], "tensor", axis=0, tiled=False
+    )
+    tensor = gain_sums.shape[0]
+    gain_sums = jnp.sum(gain_sums, axis=0).reshape(2, tensor, -1)
+    gain_sums = pick(gain_sums, zi, 1)
+
+    unit_mine = inputs * lax.rsqrt(jnp.mean(inputs * inputs, axis=-1, keepdims=True) + EPS)
+    scale_mine = lax.rsqrt(jnp.mean(inputs * inputs, axis=-1, keepdims=True) + EPS)
+    unit_one = first_grad * gain_rows[0]
+    input_grad = hidden_grad + scale_mine * (
+        unit_one - unit_mine * jnp.mean(unit_one * unit_mine, axis=-1, keepdims=True)
+    )
+    return (
+        output,
+        input_grad.astype(BF),
+        gain_sums,
+        qk_sums[0],
+        qk_sums[1],
+        vo_sums[0],
+        vo_sums[1].T,
+        bias_sums,
+        router_sum,
+        sgate_sum,
+        sup_sum,
+        sdown_sum,
+        egate_sum,
+        eup_sum,
+        routed_down,
+    )
+
+
 def solution(mesh):
+    dp, depth = mesh.shape["dp"], mesh.shape["tensor"]
+
+    def body(*arrays):
+        if arrays[5].shape[0] % 128 == 0 and dp == 8 and depth == 4:
+            return local_fused(dp, depth, *arrays)
+        return local_plain(dp, *arrays)
+
     return jax.shard_map(
-        functools.partial(local, mesh.shape["dp"]),
+        body,
         mesh=mesh,
         in_specs=(
             P(("dp", "tensor"), None),

time: 1060 us -> 901 us (0.85)
  Pallas kernels: 178 us -> 395 us
  waiting for transfers between devices: 372 us -> 160 us
  local copies, waits for them, and re-layouts: 273 us -> 172 us
  other arithmetic: 119 us -> 78.8 us
  starting transfers between devices: 35 us -> 20.3 us
  blocking collectives: 24 us -> 11.9 us
    pallas_call x0 -> x1, Pallas kernels: none -> 217 us  [forward_call(): pl.pallas_call(functools.partial(forward_body, (dp, depth, experts, hidde...]
    ppermute x49 -> x25, waiting for transfers between devices: 322 us -> 160 us  [swap(): return lax.ppermute(array, 'dp', [(i, i ^ bit) for i in range(dp)])]
    all_gather x4 -> x1, waiting for transfers between devices: 36 us -> 0.01 us  [local_fused(): lax.all_gather(jnp.concatenate([attention_grad, wide_logits], axis=1), 't...]
    dynamic_update_slice x19 -> x7, local copies, waits for them, and re-layouts: 47.6 us -> 14.8 us  [join(): lax.dynamic_update_slice_in_dim(out, theirs, n * (1 - bit_of(bit)), axis)]
    dynamic_update_slice x14 -> x5, local copies, waits for them, and re-layouts: 32.7 us -> 10.1 us  [join(): out = lax.dynamic_update_slice_in_dim(out, mine, n * bit_of(bit), axis)]
    another operation x13 -> x6, other arithmetic: 26.8 us -> 9.24 us
    unnamed x217 -> x159, local copies, waits for them, and re-layouts: 35.7 us -> 20.6 us
    ppermute x49 -> x25, starting transfers between devices: 34.5 us -> 19.9 us  [swap(): return lax.ppermute(array, 'dp', [(i, i ^ bit) for i in range(dp)])]
  transfers between devices with their start and end apart: 57 -> 29, of which waited for: 19 -> 8; matrix products, arithmetic and copies ran while one was open for 34% -> 28% of each run, Pallas kernels for 12% -> 14%
where the time goes in v2:
time: 901 us; the launch traced here: 886 us
  Pallas kernels  395 us (44%)
  local copies, waits for them, and re-layouts  172 us (19%)
  waiting for transfers between devices  160 us (18%)
  other arithmetic  78.8 us (9%)
  matrix products  34 us (4%)
  starting transfers between devices  20.3 us (2%)
  between operations  15.2 us (2%)
  blocking collectives  11.9 us (1%)
    pallas_call x1, Pallas kernels, forward_call(): pl.pallas_call(functools.partial(forward_body, (dp, depth, experts, hidde...  217 us
    ppermute x25, waiting for transfers between devices, swap(): return lax.ppermute(array, 'dp', [(i, i ^ bit) for i in range(dp)])  160 us
    pallas_call x4, Pallas kernels, back_call(): call(back_body, (width // block, count), [pl.BlockSpec((1, units - 1, seq...  72.5 us
    pallas_call x2, Pallas kernels, act_call(): call(functools.partial(act_body, experts, units), (count, units), [pl.Blo...  59.9 us
    pallas_call x4, Pallas kernels, outer_call(): call(functools.partial(outer_body, keep, pad), (units, dp // blocks), [le...  45.1 us
    dot_general x12, matrix products, einsum(): return jnp.einsum(spec, *args, preferred_element_type=F32)  34 us
    unnamed x159, local copies, waits for them, and re-layouts  20.6 us
    ppermute x25, starting transfers between devices, swap(): return lax.ppermute(array, 'dp', [(i, i ^ bit) for i in range(dp)])  19.9 us
  transfers between devices with their start and end apart: 29, of which 8 were waited for; matrix products, arithmetic and copies ran while one was open for 28% of the time, Pallas kernels for 14%

profile of v2, /device:TPU:0, one launch (start us, length us, event | category | flops | bytes accessed | tf_op | source)
XLA Modules:
  0.0 886.4 jit_solution(3691726343428553661)
XLA Ops:
  16.4 217.1 %shard_map.289 = (f32[128,2048]{1,0:T(8,128)}, bf16[2,512,2048]{2,1,0:T(8,128)(2,1)}, bf16[4,512,2048]{2,1,0:T(8,128)(2,1)}, bf16[3,2,384,2048]{3,2,1,0:T(8,128)...) custom-call(s32[16,512]{1,0:T(8,128)} %pad.32.codes_ref, ...), custom_call_target="tpu_custom_call" | custom-call | tf_op jit(solution)/shard_map/pallas_call | solution.py:775
  239.6 43.1 %collective-permute-done.1 = bf16[512,2048]{1,0:T(8,128)(2,1)} collective-permute-done((bf16[512,2048]{1,0:T(8,128)(2,1)S(1)}, bf16[512,2048]{1,0:T(8,128)(2,1)}, u32[]{:S(2)}, u32[]{:S(2)}) %collective-permute-start.1) | collective-permute-done | bytes 2097184 | tf_op jit(solution)/shard_map/ppermute | solution.py:1283
  284.6 6.0 fusion.68
  290.6 4.0 pad_maximum_fusion.2.rows_ref
  294.7 29.9 %shard_map.292 = (bf16[2,2,320,2048]{3,2,1,0:T(8,128)(2,1)}, bf16[2,2,320,2048]{3,2,1,0:T(8,128)(2,1)}, bf16[2,2,320,768]{3,2,1,0:T(8,128)(2,1)}, bf16[2,2,320,3...) custom-call(s32[1]{0:T(128)} %bitcast.14.group_ref, ...), custom_call_target="tpu_custom_call" | custom-call | flops 16240345088 | bytes 33554432 | tf_op jit(solution)/shard_map/pallas_call | solution.py:167
  324.6 20.2 %shard_map.293 = bf16[2,512,2048]{2,1,0:T(8,128)(2,1)} custom-call(s32[2,2,512,1]{3,2,1,0:T(8,128)} %copy.283.slot_ref, bf16[2,2,320,768]{3,2,1,0:T(8,128)(2,1)} %get-tuple-element.105.routed_ref, bf16[2,512,768]{2,1,0:T(8,128)(2,1)} %get-tuple-element.106.shared_ref, bf16[3,768,2048]{2,1,0:T(8,128)(2,1)} %bitcast.359), custom_call_target="tpu_custom_call" | custom-call | flops 9932111872 | bytes 13631488 | tf_op jit(solution)/shard_map/pallas_call | solution.py:224
  346.6 30.0 %shard_map.290 = (bf16[2,2,320,2048]{3,2,1,0:T(8,128)(2,1)}, bf16[2,2,320,2048]{3,2,1,0:T(8,128)(2,1)}, bf16[2,2,320,768]{3,2,1,0:T(8,128)(2,1)}, bf16[2,2,320,3...) custom-call(s32[1]{0:T(128)} %bitcast.14.group_ref, ...), custom_call_target="tpu_custom_call" | custom-call | flops 16240345088 | bytes 33554432 | tf_op jit(solution)/shard_map/pallas_call | solution.py:167
  379.7 2.7 scatter.25
  383.8 20.2 %shard_map.294 = bf16[2,512,2048]{2,1,0:T(8,128)(2,1)} custom-call(s32[2,2,512,1]{3,2,1,0:T(8,128)} %copy.284.slot_ref, bf16[2,2,320,768]{3,2,1,0:T(8,128)(2,1)} %get-tuple-element.108.routed_ref, bf16[2,512,768]{2,1,0:T(8,128)(2,1)} %get-tuple-element.109.shared_ref, bf16[3,768,2048]{2,1,0:T(8,128)(2,1)} %bitcast.361), custom_call_target="tpu_custom_call" | custom-call | flops 9932111872 | bytes 13631488 | tf_op jit(solution)/shard_map/pallas_call | solution.py:224
  404.0 3.3 slice_bitcast_fusion.7
  416.0 16.0 %shard_map.291 = bf16[2,512,2048]{2,1,0:T(8,128)(2,1)} custom-call(s32[2,2,512,1]{3,2,1,0:T(8,128)} %copy.282.slot_ref, bf16[2,2,320,384]{3,2,1,0:T(8,128)(2,1)} %get-tuple-element.103.routed_ref, bf16[2,512,384]{2,1,0:T(8,128)(2,1)} %get-tuple-element.104.shared_ref, bf16[3,384,2048]{2,1,0:T(8,128)(2,1)} %bitcast.364), custom_call_target="tpu_custom_call" | custom-call | flops 6308233216 | bytes 8912896 | tf_op jit(solution)/shard_map/pallas_call | solution.py:224
  433.9 2.9 dynamic_update_slice.53
  444.2 17.5 %collective-permute-done.10 = bf16[512,128]{1,0:T(8,128)(2,1)S(1)} collective-permute-done((bf16[512,128]{1,0:T(8,128)(2,1)S(1)}, bf16[512,128]{1,0:T(8,128)(2,1)S(1)}, u32[]{:S(2)}, u32[]{:S(2)}) %collective-permute-start.10) | collective-permute-done | bytes 131104 | tf_op jit(solution)/shard_map/ppermute | solution.py:1283
  462.7 4.2 fusion.11
  468.5 7.7 shard_map.299
  476.2 11.3 %shard_map.298 = bf16[8,2,352,256]{3,2,1,0:T(8,128)(2,1)} custom-call(bf16[2,640,384]{2,1,0:T(8,128)(2,1)} %bitcast.321, bf16[2,640,2048]{2,1,0:T(8,128)(2,1)} %bitcast.295, bf16[2,640,384]{2,1,0:T(8,128)(2,1)} %bitcast.320, bf16[2,640,2048]{2,1,0:T(8,128)(2,1)} %bitcast.294), custom_call_target="tpu_custom_call" | custom-call | flops 4026531840 | bytes 12451840 | tf_op jit(solution)/shard_map/pallas_call | solution.py:265
  495.3 10.8 %shard_map.297 = bf16[8,1,704,256]{3,2,1,0:T(8,128)(2,1)} custom-call(bf16[1,1024,768]{2,1,0:T(8,128)(2,1)} %bitcast.371, bf16[1,1024,2048]{2,1,0:T(8,128)(2,1)} %bitcast.301, bf16[1,1024,768]{2,1,0:T(8,128)(2,1)} %bitcast.370, bf16[1,1024,2048]{2,1,0:T(8,128)(2,1)} %bitcast.302), custom_call_target="tpu_custom_call" | custom-call | flops 6442450944 | bytes 11534336 | tf_op jit(solution)/shard_map/pallas_call | solution.py:265
  506.1 15.3 %shard_map.296 = bf16[8,2,704,256]{3,2,1,0:T(8,128)(2,1)} custom-call(bf16[2,640,768]{2,1,0:T(8,128)(2,1)} %bitcast.369, bf16[2,640,2048]{2,1,0:T(8,128)(2,1)} %bitcast.367, bf16[2,640,768]{2,1,0:T(8,128)(2,1)} %bitcast.368, bf16[2,640,2048]{2,1,0:T(8,128)(2,1)} %bitcast.366), custom_call_target="tpu_custom_call" | custom-call | flops 8053063680 | bytes 14417920 | tf_op jit(solution)/shard_map/pallas_call | solution.py:265
  521.4 7.6 pad_maximum_fusion
  529.0 4.6 constant_dynamic-slice_fusion.3
  535.1 16.0 %shard_map.295 = bf16[2,512,2048]{2,1,0:T(8,128)(2,1)} custom-call(s32[2,2,512,1]{3,2,1,0:T(8,128)} %copy.285.slot_ref, bf16[2,2,320,384]{3,2,1,0:T(8,128)(2,1)} %get-tuple-element.111.routed_ref, bf16[2,512,384]{2,1,0:T(8,128)(2,1)} %get-tuple-element.112.shared_ref, bf16[3,384,2048]{2,1,0:T(8,128)(2,1)} %bitcast.365), custom_call_target="tpu_custom_call" | custom-call | flops 6308233216 | bytes 8912896 | tf_op jit(solution)/shard_map/pallas_call | solution.py:224
  551.1 3.2 slice_bitcast_fusion.9
  562.6 3.2 slice_bitcast_fusion.11
  566.5 3.0 add_convert_fusion.1
  572.2 4.0 fusion.12
  578.5 17.9 %collective-permute-done.23 = bf16[2,3,352,256]{3,2,1,0:T(8,128)(2,1)S(1)} collective-permute-done((bf16[2,3,352,256]{3,2,1,0:T(8,128)(2,1)S(1)}, bf16[2,3,352,256]{3,2,1,0:T(8,128)(2,1)S(1)}, u32[]{:S(2)}, u32[]{:S(2)}) %collective-permute-start.23) | collective-permute-done | bytes 1081376 | tf_op jit(solution)/shard_map/ppermute | solution.py:1283
  599.2 35.5 %collective-permute-done.19 = bf16[1,2,2,3,704,256]{5,4,3,2,1,0:T(8,128)(2,1)} collective-permute-done((bf16[1,2,2,3,704,256]{5,4,3,2,1,0:T(8,128)(2,1)}, bf16[1,2,2,3,704,256]{5,4,3,2,1,0:T(8,128)(2,1)}, u32[]{:S(2)}, u32[]{:S(2)}) %collective-permute-start.19) | collective-permute-done | bytes 4325408 | tf_op jit(solution)/shard_map/ppermute | solution.py:1283
  634.7 3.5 add_convert_fusion
  642.8 4.1 slice_bitcast_fusion.27
  650.7 5.6 fusion.13
  662.7 26.5 %collective-permute-done.20 = bf16[2,3,704,256]{3,2,0,1:T(8,128)(2,1)} collective-permute-done((bf16[2,3,704,256]{3,2,0,1:T(8,128)(2,1)}, bf16[2,3,704,256]{3,2,0,1:T(8,128)(2,1)}, u32[]{:S(2)}, u32[]{:S(2)}) %collective-permute-start.20) | collective-permute-done | bytes 2162720 | tf_op jit(solution)/shard_map/ppermute | solution.py:1283
  695.2 3.1 fusion.24
  711.1 4.4 fusion.23
  715.6 4.3 fusion.3
  728.8 4.2 convolution_bitcast_fusion
  735.2 3.9 fusion.18
  739.0 2.5 pad_maximum_fusion.4
  741.6 5.5 copy.334
  747.2 2.8 dynamic-slice_convert_fusion.1
  752.4 6.8 fusion.16
  768.6 13.5 %concatenate.85 = f32[2,2,2,272,512]{4,3,2,1,0:T(8,128)} concatenate(f32[2,2,2,256,512]{4,3,2,1,0:T(8,128)} %bitcast.303, f32[2,2,2,9,512]{4,3,2,1,0:T(8,128)} %bitcast.318, f32[2,2,2,1,512]{4,3,2,1,0:T(1,128)} %concatenate.89, f32[2,2,2,2,512]{4,3,2,1,0:T(2,128)} %bitcast.338, f32[2,2,2,4,512]{4,3,2,1,0:T(4,128)} %broadcast_in_dim.108), dimensions={3} | concatenate | bytes 8912896 | tf_op jit(solution)/shard_map/concatenate | solution.py:1543
  787.6 3.5 slice_bitcast_fusion.1
  795.9 15.4 %collective-permute-done.13 = bf16[1,2,2,272,512]{4,3,2,1,0:T(8,128)(2,1)S(1)} collective-permute-done((bf16[1,2,2,272,512]{4,3,2,1,0:T(8,128)(2,1)S(1)}, bf16[1,2,2,272,512]{4,3,2,1,0:T(8,128)(2,1)S(1)}, u32[]{:S(2)}, u32[]{:S(2)}) %collective-permute-start.13) | collective-permute-done | bytes 1114144 | tf_op jit(solution)/shard_map/ppermute | solution.py:1283
  815.2 3.0 copy.323
  832.0 9.7 %dynamic_update_slice.54 = bf16[256,2,512]{2,1,0:T(2,128)(2,1)} dynamic-update-slice(bf16[256,2,512]{2,1,0:T(2,128)(2,1)} %broadcast.180.clone, bf16[256,1,512]{2,1,0:T(2,128)(2,1)S(1)} %copy.310, s32[]{:T(128)} %constant.347.clone.1, s32[]{:T(128)S(6)} %select_n.198, s32[]{:T(128)} %constant.347.clone.1) | dynamic-update-slice | bytes 524292 | tf_op jit(solution)/shard_map/dynamic_update_slice | solution.py:1293
  848.7 9.8 %dynamic_update_slice.55 = bf16[256,2,512]{2,1,0:T(2,128)(2,1)} dynamic-update-slice(bf16[256,2,512]{2,1,0:T(2,128)(2,1)} %dynamic_update_slice.54, bf16[256,1,512]{2,1,0:T(2,128)(2,1)S(1)} %copy.311, s32[]{:T(128)} %constant.347.clone.1, s32[]{:T(128)S(6)} %select_n.199, s32[]{:T(128)} %constant.347.clone.1) | dynamic-update-slice | bytes 524292 | tf_op jit(solution)/shard_map/dynamic_update_slice | solution.py:1294
  862.4 11.9 %all-gather.1 = f32[4,2,256]{2,1,0:T(2,128)S(1)} all-gather(f32[1,2,256]{2,1,0:T(2,128)S(1)} %slice_bitcast_fusion.25), channel_id=2, replica_groups=mesh['dp'=8,'tensor'=4] {'tensor'}, dimensions={0}, use_global_device_ids=true | all-gather | bytes 10240 | tf_op jit(solution)/shard_map/all_gather | solution.py:1578
  877.0 2.7 fusion.32
  (376 shorter events, 167.2 us)
Async XLA Ops:
  7.3 547.1 %reduce-scatter.4.cloned.1.call-start = ((), (), s32[]{:S(2)}) async-start(), calls=%async_computation.3 | async-start | bytes 2785280 | tf_op jit(solution)/shard_map/reduce_scatter | solution.py:1367
  235.2 47.4 %collective-permute-start.1 = (bf16[512,2048]{1,0:T(8,128)(2,1)S(1)}, bf16[512,2048]{1,0:T(8,128)(2,1)}, u32[]{:S(2)}, u32[]{:S(2)}) collective-permute-start(bf16[512,2048]{1,0:T(8,128)(2,1)S(1)} %slice_bitcast_fusion.13), channel_id=1, source_target_pairs={{0,8},{4,12},{8,0},{12,4},{16,24},{20,28},{24,16},{28,20},{1,9},{5... | collective-permute-start | bytes 6291464 | tf_op jit(solution)/shard_map/ppermute | solution.py:1283
  238.2 52.4 %copy-start.38 = (s32[2,2,512]{2,1,0:T(2,128)}, s32[2,2,512]{2,1,0:T(2,128)S(1)}, u32[]{:S(2)}) copy-start(s32[2,2,512]{2,1,0:T(2,128)S(1)} %get-tuple-element.222.slot_ref) | copy-start | bytes 24580
  282.6 8.0 collective-permute-start.2
  346.5 62.1 %collective-permute-start.6 = (bf16[512,2048]{1,0:T(8,128)(2,1)S(1)}, bf16[512,2048]{1,0:T(8,128)(2,1)}, u32[]{:S(2)}, u32[]{:S(2)}) collective-permute-start(bf16[512,2048]{1,0:T(8,128)(2,1)S(1)} %slice_bitcast_fusion.5), channel_id=1, source_target_pairs={{0,4},{4,0},{8,12},{12,8},{16,20},{20,16},{24,28},{28,24},{1,5},{5... | collective-permute-start | bytes 6291464 | tf_op jit(solution)/shard_map/ppermute | solution.py:1283
  382.4 21.6 %copy-start.30 = (f32[2,512,128]{2,1,0:T(8,128)}, f32[2,512,128]{2,1,0:T(8,128)S(1)}, u32[]{:S(2)}) copy-start(f32[2,512,128]{2,1,0:T(8,128)S(1)} %scatter.25) | copy-start | bytes 1572868
  407.3 55.3 %collective-permute-start.5 = (bf16[512,2048]{1,0:T(8,128)(2,1)}, bf16[512,2048]{1,0:T(8,128)(2,1)}, u32[]{:S(2)}, u32[]{:S(2)}) collective-permute-start(bf16[512,2048]{1,0:T(8,128)(2,1)} %slice_bitcast_fusion.7), channel_id=1, source_target_pairs={{0,4},{4,0},{8,12},{12,8},{16,20},{20,16},{24,28},{28,24},{1,5},{5... | collective-permute-start | bytes 6291464 | tf_op jit(solution)/shard_map/ppermute | solution.py:1283
  410.9 51.7 %collective-permute-start.7 = (bf16[512,2048]{1,0:T(8,128)(2,1)S(1)}, bf16[512,2048]{1,0:T(8,128)(2,1)}, u32[]{:S(2)}, u32[]{:S(2)}) collective-permute-start(bf16[512,2048]{1,0:T(8,128)(2,1)S(1)} %fusion.9), channel_id=1, source_target_pairs={{0,8},{4,12},{8,0},{12,4},{16,24},{20,28},{24,16},{28,20},{1,9},{5... | collective-permute-start | bytes 6291464 | tf_op jit(solution)/shard_map/ppermute | solution.py:1283
  414.6 29.5 %collective-permute-start.8 = (bf16[512,128]{1,0:T(8,128)(2,1)}, bf16[512,128]{1,0:T(8,128)(2,1)S(1)}, u32[]{:S(2)}, u32[]{:S(2)}) collective-permute-start(bf16[512,128]{1,0:T(8,128)(2,1)} %fusion.55), channel_id=1, source_target_pairs={{0,4},{4,0},{8,12},{12,8},{16,20},{20,16},{24,28},{28,24},{1,5},{5... | collective-permute-start | bytes 393224 | tf_op jit(solution)/shard_map/ppermute | solution.py:1283
  416.0 16.0 %copy-start.50 = (f32[2,2,512]{2,1,0:T(2,128)S(1)}, f32[2,2,512]{2,1,0:T(2,128)}, u32[]{:S(2)}) copy-start(f32[2,2,512]{2,1,0:T(2,128)} %get-tuple-element.115) | copy-start | bytes 24580
  432.0 10.1 %copy-start.49 = (f32[2,16,512]{2,1,0:T(8,128)S(1)}, f32[2,16,512]{2,1,0:T(8,128)}, u32[]{:S(2)}) copy-start(f32[2,16,512]{2,1,0:T(8,128)} %get-tuple-element.117) | copy-start | bytes 196612
  432.0 12.0 %copy-start.6 = (f32[128,2048]{1,0:T(8,128)S(1)}, f32[128,2048]{1,0:T(8,128)}, u32[]{:S(2)}) copy-start(f32[128,2048]{1,0:T(8,128)} %get-tuple-element.96) | copy-start | bytes 3145732
  440.2 2.7 collective-permute-start.9
  443.9 17.7 %collective-permute-start.10 = (bf16[512,128]{1,0:T(8,128)(2,1)S(1)}, bf16[512,128]{1,0:T(8,128)(2,1)S(1)}, u32[]{:S(2)}, u32[]{:S(2)}) collective-permute-start(bf16[512,128]{1,0:T(8,128)(2,1)S(1)} %fusion.49), channel_id=1, source_target_pairs={{0,8},{4,12},{8,0},{12,4},{16,24},{20,28},{24,16},{28,20},{1,9},{5... | collective-permute-start | bytes 393224 | tf_op jit(solution)/shard_map/ppermute | solution.py:1283
  468.4 174.4 %all-gather.4.cloned.1.call-start = ((), (), s32[]{:S(2)}) async-start(), calls=%async_computation.4 | async-start | bytes 2785280 | tf_op jit(solution)/shard_map/all_gather | solution.py:1483
  468.5 92.3 %copy-start.55 = (f32[128]{0:T(128)}, f32[128]{0:T(128)S(1)}, u32[]{:S(2)}) copy-start(f32[128]{0:T(128)S(1)} %add_rsqrt_fusion.2) | copy-start | bytes 1540
  476.2 11.3 %copy-start.32 = (bf16[8,1,352,256]{3,2,1,0:T(8,128)(2,1)S(1)}, bf16[8,1,352,256]{3,2,1,0:T(8,128)(2,1)}, u32[]{:S(2)}) copy-start(bf16[8,1,352,256]{3,2,1,0:T(8,128)(2,1)} %shard_map.299) | copy-start | bytes 4325380
  493.2 73.3 %collective-permute-start.22 = (bf16[1,2,2,3,352,256]{5,4,3,2,1,0:T(8,128)(2,1)}, bf16[1,2,2,3,352,256]{5,4,3,2,1,0:T(8,128)(2,1)}, u32[]{:S(2)}, u32[]{:S(2)}) collective-permute-start(bf16[1,2,2,3,352,256]{5,4,3,2,1,0:T(8,128)(2,1)} %constant_dynamic-slice_fusion), channel_id=1, source_target_pairs={{0,16},{4,20},{8,24},{12,28},{16,0},{20,4},{24,8},{28,12},{1,17},{... | collective-permute-start | bytes 6488072 | tf_op jit(solution)/shard_map/ppermute | solution.py:1283
  533.6 101.0 %collective-permute-start.19 = (bf16[1,2,2,3,704,256]{5,4,3,2,1,0:T(8,128)(2,1)}, bf16[1,2,2,3,704,256]{5,4,3,2,1,0:T(8,128)(2,1)}, u32[]{:S(2)}, u32[]{:S(2)}) collective-permute-start(bf16[1,2,2,3,704,256]{5,4,3,2,1,0:T(8,128)(2,1)} %constant_dynamic-slice_fusion.3), channel_id=1, source_target_pairs={{0,16},{4,20},{8,24},{12,28},{16,0},{20,4},{24,8},{28,12},{1,17},{... | collective-permute-start | bytes 12976136 | tf_op jit(solution)/shard_map/ppermute | solution.py:1283
  554.3 17.9 %collective-permute-start.3 = (bf16[512,2048]{1,0:T(8,128)(2,1)}, bf16[512,2048]{1,0:T(8,128)(2,1)}, u32[]{:S(2)}, u32[]{:S(2)}) collective-permute-start(bf16[512,2048]{1,0:T(8,128)(2,1)} %slice_bitcast_fusion.9), channel_id=1, source_target_pairs={{0,4},{4,0},{8,12},{12,8},{16,20},{20,16},{24,28},{28,24},{1,5},{5... | collective-permute-start | bytes 6291464 | tf_op jit(solution)/shard_map/ppermute | solution.py:1283
  562.4 313.2 %reduce-scatter.8.cloned.1.call-start = ((), (), s32[]{:S(2)}) async-start(), calls=%async_computation.6 | async-start | bytes 2621440 | tf_op jit(solution)/shard_map/reduce_scatter | solution.py:1367
  565.8 84.9 %collective-permute-start = (bf16[512,2048]{1,0:T(8,128)(2,1)}, bf16[512,2048]{1,0:T(8,128)(2,1)}, u32[]{:S(2)}, u32[]{:S(2)}) collective-permute-start(bf16[512,2048]{1,0:T(8,128)(2,1)} %slice_bitcast_fusion.11), channel_id=1, source_target_pairs={{0,4},{4,0},{8,12},{12,8},{16,20},{20,16},{24,28},{28,24},{1,5},{5... | collective-permute-start | bytes 6291464 | tf_op jit(solution)/shard_map/ppermute | solution.py:1283
  569.6 26.8 %collective-permute-start.23 = (bf16[2,3,352,256]{3,2,1,0:T(8,128)(2,1)S(1)}, bf16[2,3,352,256]{3,2,1,0:T(8,128)(2,1)S(1)}, u32[]{:S(2)}, u32[]{:S(2)}) collective-permute-start(bf16[2,3,352,256]{3,2,1,0:T(8,128)(2,1)S(1)} %dynamic-slice_bitcast_fusion.2), channel_id=1, source_target_pairs={{0,8},{4,12},{8,0},{12,4},{16,24},{20,28},{24,16},{28,20},{1,9},{5... | collective-permute-start | bytes 3244040 | tf_op jit(solution)/shard_map/ppermute | solution.py:1283
  571.3 63.4 %slice-start = ((s8[8650752]{0:T(1024)(128)(4,1)}), s8[4194304]{0:T(1024)(128)(4,1)S(1)}, s32[]{:S(2)}) async-start(s8[8650752]{0:T(1024)(128)(4,1)} %bitcast.279), calls=%async_computation.7 | async-start | bytes 8388608
  572.2 62.5 %slice-start.1 = ((s8[8650752]{0:T(1024)(128)(4,1)}), s8[4194304]{0:T(1024)(128)(4,1)S(1)}, s32[]{:S(2)}) async-start(s8[8650752]{0:T(1024)(128)(4,1)} %bitcast.279), calls=%async_computation.8 | async-start | bytes 8388608
  576.3 74.5 %collective-permute-start.4 = (bf16[512,2048]{1,0:T(8,128)(2,1)}, bf16[512,2048]{1,0:T(8,128)(2,1)}, u32[]{:S(2)}, u32[]{:S(2)}) collective-permute-start(bf16[512,2048]{1,0:T(8,128)(2,1)} %fusion.12), channel_id=1, source_target_pairs={{0,8},{4,12},{8,0},{12,4},{16,24},{20,28},{24,16},{28,20},{1,9},{5... | collective-permute-start | bytes 6291464 | tf_op jit(solution)/shard_map/ppermute | solution.py:1283
  578.5 56.2 %slice-start.2 = ((s8[8650752]{0:T(1024)(128)(4,1)}), s8[262144]{0:T(1024)(128)(4,1)S(1)}, s32[]{:S(2)}) async-start(s8[8650752]{0:T(1024)(128)(4,1)} %bitcast.279), calls=%async_computation.9 | async-start | bytes 524288
  597.8 58.5 %collective-permute-start.24 = (bf16[2,3,352,256]{3,2,1,0:T(8,128)(2,1)}, bf16[2,3,352,256]{3,2,1,0:T(8,128)(2,1)S(1)}, u32[]{:S(2)}, u32[]{:S(2)}) collective-permute-start(bf16[2,3,352,256]{3,2,1,0:T(8,128)(2,1)} %get-tuple-element.233), channel_id=1, source_target_pairs={{0,4},{4,0},{8,12},{12,8},{16,20},{20,16},{24,28},{28,24},{1,5},{5... | collective-permute-start | bytes 3244040 | tf_op jit(solution)/shard_map/ppermute | solution.py:1283
  641.4 47.8 %collective-permute-start.20 = (bf16[2,3,704,256]{3,2,0,1:T(8,128)(2,1)}, bf16[2,3,704,256]{3,2,0,1:T(8,128)(2,1)}, u32[]{:S(2)}, u32[]{:S(2)}) collective-permute-start(bf16[2,3,704,256]{3,2,0,1:T(8,128)(2,1)} %bitcast.276), channel_id=1, source_target_pairs={{0,8},{4,12},{8,0},{12,4},{16,24},{20,28},{24,16},{28,20},{1,9},{5... | collective-permute-start | bytes 6488072 | tf_op jit(solution)/shard_map/ppermute | solution.py:1283
  647.0 46.2 %collective-permute-start.11 = (bf16[512,2048]{1,0:T(8,128)(2,1)}, bf16[512,2048]{1,0:T(8,128)(2,1)}, u32[]{:S(2)}, u32[]{:S(2)}) collective-permute-start(bf16[512,2048]{1,0:T(8,128)(2,1)} %get-tuple-element.232), channel_id=1, source_target_pairs={{0,4},{4,0},{8,12},{12,8},{16,20},{20,16},{24,28},{28,24},{1,5},{5... | collective-permute-start | bytes 6291464 | tf_op jit(solution)/shard_map/ppermute | solution.py:1283
  693.2 30.2 %collective-permute-start.21 = (bf16[2,3,704,256]{3,2,0,1:T(8,128)(2,1)}, bf16[2,3,704,256]{3,2,0,1:T(8,128)(2,1)}, u32[]{:S(2)}, u32[]{:S(2)}) collective-permute-start(bf16[2,3,704,256]{3,2,0,1:T(8,128)(2,1)} %get-tuple-element.227), channel_id=1, source_target_pairs={{0,4},{4,0},{8,12},{12,8},{16,20},{20,16},{24,28},{28,24},{1,5},{5... | collective-permute-start | bytes 6488072 | tf_op jit(solution)/shard_map/ppermute | solution.py:1283
  711.1 12.3 %slice-start.3 = ((s8[4325376]{0:T(1024)(128)(4,1)}), s8[4194304]{0:T(1024)(128)(4,1)S(1)}, s32[]{:S(2)}) async-start(s8[4325376]{0:T(1024)(128)(4,1)} %bitcast.283), calls=%async_computation.10 | async-start | bytes 8388608
  720.1 12.8 %collective-permute-start.12 = (bf16[512,2048]{1,0:T(8,128)(2,1)S(1)}, bf16[512,2048]{1,0:T(8,128)(2,1)S(1)}, u32[]{:S(2)}, u32[]{:S(2)}) collective-permute-start(bf16[512,2048]{1,0:T(8,128)(2,1)S(1)} %fusion.22), channel_id=1, source_target_pairs={{0,4},{4,0},{8,12},{12,8},{16,20},{20,16},{24,28},{28,24},{1,5},{5... | collective-permute-start | bytes 6291464 | tf_op jit(solution)/shard_map/ppermute | solution.py:1283
  735.1 141.8 %reduce-scatter.6.cloned.1.call-start = ((), (), s32[]{:S(2)}) async-start(), calls=%async_computation.5 | async-start | bytes 2621440 | tf_op jit(solution)/shard_map/reduce_scatter | solution.py:1367
  750.0 41.1 %collective-permute-start.16 = (bf16[2,1,2,256,512]{4,3,2,1,0:T(8,128)(2,1)}, bf16[2,1,2,256,512]{4,3,2,1,0:T(8,128)(2,1)}, u32[]{:S(2)}, u32[]{:S(2)}) collective-permute-start(bf16[2,1,2,256,512]{4,3,2,1,0:T(8,128)(2,1)} %dynamic-slice_convert_fusion.1), channel_id=1, source_target_pairs={{0,8},{4,12},{8,0},{12,4},{16,24},{20,28},{24,16},{28,20},{1,9},{5... | collective-permute-start | bytes 3145736 | tf_op jit(solution)/shard_map/ppermute | solution.py:1283
  783.8 27.5 %collective-permute-start.13 = (bf16[1,2,2,272,512]{4,3,2,1,0:T(8,128)(2,1)S(1)}, bf16[1,2,2,272,512]{4,3,2,1,0:T(8,128)(2,1)S(1)}, u32[]{:S(2)}, u32[]{:S(2)}) collective-permute-start(bf16[1,2,2,272,512]{4,3,2,1,0:T(8,128)(2,1)S(1)} %dynamic-slice_convert_fusion), channel_id=1, source_target_pairs={{0,16},{4,20},{8,24},{12,28},{16,0},{20,4},{24,8},{28,12},{1,17},{... | collective-permute-start | bytes 3342344 | tf_op jit(solution)/shard_map/ppermute | solution.py:1283
  787.5 23.8 %slice-start.5 = ((s8[4456448]{0:T(1024)(128)(4,1)}), s8[4194304]{0:T(1024)(128)(4,1)S(1)}, s32[]{:S(2)}) async-start(s8[4456448]{0:T(1024)(128)(4,1)} %bitcast.287), calls=%async_computation.12 | async-start | bytes 8388608
  787.6 23.7 %slice-start.6 = ((s8[4456448]{0:T(1024)(128)(4,1)}), s8[262144]{0:T(1024)(128)(4,1)S(1)}, s32[]{:S(2)}) async-start(s8[4456448]{0:T(1024)(128)(4,1)} %bitcast.287), calls=%async_computation.13 | async-start | bytes 524288
  793.8 17.9 %copy-start.13 = (f32[2,1,2,256,512]{4,3,2,1,0:T(8,128)}, f32[2,1,2,256,512]{4,3,2,1,0:T(8,128)S(1)}, u32[]{:S(2)}) copy-start(f32[2,1,2,256,512]{4,3,2,1,0:T(8,128)S(1)} %convert_add_fusion.5) | copy-start | bytes 6291460
  794.8 27.1 %collective-permute-start.17 = (bf16[1,1,2,256,512]{4,3,2,1,0:T(8,128)(2,1)}, bf16[1,1,2,256,512]{4,3,2,1,0:T(8,128)(2,1)}, u32[]{:S(2)}, u32[]{:S(2)}) collective-permute-start(bf16[1,1,2,256,512]{4,3,2,1,0:T(8,128)(2,1)} %dynamic-slice_convert_fusion.3), channel_id=1, source_target_pairs={{0,16},{4,20},{8,24},{12,28},{16,0},{20,4},{24,8},{28,12},{1,17},{... | collective-permute-start | bytes 1572872 | tf_op jit(solution)/shard_map/ppermute | solution.py:1283
  812.7 13.4 %collective-permute-start.14 = (bf16[1,1,2,272,512]{4,3,2,1,0:T(8,128)(2,1)}, bf16[1,1,2,272,512]{4,3,2,1,0:T(8,128)(2,1)}, u32[]{:S(2)}, u32[]{:S(2)}) collective-permute-start(bf16[1,1,2,272,512]{4,3,2,1,0:T(8,128)(2,1)} %dynamic-slice_convert_fusion.2), channel_id=1, source_target_pairs={{0,8},{4,12},{8,0},{12,4},{16,24},{20,28},{24,16},{28,20},{1,9},{5... | collective-permute-start | bytes 1671176 | tf_op jit(solution)/shard_map/ppermute | solution.py:1283
  824.3 17.4 %collective-permute-start.18 = (bf16[256,512]{1,0:T(8,128)(2,1)}, bf16[256,512]{1,0:T(8,128)(2,1)}, u32[]{:S(2)}, u32[]{:S(2)}) collective-permute-start(bf16[256,512]{1,0:T(8,128)(2,1)} %get-tuple-element.247), channel_id=1, source_target_pairs={{0,4},{4,0},{8,12},{12,8},{16,20},{20,16},{24,28},{28,24},{1,5},{5... | collective-permute-start | bytes 786440 | tf_op jit(solution)/shard_map/ppermute | solution.py:1283
  828.7 17.7 %collective-permute-start.15 = (bf16[272,512]{1,0:T(8,128)(2,1)}, bf16[272,512]{1,0:T(8,128)(2,1)}, u32[]{:S(2)}, u32[]{:S(2)}) collective-permute-start(bf16[272,512]{1,0:T(8,128)(2,1)} %get-tuple-element.243), channel_id=1, source_target_pairs={{0,4},{4,0},{8,12},{12,8},{16,20},{20,16},{24,28},{28,24},{1,5},{5... | collective-permute-start | bytes 835592 | tf_op jit(solution)/shard_map/ppermute | solution.py:1283
  848.7 26.8 %copy-start.11 = (bf16[128,2048]{1,0:T(8,128)(2,1)S(1)}, bf16[128,2048]{1,0:T(8,128)(2,1)}, u32[]{:S(2)}) copy-start(bf16[128,2048]{1,0:T(8,128)(2,1)} %tokens_ref.1) | copy-start | bytes 1572868
  848.7 26.8 %copy-start.58 = (f32[128]{0:T(128)S(1)}, f32[128]{0:T(128)}, u32[]{:S(2)}) copy-start(f32[128]{0:T(128)} %add_rsqrt_fusion.1) | copy-start | bytes 1540
  858.5 18.4 %copy-start.18 = (bf16[128,2048]{1,0:T(8,128)(2,1)S(1)}, bf16[128,2048]{1,0:T(8,128)(2,1)}, u32[]{:S(2)}) copy-start(bf16[128,2048]{1,0:T(8,128)(2,1)} %outgrad_ref.1) | copy-start | bytes 1572868
  858.5 18.4 %copy-start.56 = (f32[128]{0:T(128)S(1)}, f32[128]{0:T(128)}, u32[]{:S(2)}) copy-start(f32[128]{0:T(128)} %copy-done.55) | copy-start | bytes 1540
  858.5 18.5 %copy-start.60 = (f32[128]{0:T(128)S(1)}, f32[128]{0:T(128)}, u32[]{:S(2)}) copy-start(f32[128]{0:T(128)} %copy-done.59) | copy-start | bytes 1540
  (52 other events, 209.5 us)
Sparse Core Ops, SparseCore 0:
  468.5 46.4 reduce-scatter.3
  562.5 48.6 all-gather.3
  735.2 44.5 reduce-scatter.7
  819.9 44.7 reduce-scatter.5

commit v3 on v2

--- a/solution.py
+++ b/solution.py
@@ -273,6 +273,62 @@
     )(left_a, right_a, left_b, right_b)
 
 
+def units_body(keep, pad, *refs):
+    lefts, rights, outs = refs[:4], refs[4:8], refs[8:]
+    unit, units = pl.program_id(0), pl.num_programs(0)
+
+    def store(first, second):
+        total = dot(lefts[first][0], rights[first][0], 0, 0)
+        total = (total + dot(lefts[second][0], rights[second][0], 0, 0)).astype(BF)
+        for part, out_ref in enumerate(outs):
+            blocks, _, _, slice_width = out_ref.shape
+            for k in range(blocks):
+                out_ref[k, 0] = total[
+                    part * pad : part * pad + keep, k * slice_width : (k + 1) * slice_width
+                ]
+
+    @pl.when(unit < units - 1)
+    def _():
+        store(0, 1)
+
+    @pl.when(unit == units - 1)
+    def _():
+        store(2, 3)
+
+
+def units_call(keep, pad, dp, routed, shared):
+    lefts = [pair[0] for pair in routed + shared]
+    rights = [pair[1] for pair in routed + shared]
+    many, _, wide = lefts[0].shape
+    width = rights[0].shape[2]
+    slice_width = width // dp
+    blocks = max(1, 512 // slice_width)
+    parts = wide // pad
+    last = dp // blocks - 1
+
+    def spec(array, cols, shared_unit):
+        def where(u, j):
+            mine = (u == many) if shared_unit else (u < many)
+            unit = 0 if shared_unit else jnp.minimum(u, many - 1)
+            if cols:
+                return (unit, 0, jnp.where(mine, j, 0 if shared_unit else last))
+            return (unit, 0, 0)
+
+        return pl.BlockSpec((1, array.shape[1], cols or wide), where)
+
+    cols = blocks * slice_width
+    return call(
+        functools.partial(units_body, keep, pad),
+        (many + 1, dp // blocks),
+        [spec(a, 0, n > 1) for n, a in enumerate(lefts)]
+        + [spec(a, cols, n > 1) for n, a in enumerate(rights)],
+        [pl.BlockSpec((blocks, 1, keep, slice_width), lambda u, j: (j, u, 0, 0))] * parts,
+        [jax.ShapeDtypeStruct((dp, many + 1, keep, slice_width), BF)] * parts,
+        4 * (many * lefts[0].shape[1] + lefts[2].shape[1]) * wide * width,
+        (many * lefts[0].shape[1] + lefts[2].shape[1]) * (wide + width) * 4,
+    )(*lefts, *rights)
+
+
 MESH = pl.DeviceIdType.MESH
 
 
@@ -324,24 +380,6 @@
         for copy, there in self.sends(0):
             pl.when(there)(copy.start)
 
-    def step(self, k, each=None):
-        z, top = self.z, self.depth - 1
-        arrivals = (
-            (self.ups[k - 1], z >= k, z - k),
-            (self.downs[k - 1], z + k <= top, z + k),
-        )
-        onward = self.sends(k) if k < top else (None, None)
-        for (copy, there, p), further in zip(arrivals, onward):
-
-            def arrive(copy=copy, p=p):
-                copy.wait_recv()
-                if each is not None:
-                    each(k, p)
-
-            pl.when(there)(arrive)
-            if further is not None:
-                pl.when(further[1])(further[0].start)
-
     def finish(self):
         for k in range(self.depth - 1):
             for copy, there in self.sends(k):
@@ -370,6 +408,40 @@
 
 def spin(field, cos_rows, sin_rows):
     return field * cos_rows + pltpu.roll(field, field.shape[-1] // 2, 1) * sin_rows
+
+
+def piece_of(buffer, p, rows):
+    return buffer.at[pl.ds(pl.multiple_of(p * rows, rows), rows)]
+
+
+def pass_on(c, source, target, z, depth, rows, sibling, passed):
+    def make(p):
+        return c.remote(piece_of(source, p, rows), piece_of(target, p, rows), dp=sibling)
+
+    ups = [make(z - k) for k in range(1, depth)]
+    downs = [make(z + k) for k in range(1, depth)]
+    for k in range(1, depth):
+        passed.append((ups[k - 1], z >= k))
+        passed.append((downs[k - 1], z + k <= depth - 1))
+
+    def each(k, up):
+        (ups if up else downs)[k - 1].start()
+
+    return each
+
+
+def line_step(line, k, each=None):
+    z, top = line.z, line.depth - 1
+    onward = line.sends(k) if k < top else (None, None)
+    for up, copy, there, further in (
+        (True, line.ups[k - 1], z >= k, onward[0]),
+        (False, line.downs[k - 1], z + k <= top, onward[1]),
+    ):
+        pl.when(there)(copy.wait_recv)
+        if further is not None:
+            pl.when(further[1])(further[0].start)
+        if each is not None:
+            pl.when(there)(functools.partial(each, k, up))
 
 
 def forward_body(
@@ -532,33 +604,9 @@
     for copy in gain_spread:
         copy.start()
 
-    def pass_on(buffer_from, buffer_to, passed):
-        ups = [c.remote(piece(buffer_from, z - k), piece(buffer_to, z - k), dp=peer_of(me, 1)) for k in range(1, depth)]
-        downs = [c.remote(piece(buffer_from, z + k), piece(buffer_to, z + k), dp=peer_of(me, 1)) for k in range(1, depth)]
-        for k in range(1, depth):
-            passed.append((ups[k - 1], z >= k))
-            passed.append((downs[k - 1], z + k <= depth - 1))
-
-        def each(k, p, up):
-            (ups if up else downs)[k - 1].start()
-
-        return each
-
     tok_passed = []
-    pass_tok = pass_on(tok.at[0], tok.at[1], tok_passed)
-
-    def line_step(line, k, each):
-        top = depth - 1
-        onward = line.sends(k) if k < top else (None, None)
-        for up, copy, there, further in (
-            (True, line.ups[k - 1], z >= k, onward[0]),
-            (False, line.downs[k - 1], z + k <= top, onward[1]),
-        ):
-            pl.when(there)(copy.wait_recv)
-            if further is not None:
-                pl.when(further[1])(further[0].start)
-            if each is not None:
-                pl.when(there)(functools.partial(each, k, None, up))
+    sibling = peer_of(me, 1)
+    pass_tok = pass_on(c, tok.at[0], tok.at[1], z, depth, rows, sibling, tok_passed)
 
     line_step(tok_line, 1, pass_tok)
     for k in range(1, len(bits) - 1):
@@ -634,7 +682,7 @@
 
     norm_rows(0)
     project(0)
-    line_step(grad_line, 1, None)
+    line_step(grad_line, 1)
     for copy in near[0]:
         copy.wait()
     for copy in far[0]:
@@ -680,7 +728,7 @@
 
     attend(1)
     if depth > 2:
-        line_step(grad_line, 2, None)
+        line_step(grad_line, 2)
     project_out(1)
     part_pass = c.remote(part.at[1], part_in, dp=peer_of(me, 1))
     part_pass.start()
@@ -706,7 +754,7 @@
             hidden_ref[...] = total + tok[0, at, :].astype(F32)
 
     for k in range(3, depth):
-        line_step(grad_line, k, None)
+        line_step(grad_line, k)
     x_grad = c.remote(grads_ref.at[0], grads_ref.at[2], dp=peer_of(me, 2))
     x_grad.start()
     own_pass = c.remote(grads_ref.at[0], grads_ref.at[1], dp=peer_of(me, 1))
@@ -732,7 +780,9 @@
     norm_own = c.remote(piece(norm_ref.at[0], z), piece(norm_ref.at[1], z), dp=peer_of(me, 1))
     norm_own.start()
     norm_passed = []
-    pass_norm = pass_on(norm_ref.at[0], norm_ref.at[1], norm_passed)
+    pass_norm = pass_on(
+        c, norm_ref.at[0], norm_ref.at[1], z, depth, rows, sibling, norm_passed
+    )
     for k in range(1, depth):
         line_step(norm_line, k, pass_norm)
 
@@ -808,6 +858,478 @@
     )(codes, misc, gains, cos_rows, sin_rows, *arrays, *units)
 
 
+def backward_body(
+    sizes,
+    terms_ref,
+    probs_mine_ref,
+    router_ref,
+    gain_rows,
+    cos_ref,
+    sin_ref,
+    hidden_ref,
+    outgrad_ref,
+    grad_a_ref,
+    grad_b_ref,
+    grad_c_ref,
+    out_a_ref,
+    out_b_ref,
+    out_c_ref,
+    down_ref,
+    gate_ref,
+    up_ref,
+    tok_hbm,
+    weights_hbm,
+    qkv_hbm,
+    probs_hbm,
+    mix_hbm,
+    norm_hbm,
+    output_ref,
+    input_ref,
+    down_out,
+    gate_out,
+    up_out,
+    attn_out,
+    misc_out,
+    gains_out,
+    own_sum,
+    arrived,
+    three,
+    scatter_in,
+    terms_sum,
+    terms_in,
+    back,
+    tok,
+    weights,
+    qkv,
+    probs_ref,
+    mix_ref,
+    scales,
+    qkv_grad,
+    part_in,
+    keep,
+    total_a,
+    first_qk,
+    first_vo,
+    second_in,
+    misc_part,
+    misc_in,
+    gains_in,
+    vectors,
+    send,
+    recv,
+    here,
+):
+    dp, depth, experts, head = sizes
+    me, z = lax.axis_index("dp"), lax.axis_index("tensor")
+    core, x, y = me % 2, (me // 2) % 2, me // 4
+    rows, width = output_ref.shape
+    seq_len = rows * depth
+    slice_width = width // dp
+    pair = mix_ref.shape[2]
+    pairs = pair // head
+    bits = [1, 2, 4]
+    c = Copies(send, recv, here)
+
+    greet(me, z, dp, depth)
+
+    matrices = ((gate_ref, gate_out), (up_ref, up_out), (down_ref, down_out))
+    over = []
+    for m, (source, _) in enumerate(matrices):
+        other = source.at[pl.ds((1 - y) * 4, 4)]
+        over.append(c.remote(other, arrived.at[m], dp=peer_of(me, 4)))
+        over[m].start()
+    grads = (grad_a_ref.at[0], grad_b_ref, grad_c_ref)
+    loads = [c.local(grads[k], three.at[k]) for k in range(3)]
+    for copy in loads:
+        copy.start()
+    own_loads = [
+        c.local(source.at[pl.ds(y * 4, 4)], own_sum) for source, _ in matrices
+    ]
+    inputs = [
+        c.local(a, b)
+        for a, b in (
+            (weights_hbm, weights),
+            (mix_hbm, mix_ref),
+            (qkv_hbm, qkv),
+            (probs_hbm, probs_ref),
+            (tok_hbm, tok),
+        )
+    ]
+    own_loads[0].start()
+    for copy in inputs:
+        copy.start()
+
+    def at_of(p):
+        return pl.ds(pl.multiple_of(p * rows, rows), rows)
+
+    for copy in loads:
+        copy.wait()
+    scatter, small = [], []
+    for r in list(range(1, depth)) + [0]:
+        at = at_of((z + r) % depth)
+        total = three[0, at, :].astype(F32) + three[1, at, :].astype(F32)
+        total = total + three[2, at, :].astype(F32)
+        extra = terms_ref[0, at, :] + terms_ref[1, at, :] + terms_ref[2, at, :]
+        if r:
+            three[0, at, :] = total.astype(BF)
+            terms_sum[at, :] = extra
+            peer = (z + r) % depth
+            scatter.append(c.remote(three.at[0, at], scatter_in.at[0, r - 1], tensor=peer))
+            small.append(c.remote(terms_sum.at[at], terms_in.at[r - 1], tensor=peer))
+            scatter[-1].start()
+            small[-1].start()
+        else:
+            keep[0] = total
+            terms_sum[at, :] = extra
+
+    def add_over(m):
+        own_loads[m].wait()
+        over[m].wait_recv()
+        copies = []
+        for r in (2, 3, 1, 0):
+            k = peer_of(me, r) % 4
+            for unit in range(own_sum.shape[1]):
+                arrived[m, k, unit] = (
+                    own_sum[k, unit].astype(F32) + arrived[m, k, unit].astype(F32)
+                ).astype(BF)
+            place = matrices[m][1].at[me % 4]
+            if r:
+                copies.append(c.remote(arrived.at[m, k], place, dp=peer_of(me, r)))
+            else:
+                copies.append(c.local(arrived.at[m, k], place))
+            copies[-1].start()
+        if m + 1 < len(own_loads):
+            own_loads[m + 1].start()
+        return copies
+
+    for copy in scatter:
+        copy.wait_recv()
+    for copy in small:
+        copy.wait_recv()
+    route = terms_sum[at_of(z), :]
+    grad = keep[0]
+    for r in range(1, depth):
+        grad = grad + scatter_in[0, r - 1].astype(F32)
+        route = route + terms_in[r - 1]
+    probs_mine = probs_mine_ref[...]
+    lane = lax.broadcasted_iota(jnp.int32, route.shape, 1)
+    inner = jnp.sum(jnp.where(lane < experts, probs_mine * route, 0.0), axis=1, keepdims=True)
+    logits = jnp.where(
+        lane < experts,
+        probs_mine * (route - inner),
+        jnp.where(lane == experts, route * probs_mine * (1.0 - probs_mine), 0.0),
+    ).astype(BF)
+    grad = grad + dot(logits, router_ref[...])
+    hidden = hidden_ref[...]
+    scale = lax.rsqrt(jnp.mean(hidden * hidden, axis=-1, keepdims=True) + EPS)
+    unit = hidden * scale
+    vectors[1:2, :] = jnp.sum(grad * unit, axis=0, keepdims=True)
+    grad = grad * gain_rows[1:2, :]
+    grad = outgrad_ref[...].astype(F32) + scale * (
+        grad - unit * jnp.mean(grad * unit, axis=-1, keepdims=True)
+    )
+    keep[0] = grad
+    back[0, at_of(z), :width] = grad.astype(BF)
+    back[0, at_of(z), width:] = logits
+
+    line = Line(c, back.at[0], z, depth, rows)
+    line.begin()
+    sibling = peer_of(me, 1)
+    back_own = c.remote(piece_of(back.at[0], z, rows), piece_of(back.at[1], z, rows), dp=sibling)
+    back_own.start()
+    passed = []
+    pass_back = pass_on(c, back.at[0], back.at[1], z, depth, rows, sibling, passed)
+    for copy in scatter:
+        copy.wait_send()
+    outs = (out_a_ref.at[0], out_b_ref, out_c_ref)
+    out_loads = [c.local(outs[k], three.at[k]) for k in range(3)]
+    for copy in out_loads:
+        copy.start()
+    units = add_over(0)
+    line_step(line, 1, pass_back)
+
+    for copy in inputs:
+        copy.wait()
+
+    def scale_rows(i, carry):
+        at = at_of(i)
+        for s in range(2):
+            data = tok[s, at, :].astype(F32)
+            scales[s, at, :] = lax.rsqrt(jnp.mean(data * data, axis=-1, keepdims=True) + EPS)
+        return carry
+
+    lax.fori_loop(0, depth, scale_rows, 0)
+    line_step(line, 2, pass_back)
+    for copy in out_loads:
+        copy.wait()
+    out_scatter = []
+    for r in list(range(1, depth)) + [0]:
+        at = at_of((z + r) % depth)
+        total = three[0, at, :].astype(F32) + three[1, at, :].astype(F32)
+        total = total + three[2, at, :].astype(F32)
+        if r:
+            three[0, at, :] = total.astype(BF)
+            peer = (z + r) % depth
+            out_scatter.append(c.remote(three.at[0, at], scatter_in.at[1, r - 1], tensor=peer))
+        else:
+            keep[1] = total + hidden_ref[...]
+    line_step(line, 3, pass_back)
+    back_own.wait()
+    for copy, there in passed:
+        pl.when(there)(copy.wait)
+    for copy in out_scatter:
+        copy.start()
+
+    def block_of(d):
+        return tuple(d // bit % 2 for bit in reversed(bits))
+
+    def slab(d):
+        return slice(d * slice_width, (d + 1) * slice_width)
+
+    def attention(s):
+        mixed = jnp.zeros((seq_len, pair), F32)
+        for d in range(dp):
+            block = weights[block_of(d) + (slice(None), slice(3 * pair, 4 * pair))]
+            mixed = mixed + dot(back[s, :, slab(d)], block)
+        mixed = mixed.astype(BF)
+        for h in range(pairs):
+            n = s * pairs + h
+            cot = mixed[:, h * head : (h + 1) * head]
+            key_total = jnp.zeros((seq_len, head), F32)
+            value_total = jnp.zeros((seq_len, head), F32)
+            for b in range(2):
+                at = slice(b * seq_len // 2, (b + 1) * seq_len // 2)
+                p_low = probs_ref[n, at, :]
+                p = p_low.astype(F32)
+                p_grad = dot(cot[at], qkv[2, n], 1, 1)
+                s_grad = p * (p_grad - jnp.sum(p * p_grad, axis=1, keepdims=True))
+                s_grad = s_grad.astype(BF)
+                q_grad = dot(s_grad, qkv[1, n]) * head ** (-0.5)
+                q_grad = spin(q_grad, cos_ref[at, :], -sin_ref[at, :])
+                qkv_grad[s, at, h * head : (h + 1) * head] = q_grad.astype(BF)
+                key_total = key_total + dot(s_grad, qkv[0, n, at, :], 0, 0)
+                value_total = value_total + dot(p_low, cot[at], 0, 0)
+            k_grad = spin(key_total * head ** (-0.5), cos_ref[...], -sin_ref[...])
+            a = pair + h * head
+            qkv_grad[s, :, a : a + head] = k_grad.astype(BF)
+            qkv_grad[s, :, a + pair : a + pair + head] = value_total.astype(BF)
+
+    def first_grad(s):
+        for d in range(dp):
+            block = weights[block_of(d) + (slice(None), slice(0, 3 * pair))]
+            total = dot(qkv_grad[s], block, 1, 1)
+            three[1 + s, :, slab(d)] = total.astype(BF)
+            unit_block = tok[s, :, slab(d)].astype(F32) * scales[s]
+            row = jnp.sum(total * unit_block, axis=0, keepdims=True)
+            vectors[2 + s : 3 + s, slab(d)] = row
+
+    attention(1)
+    first_grad(1)
+    part_pass = c.remote(three.at[2], part_in, dp=sibling)
+    part_pass.start()
+    units += add_over(1)
+    attention(0)
+    first_grad(0)
+    part_pass.wait_recv()
+    first_scatter = []
+    for r in list(range(1, depth)) + [0]:
+        at = at_of((z + r) % depth)
+        total = three[1, at, :].astype(F32) + part_in[at, :].astype(F32)
+        if r:
+            three[1, at, :] = total.astype(BF)
+            peer = (z + r) % depth
+            copy = c.remote(three.at[1, at], scatter_in.at[2, r - 1], tensor=peer)
+            copy.start()
+            first_scatter.append(copy)
+        else:
+            keep[2] = total
+
+    for d in range(dp):
+        total = jnp.zeros((slice_width, 3 * pair), F32)
+        out_total = jnp.zeros((slice_width, pair), F32)
+        for s in range(2):
+            data = tok[s, :, slab(d)].astype(F32) * scales[s] * gain_rows[0:1, slab(d)]
+            total = total + dot(data.astype(BF), qkv_grad[s], 0, 0)
+            out_total = out_total + dot(back[s, :, slab(d)], mix_ref[s], 0, 0)
+        total_a[block_of(d) + (slice(None), slice(0, 3 * pair))] = total.astype(BF)
+        total_a[block_of(d) + (slice(None), slice(3 * pair, 4 * pair))] = out_total.astype(BF)
+
+    half = 2 * pair
+
+    def index(y_at, x_at, k):
+        return (y_at, x_at, slice(None), slice(None), pl.ds(k * half, half))
+
+    every = pl.ds(0, 2)
+    qk_first = c.remote(
+        total_a.at[index(pl.ds(1 - y, 1), every, 0)], first_qk, dp=peer_of(me, 4)
+    )
+    vo_first = c.remote(
+        total_a.at[index(every, pl.ds(1 - x, 1), 1)], first_vo, dp=peer_of(me, 2)
+    )
+    qk_first.start()
+    vo_first.start()
+
+    for copy in out_scatter:
+        copy.wait_send()
+    norm_load = c.local(norm_hbm.at[0], three.at[0])
+    norm_load.start()
+    norm_load.wait()
+    router_part = dot(back[0, :, width:], three[0], 0, 0)
+    ones = jnp.ones((16, seq_len), BF)
+    bias_row = dot(ones, qkv_grad[0]) + dot(ones, qkv_grad[1])
+    lane = lax.broadcasted_iota(jnp.int32, bias_row.shape, 1)
+    sub = lax.broadcasted_iota(jnp.int32, bias_row.shape, 0)
+    head_slice = head // dp
+    bias_rows = jnp.where(lane % head // head_slice == sub, bias_row, 0.0)
+    high = bias_rows.astype(BF)
+    low = (bias_rows - high.astype(F32)).astype(BF)
+    lane = lax.broadcasted_iota(jnp.int32, (3 * pair, slice_width), 1)
+    sub = lax.broadcasted_iota(jnp.int32, (3 * pair, slice_width), 0)
+    place = (sub // head * head_slice + sub % head_slice == lane).astype(F32).astype(BF)
+    bias_rows = dot(high, place) + dot(low, place)
+    sub = lax.broadcasted_iota(jnp.int32, (16, slice_width), 0)
+    misc_copies = []
+    for d in range(dp):
+        tile = jnp.where(sub <= experts, router_part[:16, slab(d)], 0.0)
+        tile = jnp.where(sub == experts + 1 + core, bias_rows[d : d + 1], tile)
+        gain_one = vectors[2:3, slab(d)] + vectors[3:4, slab(d)]
+        tile = jnp.where(sub == experts + 3, gain_one, tile)
+        tile = jnp.where(sub == experts + 4, vectors[1:2, slab(d)], tile)
+        misc_part[d] = tile
+    for r in range(1, dp):
+        to = peer_of(me, r)
+        misc_copies.append(c.remote(misc_part.at[to], misc_in.at[r - 1], dp=to))
+        misc_copies[-1].start()
+    units += add_over(2)
+
+    qk_first.wait()
+    mine = index(pl.ds(y, 1), every, 0)
+    total_a[mine] = (total_a[mine].astype(F32) + first_qk[...].astype(F32)).astype(BF)
+    qk_second = c.remote(
+        total_a.at[index(pl.ds(y, 1), pl.ds(1 - x, 1), 0)], second_in.at[0], dp=peer_of(me, 2)
+    )
+    qk_second.start()
+    vo_first.wait()
+    mine = index(every, pl.ds(x, 1), 1)
+    total_a[mine] = (total_a[mine].astype(F32) + first_vo[...].astype(F32)).astype(BF)
+    vo_second = c.remote(
+        total_a.at[index(pl.ds(1 - y, 1), pl.ds(x, 1), 1)], second_in.at[1], dp=peer_of(me, 4)
+    )
+    vo_second.start()
+
+    total = misc_part[me]
+    for r, copy in enumerate(misc_copies):
+        copy.wait_recv()
+        total = total + misc_in[r]
+    misc_out[...] = total
+    gain_copies = []
+    for r in range(1, depth):
+        peer = (z + r) % depth
+        gain_copies.append(c.remote(misc_out.at[8:16], gains_in.at[r - 1], tensor=peer))
+        gain_copies[-1].start()
+
+    finals = []
+    for k, copy in enumerate((qk_second, vo_second)):
+        copy.wait()
+        mine = (y, x, slice(None), slice(None), pl.ds(k * half, half))
+        total_a[mine] = (
+            total_a[mine].astype(F32) + second_in[k, 0, 0].astype(F32)
+        ).astype(BF)
+        for other in (True, False):
+            to = 1 - core if other else core
+            source = total_a.at[y, x, to, :, pl.ds(k * half, half)]
+            place = attn_out.at[core, :, pl.ds(k * half, half)]
+            finals.append(c.remote(source, place, dp=sibling) if other else c.local(source, place))
+            finals[-1].start()
+
+    for copy in out_scatter:
+        copy.wait_recv()
+    total = keep[1]
+    for r in range(1, depth):
+        total = total + scatter_in[1, r - 1].astype(F32)
+    output_ref[...] = total.astype(BF)
+    for copy in first_scatter:
+        copy.wait_recv()
+    total = keep[2]
+    for r in range(1, depth):
+        total = total + scatter_in[2, r - 1].astype(F32)
+    total = total * gain_rows[0:1, :]
+    scale = scales[0, at_of(z), :]
+    unit = tok[0, at_of(z), :].astype(F32) * scale
+    total = keep[0] + scale * (total - unit * jnp.mean(total * unit, axis=-1, keepdims=True))
+    input_ref[...] = total.astype(BF)
+
+    total = misc_out[8:16, :]
+    for r, copy in enumerate(gain_copies):
+        copy.wait()
+        total = total + gains_in[r]
+    gains_out[...] = total
+    for copy in finals + units:
+        copy.wait()
+    line.finish()
+    for copy in over + small + first_scatter + misc_copies + [part_pass]:
+        copy.wait_send()
+
+
+def backward_call(dp, depth, experts, head, in_vmem, in_hbm):
+    output_rows, width = in_vmem[6].shape
+    seq_len = output_rows * depth
+    slice_width = width // dp
+    units = in_hbm[6].shape[1:]
+    pair = in_hbm[13].shape[2]
+    pairs = pair // head
+    vmem, hbm = pl.BlockSpec(memory_space=pltpu.VMEM), pl.BlockSpec(memory_space=pl.ANY)
+    shape = jax.ShapeDtypeStruct
+    final = shape((4,) + units, BF)
+    return pl.pallas_call(
+        functools.partial(backward_body, (dp, depth, experts, head)),
+        in_specs=[vmem] * len(in_vmem) + [hbm] * len(in_hbm),
+        out_specs=[vmem, vmem, hbm, hbm, hbm, vmem, vmem, vmem],
+        out_shape=[
+            shape((output_rows, width), BF),
+            shape((output_rows, width), BF),
+            final,
+            final,
+            final,
+            shape((2, slice_width, 4 * pair), BF),
+            shape((16, slice_width), F32),
+            shape((8, slice_width), F32),
+        ],
+        scratch_shapes=[
+            pltpu.VMEM((4,) + units, BF),
+            pltpu.VMEM((3, 4) + units, BF),
+            pltpu.VMEM((3, seq_len, width), BF),
+            pltpu.VMEM((3, depth - 1, output_rows, width), BF),
+            pltpu.VMEM((seq_len, 128), F32),
+            pltpu.VMEM((depth - 1, output_rows, 128), F32),
+            pltpu.VMEM((2, seq_len, width + 128), BF),
+            pltpu.VMEM((2, seq_len, width), BF),
+            pltpu.VMEM((2, 2, 2, slice_width, 4 * pair), BF),
+            pltpu.VMEM((3, 2 * pairs, seq_len, head), BF),
+            pltpu.VMEM((2 * pairs, seq_len, seq_len), BF),
+            pltpu.VMEM((2, seq_len, pair), BF),
+            pltpu.VMEM((2, seq_len, 1), F32),
+            pltpu.VMEM((2, seq_len, 3 * pair), BF),
+            pltpu.VMEM((seq_len, width), BF),
+            pltpu.VMEM((3, output_rows, width), F32),
+            pltpu.VMEM((2, 2, 2, slice_width, 4 * pair), BF),
+            pltpu.VMEM((1, 2, 2, slice_width, 2 * pair), BF),
+            pltpu.VMEM((2, 1, 2, slice_width, 2 * pair), BF),
+            pltpu.VMEM((2, 1, 1, 2, slice_width, 2 * pair), BF),
+            pltpu.VMEM((dp, 16, slice_width), F32),
+            pltpu.VMEM((dp - 1, 16, slice_width), F32),
+            pltpu.VMEM((depth - 1, 8, slice_width), F32),
+            pltpu.VMEM((8, width), F32),
+            pltpu.SemaphoreType.DMA((96,)),
+            pltpu.SemaphoreType.DMA((96,)),
+            pltpu.SemaphoreType.DMA((40,)),
+        ],
+        compiler_params=pltpu.CompilerParams(
+            collective_id=1, has_side_effects=True, vmem_limit_bytes=62 * 2**20
+        ),
+    )(*in_vmem, *in_hbm)
+
+
 def local_plain(
     dp,
     tokens,
@@ -1344,30 +1866,11 @@
     )
     gateup_all = gateup_all.reshape(mine_experts + 1, 2 * hidden_pad, width)
     down_all = down_all.reshape(mine_experts + 1, hidden_pad, width)
-    attn_weights = attn_weights.reshape(width, 4 * pair_width)
-    qk_full, vo_full = attn_weights[:, : 2 * pair_width], attn_weights[:, 2 * pair_width :]
-    out_weight = vo_full[:, pair_width:]
     router_rows = jnp.concatenate([misc_all[d] for d in range(dp)], axis=1)
     router_rows = jnp.where(jnp.arange(16)[:, None] <= experts, router_rows, 0.0).astype(BF)
     router_full = router_rows[: experts + 1].T
     codes_all = codes_all[:, : 2 * top_count]
     codes_a, codes_b = codes_all[:2], codes_all[2:]
-    misc_rows = 16
-    rows_f = tok.astype(F32)
-    first_scale = lax.rsqrt(jnp.mean(rows_f * rows_f, axis=-1, keepdims=True) + EPS)
-    score_scale = head_width ** (-0.5)
-    inputs = tokens.astype(F32)
-    second_scale = lax.rsqrt(jnp.mean(hidden * hidden, axis=-1, keepdims=True) + EPS)
-    second_unit = hidden * second_scale
-
-    def core_sum(own, sibling):
-        return own + swap(sibling.astype(BF), 1).astype(F32)
-
-    def z_scatter(array):
-        return lax.psum_scatter(
-            array.astype(BF), "tensor", scatter_dimension=0, tiled=True
-        ).astype(F32)
-
     norm_z = norm_own[0]
     norm_a = norm_own
     norm_x = swap(norm_z, 2)
@@ -1408,202 +1911,70 @@
         )
         return wide.at[..., experts].set(terms[..., mine_experts])
 
-    def group_sum(a, b):
-        across = b[0].astype(F32) + swap(b[1].astype(BF), 1).astype(F32)
-        near = a[0].astype(F32) + swap(a[1].astype(BF), 1).astype(F32)
-        return near + swap(across.astype(BF), 2).astype(F32)
-
-    grad_sum = group_sum(row_grad_a, row_grad_b)
-    term_sum = group_sum(spread(fed_a[2]), spread(fed_b[2]))
-    packed = z_scatter(jnp.concatenate([grad_sum, term_sum], axis=-1))
-    second_grad, gate_sums = packed[:, :width], packed[:, width:]
+    def over_group(a, b):
+        across = b[0].astype(F32) + swap(b[1], 1).astype(F32)
+        return a, swap(a[1], 1), swap(across.astype(b.dtype), 2)
+
+    grad_parts = over_group(row_grad_a, row_grad_b)
+    terms_a, terms_b, terms_c = over_group(spread(fed_a[2]), spread(fed_b[2]))
+    terms = jnp.stack([terms_a[0], terms_b, terms_c])
+    out_parts = over_group(row_out_a, row_out_b)
 
     data_a, data_b = fed_a[3], fed_b[3]
 
     def unit_grads(left, right):
-        return jnp.concatenate(
-            [
-                outer_call(
-                    hidden_units,
-                    hidden_pad,
-                    dp,
-                    [(data[k][left], data[k][right]) for data in (data_a, data_b)],
-                )
-                for k in range(2)
-            ],
-            axis=1,
-        )
-
-    def scatter_units(total):
-        total = total.reshape((2,) * len(bits) + total.shape[1:])
-        for bit in reversed(upper):
-            axis = len(bits) - 1 - bits.index(bit)
-            sent = half(total, 1 - bit_of(bit), axis)
-            kept = half(total, bit_of(bit), axis)
-            total = (kept.astype(F32) + swap(sent, bit).astype(F32)).astype(BF)
-        total = total.reshape((2, 2) + total.shape[len(bits) :])
-        held = join(pick(total, xi, 0)[None], swap(pick(total, 1 - xi, 0), 2)[None], 2, 0)
-        return join(pick(held, core, 1)[:, None], swap(pick(held, 1 - core, 1), 1)[:, None], 1, 1)
+        pairs = [[(data[k][left], data[k][right]) for data in (data_a, data_b)] for k in range(2)]
+        return units_call(hidden_units, hidden_pad, dp, *pairs)
+
+    gate_total, up_total = unit_grads(2, 0)
+    down_total = unit_grads(3, 1)[0]
+    probs_mine = lax.dynamic_slice_in_dim(fed_a[4][0], zi * local_rows, local_rows, 1).T
+    probs_mine = jnp.pad(probs_mine, ((0, 0), (0, 128 - probs_mine.shape[1])))
+    router_wide = jnp.pad(router_rows, ((0, 128 - router_rows.shape[0]), (0, 0)))
+    output, input_grad, down_sum, gate_sum, up_sum, attn_sum, misc_sum, gains_sum = backward_call(
+        dp,
+        depth,
+        experts,
+        head_width,
+        (terms, probs_mine, router_wide, gain_rows, cos_rows, sin_rows, hidden, out_grad),
+        grad_parts
+        + out_parts
+        + (down_total, gate_total, up_total, tok, attn_weights, qkv, probs_low, heads_out, norm_own),
+    )
 
     def split_units(held):
-        routed = held[:, :, :mine_experts].reshape(experts, -1, slice_width)
-        shared = held[:, :, mine_experts]
+        routed = held[:, :mine_experts].reshape(experts, hidden_units, slice_width)
+        shared = held[:, mine_experts].reshape(-1, slice_width)
         return routed.astype(F32), shared.astype(F32)
 
-    gateup_sum = scatter_units(unit_grads(2, 0))
-    down_sum = scatter_units(unit_grads(3, 1))
-    routed_gu, shared_gu = split_units(gateup_sum)
-    routed_down, shared_down_sum = split_units(down_sum)
-    shared_gu = shared_gu.reshape(4, 2, hidden_units, slice_width)
-    egate_sum = routed_gu[:, :hidden_units].swapaxes(1, 2)
-    eup_sum = routed_gu[:, hidden_units:].swapaxes(1, 2)
-    sgate_sum = shared_gu[:, 0].reshape(-1, slice_width).T
-    sup_sum = shared_gu[:, 1].reshape(-1, slice_width).T
-    sdown_sum = shared_down_sum.reshape(-1, slice_width)
-
-    row_start = zi * local_rows
-    probs_local = lax.dynamic_slice_in_dim(fed_a[4][0], row_start, local_rows, 1).T
-    probs_mine, weight_mine = probs_local[:, :experts], probs_local[:, experts]
-    route_grad = gate_sums[:, :experts]
-    expert_logit_grad = probs_mine * (
-        route_grad - jnp.sum(probs_mine * route_grad, axis=-1, keepdims=True)
-    )
-    weight_logit_grad = gate_sums[:, experts] * weight_mine * (1.0 - weight_mine)
-    logits_grad = jnp.concatenate([expert_logit_grad, weight_logit_grad[:, None]], axis=1).astype(
-        BF
-    )
-    second_grad = second_grad + einsum("tf,df->td", logits_grad, router_full)
-    gain_two_grad = jnp.sum(second_grad * second_unit, axis=0)
-    unit_two = second_grad * gain_rows[1]
-    hidden_grad = out_grad.astype(F32) + second_scale * (
-        unit_two - second_unit * jnp.mean(unit_two * second_unit, axis=-1, keepdims=True)
-    )
-    attention_grad = hidden_grad.astype(BF)
-    wide_logits = jnp.pad(logits_grad, ((0, 0), (0, 128 - experts - 1)))
-    back_z = lax.all_gather(
-        jnp.concatenate([attention_grad, wide_logits], axis=1), "tensor", axis=0, tiled=True
-    )
-    out_sum = after(group_sum(row_out_a, row_out_b), back_z)
-    output = (hidden + z_scatter(out_sum)).astype(BF)
-    logits_z = back_z[:, width : width + 16]
-    back_own = back_z[:, :width]
-    back_rows = jnp.stack([back_own, swap(back_own, 1)])
-
-    router_part = einsum("tf,td->fd", logits_z, norm_z)[: experts + 1]
-
-    first_norm = (rows_f * first_scale * gain_rows[0]).astype(BF)
-    out_proj = einsum("std,stf->df", back_rows, heads_out)
-    mix_grad = einsum("std,df->stf", back_rows, out_weight).astype(BF)
-    mix_grad = mix_grad.reshape(2, seq_len, pair_heads, head_width).swapaxes(1, 2)
-    mix_grad = mix_grad.reshape(2 * pair_heads, seq_len, head_width)
-    queries, keys, values = qkv[0], qkv[1], qkv[2]
-    prob_grad = einsum("nqd,nkd->nqk", mix_grad, values)
-    probs = probs_low.astype(F32)
-    score_grad = (
-        probs * (prob_grad - jnp.sum(probs * prob_grad, axis=-1, keepdims=True))
-    ).astype(BF)
-    query_rot = einsum("nqk,nkd->nqd", score_grad, keys) * score_scale
-    key_rot = einsum("nqk,nqd->nkd", score_grad, queries) * score_scale
-    value_grad = einsum("nqk,nqd->nkd", probs_low, mix_grad)
-
-    def unspin(field):
-        return field * cos_rows - jnp.roll(field, head_width // 2, axis=-1) * sin_rows
-
-    def lanes_of(field):
-        field = field.reshape(2, pair_heads, seq_len, head_width).swapaxes(1, 2)
-        return field.astype(BF).reshape(2, seq_len, pair_width)
-
-    qk_grad = jnp.concatenate([lanes_of(unspin(query_rot)), lanes_of(unspin(key_rot))], axis=-1)
-    v_grad = lanes_of(value_grad)
-    first_part = einsum("stf,df->std", qk_grad, qk_full) + einsum(
-        "stf,df->std", v_grad, vo_full[:, :pair_width]
-    )
-    first_grad = z_scatter(core_sum(first_part[0], first_part[1]))
-
-    gain_one_grad = jnp.sum(first_part * (rows_f * first_scale), axis=(0, 1))
-    bias_part = jnp.concatenate(
-        [jnp.sum(qk_grad.astype(F32), axis=(0, 1)), jnp.sum(v_grad.astype(F32), axis=(0, 1))]
-    )
-    bias_part = bias_part.reshape(3 * pair_heads, dp, -1).swapaxes(0, 1).reshape(dp, 1, -1)
-    gain_part = jnp.stack([gain_one_grad, gain_two_grad]).reshape(2, dp, slice_width)
-
-    def wide_rows(rows):
-        return jnp.pad(rows, ((0, 0), (0, 0), (0, 2 * pair_width - rows.shape[2])))
-
-    misc_part = jnp.concatenate(
-        [
-            wide_rows(router_part.reshape(experts + 1, dp, slice_width).swapaxes(0, 1)),
-            wide_rows(bias_part),
-            wide_rows(gain_part.swapaxes(0, 1)),
-            jnp.zeros((dp, misc_rows - experts - 4, 2 * pair_width), F32),
-        ],
-        axis=1,
-    )
-    qk_total = einsum("std,stf->df", first_norm, qk_grad).reshape(dp, slice_width, -1)
-    qk_total = jnp.concatenate([qk_total, misc_part], axis=1)
-    vo_total = jnp.concatenate([einsum("std,stf->df", first_norm, v_grad), out_proj], axis=1)
-    vo_total = vo_total.reshape(dp, slice_width, -1)
-
-    def scatter_attention(total, order):
-        total = total.reshape((2,) * len(bits) + total.shape[1:])
-        for bit in order:
-            axis = len(bits) - 1 - bits.index(bit)
-            sent = half(total, 1 - bit_of(bit), axis).astype(BF)
-            total = half(total, bit_of(bit), axis) + swap(sent, bit).astype(F32)
-        total = total.reshape((2,) + total.shape[-2:]).astype(BF)
-        return pick(total, core, 0), swap(pick(total, 1 - core, 0), 1)
-
-    def columns_of(mine, theirs):
-        held = join(mine[:slice_width, None], theirs[:slice_width, None], 1, 1)
-        first, second = held[..., :pair_width], held[..., pair_width:]
-        return (
-            first.reshape(slice_width, -1).astype(F32),
-            second.reshape(slice_width, -1).astype(F32),
-        )
-
-    qk_mine, qk_theirs = scatter_attention(qk_total, bits[:0:-1])
-    vo_mine, vo_theirs = scatter_attention(vo_total, bits[1:])
-    qk_sums = columns_of(qk_mine, qk_theirs)
-    vo_sums = columns_of(vo_mine, vo_theirs)
-    misc_mine = qk_mine[slice_width:].astype(F32)
-    misc_theirs = qk_theirs[slice_width:].astype(F32)
-    misc_sum = misc_mine + misc_theirs
-    router_sum = misc_sum[: experts + 1, :slice_width].T
-    bias_sums = join(
-        misc_mine[experts + 1, :bias_width].reshape(3, 1, pair_heads, -1),
-        misc_theirs[experts + 1, :bias_width].reshape(3, 1, pair_heads, -1),
-        1,
-        1,
-    ).reshape(3, heads_local, -1)
-    gain_sums = lax.all_gather(
-        misc_sum[experts + 2 : experts + 4, :slice_width], "tensor", axis=0, tiled=False
-    )
-    tensor = gain_sums.shape[0]
-    gain_sums = jnp.sum(gain_sums, axis=0).reshape(2, tensor, -1)
-    gain_sums = pick(gain_sums, zi, 1)
-
-    unit_mine = inputs * lax.rsqrt(jnp.mean(inputs * inputs, axis=-1, keepdims=True) + EPS)
-    scale_mine = lax.rsqrt(jnp.mean(inputs * inputs, axis=-1, keepdims=True) + EPS)
-    unit_one = first_grad * gain_rows[0]
-    input_grad = hidden_grad + scale_mine * (
-        unit_one - unit_mine * jnp.mean(unit_one * unit_mine, axis=-1, keepdims=True)
-    )
+    egate_sum, sgate_sum = split_units(gate_sum)
+    eup_sum, sup_sum = split_units(up_sum)
+    edown_sum, sdown_sum = split_units(down_sum)
+
+    def columns_of(kind):
+        held = attn_sum[:, :, kind * pair_width : (kind + 1) * pair_width].swapaxes(0, 1)
+        return held.reshape(slice_width, -1).astype(F32)
+
+    bias_sums = misc_sum[experts + 1 : experts + 3, :bias_width].reshape(2, 3, pair_heads, -1)
+    bias_sums = bias_sums.swapaxes(0, 1).reshape(3, heads_local, -1)
+    piece = norm_gains.shape[1]
+    gain_sums = lax.dynamic_slice(gains_sum[3:5], (jnp.int32(0), zi * piece), (2, piece))
     return (
         output,
-        input_grad.astype(BF),
+        input_grad,
         gain_sums,
-        qk_sums[0],
-        qk_sums[1],
-        vo_sums[0],
-        vo_sums[1].T,
+        columns_of(0),
+        columns_of(1),
+        columns_of(2),
+        columns_of(3).T,
         bias_sums,
-        router_sum,
-        sgate_sum,
-        sup_sum,
+        misc_sum[: experts + 1].T,
+        sgate_sum.T,
+        sup_sum.T,
         sdown_sum,
-        egate_sum,
-        eup_sum,
-        routed_down,
+        egate_sum.swapaxes(1, 2),
+        eup_sum.swapaxes(1, 2),
+        edown_sum,
     )
 
 

time: 901 us -> 803 us (0.89)
  Pallas kernels: 395 us -> 612 us
  local copies, waits for them, and re-layouts: 172 us -> 59.6 us
  waiting for transfers between devices: 160 us -> 84.5 us
  other arithmetic: 78.8 us -> 23.4 us
  matrix products: 34 us -> 0 us
  between operations: 15.2 us -> 1.69 us
  blocking collectives: 11.9 us -> 0 us
  starting transfers between devices: 20.3 us -> 11 us
    pallas_call x4 -> x3, Pallas kernels: 45.1 us -> 263 us  [the longest x1 220 us: backward_call(): pl.pallas_call(functools.partial(backward_body, (dp, depth, experts, head...]
    ppermute x25 -> x11, waiting for transfers between devices: 160 us -> 84.5 us  [swap(): return lax.ppermute(array, 'dp', [(i, i ^ bit) for i in range(dp)])]
    dot_general x12 -> x0, matrix products: 34 us -> none  [einsum(): return jnp.einsum(spec, *args, preferred_element_type=F32)]
    dynamic_update_slice x12 -> x0, local copies, waits for them, and re-layouts: 24.8 us -> none  [the longest x7 14.8 us: join(): lax.dynamic_update_slice_in_dim(out, theirs, n * (1 - bit_of(bit)), axis)]
    convert_element_type x16 -> x2, other arithmetic: 28.4 us -> 5.23 us  [over_group(): return (a, swap(a[1], 1), swap(across.astype(b.dtype), 2))]
    concatenate x4 -> x0, local copies, waits for them, and re-layouts: 15.8 us -> none  [the longest x2 14.8 us: local_fused(): qk_total = jnp.concatenate([qk_total, misc_part], axis=1)]
    concatenate x7 -> x1, other arithmetic: 15.4 us -> 1.01 us  [local_fused(): cos_rows = jnp.concatenate([cos_part, cos_part], axis=1)]
    another operation x13 -> x2, local copies, waits for them, and re-layouts: 13 us -> 0.07 us  [the longest x1 5.55 us: scatter_attention(): total = total.reshape((2,) * len(bits) + total.shape[1:])]
  transfers between devices with their start and end apart: 29 -> 11, of which waited for: 8 -> 2; matrix products, arithmetic and copies ran while one was open for 28% -> 4% of each run, Pallas kernels for 14% -> 11%
where the time goes in v3:
time: 803 us; the launch traced here: 792 us
  Pallas kernels  612 us (76%)
  waiting for transfers between devices  84.5 us (11%)
  local copies, waits for them, and re-layouts  59.6 us (7%)
  other arithmetic  23.4 us (3%)
  starting transfers between devices  11 us (1%)
    pallas_call x1, Pallas kernels, backward_call(): pl.pallas_call(functools.partial(backward_body, (dp, depth, experts, head...  220 us
    pallas_call x1, Pallas kernels, forward_call(): pl.pallas_call(functools.partial(forward_body, (dp, depth, experts, hidde...  217 us
    ppermute x11, waiting for transfers between devices, swap(): return lax.ppermute(array, 'dp', [(i, i ^ bit) for i in range(dp)])  84.5 us
    pallas_call x4, Pallas kernels, back_call(): call(back_body, (width // block, count), [pl.BlockSpec((1, units - 1, seq...  72.4 us
    pallas_call x2, Pallas kernels, act_call(): call(functools.partial(act_body, experts, units), (count, units), [pl.Blo...  59.7 us
    pallas_call x2, Pallas kernels, units_call(): call(functools.partial(units_body, keep, pad), (many + 1, dp // blocks),...  42.9 us
  transfers between devices with their start and end apart: 11, of which 2 were waited for; matrix products, arithmetic and copies ran while one was open for 4% of the time, Pallas kernels for 11%

profile of v3, /device:TPU:0, one launch (start us, length us, event | category | flops | bytes accessed | tf_op | source)
XLA Modules:
  0.0 792.4 jit_solution(11947971648355760977)
XLA Ops:
  2.4 2.2 copy.66
  4.7 1.1 copy.67
  9.7 217.1 %shard_map.289 = (f32[128,2048]{1,0:T(8,128)}, bf16[2,512,2048]{2,1,0:T(8,128)(2,1)}, bf16[4,512,2048]{2,1,0:T(8,128)(2,1)}, bf16[3,2,384,2048]{3,2,1,0:T(8,128)...) custom-call(s32[16,512]{1,0:T(8,128)} %pad.24.codes_ref, ...), custom_call_target="tpu_custom_call" | custom-call | tf_op jit(solution)/shard_map/pallas_call | solution.py:825
  226.8 1.8 slice_bitcast_fusion.6
  228.6 2.2 collective-permute-start.1
  231.1 1.3 copy.71.slot_ref
  232.5 1.3 copy.73.slot_ref
  234.6 6.0 fusion.6
  240.6 35.4 %collective-permute-done.1 = bf16[512,2048]{1,0:T(8,128)(2,1)} collective-permute-done((bf16[512,2048]{1,0:T(8,128)(2,1)S(1)}, bf16[512,2048]{1,0:T(8,128)(2,1)}, u32[]{:S(2)}, u32[]{:S(2)}) %collective-permute-start.1) | collective-permute-done | bytes 2097184 | tf_op jit(solution)/shard_map/ppermute | solution.py:1805
  276.0 1.2 collective-permute-start.2
  277.3 29.8 %shard_map.290 = (bf16[2,2,320,2048]{3,2,1,0:T(8,128)(2,1)}, bf16[2,2,320,2048]{3,2,1,0:T(8,128)(2,1)}, bf16[2,2,320,768]{3,2,1,0:T(8,128)(2,1)}, bf16[2,2,320,3...) custom-call(s32[1]{0:T(128)} %bitcast.group_ref, ...), custom_call_target="tpu_custom_call" | custom-call | flops 16240345088 | bytes 33554432 | tf_op jit(solution)/shard_map/pallas_call | solution.py:167
  307.0 16.1 %shard_map.294.out_a_ref = bf16[2,512,2048]{2,1,0:T(8,128)(2,1)} custom-call(s32[2,2,512,1]{3,2,1,0:T(8,128)} %copy.73.slot_ref, bf16[2,2,320,384]{3,2,1,0:T(8,128)(2,1)} %get-tuple-element.123.routed_ref, bf16[2,512,384]{2,1,0:T(8,128)(2,1)} %get-tuple-element.124.shared_ref, bf16[3,384,2048]{2,1,0:T(8,128)(2,1)} %bitcast.170), custom_call_target="tpu_custom_call" | custom-call | flops 6308233216 | bytes 8912896 | tf_op jit(solution)/shard_map/pallas_call | solution.py:224
  323.1 3.9 pad_maximum_fusion.rows_ref
  327.0 30.0 %shard_map.291 = (bf16[2,2,320,2048]{3,2,1,0:T(8,128)(2,1)}, bf16[2,2,320,2048]{3,2,1,0:T(8,128)(2,1)}, bf16[2,2,320,768]{3,2,1,0:T(8,128)(2,1)}, bf16[2,2,320,3...) custom-call(s32[1]{0:T(128)} %bitcast.group_ref, ...), custom_call_target="tpu_custom_call" | custom-call | flops 16240345088 | bytes 33554432 | tf_op jit(solution)/shard_map/pallas_call | solution.py:167
  357.0 20.2 %shard_map.292 = bf16[2,512,2048]{2,1,0:T(8,128)(2,1)} custom-call(s32[2,2,512,1]{3,2,1,0:T(8,128)} %copy.71.slot_ref, bf16[2,2,320,768]{3,2,1,0:T(8,128)(2,1)} %get-tuple-element.118.routed_ref, bf16[2,512,768]{2,1,0:T(8,128)(2,1)} %get-tuple-element.119.shared_ref, bf16[3,768,2048]{2,1,0:T(8,128)(2,1)} %bitcast.167), custom_call_target="tpu_custom_call" | custom-call | flops 9932111872 | bytes 13631488 | tf_op jit(solution)/shard_map/pallas_call | solution.py:224
  377.2 1.3 copy.72.slot_ref
  378.5 20.2 %shard_map.293.grad_a_ref = bf16[2,512,2048]{2,1,0:T(8,128)(2,1)} custom-call(s32[2,2,512,1]{3,2,1,0:T(8,128)} %copy.72.slot_ref, bf16[2,2,320,768]{3,2,1,0:T(8,128)(2,1)} %get-tuple-element.121.routed_ref, bf16[2,512,768]{2,1,0:T(8,128)(2,1)} %get-tuple-element.122.shared_ref, bf16[3,768,2048]{2,1,0:T(8,128)(2,1)} %bitcast.168), custom_call_target="tpu_custom_call" | custom-call | flops 9932111872 | bytes 13631488 | tf_op jit(solution)/shard_map/pallas_call | solution.py:224
  398.7 1.3 copy.74.slot_ref
  400.0 16.0 %shard_map.295 = bf16[2,512,2048]{2,1,0:T(8,128)(2,1)} custom-call(s32[2,2,512,1]{3,2,1,0:T(8,128)} %copy.74.slot_ref, bf16[2,2,320,384]{3,2,1,0:T(8,128)(2,1)} %get-tuple-element.126.routed_ref, bf16[2,512,384]{2,1,0:T(8,128)(2,1)} %get-tuple-element.127.shared_ref, bf16[3,384,2048]{2,1,0:T(8,128)(2,1)} %bitcast.172), custom_call_target="tpu_custom_call" | custom-call | flops 6308233216 | bytes 8912896 | tf_op jit(solution)/shard_map/pallas_call | solution.py:224
  416.1 3.4 slice_bitcast_fusion
  419.5 1.5 slice_bitcast_fusion.3
  422.4 1.5 slice_bitcast_fusion.2
  424.2 2.1 dynamic_update_slice.10
  426.3 2.9 scatter.25
  430.0 1.3 collective-permute-start
  432.9 3.2 slice_bitcast_fusion.5
  436.3 2.1 dynamic_update_slice.11
  438.5 2.7 scatter.26
  441.3 1.3 collective-permute-start.3
  442.6 3.1 fusion
  445.7 2.4 collective-permute-start.10
  448.1 2.1 fusion.1
  450.2 24.9 %shard_map.297 = (bf16[8,3,352,256]{3,2,1,0:T(8,128)(2,1)}, bf16[8,3,352,256]{3,2,1,0:T(8,128)(2,1)}) custom-call(bf16[2,640,768]{2,1,0:T(8,128)(2,1)} %bitcast.177, bf16[2,640,768]{2,1,0:T(8,128)(2,1)} %bitcast.178, bf16[1,1024,768]{2,1,0:T(8,128)(2,1)} %bitcast.179, bf16[1,1024,768]{2,1,0:T(8,128)(2,1)} %bitcast.180, bf16[2,640,2048]{2,1,0:T(8,128)(2,1)} %bitcast.175, ...), custom_call_target="tpu_custom_call" | custom-call | flops 14495514624 | bytes 25952256 | tf_op jit(solution)/shard_map/pallas_call | solution.py:320
  475.2 2.1 collective-permute-start.4
  477.3 18.0 %shard_map.296.down_ref = bf16[8,3,352,256]{3,2,1,0:T(8,128)(2,1)} custom-call(bf16[2,640,384]{2,1,0:T(8,128)(2,1)} %bitcast.181, bf16[2,640,384]{2,1,0:T(8,128)(2,1)} %bitcast.182, bf16[1,1024,384]{2,1,0:T(8,128)(2,1)} %bitcast.183, bf16[1,1024,384]{2,1,0:T(8,128)(2,1)} %bitcast.184, bf16[2,640,2048]{2,1,0:T(8,128)(2,1)} %bitcast.173, ...), custom_call_target="tpu_custom_call" | custom-call | flops 7247757312 | bytes 22413312 | tf_op jit(solution)/shard_map/pallas_call | solution.py:320
  495.3 49.1 %collective-permute-done.4 = f32[512,128]{1,0:T(8,128)S(1)} collective-permute-done((f32[512,128]{1,0:T(8,128)S(1)}, f32[512,128]{1,0:T(8,128)S(1)}, u32[]{:S(2)}, u32[]{:S(2)}) %collective-permute-start.4) | collective-permute-done | bytes 262176 | tf_op jit(solution)/shard_map/ppermute | solution.py:1805
  544.3 1.9 pad_maximum_fusion.1.terms_ref
  546.2 219.8 %shard_map.298 = (bf16[128,2048]{1,0:T(8,128)(2,1)}, bf16[128,2048]{1,0:T(8,128)(2,1)}, bf16[4,3,352,256]{3,2,1,0:T(8,128)(2,1)}, bf16[4,3,352,256]{3,2,1,0:T(8,...) custom-call(f32[3,512,128]{2,1,0:T(8,128)} %pad_maximum_fusion.1.ter, ...), custom_call_target="tpu_custom_call" | custom-call | tf_op jit(solution)/shard_map/pallas_call | solution.py:1284
  766.1 1.6 slice.241
  767.7 1.2 slice.238
  769.1 1.4 copy-done.3
  771.8 1.9 bitcast_convert_fusion
  773.8 1.9 convert_bitcast_fusion
  775.7 1.9 convert_bitcast_fusion.1
  777.8 1.5 copy.80
  779.5 1.5 copy.81
  781.0 1.4 convert_bitcast_fusion.2
  787.0 1.3 bitcast_convert_fusion.1
  (127 shorter events, 20.9 us)
Async XLA Ops:
  0.6 4.0 copy-start.5
  0.7 5.2 copy-start.8
  1.4 5.3 copy-start.22
  1.4 5.3 copy-start.23
  1.4 5.3 copy-start.26
  1.4 5.9 copy-start.24
  1.4 5.9 copy-start.25
  7.8 1.3 copy-start.17
  9.1 0.6 copy-start.14
  226.8 4.0 copy-start.15
  226.8 4.1 copy-start.16
  228.6 47.4 %collective-permute-start.1 = (bf16[512,2048]{1,0:T(8,128)(2,1)S(1)}, bf16[512,2048]{1,0:T(8,128)(2,1)}, u32[]{:S(2)}, u32[]{:S(2)}) collective-permute-start(bf16[512,2048]{1,0:T(8,128)(2,1)S(1)} %slice_bitcast_fusion.6), channel_id=1, source_target_pairs={{0,8},{4,12},{8,0},{12,4},{16,24},{20,28},{24,16},{28,20},{1,9},{5... | collective-permute-start | bytes 6291464 | tf_op jit(solution)/shard_map/ppermute | solution.py:1805
  231.1 9.5 %copy-start.10 = (s32[2,2,512]{2,1,0:T(2,128)}, s32[2,2,512]{2,1,0:T(2,128)S(1)}, u32[]{:S(2)}) copy-start(s32[2,2,512]{2,1,0:T(2,128)S(1)} %get-tuple-element.178.slot_ref) | copy-start | bytes 24580
  231.1 9.5 %copy-start.12 = (s32[2,2,512]{2,1,0:T(2,128)}, s32[2,2,512]{2,1,0:T(2,128)S(1)}, u32[]{:S(2)}) copy-start(s32[2,2,512]{2,1,0:T(2,128)S(1)} %get-tuple-element.177.slot_ref) | copy-start | bytes 24580
  276.0 47.1 %collective-permute-start.2 = (bf16[512,2048]{1,0:T(8,128)(2,1)}, bf16[512,2048]{1,0:T(8,128)(2,1)S(1)}, u32[]{:S(2)}, u32[]{:S(2)}) collective-permute-start(bf16[512,2048]{1,0:T(8,128)(2,1)} %collective-permute-done.1), channel_id=1, source_target_pairs={{0,4},{4,0},{8,12},{12,8},{16,20},{20,16},{24,28},{28,24},{1,5},{5... | collective-permute-start | bytes 6291464 | tf_op jit(solution)/shard_map/ppermute | solution.py:1805
  357.0 20.2 %copy-start.13 = (s32[2,2,512]{2,1,0:T(2,128)S(1)}, s32[2,2,512]{2,1,0:T(2,128)}, u32[]{:S(2)}) copy-start(s32[2,2,512]{2,1,0:T(2,128)} %copy-done.12) | copy-start | bytes 24580
  378.5 20.2 %copy-start.11 = (s32[2,2,512]{2,1,0:T(2,128)S(1)}, s32[2,2,512]{2,1,0:T(2,128)}, u32[]{:S(2)}) copy-start(s32[2,2,512]{2,1,0:T(2,128)} %copy-done.10) | copy-start | bytes 24580
  416.1 3.4 copy-start.1
  419.5 2.9 copy-start
  419.5 21.8 %collective-permute-start.9 = (bf16[512,2048]{1,0:T(8,128)(2,1)}, bf16[512,2048]{1,0:T(8,128)(2,1)}, u32[]{:S(2)}, u32[]{:S(2)}) collective-permute-start(bf16[512,2048]{1,0:T(8,128)(2,1)} %slice_bitcast_fusion), channel_id=1, source_target_pairs={{0,4},{4,0},{8,12},{12,8},{16,20},{20,16},{24,28},{28,24},{1,5},{5... | collective-permute-start | bytes 6291464 | tf_op jit(solution)/shard_map/ppermute | solution.py:1805
  420.9 2.9 copy-start.21
  420.9 24.8 %collective-permute-start.6 = (bf16[512,2048]{1,0:T(8,128)(2,1)}, bf16[512,2048]{1,0:T(8,128)(2,1)S(1)}, u32[]{:S(2)}, u32[]{:S(2)}) collective-permute-start(bf16[512,2048]{1,0:T(8,128)(2,1)} %slice_bitcast_fusion.3), channel_id=1, source_target_pairs={{0,4},{4,0},{8,12},{12,8},{16,20},{20,16},{24,28},{28,24},{1,5},{5... | collective-permute-start | bytes 6291464 | tf_op jit(solution)/shard_map/ppermute | solution.py:1805
  423.9 122.3 %collective-permute-start.8 = (bf16[512,2048]{1,0:T(8,128)(2,1)}, bf16[512,2048]{1,0:T(8,128)(2,1)}, u32[]{:S(2)}, u32[]{:S(2)}) collective-permute-start(bf16[512,2048]{1,0:T(8,128)(2,1)} %slice_bitcast_fusion.2), channel_id=1, source_target_pairs={{0,4},{4,0},{8,12},{12,8},{16,20},{20,16},{24,28},{28,24},{1,5},{5... | collective-permute-start | bytes 6291464 | tf_op jit(solution)/shard_map/ppermute | solution.py:1805
  423.9 7.4 copy-start.19
  423.9 7.5 copy-start.9
  430.0 45.2 %collective-permute-start = (f32[512,128]{1,0:T(8,128)}, f32[512,128]{1,0:T(8,128)}, u32[]{:S(2)}, u32[]{:S(2)}) collective-permute-start(f32[512,128]{1,0:T(8,128)} %get-tuple-element.186), channel_id=1, source_target_pairs={{0,4},{4,0},{8,12},{12,8},{16,20},{20,16},{24,28},{28,24},{1,5},{5... | collective-permute-start | bytes 786440 | tf_op jit(solution)/shard_map/ppermute | solution.py:1805
  432.8 3.2 copy-start.20
  436.0 110.2 %collective-permute-start.5 = (bf16[512,2048]{1,0:T(8,128)(2,1)}, bf16[512,2048]{1,0:T(8,128)(2,1)}, u32[]{:S(2)}, u32[]{:S(2)}) collective-permute-start(bf16[512,2048]{1,0:T(8,128)(2,1)} %slice_bitcast_fusion.5), channel_id=1, source_target_pairs={{0,4},{4,0},{8,12},{12,8},{16,20},{20,16},{24,28},{28,24},{1,5},{5... | collective-permute-start | bytes 6291464 | tf_op jit(solution)/shard_map/ppermute | solution.py:1805
  441.2 6.8 copy-start.2
  441.3 8.9 %collective-permute-start.3 = (f32[512,128]{1,0:T(8,128)S(1)}, f32[512,128]{1,0:T(8,128)S(1)}, u32[]{:S(2)}, u32[]{:S(2)}) collective-permute-start(f32[512,128]{1,0:T(8,128)S(1)} %slice_bitcast_fusion.7), channel_id=1, source_target_pairs={{0,4},{4,0},{8,12},{12,8},{16,20},{20,16},{24,28},{28,24},{1,5},{5... | collective-permute-start | bytes 786440 | tf_op jit(solution)/shard_map/ppermute | solution.py:1805
  445.7 100.5 %collective-permute-start.10 = (bf16[512,2048]{1,0:T(8,128)(2,1)S(1)}, bf16[512,2048]{1,0:T(8,128)(2,1)}, u32[]{:S(2)}, u32[]{:S(2)}) collective-permute-start(bf16[512,2048]{1,0:T(8,128)(2,1)S(1)} %fusion), channel_id=1, source_target_pairs={{0,8},{4,12},{8,0},{12,4},{16,24},{20,28},{24,16},{28,20},{1,9},{5... | collective-permute-start | bytes 6291464 | tf_op jit(solution)/shard_map/ppermute | solution.py:1805
  450.2 96.0 %collective-permute-start.7 = (bf16[512,2048]{1,0:T(8,128)(2,1)}, bf16[512,2048]{1,0:T(8,128)(2,1)}, u32[]{:S(2)}, u32[]{:S(2)}) collective-permute-start(bf16[512,2048]{1,0:T(8,128)(2,1)} %fusion.1), channel_id=1, source_target_pairs={{0,8},{4,12},{8,0},{12,4},{16,24},{20,28},{24,16},{28,20},{1,9},{5... | collective-permute-start | bytes 6291464 | tf_op jit(solution)/shard_map/ppermute | solution.py:1805
  475.2 69.1 %collective-permute-start.4 = (f32[512,128]{1,0:T(8,128)S(1)}, f32[512,128]{1,0:T(8,128)S(1)}, u32[]{:S(2)}, u32[]{:S(2)}) collective-permute-start(f32[512,128]{1,0:T(8,128)S(1)} %fusion.2), channel_id=1, source_target_pairs={{0,8},{4,12},{8,0},{12,4},{16,24},{20,28},{24,16},{28,20},{1,9},{5... | collective-permute-start | bytes 786440 | tf_op jit(solution)/shard_map/ppermute | solution.py:1805
  766.1 2.8 copy-start.4
  768.9 1.6 copy-start.3
  770.5 0.7 copy-start.18
  785.0 5.3 copy-start.7
  786.0 5.1 copy-start.6

commit v4 on v3

--- a/solution.py
+++ b/solution.py
@@ -68,7 +68,7 @@
     )
 
 
-def act_body(
+def plain_act_body(
     experts,
     units,
     group_ref,
@@ -148,7 +148,7 @@
         inner_s_ref[0] = inner
 
 
-def act_call(experts, capacity, group, slots, rows, grads, router, gateup, down):
+def plain_act_call(experts, capacity, group, slots, rows, grads, router, gateup, down):
     count, seq_len, width = rows.shape
     units, wide, _ = gateup.shape
     half = wide // 2
@@ -165,7 +165,7 @@
 
     work = count * (routed * capacity + seq_len) * width
     return call(
-        functools.partial(act_body, experts, units),
+        functools.partial(plain_act_body, experts, units),
         (count, units),
         [
             pl.BlockSpec(memory_space=pltpu.SMEM),
@@ -203,7 +203,7 @@
     )(group, slots, rows, grads, router, gateup, down)
 
 
-def back_body(slot_ref, routed_ref, shared_ref, weight_ref, out_ref):
+def plain_back_body(slot_ref, routed_ref, shared_ref, weight_ref, out_ref):
     routed, _, capacity, _ = routed_ref.shape
     seq_len = shared_ref.shape[1]
     total = dot(shared_ref[0], weight_ref[routed])
@@ -215,14 +215,14 @@
     out_ref[0] = total.astype(BF)
 
 
-def back_call(slots, routed, shared, weight):
+def plain_back_call(slots, routed, shared, weight):
     units, wide, width = weight.shape
     count, seq_len, _ = shared.shape
     capacity = routed.shape[2]
     block = min(width, 512)
     work = count * ((units - 1) * capacity + seq_len) * width
     return call(
-        back_body,
+        plain_back_body,
         (width // block, count),
         [
             pl.BlockSpec((1, units - 1, seq_len, 1), lambda j, s: (s, 0, 0, 0)),
@@ -237,7 +237,7 @@
     )(slots, routed, shared, weight)
 
 
-def outer_body(keep, pad, left_a, right_a, left_b, right_b, out_ref):
+def plain_outer_body(keep, pad, left_a, right_a, left_b, right_b, out_ref):
     total = dot(left_a[0], right_a[0], 0, 0) + dot(left_b[0], right_b[0], 0, 0)
     total = total.astype(BF)
     blocks, _, rows, slice_width = out_ref.shape
@@ -248,7 +248,7 @@
             ]
 
 
-def outer_call(keep, pad, dp, pairs):
+def plain_outer_call(keep, pad, dp, pairs):
     (left_a, right_a), (left_b, right_b) = pairs
     units, rows, wide = left_a.shape
     width = right_a.shape[2]
@@ -263,7 +263,7 @@
         return pl.BlockSpec((1, n, blocks * slice_width), lambda u, j: (u, 0, j))
 
     return call(
-        functools.partial(outer_body, keep, pad),
+        functools.partial(plain_outer_body, keep, pad),
         (units, dp // blocks),
         [left(rows), right(rows), left(rows), right(rows)],
         pl.BlockSpec((blocks, 1, kept, slice_width), lambda u, j: (j, u, 0, 0)),
@@ -271,6 +271,226 @@
         4 * units * rows * wide * width,
         units * rows * (wide + width) * 4,
     )(left_a, right_a, left_b, right_b)
+
+
+def act_body(
+    experts,
+    top_count,
+    group_ref,
+    codes_ref,
+    rows_ref,
+    grads_ref,
+    router_ref,
+    gateup_ref,
+    down_ref,
+    slotted_ref,
+    slotgrad_ref,
+    pair_ref,
+    act_ref,
+    pair_s_ref,
+    act_s_ref,
+    terms_ref,
+    probs_ref,
+):
+    unit, units = pl.program_id(0), pl.num_programs(0)
+    half = gateup_ref.shape[1] // 2
+    count, seq_len, width = rows_ref.shape
+    capacity = slotted_ref.shape[2]
+
+    @pl.when(unit == 0)
+    def _():
+        for s in range(count):
+            logits = dot(router_ref[...], rows_ref[s], 1, 1)
+            row = lax.broadcasted_iota(jnp.int32, logits.shape, 0)
+            routed = jnp.where(row < experts, logits, -1e30)
+            raised = jnp.exp(routed - jnp.max(routed, axis=0, keepdims=True))
+            soft = raised / jnp.sum(raised, axis=0, keepdims=True)
+            probs_ref[s] = jnp.where(row < experts, soft, jax.nn.sigmoid(logits))
+        terms_ref[...] = jnp.zeros_like(terms_ref)
+
+    def parts(data, cot, weight):
+        both = dot(data, gateup_ref[0], 1, 1)
+        cot_in = dot(cot, down_ref[0], 1, 1)
+        gate_in, up_in = both[:, :half], both[:, half:]
+        gate_act, gate_slope = silu_parts(gate_in)
+        act = gate_act * up_in
+        inner = jnp.sum(act.astype(BF).astype(F32) * cot_in, axis=1, keepdims=True)
+        cot_in = cot_in * weight
+        return (
+            (act * weight).astype(BF),
+            (cot_in * up_in * gate_slope).astype(BF),
+            (cot_in * gate_act).astype(BF),
+            inner,
+        )
+
+    @pl.when(unit < units - 1)
+    def _():
+        expert = group_ref[0] * (units - 1) + unit
+        masks, weights = [], []
+        for s in range(count):
+            mask = slot_mask(codes_ref, s, expert, top_count, capacity)
+            onehot = mask.astype(F32).astype(BF)
+            slotted_ref[0, s] = dot(onehot, rows_ref[s]).astype(BF)
+            slotgrad_ref[0, s] = dot(onehot, grads_ref[s]).astype(BF)
+            probs = probs_ref[s]
+            row = lax.broadcasted_iota(jnp.int32, probs.shape, 0)
+            gate = jnp.sum(jnp.where(row == expert, probs, 0.0), axis=0, keepdims=True)
+            weights.append(jnp.sum(jnp.where(mask, gate, 0.0), axis=1, keepdims=True))
+            masks.append(onehot)
+        act, gate_grad, up_grad, inner = parts(
+            slotted_ref[0].reshape(count * capacity, width),
+            slotgrad_ref[0].reshape(count * capacity, width),
+            jnp.concatenate(weights, axis=0),
+        )
+        lane = lax.broadcasted_iota(jnp.int32, (capacity, terms_ref.shape[2]), 1)
+        for s in range(count):
+            at = slice(s * capacity, (s + 1) * capacity)
+            act_ref[0, s] = act[at]
+            pair_ref[0, s, :, :half] = gate_grad[at]
+            pair_ref[0, s, :, half:] = up_grad[at]
+            placed = jnp.where(lane == expert, inner[at], 0.0)
+            high = placed.astype(BF)
+            low = (placed - high.astype(F32)).astype(BF)
+            terms_ref[s] += dot(masks[s], high, 0, 0) + dot(masks[s], low, 0, 0)
+
+    @pl.when(unit == units - 1)
+    def _():
+        data = rows_ref[...].reshape(count * seq_len, width)
+        logits = dot(data, router_ref[...], 1, 1)
+        weight = jax.nn.sigmoid(logits[:, experts : experts + 1])
+        act, gate_grad, up_grad, inner = parts(
+            data, grads_ref[...].reshape(count * seq_len, width), weight
+        )
+        lane = lax.broadcasted_iota(jnp.int32, (seq_len, terms_ref.shape[2]), 1)
+        for s in range(count):
+            at = slice(s * seq_len, (s + 1) * seq_len)
+            act_s_ref[s] = act[at]
+            pair_s_ref[s, :, :half] = gate_grad[at]
+            pair_s_ref[s, :, half:] = up_grad[at]
+            terms_ref[s] += jnp.where(lane == experts, inner[at], 0.0)
+
+
+def slot_mask(codes_ref, s, expert, top_count, capacity):
+    codes = codes_ref[s]
+    slot = jnp.full((1, codes.shape[1]), -1, jnp.int32)
+    for k in range(top_count):
+        slot = jnp.where(codes[k : k + 1] == expert, codes[top_count + k : top_count + k + 1], slot)
+    return lax.broadcasted_iota(jnp.int32, (capacity, codes.shape[1]), 0) == slot
+
+
+def act_call(experts, top_count, capacity, chunk, group, codes, rows, grads, router, gateup, down):
+    _, seq_len, width = rows.shape
+    units, wide, _ = gateup.shape
+    half = wide // 2
+    routed, count = units - 1, 2
+
+    def unit(u):
+        return (u, 0, 0)
+
+    def slot(u):
+        return (jnp.minimum(u, routed - 1), 0, 0, 0)
+
+    def whole(*shape):
+        return pl.BlockSpec(shape, lambda u: (0,) * len(shape))
+
+    def part(*shape):
+        return pl.BlockSpec(
+            shape,
+            lambda u: (chunk,) + (0,) * (len(shape) - 1),
+            pipeline_mode=pl.Buffered(1),
+        )
+
+    work = count * (routed * capacity + seq_len) * width
+    return call(
+        functools.partial(act_body, experts, top_count),
+        (units,),
+        [
+            pl.BlockSpec(memory_space=pltpu.SMEM),
+            part(count, codes.shape[1], seq_len),
+            part(count, seq_len, width),
+            part(count, seq_len, width),
+            whole(*router.shape),
+            pl.BlockSpec((1, wide, width), unit),
+            pl.BlockSpec((1, half, width), unit),
+        ],
+        [
+            pl.BlockSpec((1, count, capacity, width), slot),
+            pl.BlockSpec((1, count, capacity, width), slot),
+            pl.BlockSpec((1, count, capacity, wide), slot),
+            pl.BlockSpec((1, count, capacity, half), slot),
+            whole(count, seq_len, wide),
+            whole(count, seq_len, half),
+            whole(count, seq_len, 128),
+            whole(count, router.shape[0], seq_len),
+        ],
+        [
+            jax.ShapeDtypeStruct((routed, count, capacity, width), BF),
+            jax.ShapeDtypeStruct((routed, count, capacity, width), BF),
+            jax.ShapeDtypeStruct((routed, count, capacity, wide), BF),
+            jax.ShapeDtypeStruct((routed, count, capacity, half), BF),
+            jax.ShapeDtypeStruct((count, seq_len, wide), BF),
+            jax.ShapeDtypeStruct((count, seq_len, half), BF),
+            jax.ShapeDtypeStruct((count, seq_len, 128), F32),
+            jax.ShapeDtypeStruct((count, router.shape[0], seq_len), F32),
+        ],
+        2 * work * 3 * half + 4 * count * routed * capacity * seq_len * width,
+        8 * count * seq_len * width * 2,
+    )(group, codes, rows, grads, router, gateup, down)
+
+
+def back_body(top_count, group_ref, codes_ref, routed_ref, shared_ref, weight_ref, *refs):
+    out_refs, onehot_ref = refs[:-1], refs[-1]
+    routed, count, capacity, wide = routed_ref.shape
+    seq_len = shared_ref.shape[1]
+    cols = weight_ref.shape[2]
+
+    @pl.when(pl.program_id(0) == 0)
+    def _():
+        for s in range(count):
+            for e in range(routed):
+                mask = slot_mask(codes_ref, s, group_ref[0] * routed + e, top_count, capacity)
+                onehot_ref[s, e * capacity : (e + 1) * capacity] = mask.astype(F32).astype(BF)
+
+    shared = dot(shared_ref[...].reshape(count * seq_len, wide), weight_ref[routed])
+    slots = [
+        dot(routed_ref[e].reshape(count * capacity, wide), weight_ref[e])
+        .astype(BF)
+        .reshape(count, capacity, cols)
+        for e in range(routed)
+    ]
+    for s in range(count):
+        total = dot(onehot_ref[s], jnp.concatenate([rows[s] for rows in slots], axis=0), 0, 0)
+        out_refs[s][...] = (total + shared[s * seq_len : (s + 1) * seq_len]).astype(BF)
+
+
+def back_call(top_count, chunk, group, codes, routed, shared, weight):
+    units, wide, width = weight.shape
+    count, seq_len, _ = shared.shape
+    capacity = routed.shape[2]
+    block = min(width, 512)
+    work = count * ((units - 1) * capacity + seq_len) * width
+
+    def whole(*shape):
+        return pl.BlockSpec(
+            shape, lambda j: (0,) * len(shape), pipeline_mode=pl.Buffered(1)
+        )
+
+    return call(
+        functools.partial(back_body, top_count),
+        (width // block,),
+        [
+            pl.BlockSpec(memory_space=pltpu.SMEM),
+            pl.BlockSpec((count, codes.shape[1], seq_len), lambda j: (chunk, 0, 0)),
+            whole(*routed.shape),
+            whole(*shared.shape),
+            pl.BlockSpec((units, wide, block), lambda j: (0, 0, j)),
+        ],
+        [pl.BlockSpec((seq_len, block), lambda j: (0, j))] * count,
+        [jax.ShapeDtypeStruct((seq_len, width), BF)] * count,
+        2 * work * wide + 2 * count * (units - 1) * capacity * seq_len * width,
+        units * wide * width * 2 + count * seq_len * width * 2,
+        [pltpu.VMEM((count, (units - 1) * capacity, seq_len), BF)],
+    )(group, codes, routed, shared, weight)
 
 
 def units_body(keep, pad, *refs):
@@ -297,35 +517,38 @@
 
 
 def units_call(keep, pad, dp, routed, shared):
-    lefts = [pair[0] for pair in routed + shared]
-    rights = [pair[1] for pair in routed + shared]
+    lefts = [pair[0] for pair in routed] + [entry[0] for entry in shared]
+    rights = [pair[1] for pair in routed] + [entry[1] for entry in shared]
+    chunks = [0, 0] + [entry[2] for entry in shared]
     many, _, wide = lefts[0].shape
     width = rights[0].shape[2]
     slice_width = width // dp
-    blocks = max(1, 512 // slice_width)
+    blocks = max(1, 1024 // slice_width)
     parts = wide // pad
     last = dp // blocks - 1
 
-    def spec(array, cols, shared_unit):
+    def spec(n, array, cols):
         def where(u, j):
-            mine = (u == many) if shared_unit else (u < many)
-            unit = 0 if shared_unit else jnp.minimum(u, many - 1)
+            of_shared = n > 1
+            mine = (u == many) if of_shared else (u < many)
+            unit = chunks[n] if of_shared else jnp.minimum(u, many - 1)
             if cols:
-                return (unit, 0, jnp.where(mine, j, 0 if shared_unit else last))
-            return (unit, 0, 0)
+                return (unit, 0, jnp.where(mine, j, 0 if of_shared else last))
+            return (0 if of_shared else unit, 0, 0)
 
         return pl.BlockSpec((1, array.shape[1], cols or wide), where)
 
     cols = blocks * slice_width
+    rows = many * lefts[0].shape[1] + lefts[2].shape[1]
     return call(
         functools.partial(units_body, keep, pad),
         (many + 1, dp // blocks),
-        [spec(a, 0, n > 1) for n, a in enumerate(lefts)]
-        + [spec(a, cols, n > 1) for n, a in enumerate(rights)],
+        [spec(n, a, 0) for n, a in enumerate(lefts)]
+        + [spec(n, a, cols) for n, a in enumerate(rights)],
         [pl.BlockSpec((blocks, 1, keep, slice_width), lambda u, j: (j, u, 0, 0))] * parts,
         [jax.ShapeDtypeStruct((dp, many + 1, keep, slice_width), BF)] * parts,
-        4 * (many * lefts[0].shape[1] + lefts[2].shape[1]) * wide * width,
-        (many * lefts[0].shape[1] + lefts[2].shape[1]) * (wide + width) * 4,
+        4 * rows * wide * width,
+        rows * (wide + width) * 4,
     )(*lefts, *rights)
 
 
@@ -777,14 +1000,23 @@
     ).astype(BF)
     norm_line = Line(c, norm_ref.at[0], z, depth, rows)
     norm_line.begin()
-    norm_own = c.remote(piece(norm_ref.at[0], z), piece(norm_ref.at[1], z), dp=peer_of(me, 1))
+    beside = peer_of(me, 2)
+    norm_own = c.remote(piece(norm_ref.at[0], z), piece(norm_ref.at[1], z), dp=sibling)
+    norm_far = c.remote(piece(norm_ref.at[0], z), piece(norm_ref.at[2], z), dp=beside)
+    norm_far.start()
     norm_own.start()
-    norm_passed = []
+    norm_passed, far_passed = [], []
     pass_norm = pass_on(
         c, norm_ref.at[0], norm_ref.at[1], z, depth, rows, sibling, norm_passed
     )
+    pass_far = pass_on(c, norm_ref.at[0], norm_ref.at[2], z, depth, rows, beside, far_passed)
+
+    def pass_both(k, up):
+        pass_far(k, up)
+        pass_norm(k, up)
+
     for k in range(1, depth):
-        line_step(norm_line, k, pass_norm)
+        line_step(norm_line, k, pass_both)
 
     x_grad.wait_recv()
     grad_pass = c.remote(grads_ref.at[2], grads_ref.at[3], dp=peer_of(me, 1))
@@ -795,9 +1027,15 @@
             chain[k].start()
     for chain in over:
         chain[-1].wait_recv()
+    norm_far.wait()
+    for copy, there in far_passed:
+        pl.when(there)(copy.wait)
+    norm_pass = c.remote(norm_ref.at[2], norm_ref.at[3], dp=sibling)
+    norm_pass.start()
     norm_own.wait()
     for copy, there in norm_passed:
         pl.when(there)(copy.wait)
+    norm_pass.wait()
     own_pass.wait()
     grad_pass.wait()
     for line in (tok_line, grad_line, norm_line):
@@ -828,7 +1066,7 @@
         out_specs=[vmem, vmem, hbm, hbm, hbm] + [vmem] * 8,
         out_shape=[
             shape((rows, width), F32),
-            shape((2, seq_len, width), BF),
+            shape((4, seq_len, width), BF),
             shape((4, seq_len, width), BF),
             shape((routed + 1, 2, hidden_pad, width), BF),
             shape((routed + 1, 1, hidden_pad, width), BF),
@@ -873,10 +1111,11 @@
     grad_c_ref,
     out_a_ref,
     out_b_ref,
-    out_c_ref,
-    down_ref,
+    out_far_ref,
+    gate_in_ref,
     gate_ref,
     up_ref,
+    down_ref,
     tok_hbm,
     weights_hbm,
     qkv_hbm,
@@ -885,9 +1124,10 @@
     norm_hbm,
     output_ref,
     input_ref,
-    down_out,
     gate_out,
     up_out,
+    down_out,
+    out_c_ref,
     attn_out,
     misc_out,
     gains_out,
@@ -933,12 +1173,15 @@
     greet(me, z, dp, depth)
 
     matrices = ((gate_ref, gate_out), (up_ref, up_out), (down_ref, down_out))
-    over = []
-    for m, (source, _) in enumerate(matrices):
-        other = source.at[pl.ds((1 - y) * 4, 4)]
+    over = [None]
+    for m in (1, 2):
+        other = matrices[m][0].at[pl.ds((1 - y) * 4, 4)]
         over.append(c.remote(other, arrived.at[m], dp=peer_of(me, 4)))
         over[m].start()
-    grads = (grad_a_ref.at[0], grad_b_ref, grad_c_ref)
+    out_far = c.remote(out_far_ref, out_c_ref, dp=peer_of(me, 2))
+    out_far.start()
+    gate_in = c.local(gate_in_ref, arrived.at[0])
+    grads = (grad_a_ref, grad_b_ref, grad_c_ref)
     loads = [c.local(grads[k], three.at[k]) for k in range(3)]
     for copy in loads:
         copy.start()
@@ -956,6 +1199,7 @@
         )
     ]
     own_loads[0].start()
+    gate_in.start()
     for copy in inputs:
         copy.start()
 
@@ -984,7 +1228,10 @@
 
     def add_over(m):
         own_loads[m].wait()
-        over[m].wait_recv()
+        if m:
+            over[m].wait_recv()
+        else:
+            gate_in.wait()
         copies = []
         for r in (2, 3, 1, 0):
             k = peer_of(me, r) % 4
@@ -1002,6 +1249,7 @@
             own_loads[m + 1].start()
         return copies
 
+    units = add_over(0)
     for copy in scatter:
         copy.wait_recv()
     for copy in small:
@@ -1041,12 +1289,13 @@
     pass_back = pass_on(c, back.at[0], back.at[1], z, depth, rows, sibling, passed)
     for copy in scatter:
         copy.wait_send()
-    outs = (out_a_ref.at[0], out_b_ref, out_c_ref)
+    outs = (out_a_ref, out_b_ref, out_c_ref)
     out_loads = [c.local(outs[k], three.at[k]) for k in range(3)]
-    for copy in out_loads:
+    for copy in out_loads[:2]:
         copy.start()
-    units = add_over(0)
     line_step(line, 1, pass_back)
+    out_far.wait_recv()
+    out_loads[2].start()
 
     for copy in inputs:
         copy.wait()
@@ -1060,6 +1309,7 @@
 
     lax.fori_loop(0, depth, scale_rows, 0)
     line_step(line, 2, pass_back)
+    units += add_over(1)
     for copy in out_loads:
         copy.wait()
     out_scatter = []
@@ -1127,7 +1377,7 @@
     first_grad(1)
     part_pass = c.remote(three.at[2], part_in, dp=sibling)
     part_pass.start()
-    units += add_over(1)
+    units += add_over(2)
     attention(0)
     first_grad(0)
     part_pass.wait_recv()
@@ -1200,7 +1450,6 @@
         to = peer_of(me, r)
         misc_copies.append(c.remote(misc_part.at[to], misc_in.at[r - 1], dp=to))
         misc_copies[-1].start()
-    units += add_over(2)
 
     qk_first.wait()
     mine = index(pl.ds(y, 1), every, 0)
@@ -1267,7 +1516,7 @@
     for copy in finals + units:
         copy.wait()
     line.finish()
-    for copy in over + small + first_scatter + misc_copies + [part_pass]:
+    for copy in over[1:] + small + first_scatter + misc_copies + [part_pass, out_far]:
         copy.wait_send()
 
 
@@ -1276,7 +1525,7 @@
     seq_len = output_rows * depth
     slice_width = width // dp
     units = in_hbm[6].shape[1:]
-    pair = in_hbm[13].shape[2]
+    pair = in_hbm[14].shape[2]
     pairs = pair // head
     vmem, hbm = pl.BlockSpec(memory_space=pltpu.VMEM), pl.BlockSpec(memory_space=pl.ANY)
     shape = jax.ShapeDtypeStruct
@@ -1284,13 +1533,14 @@
     return pl.pallas_call(
         functools.partial(backward_body, (dp, depth, experts, head)),
         in_specs=[vmem] * len(in_vmem) + [hbm] * len(in_hbm),
-        out_specs=[vmem, vmem, hbm, hbm, hbm, vmem, vmem, vmem],
+        out_specs=[vmem, vmem, hbm, hbm, hbm, hbm, vmem, vmem, vmem],
         out_shape=[
             shape((output_rows, width), BF),
             shape((output_rows, width), BF),
             final,
             final,
             final,
+            shape((seq_len, width), BF),
             shape((2, slice_width, 4 * pair), BF),
             shape((16, slice_width), F32),
             shape((8, slice_width), F32),
@@ -1545,7 +1795,7 @@
         return jnp.max(jnp.where(matches, slots_in, -1), axis=2)
 
     def feed(slots, rows, grads):
-        slotted, slot_grad, pair, act, terms, pair_s, act_s, inner_s, probs_out = act_call(
+        slotted, slot_grad, pair, act, terms, pair_s, act_s, inner_s, probs_out = plain_act_call(
             experts, capacity, group_ids, slots, rows, grads, router_rows, gateup_all, down_all
         )
         terms = jnp.concatenate([terms.swapaxes(1, 2), inner_s], axis=-1)
@@ -1557,10 +1807,10 @@
     fed_a = feed(slots_a, norm_a, grad_a)
     fed_b = feed(slots_b, norm_b, grad_b)
     columns_a, columns_b = slots_a[..., None], slots_b[..., None]
-    row_grad_b = back_call(columns_b, *fed_b[0], gateup_all)
-    row_grad_a = back_call(after(columns_a, row_grad_b), *fed_a[0], gateup_all)
-    row_out_b = back_call(after(columns_b, row_grad_a), *fed_b[1], down_all)
-    row_out_a = back_call(columns_a, *fed_a[1], down_all)
+    row_grad_b = plain_back_call(columns_b, *fed_b[0], gateup_all)
+    row_grad_a = plain_back_call(after(columns_a, row_grad_b), *fed_a[0], gateup_all)
+    row_out_b = plain_back_call(after(columns_b, row_grad_a), *fed_b[1], down_all)
+    row_out_a = plain_back_call(columns_a, *fed_a[1], down_all)
 
     def spread(terms):
         wide = jnp.zeros(terms.shape[:-1] + (128,), F32)
@@ -1584,7 +1834,7 @@
     def unit_grads(left, right):
         return jnp.concatenate(
             [
-                outer_call(
+                plain_outer_call(
                     hidden_units,
                     hidden_pad,
                     dp,
@@ -1836,7 +2086,7 @@
     sin_rows = jnp.concatenate([-sin_part, sin_part], axis=1)
     (
         hidden,
-        norm_own,
+        norm_all,
         grads_all,
         gateup_all,
         down_all,
@@ -1869,69 +2119,78 @@
     router_rows = jnp.concatenate([misc_all[d] for d in range(dp)], axis=1)
     router_rows = jnp.where(jnp.arange(16)[:, None] <= experts, router_rows, 0.0).astype(BF)
     router_full = router_rows[: experts + 1].T
-    codes_all = codes_all[:, : 2 * top_count]
-    codes_a, codes_b = codes_all[:2], codes_all[2:]
-    norm_z = norm_own[0]
-    norm_a = norm_own
-    norm_x = swap(norm_z, 2)
-    norm_b = jnp.stack([norm_x, swap(norm_x, 1)])
-    grad_a, grad_b = grads_all[:2], grads_all[2:]
-
-    expert_ids = group * mine_experts + jnp.arange(mine_experts, dtype=jnp.int32)
-
     group_ids = group.astype(jnp.int32).reshape(1)
 
-    def slots_of(codes_in):
-        routes_in, slots_in = codes_in[:, None, :top_count], codes_in[:, None, top_count:]
-        matches = routes_in == expert_ids[None, :, None, None]
-        return jnp.max(jnp.where(matches, slots_in, -1), axis=2)
-
-    def feed(slots, rows, grads):
-        slotted, slot_grad, pair, act, terms, pair_s, act_s, inner_s, probs_out = act_call(
-            experts, capacity, group_ids, slots, rows, grads, router_rows, gateup_all, down_all
+    def feed(chunk, group_in):
+        return act_call(
+            experts,
+            top_count,
+            capacity,
+            chunk,
+            group_in,
+            codes_all,
+            norm_all,
+            grads_all,
+            router_rows,
+            gateup_all,
+            down_all,
         )
-        terms = jnp.concatenate([terms.swapaxes(1, 2), inner_s], axis=-1)
-        flat = [a.reshape(mine_experts, -1, a.shape[-1]) for a in (slotted, slot_grad, pair, act)]
-        shared = [a.reshape(1, -1, a.shape[-1]) for a in (rows, grads, pair_s, act_s)]
-        return (pair, pair_s), (act, act_s), terms, (flat, shared), probs_out
-
-    slots_a, slots_b = slots_of(codes_a), slots_of(codes_b)
-    fed_a = feed(slots_a, norm_a, grad_a)
-    fed_b = feed(slots_b, norm_b, grad_b)
-    columns_a, columns_b = slots_a[..., None], slots_b[..., None]
-    row_grad_b = back_call(columns_b, *fed_b[0], gateup_all)
-    row_grad_a = back_call(after(columns_a, row_grad_b), *fed_a[0], gateup_all)
-    row_out_b = back_call(after(columns_b, row_grad_a), *fed_b[1], down_all)
-    row_out_a = back_call(columns_a, *fed_a[1], down_all)
-
-    def spread(terms):
-        wide = jnp.zeros(terms.shape[:-1] + (128,), F32)
-        wide = lax.dynamic_update_slice_in_dim(
-            wide, terms[..., :mine_experts], group * mine_experts, terms.ndim - 1
-        )
-        return wide.at[..., experts].set(terms[..., mine_experts])
-
-    def over_group(a, b):
-        across = b[0].astype(F32) + swap(b[1], 1).astype(F32)
-        return a, swap(a[1], 1), swap(across.astype(b.dtype), 2)
-
-    grad_parts = over_group(row_grad_a, row_grad_b)
-    terms_a, terms_b, terms_c = over_group(spread(fed_a[2]), spread(fed_b[2]))
-    terms = jnp.stack([terms_a[0], terms_b, terms_c])
-    out_parts = over_group(row_out_a, row_out_b)
-
-    data_a, data_b = fed_a[3], fed_b[3]
-
-    def unit_grads(left, right):
-        pairs = [[(data[k][left], data[k][right]) for data in (data_a, data_b)] for k in range(2)]
-        return units_call(hidden_units, hidden_pad, dp, *pairs)
-
-    gate_total, up_total = unit_grads(2, 0)
-    down_total = unit_grads(3, 1)[0]
-    probs_mine = lax.dynamic_slice_in_dim(fed_a[4][0], zi * local_rows, local_rows, 1).T
+
+    def back(chunk, group_in, routed, shared, weight):
+        return back_call(top_count, chunk, group_in, codes_all, routed, shared, weight)
+
+    def across(own, sibling):
+        total = own.astype(F32) + swap(sibling, 1).astype(F32)
+        return total.astype(own.dtype)
+
+    slots_b, slot_grads_b, pair_b, act_b, pair_sb, act_sb, terms_b, _ = feed(1, group_ids)
+    terms_far = swap(across(terms_b[0], terms_b[1]), 2)
+    grad_b = back(1, group_ids, pair_b, pair_sb, gateup_all)
+    grad_far = across(*grad_b)
+    slots_a, slot_grads_a, pair_a, act_a, pair_sa, act_sa, terms_a, probs_out = feed(
+        0, after(group_ids, grad_far, terms_far)
+    )
+    grad_far = swap(grad_far, 2)
+
+    def rows_of(array):
+        return array.reshape(array.shape[0], -1, array.shape[-1])
+
+    def chunks_of(array):
+        return array.reshape(2, 2 * seq_len, width)
+
+    def flat(array):
+        return array.reshape(1, -1, array.shape[-1])
+
+    gate_total, up_total = units_call(
+        hidden_units,
+        hidden_pad,
+        dp,
+        [(rows_of(pair_a), rows_of(slots_a)), (rows_of(pair_b), rows_of(slots_b))],
+        [(flat(pair_sa), chunks_of(norm_all), 0), (flat(pair_sb), chunks_of(norm_all), 1)],
+    )
+    gate_sent = lax.dynamic_slice_in_dim(gate_total, (1 - me // 4) * 4, 4, 0)
+    out_b = back(1, after(group_ids, gate_sent), act_b, act_sb, down_all)
+    out_far = across(*out_b)
+    gate_in = swap(gate_sent, 4)
+    grad_a = back(0, after(group_ids, out_far), pair_a, pair_sa, gateup_all)
+    out_a = back(0, after(group_ids, grad_a[0]), act_a, act_sa, down_all)
+    (down_total,) = units_call(
+        hidden_units,
+        hidden_pad,
+        dp,
+        [
+            (rows_of(act_a), rows_of(slot_grads_a)),
+            (after(rows_of(act_b), out_a[0]), rows_of(slot_grads_b)),
+        ],
+        [(flat(act_sa), chunks_of(grads_all), 0), (flat(act_sb), chunks_of(grads_all), 1)],
+    )
+    grad_parts = (grad_a[0], swap(grad_a[1], 1), grad_far)
+    out_parts = (out_a[0], swap(out_a[1], 1), out_far)
+    terms = jnp.stack([terms_a[0], swap(terms_a[1], 1), terms_far])
+    probs_mine = lax.dynamic_slice_in_dim(probs_out[0], zi * local_rows, local_rows, 1).T
     probs_mine = jnp.pad(probs_mine, ((0, 0), (0, 128 - probs_mine.shape[1])))
     router_wide = jnp.pad(router_rows, ((0, 128 - router_rows.shape[0]), (0, 0)))
-    output, input_grad, down_sum, gate_sum, up_sum, attn_sum, misc_sum, gains_sum = backward_call(
+    output, input_grad, gate_sum, up_sum, down_sum, _, attn_sum, misc_sum, gains_sum = backward_call(
         dp,
         depth,
         experts,
@@ -1939,7 +2198,8 @@
         (terms, probs_mine, router_wide, gain_rows, cos_rows, sin_rows, hidden, out_grad),
         grad_parts
         + out_parts
-        + (down_total, gate_total, up_total, tok, attn_weights, qkv, probs_low, heads_out, norm_own),
+        + (gate_in, gate_total, up_total, down_total)
+        + (tok, attn_weights, qkv, probs_low, heads_out, norm_all),
     )
 
     def split_units(held):

time: 803 us -> 673 us (0.84)
  waiting for transfers between devices: 84.5 us -> 11.4 us
  local copies, waits for them, and re-layouts: 59.6 us -> 32.3 us
  Pallas kernels: 612 us -> 591 us
    ppermute x11 -> x9, waiting for transfers between devices: 84.5 us -> 11.4 us  [swap(): return lax.ppermute(array, 'dp', [(i, i ^ bit) for i in range(dp)])]
    pallas_call x1, Pallas kernels: 220 us -> 198 us  [backward_call(): pl.pallas_call(functools.partial(backward_body, (dp, depth, experts, head...]
    squeeze x6 -> x1, local copies, waits for them, and re-layouts: 11.3 us -> 0.02 us  [local_fused(): terms_far = swap(across(terms_b[0], terms_b[1]), 2)]
  transfers between devices with their start and end apart: 11 -> 9, of which waited for: 2 -> 4; matrix products, arithmetic and copies ran while one was open for 4% -> 2% of each run, Pallas kernels for 11% -> 6%
where the time goes in v4:
time: 673 us; the launch traced here: 663 us
  Pallas kernels  591 us (88%)
  local copies, waits for them, and re-layouts  32.3 us (5%)
  other arithmetic  20.5 us (3%)
  waiting for transfers between devices  11.4 us (2%)
    pallas_call x1, Pallas kernels, forward_call(): pl.pallas_call(functools.partial(forward_body, (dp, depth, experts, hidde...  224 us
    pallas_call x1, Pallas kernels, backward_call(): pl.pallas_call(functools.partial(backward_body, (dp, depth, experts, head...  198 us
    pallas_call x2, Pallas kernels, act_call(): call(functools.partial(act_body, experts, top_count), (units,), [pl.Block...  76.1 us
    pallas_call x4, Pallas kernels, back_call(): call(functools.partial(back_body, top_count), (width // block,), [pl.Bloc...  54 us
    pallas_call x2, Pallas kernels, units_call(): call(functools.partial(units_body, keep, pad), (many + 1, dp // blocks),...  39.9 us
  transfers between devices with their start and end apart: 9, of which 4 were waited for; matrix products, arithmetic and copies ran while one was open for 2% of the time, Pallas kernels for 6%

profile of v4, /device:TPU:0, one launch (start us, length us, event | category | flops | bytes accessed | tf_op | source)
XLA Modules:
  0.0 663.1 jit_solution(10510712706837544144)
XLA Ops:
  0.7 0.7 convert_element_type.111
  1.5 1.0 fusion.2
  2.5 2.2 copy.43
  4.7 1.1 copy.44
  5.9 0.8 copy.42
  7.9 1.0 pad_maximum_fusion.1
  9.7 223.7 %shard_map.289 = (f32[128,2048]{1,0:T(8,128)}, bf16[4,512,2048]{2,1,0:T(8,128)(2,1)}, bf16[4,512,2048]{2,1,0:T(8,128)(2,1)}, bf16[3,2,384,2048]{3,2,1,0:T(8,128)...) custom-call(s32[16,512]{1,0:T(8,128)} %pad.20.codes_ref, ...), custom_call_target="tpu_custom_call" | custom-call | tf_op jit(solution)/shard_map/pallas_call | solution.py:1063
  233.4 0.7 constant_dynamic-update-slice_fusion.7
  234.1 0.7 constant_dynamic-update-slice_fusion.6
  234.8 0.7 constant_dynamic-update-slice_fusion.5
  235.6 0.7 constant_dynamic-update-slice_fusion.4
  236.3 0.7 constant_dynamic-update-slice_fusion.3
  239.9 43.3 %shard_map.290 = (bf16[2,2,320,2048]{3,2,1,0:T(8,128)(2,1)}, bf16[2,2,320,2048]{3,2,1,0:T(8,128)(2,1)}, bf16[2,2,320,768]{3,2,1,0:T(8,128)(2,1)}, bf16[2,2,320,3...) custom-call(s32[1]{0:T(128)} %bitcast.group_ref, ...), custom_call_target="tpu_custom_call" | custom-call | flops 16240345088 | bytes 33554432 | tf_op jit(solution)/shard_map/pallas_call | solution.py:404
  283.2 15.2 %shard_map.291 = (bf16[512,2048]{1,0:T(8,128)(2,1)}, bf16[512,2048]{1,0:T(8,128)(2,1)}) custom-call(s32[1]{0:T(128)} %bitcast.group_ref, s32[4,16,512]{2,1,0:T(8,128)} %get-tuple-element.90.codes_ref, bf16[2,2,320,768]{3,2,1,0:T(8,128)(2,1)} %get-tuple-element.96.routed_ref, bf16[2,512,768]{2,1,0:T(8,128)(2,1)} %get-tuple-element.97.shared_ref, ...), custom_call_target="tpu_custom_call" | custom-call | flops 9932111872 | bytes 13631488 | tf_op jit(solution)/shard_map/pallas_call | solution.py:478
  299.0 3.7 collective-permute-done.1
  302.7 2.5 collective-permute-start.2
  305.3 3.7 add_convert_fusion.1
  308.9 3.1 collective-permute-done.2
  312.1 32.8 %shard_map.292 = (bf16[2,2,320,2048]{3,2,1,0:T(8,128)(2,1)}, bf16[2,2,320,2048]{3,2,1,0:T(8,128)(2,1)}, bf16[2,2,320,768]{3,2,1,0:T(8,128)(2,1)}, bf16[2,2,320,3...) custom-call(s32[1]{0:T(128)} %bitcast.group_ref, ...), custom_call_target="tpu_custom_call" | custom-call | flops 16240345088 | bytes 33554432 | tf_op jit(solution)/shard_map/pallas_call | solution.py:404
  344.9 24.0 %shard_map.293 = (bf16[8,3,352,256]{3,2,1,0:T(8,128)(2,1)}, bf16[8,3,352,256]{3,2,1,0:T(8,128)(2,1)}) custom-call(bf16[2,640,768]{2,1,0:T(8,128)(2,1)} %bitcast.146, bf16[2,640,768]{2,1,0:T(8,128)(2,1)} %bitcast.145, bf16[1,1024,768]{2,1,0:T(8,128)(2,1)} %bitcast.148, bf16[1,1024,768]{2,1,0:T(8,128)(2,1)} %bitcast.147, bf16[2,640,2048]{2,1,0:T(8,128)(2,1)} %bitcast.144, ...), custom_call_target="tpu_custom_call" | custom-call | flops 14495514624 | bytes 25952256 | tf_op jit(solution)/shard_map/pallas_call | solution.py:543
  368.9 1.7 constant_dynamic-slice_fusion.1
  370.6 11.8 %shard_map.294 = (bf16[512,2048]{1,0:T(8,128)(2,1)}, bf16[512,2048]{1,0:T(8,128)(2,1)}) custom-call(s32[1]{0:T(128)} %bitcast.group_ref, s32[4,16,512]{2,1,0:T(8,128)} %get-tuple-element.90.codes_ref, bf16[2,2,320,384]{3,2,1,0:T(8,128)(2,1)} %get-tuple-element.112.routed_ref, bf16[2,512,384]{2,1,0:T(8,128)(2,1)} %get-tuple-element.113.shared_ref, ...), custom_call_target="tpu_custom_call" | custom-call | flops 6308233216 | bytes 8912896 | tf_op jit(solution)/shard_map/pallas_call | solution.py:478
  382.4 1.7 collective-permute-start.8
  384.8 2.0 collective-permute-done.4
  386.8 3.7 add_convert_fusion.out_far_ref
  390.4 15.1 %shard_map.295 = (bf16[512,2048]{1,0:T(8,128)(2,1)}, bf16[512,2048]{1,0:T(8,128)(2,1)}) custom-call(s32[1]{0:T(128)} %bitcast.group_ref, s32[4,16,512]{2,1,0:T(8,128)} %get-tuple-element.90.codes_ref, bf16[2,2,320,768]{3,2,1,0:T(8,128)(2,1)} %get-tuple-element.106.routed_ref, bf16[2,512,768]{2,1,0:T(8,128)(2,1)} %get-tuple-element.107.shared_ref, ...), custom_call_target="tpu_custom_call" | custom-call | flops 9932111872 | bytes 13631488 | tf_op jit(solution)/shard_map/pallas_call | solution.py:478
  405.6 11.9 %shard_map.296 = (bf16[512,2048]{1,0:T(8,128)(2,1)}, bf16[512,2048]{1,0:T(8,128)(2,1)}) custom-call(s32[1]{0:T(128)} %bitcast.group_ref, s32[4,16,512]{2,1,0:T(8,128)} %get-tuple-element.90.codes_ref, bf16[2,2,320,384]{3,2,1,0:T(8,128)(2,1)} %get-tuple-element.120.routed_ref, bf16[2,512,384]{2,1,0:T(8,128)(2,1)} %get-tuple-element.121.shared_ref, ...), custom_call_target="tpu_custom_call" | custom-call | flops 6308233216 | bytes 8912896 | tf_op jit(solution)/shard_map/pallas_call | solution.py:478
  418.2 0.8 pad.22.router_ref
  419.8 2.6 collective-permute-done.3
  422.4 0.9 pad_maximum_fusion.terms_ref
  423.3 15.9 %shard_map.297.down_ref = bf16[8,3,352,256]{3,2,1,0:T(8,128)(2,1)} custom-call(bf16[2,640,384]{2,1,0:T(8,128)(2,1)} %bitcast.118, bf16[2,640,384]{2,1,0:T(8,128)(2,1)} %bitcast.117, bf16[1,1024,384]{2,1,0:T(8,128)(2,1)} %bitcast.120, bf16[1,1024,384]{2,1,0:T(8,128)(2,1)} %bitcast.119, bf16[2,640,2048]{2,1,0:T(8,128)(2,1)} %bitcast.106, ...), custom_call_target="tpu_custom_call" | custom-call | flops 7247757312 | bytes 22413312 | tf_op jit(solution)/shard_map/pallas_call | solution.py:543
  439.3 197.6 %shard_map.298 = (bf16[128,2048]{1,0:T(8,128)(2,1)}, bf16[128,2048]{1,0:T(8,128)(2,1)}, bf16[4,3,352,256]{3,2,1,0:T(8,128)(2,1)}, bf16[4,3,352,256]{3,2,1,0:T(8,...) custom-call(f32[3,512,128]{2,1,0:T(8,128)} %pad_maximum_fusion.terms, ...), custom_call_target="tpu_custom_call" | custom-call | tf_op jit(solution)/shard_map/pallas_call | solution.py:1533
  636.9 1.6 slice.140
  638.5 1.2 slice.137
  639.9 1.4 copy-done
  642.6 1.9 bitcast_convert_fusion
  644.6 1.9 convert_bitcast_fusion
  646.5 1.9 convert_bitcast_fusion.1
  648.6 1.5 copy.51
  650.3 1.5 copy.52
  651.8 1.4 convert_bitcast_fusion.2
  653.4 1.0 copy.53
  654.6 1.0 copy.54
  655.8 1.0 copy.55
  656.8 1.0 copy.49
  657.8 1.3 bitcast_convert_fusion.1
  661.1 0.8 copy.69
  661.9 0.8 copy.70
  (84 shorter events, 12.1 us)
Async XLA Ops:
  0.6 4.1 copy-start.2
  0.7 5.2 copy-start.7
  1.4 5.3 copy-start.13
  1.4 5.3 copy-start.14
  1.4 5.3 copy-start.17
  1.5 5.9 copy-start.15
  1.5 5.9 copy-start.16
  7.8 1.3 copy-start.10
  9.1 0.6 copy-start.9
  283.2 15.3 %copy-start.3 = (f32[2,512,128]{2,1,0:T(8,128)S(1)}, f32[2,512,128]{2,1,0:T(8,128)}, u32[]{:S(2)}) copy-start(f32[2,512,128]{2,1,0:T(8,128)} %get-tuple-element.100) | copy-start | bytes 1572868
  298.4 6.8 %collective-permute-start = (bf16[512,2048]{1,0:T(8,128)(2,1)}, bf16[512,2048]{1,0:T(8,128)(2,1)S(1)}, u32[]{:S(2)}, u32[]{:S(2)}) collective-permute-start(bf16[512,2048]{1,0:T(8,128)(2,1)} %get-tuple-element.99), channel_id=1, source_target_pairs={{0,4},{4,0},{8,12},{12,8},{16,20},{20,16},{24,28},{28,24},{1,5},{5... | collective-permute-start | bytes 6291464 | tf_op jit(solution)/shard_map/ppermute | solution.py:2055
  298.6 4.1 collective-permute-start.1
  302.7 9.3 %collective-permute-start.2 = (f32[512,128]{1,0:T(8,128)S(1)}, f32[512,128]{1,0:T(8,128)S(1)}, u32[]{:S(2)}, u32[]{:S(2)}) collective-permute-start(f32[512,128]{1,0:T(8,128)S(1)} %bitcast_add_fusion), channel_id=1, source_target_pairs={{0,8},{4,12},{8,0},{12,4},{16,24},{20,28},{24,16},{28,20},{1,9},{5... | collective-permute-start | bytes 786440 | tf_op jit(solution)/shard_map/ppermute | solution.py:2055
  382.4 4.4 collective-permute-start.4
  382.4 56.8 %collective-permute-start.8 = (bf16[4,3,352,256]{3,2,1,0:T(8,128)(2,1)S(1)}, bf16[4,3,352,256]{3,2,1,0:T(8,128)(2,1)}, u32[]{:S(2)}, u32[]{:S(2)}) collective-permute-start(bf16[4,3,352,256]{3,2,1,0:T(8,128)(2,1)S(1)} %constant_dynamic-slice_fusion.1), channel_id=1, source_target_pairs={{0,16},{4,20},{8,24},{12,28},{16,0},{20,4},{24,8},{28,12},{1,17},{... | collective-permute-start | bytes 6488072 | tf_op jit(solution)/shard_map/ppermute | solution.py:2055
  384.1 55.1 %collective-permute-start.6 = (bf16[512,2048]{1,0:T(8,128)(2,1)}, bf16[512,2048]{1,0:T(8,128)(2,1)}, u32[]{:S(2)}, u32[]{:S(2)}) collective-permute-start(bf16[512,2048]{1,0:T(8,128)(2,1)} %add_convert_fusion.1), channel_id=1, source_target_pairs={{0,8},{4,12},{8,0},{12,4},{16,24},{20,28},{24,16},{28,20},{1,9},{5... | collective-permute-start | bytes 6291464 | tf_op jit(solution)/shard_map/ppermute | solution.py:2055
  405.6 12.4 %copy-start.6 = (f32[2,512,128]{2,1,0:T(8,128)S(1)}, f32[2,512,128]{2,1,0:T(8,128)}, u32[]{:S(2)}) copy-start(f32[2,512,128]{2,1,0:T(8,128)} %get-tuple-element.102) | copy-start | bytes 1572868
  405.6 12.7 %copy-start.8 = (bf16[16,2048]{1,0:T(8,128)(2,1)S(1)}, bf16[16,2048]{1,0:T(8,128)(2,1)}, u32[]{:S(2)}) copy-start(bf16[16,2048]{1,0:T(8,128)(2,1)} %select_convert_fusion.router_ref) | copy-start | bytes 196612
  405.6 13.5 %copy-start.12 = (f32[2,16,512]{2,1,0:T(8,128)S(1)}, f32[2,16,512]{2,1,0:T(8,128)}, u32[]{:S(2)}) copy-start(f32[2,16,512]{2,1,0:T(8,128)} %get-tuple-element.103) | copy-start | bytes 196612
  417.5 21.8 %collective-permute-start.7 = (bf16[512,2048]{1,0:T(8,128)(2,1)}, bf16[512,2048]{1,0:T(8,128)(2,1)}, u32[]{:S(2)}, u32[]{:S(2)}) collective-permute-start(bf16[512,2048]{1,0:T(8,128)(2,1)} %get-tuple-element.123), channel_id=1, source_target_pairs={{0,4},{4,0},{8,12},{12,8},{16,20},{20,16},{24,28},{28,24},{1,5},{5... | collective-permute-start | bytes 6291464 | tf_op jit(solution)/shard_map/ppermute | solution.py:2055
  417.6 21.6 %collective-permute-start.5 = (bf16[512,2048]{1,0:T(8,128)(2,1)}, bf16[512,2048]{1,0:T(8,128)(2,1)}, u32[]{:S(2)}, u32[]{:S(2)}) collective-permute-start(bf16[512,2048]{1,0:T(8,128)(2,1)} %get-tuple-element.118), channel_id=1, source_target_pairs={{0,4},{4,0},{8,12},{12,8},{16,20},{20,16},{24,28},{28,24},{1,5},{5... | collective-permute-start | bytes 6291464 | tf_op jit(solution)/shard_map/ppermute | solution.py:2055
  418.0 4.4 collective-permute-start.3
  636.9 2.8 copy-start.1
  639.7 1.6 copy-start
  641.3 0.7 copy-start.11
  655.8 5.3 copy-start.5
  656.8 5.1 copy-start.4

commit v5 on v4

--- a/solution.py
+++ b/solution.py
@@ -283,115 +283,64 @@
     router_ref,
     gateup_ref,
     down_ref,
-    slotted_ref,
-    slotgrad_ref,
     pair_ref,
     act_ref,
-    pair_s_ref,
-    act_s_ref,
     terms_ref,
     probs_ref,
+    weights,
+    routed,
 ):
     unit, units = pl.program_id(0), pl.num_programs(0)
     half = gateup_ref.shape[1] // 2
     count, seq_len, width = rows_ref.shape
-    capacity = slotted_ref.shape[2]
+    data = rows_ref[...].reshape(count * seq_len, width)
+    cot = grads_ref[...].reshape(count * seq_len, width)
+    lane = lax.broadcasted_iota(jnp.int32, weights.shape, 1)
 
     @pl.when(unit == 0)
     def _():
+        logits = dot(data, router_ref[...], 1, 1)
+        chosen = jnp.where(lane < experts, logits, -1e30)
+        raised = jnp.exp(chosen - jnp.max(chosen, axis=1, keepdims=True))
+        soft = raised / jnp.sum(raised, axis=1, keepdims=True)
+        probs = jnp.where(lane < experts, soft, jax.nn.sigmoid(logits))
         for s in range(count):
-            logits = dot(router_ref[...], rows_ref[s], 1, 1)
-            row = lax.broadcasted_iota(jnp.int32, logits.shape, 0)
-            routed = jnp.where(row < experts, logits, -1e30)
-            raised = jnp.exp(routed - jnp.max(routed, axis=0, keepdims=True))
-            soft = raised / jnp.sum(raised, axis=0, keepdims=True)
-            probs_ref[s] = jnp.where(row < experts, soft, jax.nn.sigmoid(logits))
+            codes = codes_ref[s]
+            row = lax.broadcasted_iota(jnp.int32, codes.shape, 0)
+            named = row == experts
+            for k in range(top_count):
+                named = jnp.logical_or(named, codes[k : k + 1] == row)
+            named = jnp.logical_and(named, row <= experts).astype(F32).astype(BF)
+            place = (codes.shape[0], weights.shape[1])
+            same = lax.broadcasted_iota(jnp.int32, place, 0) == lax.broadcasted_iota(
+                jnp.int32, place, 1
+            )
+            at = slice(s * seq_len, (s + 1) * seq_len)
+            routed[at] = dot(named, same.astype(F32).astype(BF), 0, 0)
+            probs_ref[s] = probs[at]
+        weights[...] = probs * routed[...]
         terms_ref[...] = jnp.zeros_like(terms_ref)
 
-    def parts(data, cot, weight):
-        both = dot(data, gateup_ref[0], 1, 1)
-        cot_in = dot(cot, down_ref[0], 1, 1)
-        gate_in, up_in = both[:, :half], both[:, half:]
-        gate_act, gate_slope = silu_parts(gate_in)
-        act = gate_act * up_in
-        inner = jnp.sum(act.astype(BF).astype(F32) * cot_in, axis=1, keepdims=True)
-        cot_in = cot_in * weight
-        return (
-            (act * weight).astype(BF),
-            (cot_in * up_in * gate_slope).astype(BF),
-            (cot_in * gate_act).astype(BF),
-            inner,
-        )
-
-    @pl.when(unit < units - 1)
-    def _():
-        expert = group_ref[0] * (units - 1) + unit
-        masks, weights = [], []
-        for s in range(count):
-            mask = slot_mask(codes_ref, s, expert, top_count, capacity)
-            onehot = mask.astype(F32).astype(BF)
-            slotted_ref[0, s] = dot(onehot, rows_ref[s]).astype(BF)
-            slotgrad_ref[0, s] = dot(onehot, grads_ref[s]).astype(BF)
-            probs = probs_ref[s]
-            row = lax.broadcasted_iota(jnp.int32, probs.shape, 0)
-            gate = jnp.sum(jnp.where(row == expert, probs, 0.0), axis=0, keepdims=True)
-            weights.append(jnp.sum(jnp.where(mask, gate, 0.0), axis=1, keepdims=True))
-            masks.append(onehot)
-        act, gate_grad, up_grad, inner = parts(
-            slotted_ref[0].reshape(count * capacity, width),
-            slotgrad_ref[0].reshape(count * capacity, width),
-            jnp.concatenate(weights, axis=0),
-        )
-        lane = lax.broadcasted_iota(jnp.int32, (capacity, terms_ref.shape[2]), 1)
-        for s in range(count):
-            at = slice(s * capacity, (s + 1) * capacity)
-            act_ref[0, s] = act[at]
-            pair_ref[0, s, :, :half] = gate_grad[at]
-            pair_ref[0, s, :, half:] = up_grad[at]
-            placed = jnp.where(lane == expert, inner[at], 0.0)
-            high = placed.astype(BF)
-            low = (placed - high.astype(F32)).astype(BF)
-            terms_ref[s] += dot(masks[s], high, 0, 0) + dot(masks[s], low, 0, 0)
-
-    @pl.when(unit == units - 1)
-    def _():
-        data = rows_ref[...].reshape(count * seq_len, width)
-        logits = dot(data, router_ref[...], 1, 1)
-        weight = jax.nn.sigmoid(logits[:, experts : experts + 1])
-        act, gate_grad, up_grad, inner = parts(
-            data, grads_ref[...].reshape(count * seq_len, width), weight
-        )
-        lane = lax.broadcasted_iota(jnp.int32, (seq_len, terms_ref.shape[2]), 1)
-        for s in range(count):
-            at = slice(s * seq_len, (s + 1) * seq_len)
-            act_s_ref[s] = act[at]
-            pair_s_ref[s, :, :half] = gate_grad[at]
-            pair_s_ref[s, :, half:] = up_grad[at]
-            terms_ref[s] += jnp.where(lane == experts, inner[at], 0.0)
-
-
-def slot_mask(codes_ref, s, expert, top_count, capacity):
-    codes = codes_ref[s]
-    slot = jnp.full((1, codes.shape[1]), -1, jnp.int32)
-    for k in range(top_count):
-        slot = jnp.where(codes[k : k + 1] == expert, codes[top_count + k : top_count + k + 1], slot)
-    return lax.broadcasted_iota(jnp.int32, (capacity, codes.shape[1]), 0) == slot
-
-
-def act_call(experts, top_count, capacity, chunk, group, codes, rows, grads, router, gateup, down):
+    mine = lane == jnp.where(unit < units - 1, group_ref[0] * (units - 1) + unit, experts)
+    weight = jnp.sum(jnp.where(mine, weights[...], 0.0), axis=1, keepdims=True)
+    both = dot(data, gateup_ref[0], 1, 1)
+    cot_in = dot(cot, down_ref[0], 1, 1)
+    gate_in, up_in = both[:, :half], both[:, half:]
+    gate_act, gate_slope = silu_parts(gate_in)
+    act = gate_act * up_in
+    inner = jnp.sum(act.astype(BF).astype(F32) * cot_in, axis=1, keepdims=True)
+    cot_in = cot_in * weight
+    act_ref[...] = (act * weight).astype(BF)
+    pair_ref[:, :half] = (cot_in * up_in * gate_slope).astype(BF)
+    pair_ref[:, half:] = (cot_in * gate_act).astype(BF)
+    terms_ref[...] += jnp.where(mine, inner * routed[...], 0.0).reshape(terms_ref.shape)
+
+
+def act_call(experts, top_count, chunk, group, codes, rows, grads, router, gateup, down):
     _, seq_len, width = rows.shape
     units, wide, _ = gateup.shape
-    half = wide // 2
-    routed, count = units - 1, 2
-
-    def unit(u):
-        return (u, 0, 0)
-
-    def slot(u):
-        return (jnp.minimum(u, routed - 1), 0, 0, 0)
-
-    def whole(*shape):
-        return pl.BlockSpec(shape, lambda u: (0,) * len(shape))
+    half, count = wide // 2, 2
+    total = count * seq_len
 
     def part(*shape):
         return pl.BlockSpec(
@@ -400,7 +349,12 @@
             pipeline_mode=pl.Buffered(1),
         )
 
-    work = count * (routed * capacity + seq_len) * width
+    def unit(u):
+        return (u, 0, 0)
+
+    def whole(u):
+        return (0, 0, 0)
+
     return call(
         functools.partial(act_body, experts, top_count),
         (units,),
@@ -409,147 +363,86 @@
             part(count, codes.shape[1], seq_len),
             part(count, seq_len, width),
             part(count, seq_len, width),
-            whole(*router.shape),
+            pl.BlockSpec(router.shape, lambda u: (0, 0)),
             pl.BlockSpec((1, wide, width), unit),
             pl.BlockSpec((1, half, width), unit),
         ],
         [
-            pl.BlockSpec((1, count, capacity, width), slot),
-            pl.BlockSpec((1, count, capacity, width), slot),
-            pl.BlockSpec((1, count, capacity, wide), slot),
-            pl.BlockSpec((1, count, capacity, half), slot),
-            whole(count, seq_len, wide),
-            whole(count, seq_len, half),
-            whole(count, seq_len, 128),
-            whole(count, router.shape[0], seq_len),
+            pl.BlockSpec((total, wide), lambda u: (0, u)),
+            pl.BlockSpec((total, half), lambda u: (0, u)),
+            pl.BlockSpec((count, seq_len, 128), whole),
+            pl.BlockSpec((count, seq_len, 128), whole),
         ],
         [
-            jax.ShapeDtypeStruct((routed, count, capacity, width), BF),
-            jax.ShapeDtypeStruct((routed, count, capacity, width), BF),
-            jax.ShapeDtypeStruct((routed, count, capacity, wide), BF),
-            jax.ShapeDtypeStruct((routed, count, capacity, half), BF),
-            jax.ShapeDtypeStruct((count, seq_len, wide), BF),
-            jax.ShapeDtypeStruct((count, seq_len, half), BF),
+            jax.ShapeDtypeStruct((total, units * wide), BF),
+            jax.ShapeDtypeStruct((total, units * half), BF),
             jax.ShapeDtypeStruct((count, seq_len, 128), F32),
-            jax.ShapeDtypeStruct((count, router.shape[0], seq_len), F32),
+            jax.ShapeDtypeStruct((count, seq_len, 128), F32),
         ],
-        2 * work * 3 * half + 4 * count * routed * capacity * seq_len * width,
-        8 * count * seq_len * width * 2,
+        2 * total * units * 3 * half * width,
+        4 * total * width + units * 3 * half * width * 2,
+        [pltpu.VMEM((total, 128), F32), pltpu.VMEM((total, 128), F32)],
     )(group, codes, rows, grads, router, gateup, down)
 
 
-def back_body(top_count, group_ref, codes_ref, routed_ref, shared_ref, weight_ref, *refs):
-    out_refs, onehot_ref = refs[:-1], refs[-1]
-    routed, count, capacity, wide = routed_ref.shape
-    seq_len = shared_ref.shape[1]
-    cols = weight_ref.shape[2]
-
-    @pl.when(pl.program_id(0) == 0)
-    def _():
-        for s in range(count):
-            for e in range(routed):
-                mask = slot_mask(codes_ref, s, group_ref[0] * routed + e, top_count, capacity)
-                onehot_ref[s, e * capacity : (e + 1) * capacity] = mask.astype(F32).astype(BF)
-
-    shared = dot(shared_ref[...].reshape(count * seq_len, wide), weight_ref[routed])
-    slots = [
-        dot(routed_ref[e].reshape(count * capacity, wide), weight_ref[e])
-        .astype(BF)
-        .reshape(count, capacity, cols)
-        for e in range(routed)
-    ]
-    for s in range(count):
-        total = dot(onehot_ref[s], jnp.concatenate([rows[s] for rows in slots], axis=0), 0, 0)
-        out_refs[s][...] = (total + shared[s * seq_len : (s + 1) * seq_len]).astype(BF)
-
-
-def back_call(top_count, chunk, group, codes, routed, shared, weight):
+def back_body(left_ref, weight_ref, *out_refs):
+    seq_len = out_refs[0].shape[0]
+    total = dot(left_ref[...], weight_ref[...]).astype(BF)
+    for s, out_ref in enumerate(out_refs):
+        out_ref[...] = total[s * seq_len : (s + 1) * seq_len]
+
+
+def back_call(left, weight):
     units, wide, width = weight.shape
-    count, seq_len, _ = shared.shape
-    capacity = routed.shape[2]
+    weight = weight.reshape(units * wide, width)
+    total, depth = left.shape
     block = min(width, 512)
-    work = count * ((units - 1) * capacity + seq_len) * width
-
-    def whole(*shape):
-        return pl.BlockSpec(
-            shape, lambda j: (0,) * len(shape), pipeline_mode=pl.Buffered(1)
-        )
-
     return call(
-        functools.partial(back_body, top_count),
+        back_body,
         (width // block,),
         [
-            pl.BlockSpec(memory_space=pltpu.SMEM),
-            pl.BlockSpec((count, codes.shape[1], seq_len), lambda j: (chunk, 0, 0)),
-            whole(*routed.shape),
-            whole(*shared.shape),
-            pl.BlockSpec((units, wide, block), lambda j: (0, 0, j)),
+            pl.BlockSpec((total, depth), lambda j: (0, 0), pipeline_mode=pl.Buffered(1)),
+            pl.BlockSpec((depth, block), lambda j: (0, j)),
         ],
-        [pl.BlockSpec((seq_len, block), lambda j: (0, j))] * count,
-        [jax.ShapeDtypeStruct((seq_len, width), BF)] * count,
-        2 * work * wide + 2 * count * (units - 1) * capacity * seq_len * width,
-        units * wide * width * 2 + count * seq_len * width * 2,
-        [pltpu.VMEM((count, (units - 1) * capacity, seq_len), BF)],
-    )(group, codes, routed, shared, weight)
-
-
-def units_body(keep, pad, *refs):
-    lefts, rights, outs = refs[:4], refs[4:8], refs[8:]
-    unit, units = pl.program_id(0), pl.num_programs(0)
-
-    def store(first, second):
-        total = dot(lefts[first][0], rights[first][0], 0, 0)
-        total = (total + dot(lefts[second][0], rights[second][0], 0, 0)).astype(BF)
-        for part, out_ref in enumerate(outs):
-            blocks, _, _, slice_width = out_ref.shape
-            for k in range(blocks):
-                out_ref[k, 0] = total[
-                    part * pad : part * pad + keep, k * slice_width : (k + 1) * slice_width
-                ]
-
-    @pl.when(unit < units - 1)
-    def _():
-        store(0, 1)
-
-    @pl.when(unit == units - 1)
-    def _():
-        store(2, 3)
-
-
-def units_call(keep, pad, dp, routed, shared):
-    lefts = [pair[0] for pair in routed] + [entry[0] for entry in shared]
-    rights = [pair[1] for pair in routed] + [entry[1] for entry in shared]
-    chunks = [0, 0] + [entry[2] for entry in shared]
-    many, _, wide = lefts[0].shape
-    width = rights[0].shape[2]
+        [pl.BlockSpec((total // 2, block), lambda j: (0, j))] * 2,
+        [jax.ShapeDtypeStruct((total // 2, width), BF)] * 2,
+        2 * total * depth * width,
+        (total * depth + depth * width + total * width) * 2,
+    )(left, weight)
+
+
+def units_body(keep, pad, left_a, left_b, right_a, right_b, *outs):
+    total = dot(left_a[...], right_a[0], 0, 0) + dot(left_b[...], right_b[0], 0, 0)
+    total = total.astype(BF)
+    for part, out_ref in enumerate(outs):
+        blocks, _, _, slice_width = out_ref.shape
+        for k in range(blocks):
+            out_ref[k, 0] = total[
+                part * pad : part * pad + keep, k * slice_width : (k + 1) * slice_width
+            ]
+
+
+def units_call(keep, pad, dp, units, left_a, left_b, right):
+    right = right.reshape(2, left_a.shape[0], -1)
+    total, width = right.shape[1:]
+    wide = left_a.shape[1] // units
     slice_width = width // dp
     blocks = max(1, 1024 // slice_width)
     parts = wide // pad
-    last = dp // blocks - 1
-
-    def spec(n, array, cols):
-        def where(u, j):
-            of_shared = n > 1
-            mine = (u == many) if of_shared else (u < many)
-            unit = chunks[n] if of_shared else jnp.minimum(u, many - 1)
-            if cols:
-                return (unit, 0, jnp.where(mine, j, 0 if of_shared else last))
-            return (0 if of_shared else unit, 0, 0)
-
-        return pl.BlockSpec((1, array.shape[1], cols or wide), where)
-
-    cols = blocks * slice_width
-    rows = many * lefts[0].shape[1] + lefts[2].shape[1]
+    left = pl.BlockSpec((total, wide), lambda u, j: (0, u))
+
+    def chunk(k):
+        return pl.BlockSpec((1, total, blocks * slice_width), lambda u, j: (k, 0, j))
+
     return call(
         functools.partial(units_body, keep, pad),
-        (many + 1, dp // blocks),
-        [spec(n, a, 0) for n, a in enumerate(lefts)]
-        + [spec(n, a, cols) for n, a in enumerate(rights)],
+        (units, dp // blocks),
+        [left, left, chunk(0), chunk(1)],
         [pl.BlockSpec((blocks, 1, keep, slice_width), lambda u, j: (j, u, 0, 0))] * parts,
-        [jax.ShapeDtypeStruct((dp, many + 1, keep, slice_width), BF)] * parts,
-        4 * rows * wide * width,
-        rows * (wide + width) * 4,
-    )(*lefts, *rights)
+        [jax.ShapeDtypeStruct((dp, units, keep, slice_width), BF)] * parts,
+        4 * total * units * wide * width,
+        (4 * total * width + 4 * total * units * wide + units * wide * width) * 2,
+    )(left_a, left_b, right, right)
 
 
 MESH = pl.DeviceIdType.MESH
@@ -713,7 +606,6 @@
     me, z = lax.axis_index("dp"), lax.axis_index("tensor")
     core, x = me % 2, (me // 2) % 2
     bits = [2**k for k in range(dp.bit_length() - 1)]
-    upper = bits[2:]
     rows, width = tokens_ref.shape
     seq_len = rows * depth
     slice_width = width // dp
@@ -786,16 +678,15 @@
     near = [[copy for r in (0, 1) for copy in group_copies(*m, r)] for m in matrices]
     far = [[copy for r in (2, 3) for copy in group_copies(*m, r)] for m in matrices]
 
-    def upper_copies(dst, k):
-        copies = []
-        for bit in upper:
-            n = bit * slice_width
-            cols = pl.ds(pl.multiple_of(me // bit * n, n), n)
-            place = dst.at[:, k, pl.ds(0, hidden_units), cols]
-            copies.append(c.remote(place, place, dp=peer_of(me, bit)))
-        return copies
-
-    over = [upper_copies(m[2], m[3]) for m in matrices]
+    def over_copy(dst, k, far_chip):
+        n = 2 * slice_width
+        chip = me // 2 + far_chip * (1 - 2 * x)
+        cols = pl.ds(pl.multiple_of(chip * n, n), n)
+        place = dst.at[:, k, pl.ds(0, hidden_units), cols]
+        return c.remote(place, place, dp=peer_of(me, 4))
+
+    over_near = [over_copy(m[2], m[3], 0) for m in matrices]
+    over = [over_copy(m[2], m[3], 1) for m in matrices]
 
     for copy in core_copies:
         copy.wait()
@@ -840,6 +731,10 @@
     for m in far:
         for copy in m:
             copy.start()
+    for m, copy in zip(near, over_near):
+        for part_copy in m:
+            part_copy.wait()
+        copy.start()
     own_grad.wait()
     grad_line = Line(c, grads_ref.at[0], z, depth, rows)
     for k in range(2, depth):
@@ -906,11 +801,9 @@
     norm_rows(0)
     project(0)
     line_step(grad_line, 1)
-    for copy in near[0]:
-        copy.wait()
     for copy in far[0]:
         copy.wait_recv()
-    over[0][0].start()
+    over[0].start()
     tok_pass[0].wait()
     for copy, there in tok_passed:
         pl.when(there)(copy.wait)
@@ -957,11 +850,6 @@
     part_pass.start()
     attend(0)
     project_out(0)
-    for copy in near[1]:
-        copy.wait()
-    for copy in far[1]:
-        copy.wait_recv()
-    over[1][0].start()
     part_pass.wait_recv()
 
     scatter = []
@@ -982,11 +870,10 @@
     x_grad.start()
     own_pass = c.remote(grads_ref.at[0], grads_ref.at[1], dp=peer_of(me, 1))
     own_pass.start()
-    for copy in near[2]:
-        copy.wait()
-    for copy in far[2]:
-        copy.wait_recv()
-    over[2][0].start()
+    for k in (1, 2):
+        for copy in far[k]:
+            copy.wait_recv()
+        over[k].start()
 
     for copy in scatter:
         copy.wait_recv()
@@ -1021,12 +908,8 @@
     x_grad.wait_recv()
     grad_pass = c.remote(grads_ref.at[2], grads_ref.at[3], dp=peer_of(me, 1))
     grad_pass.start()
-    for k in range(1, len(upper)):
-        for chain in over:
-            chain[k - 1].wait_recv()
-            chain[k].start()
-    for chain in over:
-        chain[-1].wait_recv()
+    for copy in over_near + over:
+        copy.wait()
     norm_far.wait()
     for copy, there in far_passed:
         pl.when(there)(copy.wait)
@@ -1044,7 +927,7 @@
         copy.wait()
     for copy in gain_copies + misc_copies + gain_spread + qk_copies + vo_copies + scatter:
         copy.wait_send()
-    for copy in [part_pass, x_grad] + [y for m in far for y in m] + [y for m in over for y in m]:
+    for copy in [part_pass, x_grad] + [y for m in far for y in m]:
         copy.wait_send()
 
 
@@ -1109,9 +992,6 @@
     grad_a_ref,
     grad_b_ref,
     grad_c_ref,
-    out_a_ref,
-    out_b_ref,
-    out_far_ref,
     gate_in_ref,
     gate_ref,
     up_ref,
@@ -1122,12 +1002,10 @@
     probs_hbm,
     mix_hbm,
     norm_hbm,
-    output_ref,
     input_ref,
     gate_out,
     up_out,
     down_out,
-    out_c_ref,
     attn_out,
     misc_out,
     gains_out,
@@ -1162,7 +1040,7 @@
     dp, depth, experts, head = sizes
     me, z = lax.axis_index("dp"), lax.axis_index("tensor")
     core, x, y = me % 2, (me // 2) % 2, me // 4
-    rows, width = output_ref.shape
+    rows, width = input_ref.shape
     seq_len = rows * depth
     slice_width = width // dp
     pair = mix_ref.shape[2]
@@ -1178,8 +1056,6 @@
         other = matrices[m][0].at[pl.ds((1 - y) * 4, 4)]
         over.append(c.remote(other, arrived.at[m], dp=peer_of(me, 4)))
         over[m].start()
-    out_far = c.remote(out_far_ref, out_c_ref, dp=peer_of(me, 2))
-    out_far.start()
     gate_in = c.local(gate_in_ref, arrived.at[0])
     grads = (grad_a_ref, grad_b_ref, grad_c_ref)
     loads = [c.local(grads[k], three.at[k]) for k in range(3)]
@@ -1289,13 +1165,7 @@
     pass_back = pass_on(c, back.at[0], back.at[1], z, depth, rows, sibling, passed)
     for copy in scatter:
         copy.wait_send()
-    outs = (out_a_ref, out_b_ref, out_c_ref)
-    out_loads = [c.local(outs[k], three.at[k]) for k in range(3)]
-    for copy in out_loads[:2]:
-        copy.start()
     line_step(line, 1, pass_back)
-    out_far.wait_recv()
-    out_loads[2].start()
 
     for copy in inputs:
         copy.wait()
@@ -1310,26 +1180,10 @@
     lax.fori_loop(0, depth, scale_rows, 0)
     line_step(line, 2, pass_back)
     units += add_over(1)
-    for copy in out_loads:
-        copy.wait()
-    out_scatter = []
-    for r in list(range(1, depth)) + [0]:
-        at = at_of((z + r) % depth)
-        total = three[0, at, :].astype(F32) + three[1, at, :].astype(F32)
-        total = total + three[2, at, :].astype(F32)
-        if r:
-            three[0, at, :] = total.astype(BF)
-            peer = (z + r) % depth
-            out_scatter.append(c.remote(three.at[0, at], scatter_in.at[1, r - 1], tensor=peer))
-        else:
-            keep[1] = total + hidden_ref[...]
     line_step(line, 3, pass_back)
     back_own.wait()
     for copy, there in passed:
         pl.when(there)(copy.wait)
-    for copy in out_scatter:
-        copy.start()
-
     def block_of(d):
         return tuple(d // bit % 2 for bit in reversed(bits))
 
@@ -1388,11 +1242,11 @@
         if r:
             three[1, at, :] = total.astype(BF)
             peer = (z + r) % depth
-            copy = c.remote(three.at[1, at], scatter_in.at[2, r - 1], tensor=peer)
+            copy = c.remote(three.at[1, at], scatter_in.at[1, r - 1], tensor=peer)
             copy.start()
             first_scatter.append(copy)
         else:
-            keep[2] = total
+            keep[1] = total
 
     for d in range(dp):
         total = jnp.zeros((slice_width, 3 * pair), F32)
@@ -1419,8 +1273,6 @@
     qk_first.start()
     vo_first.start()
 
-    for copy in out_scatter:
-        copy.wait_send()
     norm_load = c.local(norm_hbm.at[0], three.at[0])
     norm_load.start()
     norm_load.wait()
@@ -1491,17 +1343,11 @@
             finals.append(c.remote(source, place, dp=sibling) if other else c.local(source, place))
             finals[-1].start()
 
-    for copy in out_scatter:
+    for copy in first_scatter:
         copy.wait_recv()
     total = keep[1]
     for r in range(1, depth):
         total = total + scatter_in[1, r - 1].astype(F32)
-    output_ref[...] = total.astype(BF)
-    for copy in first_scatter:
-        copy.wait_recv()
-    total = keep[2]
-    for r in range(1, depth):
-        total = total + scatter_in[2, r - 1].astype(F32)
     total = total * gain_rows[0:1, :]
     scale = scales[0, at_of(z), :]
     unit = tok[0, at_of(z), :].astype(F32) * scale
@@ -1516,7 +1362,7 @@
     for copy in finals + units:
         copy.wait()
     line.finish()
-    for copy in over[1:] + small + first_scatter + misc_copies + [part_pass, out_far]:
+    for copy in over[1:] + small + first_scatter + misc_copies + [part_pass]:
         copy.wait_send()
 
 
@@ -1524,8 +1370,8 @@
     output_rows, width = in_vmem[6].shape
     seq_len = output_rows * depth
     slice_width = width // dp
-    units = in_hbm[6].shape[1:]
-    pair = in_hbm[14].shape[2]
+    units = in_hbm[3].shape[1:]
+    pair = in_hbm[11].shape[2]
     pairs = pair // head
     vmem, hbm = pl.BlockSpec(memory_space=pltpu.VMEM), pl.BlockSpec(memory_space=pl.ANY)
     shape = jax.ShapeDtypeStruct
@@ -1533,14 +1379,12 @@
     return pl.pallas_call(
         functools.partial(backward_body, (dp, depth, experts, head)),
         in_specs=[vmem] * len(in_vmem) + [hbm] * len(in_hbm),
-        out_specs=[vmem, vmem, hbm, hbm, hbm, hbm, vmem, vmem, vmem],
+        out_specs=[vmem, hbm, hbm, hbm, vmem, vmem, vmem],
         out_shape=[
-            shape((output_rows, width), BF),
             shape((output_rows, width), BF),
             final,
             final,
             final,
-            shape((seq_len, width), BF),
             shape((2, slice_width, 4 * pair), BF),
             shape((16, slice_width), F32),
             shape((8, slice_width), F32),
@@ -1549,7 +1393,7 @@
             pltpu.VMEM((4,) + units, BF),
             pltpu.VMEM((3, 4) + units, BF),
             pltpu.VMEM((3, seq_len, width), BF),
-            pltpu.VMEM((3, depth - 1, output_rows, width), BF),
+            pltpu.VMEM((2, depth - 1, output_rows, width), BF),
             pltpu.VMEM((seq_len, 128), F32),
             pltpu.VMEM((depth - 1, output_rows, 128), F32),
             pltpu.VMEM((2, seq_len, width + 128), BF),
@@ -1561,7 +1405,7 @@
             pltpu.VMEM((2, seq_len, 1), F32),
             pltpu.VMEM((2, seq_len, 3 * pair), BF),
             pltpu.VMEM((seq_len, width), BF),
-            pltpu.VMEM((3, output_rows, width), F32),
+            pltpu.VMEM((2, output_rows, width), F32),
             pltpu.VMEM((2, 2, 2, slice_width, 4 * pair), BF),
             pltpu.VMEM((1, 2, 2, slice_width, 2 * pair), BF),
             pltpu.VMEM((2, 1, 2, slice_width, 2 * pair), BF),
@@ -2046,28 +1890,8 @@
     zi = lax.axis_index("tensor")
     core, xi = me % 2, (me // 2) % 2
     group = me % 4
-    bits = []
-    while 2 ** (len(bits) + 1) <= dp:
-        bits.append(2 ** len(bits))
-    upper = bits[2:]
-
     def swap(array, bit):
         return lax.ppermute(array, "dp", [(i, i ^ bit) for i in range(dp)])
-
-    def bit_of(bit):
-        return (me // bit) % 2
-
-    def join(mine, theirs, bit, axis):
-        n = mine.shape[axis]
-        shape = list(mine.shape)
-        shape[axis] = 2 * n
-        out = jnp.zeros(shape, mine.dtype)
-        out = lax.dynamic_update_slice_in_dim(out, mine, n * bit_of(bit), axis)
-        return lax.dynamic_update_slice_in_dim(out, theirs, n * (1 - bit_of(bit)), axis)
-
-    def half(array, which, axis):
-        n = array.shape[axis] // 2
-        return lax.dynamic_slice_in_dim(array, which * n, n, axis)
 
     codes = jnp.concatenate([routes.T, slot_order.T, picture_ids[None]], axis=0)
     codes = jnp.pad(codes, ((0, 16 - codes.shape[0]), (0, 0)))
@@ -2118,14 +1942,13 @@
     down_all = down_all.reshape(mine_experts + 1, hidden_pad, width)
     router_rows = jnp.concatenate([misc_all[d] for d in range(dp)], axis=1)
     router_rows = jnp.where(jnp.arange(16)[:, None] <= experts, router_rows, 0.0).astype(BF)
-    router_full = router_rows[: experts + 1].T
+    router_rows = jnp.pad(router_rows, ((0, 128 - router_rows.shape[0]), (0, 0)))
     group_ids = group.astype(jnp.int32).reshape(1)
 
     def feed(chunk, group_in):
         return act_call(
             experts,
             top_count,
-            capacity,
             chunk,
             group_in,
             codes_all,
@@ -2136,68 +1959,40 @@
             down_all,
         )
 
-    def back(chunk, group_in, routed, shared, weight):
-        return back_call(top_count, chunk, group_in, codes_all, routed, shared, weight)
-
     def across(own, sibling):
         total = own.astype(F32) + swap(sibling, 1).astype(F32)
         return total.astype(own.dtype)
 
-    slots_b, slot_grads_b, pair_b, act_b, pair_sb, act_sb, terms_b, _ = feed(1, group_ids)
+    pair_b, act_b, terms_b, _ = feed(1, group_ids)
     terms_far = swap(across(terms_b[0], terms_b[1]), 2)
-    grad_b = back(1, group_ids, pair_b, pair_sb, gateup_all)
-    grad_far = across(*grad_b)
-    slots_a, slot_grads_a, pair_a, act_a, pair_sa, act_sa, terms_a, probs_out = feed(
-        0, after(group_ids, grad_far, terms_far)
-    )
-    grad_far = swap(grad_far, 2)
-
-    def rows_of(array):
-        return array.reshape(array.shape[0], -1, array.shape[-1])
-
-    def chunks_of(array):
-        return array.reshape(2, 2 * seq_len, width)
-
-    def flat(array):
-        return array.reshape(1, -1, array.shape[-1])
-
+    out_far = across(*back_call(act_b, down_all))
+    grad_far = across(*back_call(after(pair_b, out_far), gateup_all))
+    pair_a, act_a, terms_a, probs_out = feed(0, after(group_ids, grad_far, terms_far))
+    out_a = back_call(act_a, down_all)
+    out_sum = out_a[0].astype(F32) + swap(out_a[1], 1).astype(F32) + swap(out_far, 2).astype(F32)
     gate_total, up_total = units_call(
-        hidden_units,
-        hidden_pad,
-        dp,
-        [(rows_of(pair_a), rows_of(slots_a)), (rows_of(pair_b), rows_of(slots_b))],
-        [(flat(pair_sa), chunks_of(norm_all), 0), (flat(pair_sb), chunks_of(norm_all), 1)],
+        hidden_units, hidden_pad, dp, mine_experts + 1, after(pair_a, out_a[0]), pair_b, norm_all
     )
     gate_sent = lax.dynamic_slice_in_dim(gate_total, (1 - me // 4) * 4, 4, 0)
-    out_b = back(1, after(group_ids, gate_sent), act_b, act_sb, down_all)
-    out_far = across(*out_b)
     gate_in = swap(gate_sent, 4)
-    grad_a = back(0, after(group_ids, out_far), pair_a, pair_sa, gateup_all)
-    out_a = back(0, after(group_ids, grad_a[0]), act_a, act_sa, down_all)
+    grad_a = back_call(after(pair_a, gate_sent), gateup_all)
     (down_total,) = units_call(
-        hidden_units,
-        hidden_pad,
-        dp,
-        [
-            (rows_of(act_a), rows_of(slot_grads_a)),
-            (after(rows_of(act_b), out_a[0]), rows_of(slot_grads_b)),
-        ],
-        [(flat(act_sa), chunks_of(grads_all), 0), (flat(act_sb), chunks_of(grads_all), 1)],
-    )
-    grad_parts = (grad_a[0], swap(grad_a[1], 1), grad_far)
-    out_parts = (out_a[0], swap(out_a[1], 1), out_far)
+        hidden_units, hidden_pad, dp, mine_experts + 1, act_a, after(act_b, grad_a[0]), grads_all
+    )
+    grad_parts = (grad_a[0], swap(grad_a[1], 1), swap(grad_far, 2))
     terms = jnp.stack([terms_a[0], swap(terms_a[1], 1), terms_far])
-    probs_mine = lax.dynamic_slice_in_dim(probs_out[0], zi * local_rows, local_rows, 1).T
-    probs_mine = jnp.pad(probs_mine, ((0, 0), (0, 128 - probs_mine.shape[1])))
-    router_wide = jnp.pad(router_rows, ((0, 128 - router_rows.shape[0]), (0, 0)))
-    output, input_grad, gate_sum, up_sum, down_sum, _, attn_sum, misc_sum, gains_sum = backward_call(
+    feed_out = lax.psum_scatter(
+        out_sum.astype(BF), "tensor", scatter_dimension=0, tiled=True
+    ).astype(F32)
+    output = (hidden + feed_out).astype(BF)
+    probs_mine = lax.dynamic_slice_in_dim(probs_out[0], zi * local_rows, local_rows, 0)
+    input_grad, gate_sum, up_sum, down_sum, attn_sum, misc_sum, gains_sum = backward_call(
         dp,
         depth,
         experts,
         head_width,
-        (terms, probs_mine, router_wide, gain_rows, cos_rows, sin_rows, hidden, out_grad),
+        (terms, probs_mine, router_rows, gain_rows, cos_rows, sin_rows, hidden, out_grad),
         grad_parts
-        + out_parts
         + (gate_in, gate_total, up_total, down_total)
         + (tok, attn_weights, qkv, probs_low, heads_out, norm_all),
     )

time: 673 us -> 689 us (1.024)
  Pallas kernels: 591 us -> 562 us
  other arithmetic: 20.5 us -> 35.5 us
  between operations: 1.44 us -> 14.5 us
  local copies, waits for them, and re-layouts: 32.3 us -> 41.3 us
  waiting for transfers between devices: 11.4 us -> 18.7 us
    pallas_call x1, Pallas kernels: 198 us -> 178 us  [backward_call(): pl.pallas_call(functools.partial(backward_body, (dp, depth, experts, head...]
    pallas_call x2, Pallas kernels: 76.1 us -> 57.9 us  [act_call(): call(functools.partial(act_body, experts, top_count), (units,), [pl.Block...]
    pallas_call x1, Pallas kernels: 224 us -> 236 us  [forward_call(): pl.pallas_call(functools.partial(forward_body, (dp, depth, experts, hidde...]
    convert_element_type x0 -> x2, other arithmetic: none -> 7.57 us  [the longest x1 5.63 us: local_fused(): out_sum.astype(BF)]
    ppermute x9 -> x10, waiting for transfers between devices: 11.4 us -> 18.7 us  [swap(): return lax.ppermute(array, 'dp', [(i, i ^ bit) for i in range(dp)])]
  transfers between devices with their start and end apart: 9 -> 11, of which waited for: 4 -> 4; matrix products, arithmetic and copies ran while one was open for 2% -> 7% of each run, Pallas kernels for 6% -> 40%
where the time goes in v5:
time: 689 us; the launch traced here: 679 us
  Pallas kernels  562 us (82%)
  local copies, waits for them, and re-layouts  41.3 us (6%)
  other arithmetic  35.5 us (5%)
  waiting for transfers between devices  18.7 us (3%)
  between operations  14.5 us (2%)
    pallas_call x1, Pallas kernels, forward_call(): pl.pallas_call(functools.partial(forward_body, (dp, depth, experts, hidde...  236 us
    pallas_call x1, Pallas kernels, backward_call(): pl.pallas_call(functools.partial(backward_body, (dp, depth, experts, head...  178 us
    pallas_call x2, Pallas kernels, act_call(): call(functools.partial(act_body, experts, top_count), (units,), [pl.Block...  57.9 us
    pallas_call x4, Pallas kernels, back_call(): call(back_body, (width // block,), [pl.BlockSpec((total, depth), lambda j...  46.9 us
    pallas_call x2, Pallas kernels, units_call(): call(functools.partial(units_body, keep, pad), (units, dp // blocks), [le...  43.3 us
    ppermute x10, waiting for transfers between devices, swap(): return lax.ppermute(array, 'dp', [(i, i ^ bit) for i in range(dp)])  18.7 us
  transfers between devices with their start and end apart: 11, of which 4 were waited for; matrix products, arithmetic and copies ran while one was open for 7% of the time, Pallas kernels for 40%

profile of v5, /device:TPU:0, one launch (start us, length us, event | category | flops | bytes accessed | tf_op | source)
XLA Modules:
  0.0 678.9 jit_solution(1248327858071784373)
XLA Ops:
  10.9 1.8 copy.41
  12.7 2.2 copy.42
  15.0 1.1 copy.43
  16.1 1.0 fusion.2
  17.9 1.1 pad_maximum_fusion.1
  18.9 235.9 %shard_map.289 = (f32[128,2048]{1,0:T(8,128)}, bf16[4,512,2048]{2,1,0:T(8,128)(2,1)}, bf16[4,512,2048]{2,1,0:T(8,128)(2,1)}, bf16[3,2,384,2048]{3,2,1,0:T(8,128)...) custom-call(s32[16,512]{1,0:T(8,128)} %pad.16.codes_ref, ...), custom_call_target="tpu_custom_call" | custom-call | tf_op jit(solution)/shard_map/pallas_call | solution.py:946
  261.5 29.0 %shard_map.290 = (bf16[1024,2304]{1,0:T(8,128)(2,1)}, bf16[1024,1152]{1,0:T(8,128)(2,1)}, f32[2,512,128]{2,1,0:T(8,128)}, f32[2,512,128]{2,1,0:T(8,128)}) custom-call(s32[1]{0:T(128)} %bitcast.13.group_ref, s32[4,16,512]{2,1,0:T(8,128)} %get-tuple-element.82.codes_ref, bf16[4,512,2048]{2,1,0:T(8,128)(2,1)} %get-tuple-element.83.rows_ref.norm_hbm, ...), custom_call_target="tpu_custom_call" | custom-call | flops 14495514624 | bytes 22544384 | tf_op jit(solution)/shard_map/pallas_call | solution.py:358
  290.6 9.0 %shard_map.291 = (bf16[512,2048]{1,0:T(8,128)(2,1)}, bf16[512,2048]{1,0:T(8,128)(2,1)}) custom-call(bf16[1024,1152]{1,0:T(8,128)(2,1)} %get-tuple-element.110.left_ref.left_b, bf16[1152,2048]{1,0:T(8,128)(2,1)} %bitcast.122), custom_call_target="tpu_custom_call" | custom-call | flops 4831838208 | bytes 11272192 | tf_op jit(solution)/shard_map/pallas_call | solution.py:400
  299.9 4.0 collective-permute-done
  303.9 3.7 add_convert_fusion.2
  307.6 14.4 %shard_map.292 = (bf16[512,2048]{1,0:T(8,128)(2,1)}, bf16[512,2048]{1,0:T(8,128)(2,1)}) custom-call(bf16[1024,2304]{1,0:T(8,128)(2,1)} %get-tuple-element.92.left_ref.left_b, bf16[2304,2048]{1,0:T(8,128)(2,1)} %bitcast.116), custom_call_target="tpu_custom_call" | custom-call | flops 9663676416 | bytes 18350080 | tf_op jit(solution)/shard_map/pallas_call | solution.py:400
  322.6 3.9 collective-permute-done.2
  326.6 2.5 collective-permute-start.3
  329.2 3.7 add_convert_fusion.1
  332.9 1.9 collective-permute-start.8
  334.9 1.4 collective-permute-done.3
  336.3 28.9 %shard_map.293 = (bf16[1024,2304]{1,0:T(8,128)(2,1)}, bf16[1024,1152]{1,0:T(8,128)(2,1)}, f32[2,512,128]{2,1,0:T(8,128)}, f32[2,512,128]{2,1,0:T(8,128)}) custom-call(s32[1]{0:T(128)} %bitcast.13.group_ref, s32[4,16,512]{2,1,0:T(8,128)} %get-tuple-element.82.codes_ref, bf16[4,512,2048]{2,1,0:T(8,128)(2,1)} %get-tuple-element.83.rows_ref.norm_hbm, ...), custom_call_target="tpu_custom_call" | custom-call | flops 14495514624 | bytes 22544384 | tf_op jit(solution)/shard_map/pallas_call | solution.py:358
  365.1 9.1 %shard_map.294 = (bf16[512,2048]{1,0:T(8,128)(2,1)}, bf16[512,2048]{1,0:T(8,128)(2,1)}) custom-call(bf16[1024,1152]{1,0:T(8,128)(2,1)} %get-tuple-element.97.left_ref.left_a, bf16[1152,2048]{1,0:T(8,128)(2,1)} %bitcast.124), custom_call_target="tpu_custom_call" | custom-call | flops 4831838208 | bytes 11272192 | tf_op jit(solution)/shard_map/pallas_call | solution.py:400
  374.2 25.6 %shard_map.295 = (bf16[8,3,352,256]{3,2,1,0:T(8,128)(2,1)}, bf16[8,3,352,256]{3,2,1,0:T(8,128)(2,1)}) custom-call(bf16[1024,2304]{1,0:T(8,128)(2,1)} %get-tuple-element.106.left_a.left_ref, bf16[1024,2304]{1,0:T(8,128)(2,1)} %get-tuple-element.92.left_ref.left_b, bf16[2,1024,2048]{2,1,0:T(8,128)(2,1)} %bitcast.90, bf16[2,1024,2048]{2,1,0:T(8,128)(2,1)} %bitcast.91), custom_call_target="tpu_custom_call" | custom-call | flops 19327352832 | bytes 45088768 | tf_op jit(solution)/shard_map/pallas_call | solution.py:437
  399.9 1.7 constant_dynamic-slice_fusion.1
  401.9 14.4 %shard_map.296 = (bf16[512,2048]{1,0:T(8,128)(2,1)}, bf16[512,2048]{1,0:T(8,128)(2,1)}) custom-call(bf16[1024,2304]{1,0:T(8,128)(2,1)} %get-tuple-element.106.left_a.left_ref, bf16[2304,2048]{1,0:T(8,128)(2,1)} %bitcast.118), custom_call_target="tpu_custom_call" | custom-call | flops 9663676416 | bytes 18350080 | tf_op jit(solution)/shard_map/pallas_call | solution.py:400
  417.0 5.6 add_convert_fusion
  422.6 17.6 %shard_map.297.down_ref = bf16[8,3,352,256]{3,2,1,0:T(8,128)(2,1)} custom-call(bf16[1024,1152]{1,0:T(8,128)(2,1)} %get-tuple-element.97.left_ref.left_a, bf16[1024,1152]{1,0:T(8,128)(2,1)} %get-tuple-element.110.left_ref.left_b, bf16[2,1024,2048]{2,1,0:T(8,128)(2,1)} %bitcast.119, bf16[2,1024,2048]{2,1,0:T(8,128)(2,1)} %bitcast.120), custom_call_target="tpu_custom_call" | custom-call | flops 9663676416 | bytes 30932992 | tf_op jit(solution)/shard_map/pallas_call | solution.py:437
  440.9 0.9 pad_maximum_fusion.terms_ref
  441.9 9.3 %collective-permute-done.9.gate_in_ref = bf16[4,3,352,256]{3,2,1,0:T(8,128)(2,1)} collective-permute-done((bf16[4,3,352,256]{3,2,1,0:T(8,128)(2,1)S(1)}, bf16[4,3,352,256]{3,2,1,0:T(8,128)(2,1)}, u32[]{:S(2)}, u32[]{:S(2)}) %collective-permute-start.9) | collective-permute-done | bytes 2162720 | tf_op jit(solution)/shard_map/ppermute | solution.py:1894
  451.2 178.5 %shard_map.298 = (bf16[128,2048]{1,0:T(8,128)(2,1)}, bf16[4,3,352,256]{3,2,1,0:T(8,128)(2,1)}, bf16[4,3,352,256]{3,2,1,0:T(8,128)(2,1)}, bf16[4,3,352,256]{3,2,1...) custom-call(f32[3,512,128]{2,1,0:T(8,128)} %pad_maximum_fusion.terms_ref, ...), custom_call_target="tpu_custom_call" | custom-call | tf_op jit(solution)/shard_map/pallas_call | solution.py:1379
  629.7 2.2 slice.137
  631.9 1.5 slice.140
  633.4 0.9 slice.138
  635.2 0.9 slice.139
  636.1 1.2 slice.142
  638.7 2.3 bitcast_convert_fusion.3
  641.0 2.9 copy.49
  643.9 2.3 bitcast_convert_fusion.2
  646.2 2.9 copy.50
  649.1 2.4 convert_bitcast_fusion.2
  651.5 1.0 copy.47
  652.5 1.2 copy.46
  653.8 1.0 copy.53
  654.8 1.2 copy.45
  656.0 1.0 copy.52
  657.0 1.2 copy.44
  658.2 1.0 copy.51
  660.5 3.2 bitcast_convert_fusion
  663.7 1.9 convert_bitcast_fusion
  665.6 1.9 convert_bitcast_fusion.1
  667.6 1.3 bitcast_convert_fusion.1
  669.1 1.9 add_convert_fusion.3
  (76 shorter events, 18.5 us)
Async XLA Ops:
  7.2 7.8 %copy-start.4 = (bf16[256,1408]{1,0:T(8,128)(2,1)S(1)}, bf16[256,1408]{1,0:T(8,128)(2,1)}, u32[]{:S(2)}) copy-start(bf16[256,1408]{1,0:T(8,128)(2,1)} %param.34) | copy-start | bytes 2162692
  7.2 661.6 %reduce-scatter.2.cloned.1.call-start = ((), (), s32[]{:S(2)}) async-start(), calls=%async_computation.1 | async-start | bytes 2621440 | tf_op jit(solution)/shard_map/reduce_scatter | solution.py:1984
  17.5 1.5 copy-start.10
  17.9 1.1 copy-start.9
  299.6 4.4 collective-permute-start
  307.6 14.8 %copy-start.5 = (f32[2,512,128]{2,1,0:T(8,128)S(1)}, f32[2,512,128]{2,1,0:T(8,128)}, u32[]{:S(2)}) copy-start(f32[2,512,128]{2,1,0:T(8,128)} %get-tuple-element.95) | copy-start | bytes 1572868
  322.0 7.2 %collective-permute-start.1 = (bf16[512,2048]{1,0:T(8,128)(2,1)}, bf16[512,2048]{1,0:T(8,128)(2,1)S(1)}, u32[]{:S(2)}, u32[]{:S(2)}) collective-permute-start(bf16[512,2048]{1,0:T(8,128)(2,1)} %get-tuple-element.94), channel_id=1, source_target_pairs={{0,4},{4,0},{8,12},{12,8},{16,20},{20,16},{24,28},{28,24},{1,5},{5... | collective-permute-start | bytes 6291464 | tf_op jit(solution)/shard_map/ppermute | solution.py:1894
  322.4 4.1 collective-permute-start.2
  326.6 9.6 %collective-permute-start.3 = (f32[512,128]{1,0:T(8,128)S(1)}, f32[512,128]{1,0:T(8,128)S(1)}, u32[]{:S(2)}, u32[]{:S(2)}) collective-permute-start(f32[512,128]{1,0:T(8,128)S(1)} %bitcast_add_fusion), channel_id=1, source_target_pairs={{0,8},{4,12},{8,0},{12,4},{16,24},{20,28},{24,16},{28,20},{1,9},{5... | collective-permute-start | bytes 786440 | tf_op jit(solution)/shard_map/ppermute | solution.py:1894
  329.2 87.5 %collective-permute-start.5 = (bf16[512,2048]{1,0:T(8,128)(2,1)}, bf16[512,2048]{1,0:T(8,128)(2,1)}, u32[]{:S(2)}, u32[]{:S(2)}) collective-permute-start(bf16[512,2048]{1,0:T(8,128)(2,1)} %add_convert_fusion.2), channel_id=1, source_target_pairs={{0,8},{4,12},{8,0},{12,4},{16,24},{20,28},{24,16},{28,20},{1,9},{5... | collective-permute-start | bytes 6291464 | tf_op jit(solution)/shard_map/ppermute | solution.py:1894
  332.9 109.0 %collective-permute-start.8 = (bf16[512,2048]{1,0:T(8,128)(2,1)}, bf16[512,2048]{1,0:T(8,128)(2,1)}, u32[]{:S(2)}, u32[]{:S(2)}) collective-permute-start(bf16[512,2048]{1,0:T(8,128)(2,1)} %add_convert_fusion.1), channel_id=1, source_target_pairs={{0,8},{4,12},{8,0},{12,4},{16,24},{20,28},{24,16},{28,20},{1,9},{5... | collective-permute-start | bytes 6291464 | tf_op jit(solution)/shard_map/ppermute | solution.py:1894
  374.2 42.7 %collective-permute-start.4 = (bf16[512,2048]{1,0:T(8,128)(2,1)}, bf16[512,2048]{1,0:T(8,128)(2,1)}, u32[]{:S(2)}, u32[]{:S(2)}) collective-permute-start(bf16[512,2048]{1,0:T(8,128)(2,1)} %get-tuple-element.99), channel_id=1, source_target_pairs={{0,4},{4,0},{8,12},{12,8},{16,20},{20,16},{24,28},{28,24},{1,5},{5... | collective-permute-start | bytes 6291464 | tf_op jit(solution)/shard_map/ppermute | solution.py:1894
  401.6 15.0 %copy-start.7 = (f32[2,512,128]{2,1,0:T(8,128)S(1)}, f32[2,512,128]{2,1,0:T(8,128)}, u32[]{:S(2)}) copy-start(f32[2,512,128]{2,1,0:T(8,128)} %get-tuple-element.100) | copy-start | bytes 1572868
  401.6 49.6 %collective-permute-start.9 = (bf16[4,3,352,256]{3,2,1,0:T(8,128)(2,1)S(1)}, bf16[4,3,352,256]{3,2,1,0:T(8,128)(2,1)}, u32[]{:S(2)}, u32[]{:S(2)}) collective-permute-start(bf16[4,3,352,256]{3,2,1,0:T(8,128)(2,1)S(1)} %constant_dynamic-slice_fusion.1), channel_id=1, source_target_pairs={{0,16},{4,20},{8,24},{12,28},{16,0},{20,4},{24,8},{28,12},{1,17},{... | collective-permute-start | bytes 6488072 | tf_op jit(solution)/shard_map/ppermute | solution.py:1894
  416.3 25.5 %collective-permute-start.7 = (bf16[512,2048]{1,0:T(8,128)(2,1)}, bf16[512,2048]{1,0:T(8,128)(2,1)}, u32[]{:S(2)}, u32[]{:S(2)}) collective-permute-start(bf16[512,2048]{1,0:T(8,128)(2,1)} %get-tuple-element.108), channel_id=1, source_target_pairs={{0,4},{4,0},{8,12},{12,8},{16,20},{20,16},{24,28},{28,24},{1,5},{5... | collective-permute-start | bytes 6291464 | tf_op jit(solution)/shard_map/ppermute | solution.py:1894
  416.7 24.2 %collective-permute-start.6 = (f32[512,128]{1,0:T(8,128)S(1)}, f32[512,128]{1,0:T(8,128)S(1)}, u32[]{:S(2)}, u32[]{:S(2)}) collective-permute-start(f32[512,128]{1,0:T(8,128)S(1)} %get-tuple-element.143), channel_id=1, source_target_pairs={{0,4},{4,0},{8,12},{12,8},{16,20},{20,16},{24,28},{28,24},{1,5},{5... | collective-permute-start | bytes 786440 | tf_op jit(solution)/shard_map/ppermute | solution.py:1894
  422.6 17.7 %copy-start.8 = (f32[2,512,128]{2,1,0:T(8,128)S(1)}, f32[2,512,128]{2,1,0:T(8,128)}, u32[]{:S(2)}) copy-start(f32[2,512,128]{2,1,0:T(8,128)} %get-tuple-element.101) | copy-start | bytes 1572868
  629.7 3.6 copy-start.3
  633.3 1.9 copy-start.2
  635.2 2.1 copy-start.11
  665.6 1.9 copy-start.1
  667.6 1.6 copy-start
  667.6 3.5 copy-start.6
Sparse Core Ops, SparseCore 0:
  422.7 57.3 reduce-scatter.1

commit v6 on v5

--- a/solution.py
+++ b/solution.py
@@ -585,8 +585,15 @@
     gateup_ref,
     down_ref,
     codes_all,
+    router_out,
+    gain_rows,
+    tok_out,
+    weights_out,
+    qkv_out,
+    probs_out,
+    mix_out,
     misc_all,
-    gain_rows,
+    norm_mine,
     tok,
     weights,
     qkv_ref,
@@ -728,13 +735,6 @@
         qk_copies[k].start()
         vo_copies[k - 1].wait_recv()
         vo_copies[k].start()
-    for m in far:
-        for copy in m:
-            copy.start()
-    for m, copy in zip(near, over_near):
-        for part_copy in m:
-            part_copy.wait()
-        copy.start()
     own_grad.wait()
     grad_line = Line(c, grads_ref.at[0], z, depth, rows)
     for k in range(2, depth):
@@ -762,6 +762,11 @@
     own_misc.wait()
     for copy in misc_copies:
         copy.wait_recv()
+    router_out[...] = jnp.zeros_like(router_out)
+    row = lax.broadcasted_iota(jnp.int32, misc_ref.shape, 0)
+    for d in range(dp):
+        block = jnp.where(row <= experts, misc_all[d], 0.0).astype(BF)
+        router_out[: misc_ref.shape[0], d * slice_width : (d + 1) * slice_width] = block
     bias_in = jnp.zeros(misc_ref.shape, F32)
     sub = lax.broadcasted_iota(jnp.int32, misc_ref.shape, 0)
     for d in range(dp):
@@ -779,6 +784,13 @@
 
     qk_copies[-1].wait_recv()
     vo_copies[-1].wait_recv()
+    for m in far:
+        for copy in m:
+            copy.start()
+    for m, copy in zip(near, over_near):
+        for part_copy in m:
+            part_copy.wait()
+        copy.start()
     pairs = pair // head
 
     def project(s):
@@ -852,6 +864,18 @@
     project_out(0)
     part_pass.wait_recv()
 
+    saved = [
+        c.local(a, b)
+        for a, b in (
+            (tok, tok_out),
+            (weights, weights_out),
+            (qkv_ref, qkv_out),
+            (probs_ref, probs_out),
+            (mix_ref, mix_out),
+        )
+    ]
+    for copy in saved:
+        copy.start()
     scatter = []
     for r in list(range(1, depth)) + [0]:
         at = pl.ds(pl.multiple_of((z + r) % depth * rows, rows), rows)
@@ -882,9 +906,10 @@
         total = total + scatter_in[r - 1].astype(F32)
     hidden_ref[...] = total
     scale = lax.rsqrt(jnp.mean(total * total, axis=-1, keepdims=True) + EPS)
-    norm_ref[0, pl.ds(pl.multiple_of(z * rows, rows), rows), :] = (
-        total * scale * gain_rows[1:2, :]
-    ).astype(BF)
+    norm_mine[...] = (total * scale * gain_rows[1:2, :]).astype(BF)
+    norm_here = c.local(norm_mine, piece(norm_ref.at[0], z))
+    norm_here.start()
+    norm_here.wait()
     norm_line = Line(c, norm_ref.at[0], z, depth, rows)
     norm_line.begin()
     beside = peer_of(me, 2)
@@ -923,7 +948,7 @@
     grad_pass.wait()
     for line in (tok_line, grad_line, norm_line):
         line.finish()
-    for copy in pads:
+    for copy in pads + saved:
         copy.wait()
     for copy in gain_copies + misc_copies + gain_spread + qk_copies + vo_copies + scatter:
         copy.wait_send()
@@ -946,7 +971,7 @@
     return pl.pallas_call(
         functools.partial(forward_body, (dp, depth, experts, hidden_units, head)),
         in_specs=[vmem] * 5 + [hbm] * 12,
-        out_specs=[vmem, vmem, hbm, hbm, hbm] + [vmem] * 8,
+        out_specs=[vmem] + [hbm] * 4 + [vmem] * 3 + [hbm] * 5,
         out_shape=[
             shape((rows, width), F32),
             shape((4, seq_len, width), BF),
@@ -954,7 +979,7 @@
             shape((routed + 1, 2, hidden_pad, width), BF),
             shape((routed + 1, 1, hidden_pad, width), BF),
             shape((4,) + codes.shape, codes.dtype),
-            shape((dp,) + misc.shape, F32),
+            shape((128, width), BF),
             shape((8, width), F32),
             shape((2, seq_len, width), BF),
             shape((2,) * bits + (width // dp, 4 * pair), BF),
@@ -963,6 +988,13 @@
             shape((2, seq_len, pair), BF),
         ],
         scratch_shapes=[
+            pltpu.VMEM((dp,) + misc.shape, F32),
+            pltpu.VMEM((rows, width), BF),
+            pltpu.VMEM((2, seq_len, width), BF),
+            pltpu.VMEM((2,) * bits + (width // dp, 4 * pair), BF),
+            pltpu.VMEM((3, 2 * pairs, seq_len, head), BF),
+            pltpu.VMEM((2 * pairs, seq_len, seq_len), BF),
+            pltpu.VMEM((2, seq_len, pair), BF),
             pltpu.VMEM((seq_len, width), BF),
             pltpu.VMEM((2, seq_len, width), BF),
             pltpu.VMEM((seq_len, width), BF),
@@ -971,7 +1003,7 @@
             pltpu.VMEM((routed + 1, hidden_pad - hidden_units, width), BF),
             pltpu.SemaphoreType.DMA((160,)),
             pltpu.SemaphoreType.DMA((160,)),
-            pltpu.SemaphoreType.DMA((32,)),
+            pltpu.SemaphoreType.DMA((40,)),
         ],
         compiler_params=pltpu.CompilerParams(
             collective_id=0, has_side_effects=True, vmem_limit_bytes=VMEM_LIMIT
@@ -1424,6 +1456,66 @@
     )(*in_vmem, *in_hbm)
 
 
+def finish_body(
+    gate_ref, up_ref, down_ref, attn_ref, eg_ref, eu_ref, ed_ref, sg_ref, su_ref, sd_ref,
+    q_ref, k_ref, v_ref, o_ref, sg_rows, su_rows
+):
+    group, groups = pl.program_id(0), pl.num_programs(0)
+    many, rows, _ = eg_ref.shape
+    for source, routed, shared in (
+        (gate_ref, eg_ref, sg_rows.at[group]),
+        (up_ref, eu_ref, su_rows.at[group]),
+        (down_ref, ed_ref, sd_ref),
+    ):
+        for unit in range(many):
+            routed[unit] = source[0, unit].astype(F32)
+        shared[...] = source[0, many].astype(F32)
+
+    @pl.when(group == 0)
+    def _():
+        pair = attn_ref.shape[2] // 4
+        for c in range(2):
+            at = slice(c * pair, (c + 1) * pair)
+            for kind, out_ref in enumerate((q_ref, k_ref, v_ref)):
+                out_ref[:, at] = attn_ref[c, :, kind * pair : (kind + 1) * pair].astype(F32)
+            o_ref[at, :] = jnp.transpose(attn_ref[c, :, 3 * pair :].astype(F32))
+
+    @pl.when(group == groups - 1)
+    def _():
+        for source, out_ref in ((sg_rows, sg_ref), (su_rows, su_ref)):
+            out_ref[...] = jnp.transpose(source[...].reshape(groups * rows, -1))
+
+
+def finish_call(gate, up, down, attn):
+    groups, units, rows, slice_width = gate.shape
+    many, pair = units - 1, attn.shape[2] // 4
+    shape = jax.ShapeDtypeStruct
+
+    def whole(*dims):
+        return pl.BlockSpec(dims, lambda g: (0,) * len(dims))
+
+    source = pl.BlockSpec((1, units, rows, slice_width), lambda g: (g, 0, 0, 0))
+    routed = pl.BlockSpec((many, rows, slice_width), lambda g: (g, 0, 0))
+    return call(
+        finish_body,
+        (groups,),
+        [source] * 3 + [whole(*attn.shape)],
+        [routed] * 3
+        + [whole(slice_width, groups * rows)] * 2
+        + [pl.BlockSpec((rows, slice_width), lambda g: (g, 0))]
+        + [whole(slice_width, 2 * pair)] * 3
+        + [whole(2 * pair, slice_width)],
+        [shape((groups * many, rows, slice_width), F32)] * 3
+        + [shape((slice_width, groups * rows), F32)] * 2
+        + [shape((groups * rows, slice_width), F32)]
+        + [shape((slice_width, 2 * pair), F32)] * 3
+        + [shape((2 * pair, slice_width), F32)],
+        0,
+        groups * units * rows * slice_width * 18,
+        [pltpu.VMEM((groups, rows, slice_width), F32)] * 2,
+    )(gate, up, down, attn)
+
+
 def local_plain(
     dp,
     tokens,
@@ -1915,7 +2007,7 @@
         gateup_all,
         down_all,
         codes_all,
-        misc_all,
+        router_rows,
         gain_rows,
         tok,
         attn_weights,
@@ -1940,9 +2032,6 @@
     )
     gateup_all = gateup_all.reshape(mine_experts + 1, 2 * hidden_pad, width)
     down_all = down_all.reshape(mine_experts + 1, hidden_pad, width)
-    router_rows = jnp.concatenate([misc_all[d] for d in range(dp)], axis=1)
-    router_rows = jnp.where(jnp.arange(16)[:, None] <= experts, router_rows, 0.0).astype(BF)
-    router_rows = jnp.pad(router_rows, ((0, 128 - router_rows.shape[0]), (0, 0)))
     group_ids = group.astype(jnp.int32).reshape(1)
 
     def feed(chunk, group_in):
@@ -1963,53 +2052,49 @@
         total = own.astype(F32) + swap(sibling, 1).astype(F32)
         return total.astype(own.dtype)
 
+    units = mine_experts + 1
     pair_b, act_b, terms_b, _ = feed(1, group_ids)
+    out_b = back_call(act_b, down_all)
+    grad_b = back_call(after(pair_b, out_b[0]), gateup_all)
+    out_far = across(*out_b)
+    pair_a, act_a, terms_a, probs_out = feed(0, after(group_ids, out_far, grad_b[0]))
+    grad_far = across(*grad_b)
     terms_far = swap(across(terms_b[0], terms_b[1]), 2)
-    out_far = across(*back_call(act_b, down_all))
-    grad_far = across(*back_call(after(pair_b, out_far), gateup_all))
-    pair_a, act_a, terms_a, probs_out = feed(0, after(group_ids, grad_far, terms_far))
-    out_a = back_call(act_a, down_all)
-    out_sum = out_a[0].astype(F32) + swap(out_a[1], 1).astype(F32) + swap(out_far, 2).astype(F32)
+    out_a = back_call(after(act_a, grad_far, terms_far), down_all)
     gate_total, up_total = units_call(
-        hidden_units, hidden_pad, dp, mine_experts + 1, after(pair_a, out_a[0]), pair_b, norm_all
+        hidden_units, hidden_pad, dp, units, after(pair_a, out_a[0]), pair_b, norm_all
     )
     gate_sent = lax.dynamic_slice_in_dim(gate_total, (1 - me // 4) * 4, 4, 0)
     gate_in = swap(gate_sent, 4)
+    out_sum = out_a[0].astype(F32) + swap(out_a[1], 1).astype(F32) + swap(out_far, 2).astype(F32)
     grad_a = back_call(after(pair_a, gate_sent), gateup_all)
     (down_total,) = units_call(
-        hidden_units, hidden_pad, dp, mine_experts + 1, act_a, after(act_b, grad_a[0]), grads_all
-    )
+        hidden_units, hidden_pad, dp, units, act_a, after(act_b, grad_a[0], out_sum), grads_all
+    )
+    output = hidden + lax.dynamic_slice_in_dim(out_sum, zi * local_rows, local_rows, 0)
+    for r in range(1, depth):
+        start = (zi + r) % depth * local_rows
+        sent = lax.dynamic_slice_in_dim(out_sum, start, local_rows, 0).astype(BF)
+        moved = lax.ppermute(sent, "tensor", [(i, (i + r) % depth) for i in range(depth)])
+        output = output + moved.astype(F32)
+    output = output.astype(BF)
     grad_parts = (grad_a[0], swap(grad_a[1], 1), swap(grad_far, 2))
     terms = jnp.stack([terms_a[0], swap(terms_a[1], 1), terms_far])
-    feed_out = lax.psum_scatter(
-        out_sum.astype(BF), "tensor", scatter_dimension=0, tiled=True
-    ).astype(F32)
-    output = (hidden + feed_out).astype(BF)
     probs_mine = lax.dynamic_slice_in_dim(probs_out[0], zi * local_rows, local_rows, 0)
     input_grad, gate_sum, up_sum, down_sum, attn_sum, misc_sum, gains_sum = backward_call(
         dp,
         depth,
         experts,
         head_width,
-        (terms, probs_mine, router_rows, gain_rows, cos_rows, sin_rows, hidden, out_grad),
+        (after(terms, output), probs_mine, router_rows, gain_rows, cos_rows, sin_rows, hidden, out_grad),
         grad_parts
         + (gate_in, gate_total, up_total, down_total)
         + (tok, attn_weights, qkv, probs_low, heads_out, norm_all),
     )
 
-    def split_units(held):
-        routed = held[:, :mine_experts].reshape(experts, hidden_units, slice_width)
-        shared = held[:, mine_experts].reshape(-1, slice_width)
-        return routed.astype(F32), shared.astype(F32)
-
-    egate_sum, sgate_sum = split_units(gate_sum)
-    eup_sum, sup_sum = split_units(up_sum)
-    edown_sum, sdown_sum = split_units(down_sum)
-
-    def columns_of(kind):
-        held = attn_sum[:, :, kind * pair_width : (kind + 1) * pair_width].swapaxes(0, 1)
-        return held.reshape(slice_width, -1).astype(F32)
-
+    egate_sum, eup_sum, edown_sum, sgate_sum, sup_sum, sdown_sum, *attn_sums = finish_call(
+        gate_sum, up_sum, down_sum, attn_sum
+    )
     bias_sums = misc_sum[experts + 1 : experts + 3, :bias_width].reshape(2, 3, pair_heads, -1)
     bias_sums = bias_sums.swapaxes(0, 1).reshape(3, heads_local, -1)
     piece = norm_gains.shape[1]
@@ -2018,14 +2103,11 @@
         output,
         input_grad,
         gain_sums,
-        columns_of(0),
-        columns_of(1),
-        columns_of(2),
-        columns_of(3).T,
+        *attn_sums,
         bias_sums,
         misc_sum[: experts + 1].T,
-        sgate_sum.T,
-        sup_sum.T,
+        sgate_sum,
+        sup_sum,
         sdown_sum,
         egate_sum.swapaxes(1, 2),
         eup_sum.swapaxes(1, 2),

time: 689 us -> 634 us (0.920)
  local copies, waits for them, and re-layouts: 41.3 us -> 19.7 us
  other arithmetic: 35.5 us -> 16.9 us
  between operations: 14.5 us -> 1.05 us
  Pallas kernels: 562 us -> 549 us
  waiting for transfers between devices: 18.7 us -> 29.4 us
    ppermute x0 -> x3, waiting for transfers between devices: none -> 24.6 us  [local_fused(): lax.ppermute(sent, 'tensor', [(i, (i + r) % depth) for i in range(depth)])]
    pallas_call x1, Pallas kernels: 236 us -> 219 us  [forward_call(): pl.pallas_call(functools.partial(forward_body, (dp, depth, experts, hidde...]
    ppermute x10, waiting for transfers between devices: 18.7 us -> 4.78 us  [swap(): return lax.ppermute(array, 'dp', [(i, i ^ bit) for i in range(dp)])]
    transpose x5 -> x0, other arithmetic: 10.9 us -> none  [the longest x2 4.63 us: local_fused(): return (output, input_grad, gain_sums, columns_of(0), columns_of(1), colu...]
    pallas_call x0 -> x1, Pallas kernels: none -> 10.3 us  [finish_call(): call(finish_body, (groups,), [source] * 3 + [whole(*attn.shape)], [routed...]
    convert_element_type x5 -> x1, other arithmetic: 12.1 us -> 2.36 us  [local_fused(): output = output.astype(BF)]
  transfers between devices with their start and end apart: 11 -> 13, of which waited for: 4 -> 4; matrix products, arithmetic and copies ran while one was open for 7% -> 3% of each run, Pallas kernels for 40% -> 18%
where the time goes in v6:
time: 634 us; the launch traced here: 625 us
  Pallas kernels  549 us (87%)
  waiting for transfers between devices  29.4 us (5%)
  local copies, waits for them, and re-layouts  19.7 us (3%)
  other arithmetic  16.9 us (3%)
  starting transfers between devices  8.75 us (1%)
    pallas_call x1, Pallas kernels, forward_call(): pl.pallas_call(functools.partial(forward_body, (dp, depth, experts, hidde...  219 us
    pallas_call x1, Pallas kernels, backward_call(): pl.pallas_call(functools.partial(backward_body, (dp, depth, experts, head...  172 us
    pallas_call x2, Pallas kernels, act_call(): call(functools.partial(act_body, experts, top_count), (units,), [pl.Block...  57.9 us
    pallas_call x4, Pallas kernels, back_call(): call(back_body, (width // block,), [pl.BlockSpec((total, depth), lambda j...  47 us
    pallas_call x2, Pallas kernels, units_call(): call(functools.partial(units_body, keep, pad), (units, dp // blocks), [le...  43.2 us
    ppermute x3, waiting for transfers between devices, local_fused(): lax.ppermute(sent, 'tensor', [(i, (i + r) % depth) for i in range(depth)])  24.6 us
  transfers between devices with their start and end apart: 13, of which 4 were waited for; matrix products, arithmetic and copies ran while one was open for 3% of the time, Pallas kernels for 18%

profile of v6, /device:TPU:0, one launch (start us, length us, event | category | flops | bytes accessed | tf_op | source)
XLA Modules:
  0.0 625.0 jit_solution(7715092596773867858)
XLA Ops:
  0.7 0.7 convert_element_type.72
  1.4 0.8 reshape.142
  2.3 0.7 pad_convert_fusion
  3.0 0.7 pad_add_fusion
  3.7 0.6 pad.12.codes_ref
  4.3 1.8 copy.39
  6.1 2.2 copy.40
  8.4 1.1 copy.41
  9.5 1.0 fusion.2
  10.9 0.4 scatter.14.misc_ref
  11.3 1.0 pad_maximum_fusion.1
  12.3 218.7 %shard_map.289 = (f32[128,2048]{1,0:T(8,128)}, bf16[4,512,2048]{2,1,0:T(8,128)(2,1)}, bf16[4,512,2048]{2,1,0:T(8,128)(2,1)}, bf16[3,2,384,2048]{3,2,1,0:T(8,128)...) custom-call(s32[16,512]{1,0:T(8,128)} %pad.12.codes_ref, ...), custom_call_target="tpu_custom_call" | custom-call | tf_op jit(solution)/shard_map/pallas_call | solution.py:971
  231.0 29.1 %shard_map.290 = (bf16[1024,2304]{1,0:T(8,128)(2,1)}, bf16[1024,1152]{1,0:T(8,128)(2,1)}, f32[2,512,128]{2,1,0:T(8,128)}, f32[2,512,128]{2,1,0:T(8,128)}) custom-call(s32[1]{0:T(128)} %bitcast.13.group_ref, s32[4,16,512]{2,1,0:T(8,128)} %get-tuple-element.94.codes_ref, bf16[4,512,2048]{2,1,0:T(8,128)(2,1)} %get-tuple-element.95.rows_ref.norm_hbm, ...), custom_call_target="tpu_custom_call" | custom-call | flops 14495514624 | bytes 22544384 | tf_op jit(solution)/shard_map/pallas_call | solution.py:358
  260.1 9.0 %shard_map.291 = (bf16[512,2048]{1,0:T(8,128)(2,1)}, bf16[512,2048]{1,0:T(8,128)(2,1)}) custom-call(bf16[1024,1152]{1,0:T(8,128)(2,1)} %get-tuple-element.124.left_ref.left_b, bf16[1152,2048]{1,0:T(8,128)(2,1)} %bitcast.64), custom_call_target="tpu_custom_call" | custom-call | flops 4831838208 | bytes 11272192 | tf_op jit(solution)/shard_map/pallas_call | solution.py:400
  269.1 0.4 collective-permute-start
  269.4 14.4 %shard_map.292 = (bf16[512,2048]{1,0:T(8,128)(2,1)}, bf16[512,2048]{1,0:T(8,128)(2,1)}) custom-call(bf16[1024,2304]{1,0:T(8,128)(2,1)} %get-tuple-element.104.left_ref.left_b, bf16[2304,2048]{1,0:T(8,128)(2,1)} %bitcast.58), custom_call_target="tpu_custom_call" | custom-call | flops 9663676416 | bytes 18350080 | tf_op jit(solution)/shard_map/pallas_call | solution.py:400
  284.0 0.4 collective-permute-start.2
  284.4 3.7 collective-permute-done.2
  288.2 2.1 collective-permute-start.3
  290.3 4.5 add_convert_fusion.1
  295.0 2.1 add_convert_fusion
  297.1 1.9 collective-permute-start.11
  299.0 28.9 %shard_map.293 = (bf16[1024,2304]{1,0:T(8,128)(2,1)}, bf16[1024,1152]{1,0:T(8,128)(2,1)}, f32[2,512,128]{2,1,0:T(8,128)}, f32[2,512,128]{2,1,0:T(8,128)}) custom-call(s32[1]{0:T(128)} %bitcast.13.group_ref, s32[4,16,512]{2,1,0:T(8,128)} %get-tuple-element.94.codes_ref, bf16[4,512,2048]{2,1,0:T(8,128)(2,1)} %get-tuple-element.95.rows_ref.norm_hbm, ...), custom_call_target="tpu_custom_call" | custom-call | flops 14495514624 | bytes 22544384 | tf_op jit(solution)/shard_map/pallas_call | solution.py:358
  327.8 9.1 %shard_map.294 = (bf16[512,2048]{1,0:T(8,128)(2,1)}, bf16[512,2048]{1,0:T(8,128)(2,1)}) custom-call(bf16[1024,1152]{1,0:T(8,128)(2,1)} %get-tuple-element.110.left_ref.left_a, bf16[1152,2048]{1,0:T(8,128)(2,1)} %bitcast.66), custom_call_target="tpu_custom_call" | custom-call | flops 4831838208 | bytes 11272192 | tf_op jit(solution)/shard_map/pallas_call | solution.py:400
  336.9 25.6 %shard_map.295 = (bf16[8,3,352,256]{3,2,1,0:T(8,128)(2,1)}, bf16[8,3,352,256]{3,2,1,0:T(8,128)(2,1)}) custom-call(bf16[1024,2304]{1,0:T(8,128)(2,1)} %get-tuple-element.120.left_a.left_ref, bf16[1024,2304]{1,0:T(8,128)(2,1)} %get-tuple-element.104.left_ref.left_b, bf16[2,1024,2048]{2,1,0:T(8,128)(2,1)} %bitcast.38, bf16[2,1024,2048]{2,1,0:T(8,128)(2,1)} %bitcast.39), custom_call_target="tpu_custom_call" | custom-call | flops 19327352832 | bytes 45088768 | tf_op jit(solution)/shard_map/pallas_call | solution.py:437
  362.6 3.1 constant_dynamic-slice_fusion.1
  365.6 14.5 %shard_map.296 = (bf16[512,2048]{1,0:T(8,128)(2,1)}, bf16[512,2048]{1,0:T(8,128)(2,1)}) custom-call(bf16[1024,2304]{1,0:T(8,128)(2,1)} %get-tuple-element.120.left_a.left_ref, bf16[2304,2048]{1,0:T(8,128)(2,1)} %bitcast.60), custom_call_target="tpu_custom_call" | custom-call | flops 9663676416 | bytes 18350080 | tf_op jit(solution)/shard_map/pallas_call | solution.py:400
  380.2 0.5 collective-permute-start.10
  380.7 2.8 convert_add_fusion
  383.5 2.0 copy-done
  385.8 0.7 copy-done.6
  386.5 0.7 fusion.3
  387.3 0.6 dynamic-slice_bitcast_fusion.probs_mine_ref
  388.0 1.1 collective-permute-done.9
  389.0 0.9 pad_maximum_fusion.terms_ref
  389.9 3.1 collective-permute-start.8
  393.0 9.4 %collective-permute-done.6 = bf16[128,2048]{1,0:T(8,128)(2,1)S(1)} collective-permute-done((bf16[128,2048]{1,0:T(8,128)(2,1)S(1)}, bf16[128,2048]{1,0:T(8,128)(2,1)S(1)}, u32[]{:S(2)}, u32[]{:S(2)}) %collective-permute-start.6) | collective-permute-done | bytes 524320 | tf_op jit(solution)/shard_map/ppermute | solution.py:2078
  402.4 17.5 %shard_map.297.down_ref = bf16[8,3,352,256]{3,2,1,0:T(8,128)(2,1)} custom-call(bf16[1024,1152]{1,0:T(8,128)(2,1)} %get-tuple-element.110.left_ref.left_a, bf16[1024,1152]{1,0:T(8,128)(2,1)} %get-tuple-element.124.left_ref.left_b, bf16[2,1024,2048]{2,1,0:T(8,128)(2,1)} %bitcast.61, bf16[2,1024,2048]{2,1,0:T(8,128)(2,1)} %bitcast.62), custom_call_target="tpu_custom_call" | custom-call | flops 9663676416 | bytes 30932992 | tf_op jit(solution)/shard_map/pallas_call | solution.py:437
  419.9 15.2 %collective-permute-done.7 = bf16[128,2048]{1,0:T(8,128)(2,1)S(1)} collective-permute-done((bf16[128,2048]{1,0:T(8,128)(2,1)S(1)}, bf16[128,2048]{1,0:T(8,128)(2,1)S(1)}, u32[]{:S(2)}, u32[]{:S(2)}) %collective-permute-start.7) | collective-permute-done | bytes 524320 | tf_op jit(solution)/shard_map/ppermute | solution.py:2078
  435.1 2.4 add_convert_fusion.2
  437.5 172.1 %shard_map.298 = (bf16[128,2048]{1,0:T(8,128)(2,1)}, bf16[4,3,352,256]{3,2,1,0:T(8,128)(2,1)}, bf16[4,3,352,256]{3,2,1,0:T(8,128)(2,1)}, bf16[4,3,352,256]{3,2,1...) custom-call(f32[3,512,128]{2,1,0:T(8,128)} %pad_maximum_fusion.terms_ref, ...), custom_call_target="tpu_custom_call" | custom-call | tf_op jit(solution)/shard_map/pallas_call | solution.py:1411
  609.6 0.7 slice.69
  610.3 1.3 slice_bitcast_fusion.2
  611.6 0.7 slice.68
  612.3 0.6 constant_dynamic-slice_fusion
  613.0 0.6 copy.42
  613.6 10.3 %shard_map.299 = (f32[8,352,256]{2,1,0:T(8,128)}, f32[8,352,256]{2,1,0:T(8,128)}, f32[8,352,256]{2,1,0:T(8,128)}, f32[256,1408]{1,0:T(8,128)}, f32[256,1408]{1,0...) custom-call(bf16[4,3,352,256]{3,2,1,0:T(8,128)(2,1)} %get-tuple-elem, ...), custom_call_target="tpu_custom_call" | custom-call | bytes 19464192 | tf_op jit(solution)/shard_map/pallas_call | solution.py:1499
  624.0 0.8 copy.48
  (46 shorter events, 1.3 us)
Async XLA Ops:
  0.6 7.7 %copy-start.4 = (bf16[256,1408]{1,0:T(8,128)(2,1)S(1)}, bf16[256,1408]{1,0:T(8,128)(2,1)}, u32[]{:S(2)}) copy-start(bf16[256,1408]{1,0:T(8,128)(2,1)} %param.34) | copy-start | bytes 2162692
  10.9 1.4 copy-start.10
  11.3 1.0 copy-start.9
  269.1 21.2 %collective-permute-start = (bf16[512,2048]{1,0:T(8,128)(2,1)}, bf16[512,2048]{1,0:T(8,128)(2,1)}, u32[]{:S(2)}, u32[]{:S(2)}) collective-permute-start(bf16[512,2048]{1,0:T(8,128)(2,1)} %get-tuple-element.102), channel_id=1, source_target_pairs={{0,4},{4,0},{8,12},{12,8},{16,20},{20,16},{24,28},{28,24},{1,5},{5... | collective-permute-start | bytes 6291464 | tf_op jit(solution)/shard_map/ppermute | solution.py:1986
  269.4 14.5 %copy-start.5 = (f32[2,512,128]{2,1,0:T(8,128)S(1)}, f32[2,512,128]{2,1,0:T(8,128)}, u32[]{:S(2)}) copy-start(f32[2,512,128]{2,1,0:T(8,128)} %get-tuple-element.109) | copy-start | bytes 1572868
  283.8 11.1 %collective-permute-start.1 = (bf16[512,2048]{1,0:T(8,128)(2,1)}, bf16[512,2048]{1,0:T(8,128)(2,1)S(1)}, u32[]{:S(2)}, u32[]{:S(2)}) collective-permute-start(bf16[512,2048]{1,0:T(8,128)(2,1)} %get-tuple-element.108), channel_id=1, source_target_pairs={{0,4},{4,0},{8,12},{12,8},{16,20},{20,16},{24,28},{28,24},{1,5},{5... | collective-permute-start | bytes 6291464 | tf_op jit(solution)/shard_map/ppermute | solution.py:1986
  284.0 4.1 collective-permute-start.2
  288.2 6.8 %copy-start.2 = (bf16[512,2048]{1,0:T(8,128)(2,1)S(1)}, bf16[512,2048]{1,0:T(8,128)(2,1)}, u32[]{:S(2)}) copy-start(bf16[512,2048]{1,0:T(8,128)(2,1)} %get-tuple-element.105) | copy-start | bytes 6291460
  288.2 39.6 %collective-permute-start.3 = (f32[512,128]{1,0:T(8,128)S(1)}, f32[512,128]{1,0:T(8,128)S(1)}, u32[]{:S(2)}, u32[]{:S(2)}) collective-permute-start(f32[512,128]{1,0:T(8,128)S(1)} %bitcast_add_fusion), channel_id=1, source_target_pairs={{0,8},{4,12},{8,0},{12,4},{16,24},{20,28},{24,16},{28,20},{1,9},{5... | collective-permute-start | bytes 786440 | tf_op jit(solution)/shard_map/ppermute | solution.py:1986
  294.8 85.9 %collective-permute-start.5 = (bf16[512,2048]{1,0:T(8,128)(2,1)}, bf16[512,2048]{1,0:T(8,128)(2,1)S(1)}, u32[]{:S(2)}, u32[]{:S(2)}) collective-permute-start(bf16[512,2048]{1,0:T(8,128)(2,1)} %add_convert_fusion.1), channel_id=1, source_target_pairs={{0,8},{4,12},{8,0},{12,4},{16,24},{20,28},{24,16},{28,20},{1,9},{5... | collective-permute-start | bytes 6291464 | tf_op jit(solution)/shard_map/ppermute | solution.py:1986
  297.1 140.4 %collective-permute-start.11 = (bf16[512,2048]{1,0:T(8,128)(2,1)}, bf16[512,2048]{1,0:T(8,128)(2,1)}, u32[]{:S(2)}, u32[]{:S(2)}) collective-permute-start(bf16[512,2048]{1,0:T(8,128)(2,1)} %add_convert_fusion), channel_id=1, source_target_pairs={{0,8},{4,12},{8,0},{12,4},{16,24},{20,28},{24,16},{28,20},{1,9},{5... | collective-permute-start | bytes 6291464 | tf_op jit(solution)/shard_map/ppermute | solution.py:1986
  336.9 43.8 %collective-permute-start.4 = (bf16[512,2048]{1,0:T(8,128)(2,1)}, bf16[512,2048]{1,0:T(8,128)(2,1)}, u32[]{:S(2)}, u32[]{:S(2)}) collective-permute-start(bf16[512,2048]{1,0:T(8,128)(2,1)} %get-tuple-element.112), channel_id=1, source_target_pairs={{0,4},{4,0},{8,12},{12,8},{16,20},{20,16},{24,28},{28,24},{1,5},{5... | collective-permute-start | bytes 6291464 | tf_op jit(solution)/shard_map/ppermute | solution.py:1986
  365.6 15.0 %copy-start.3 = (bf16[512,2048]{1,0:T(8,128)(2,1)S(1)}, bf16[512,2048]{1,0:T(8,128)(2,1)}, u32[]{:S(2)}) copy-start(bf16[512,2048]{1,0:T(8,128)(2,1)} %get-tuple-element.111) | copy-start | bytes 6291460
  365.6 71.9 %collective-permute-start.12 = (bf16[4,3,352,256]{3,2,1,0:T(8,128)(2,1)}, bf16[4,3,352,256]{3,2,1,0:T(8,128)(2,1)}, u32[]{:S(2)}, u32[]{:S(2)}) collective-permute-start(bf16[4,3,352,256]{3,2,1,0:T(8,128)(2,1)} %constant_dynamic-slice_fusion.1), channel_id=1, source_target_pairs={{0,16},{4,20},{8,24},{12,28},{16,0},{20,4},{24,8},{28,12},{1,17},{... | collective-permute-start | bytes 6488072 | tf_op jit(solution)/shard_map/ppermute | solution.py:1986
  380.2 57.3 %collective-permute-start.10 = (bf16[512,2048]{1,0:T(8,128)(2,1)}, bf16[512,2048]{1,0:T(8,128)(2,1)}, u32[]{:S(2)}, u32[]{:S(2)}) collective-permute-start(bf16[512,2048]{1,0:T(8,128)(2,1)} %get-tuple-element.122), channel_id=1, source_target_pairs={{0,4},{4,0},{8,12},{12,8},{16,20},{20,16},{24,28},{28,24},{1,5},{5... | collective-permute-start | bytes 6291464 | tf_op jit(solution)/shard_map/ppermute | solution.py:1986
  383.5 2.0 copy-start
  385.5 1.0 copy-start.6
  385.5 1.8 copy-start.8
  385.7 16.7 %collective-permute-start.6 = (bf16[128,2048]{1,0:T(8,128)(2,1)S(1)}, bf16[128,2048]{1,0:T(8,128)(2,1)S(1)}, u32[]{:S(2)}, u32[]{:S(2)}) collective-permute-start(bf16[128,2048]{1,0:T(8,128)(2,1)S(1)} %get-tuple-element.147), channel_id=1, source_target_pairs={{0,1},{1,2},{2,3},{3,0},{4,5},{5,6},{6,7},{7,4},{8,9},{9,10},{10,1... | collective-permute-start | bytes 1572872 | tf_op jit(solution)/shard_map/ppermute | solution.py:2078
  387.3 1.7 collective-permute-start.9
  389.9 30.0 %collective-permute-start.8 = (bf16[128,2048]{1,0:T(8,128)(2,1)S(1)}, bf16[128,2048]{1,0:T(8,128)(2,1)S(1)}, u32[]{:S(2)}, u32[]{:S(2)}) collective-permute-start(bf16[128,2048]{1,0:T(8,128)(2,1)S(1)} %get-tuple-element.148), channel_id=1, source_target_pairs={{0,3},{1,0},{2,1},{3,2},{4,7},{5,4},{6,5},{7,6},{8,11},{9,8},{10,9... | collective-permute-start | bytes 1572872 | tf_op jit(solution)/shard_map/ppermute | solution.py:2078
  402.4 32.7 %collective-permute-start.7 = (bf16[128,2048]{1,0:T(8,128)(2,1)S(1)}, bf16[128,2048]{1,0:T(8,128)(2,1)S(1)}, u32[]{:S(2)}, u32[]{:S(2)}) collective-permute-start(bf16[128,2048]{1,0:T(8,128)(2,1)S(1)} %get-tuple-element.149), channel_id=1, source_target_pairs={{0,2},{1,3},{2,0},{3,1},{4,6},{5,7},{6,4},{7,5},{8,10},{9,11},{10,... | collective-permute-start | bytes 1572872 | tf_op jit(solution)/shard_map/ppermute | solution.py:2078
  402.4 32.7 %copy-start.1 = (f32[128,2048]{1,0:T(8,128)S(1)}, f32[128,2048]{1,0:T(8,128)}, u32[]{:S(2)}) copy-start(f32[128,2048]{1,0:T(8,128)} %get-tuple-element.93.hidden_ref) | copy-start | bytes 3145732
  613.6 10.3 %copy-start.7 = (bf16[128,2048]{1,0:T(8,128)(2,1)S(1)}, bf16[128,2048]{1,0:T(8,128)(2,1)}, u32[]{:S(2)}) copy-start(bf16[128,2048]{1,0:T(8,128)(2,1)} %get-tuple-element.173) | copy-start | bytes 1572868

commit v7 on v6

--- a/solution.py
+++ b/solution.py
@@ -271,178 +271,6 @@
         4 * units * rows * wide * width,
         units * rows * (wide + width) * 4,
     )(left_a, right_a, left_b, right_b)
-
-
-def act_body(
-    experts,
-    top_count,
-    group_ref,
-    codes_ref,
-    rows_ref,
-    grads_ref,
-    router_ref,
-    gateup_ref,
-    down_ref,
-    pair_ref,
-    act_ref,
-    terms_ref,
-    probs_ref,
-    weights,
-    routed,
-):
-    unit, units = pl.program_id(0), pl.num_programs(0)
-    half = gateup_ref.shape[1] // 2
-    count, seq_len, width = rows_ref.shape
-    data = rows_ref[...].reshape(count * seq_len, width)
-    cot = grads_ref[...].reshape(count * seq_len, width)
-    lane = lax.broadcasted_iota(jnp.int32, weights.shape, 1)
-
-    @pl.when(unit == 0)
-    def _():
-        logits = dot(data, router_ref[...], 1, 1)
-        chosen = jnp.where(lane < experts, logits, -1e30)
-        raised = jnp.exp(chosen - jnp.max(chosen, axis=1, keepdims=True))
-        soft = raised / jnp.sum(raised, axis=1, keepdims=True)
-        probs = jnp.where(lane < experts, soft, jax.nn.sigmoid(logits))
-        for s in range(count):
-            codes = codes_ref[s]
-            row = lax.broadcasted_iota(jnp.int32, codes.shape, 0)
-            named = row == experts
-            for k in range(top_count):
-                named = jnp.logical_or(named, codes[k : k + 1] == row)
-            named = jnp.logical_and(named, row <= experts).astype(F32).astype(BF)
-            place = (codes.shape[0], weights.shape[1])
-            same = lax.broadcasted_iota(jnp.int32, place, 0) == lax.broadcasted_iota(
-                jnp.int32, place, 1
-            )
-            at = slice(s * seq_len, (s + 1) * seq_len)
-            routed[at] = dot(named, same.astype(F32).astype(BF), 0, 0)
-            probs_ref[s] = probs[at]
-        weights[...] = probs * routed[...]
-        terms_ref[...] = jnp.zeros_like(terms_ref)
-
-    mine = lane == jnp.where(unit < units - 1, group_ref[0] * (units - 1) + unit, experts)
-    weight = jnp.sum(jnp.where(mine, weights[...], 0.0), axis=1, keepdims=True)
-    both = dot(data, gateup_ref[0], 1, 1)
-    cot_in = dot(cot, down_ref[0], 1, 1)
-    gate_in, up_in = both[:, :half], both[:, half:]
-    gate_act, gate_slope = silu_parts(gate_in)
-    act = gate_act * up_in
-    inner = jnp.sum(act.astype(BF).astype(F32) * cot_in, axis=1, keepdims=True)
-    cot_in = cot_in * weight
-    act_ref[...] = (act * weight).astype(BF)
-    pair_ref[:, :half] = (cot_in * up_in * gate_slope).astype(BF)
-    pair_ref[:, half:] = (cot_in * gate_act).astype(BF)
-    terms_ref[...] += jnp.where(mine, inner * routed[...], 0.0).reshape(terms_ref.shape)
-
-
-def act_call(experts, top_count, chunk, group, codes, rows, grads, router, gateup, down):
-    _, seq_len, width = rows.shape
-    units, wide, _ = gateup.shape
-    half, count = wide // 2, 2
-    total = count * seq_len
-
-    def part(*shape):
-        return pl.BlockSpec(
-            shape,
-            lambda u: (chunk,) + (0,) * (len(shape) - 1),
-            pipeline_mode=pl.Buffered(1),
-        )
-
-    def unit(u):
-        return (u, 0, 0)
-
-    def whole(u):
-        return (0, 0, 0)
-
-    return call(
-        functools.partial(act_body, experts, top_count),
-        (units,),
-        [
-            pl.BlockSpec(memory_space=pltpu.SMEM),
-            part(count, codes.shape[1], seq_len),
-            part(count, seq_len, width),
-            part(count, seq_len, width),
-            pl.BlockSpec(router.shape, lambda u: (0, 0)),
-            pl.BlockSpec((1, wide, width), unit),
-            pl.BlockSpec((1, half, width), unit),
-        ],
-        [
-            pl.BlockSpec((total, wide), lambda u: (0, u)),
-            pl.BlockSpec((total, half), lambda u: (0, u)),
-            pl.BlockSpec((count, seq_len, 128), whole),
-            pl.BlockSpec((count, seq_len, 128), whole),
-        ],
-        [
-            jax.ShapeDtypeStruct((total, units * wide), BF),
-            jax.ShapeDtypeStruct((total, units * half), BF),
-            jax.ShapeDtypeStruct((count, seq_len, 128), F32),
-            jax.ShapeDtypeStruct((count, seq_len, 128), F32),
-        ],
-        2 * total * units * 3 * half * width,
-        4 * total * width + units * 3 * half * width * 2,
-        [pltpu.VMEM((total, 128), F32), pltpu.VMEM((total, 128), F32)],
-    )(group, codes, rows, grads, router, gateup, down)
-
-
-def back_body(left_ref, weight_ref, *out_refs):
-    seq_len = out_refs[0].shape[0]
-    total = dot(left_ref[...], weight_ref[...]).astype(BF)
-    for s, out_ref in enumerate(out_refs):
-        out_ref[...] = total[s * seq_len : (s + 1) * seq_len]
-
-
-def back_call(left, weight):
-    units, wide, width = weight.shape
-    weight = weight.reshape(units * wide, width)
-    total, depth = left.shape
-    block = min(width, 512)
-    return call(
-        back_body,
-        (width // block,),
-        [
-            pl.BlockSpec((total, depth), lambda j: (0, 0), pipeline_mode=pl.Buffered(1)),
-            pl.BlockSpec((depth, block), lambda j: (0, j)),
-        ],
-        [pl.BlockSpec((total // 2, block), lambda j: (0, j))] * 2,
-        [jax.ShapeDtypeStruct((total // 2, width), BF)] * 2,
-        2 * total * depth * width,
-        (total * depth + depth * width + total * width) * 2,
-    )(left, weight)
-
-
-def units_body(keep, pad, left_a, left_b, right_a, right_b, *outs):
-    total = dot(left_a[...], right_a[0], 0, 0) + dot(left_b[...], right_b[0], 0, 0)
-    total = total.astype(BF)
-    for part, out_ref in enumerate(outs):
-        blocks, _, _, slice_width = out_ref.shape
-        for k in range(blocks):
-            out_ref[k, 0] = total[
-                part * pad : part * pad + keep, k * slice_width : (k + 1) * slice_width
-            ]
-
-
-def units_call(keep, pad, dp, units, left_a, left_b, right):
-    right = right.reshape(2, left_a.shape[0], -1)
-    total, width = right.shape[1:]
-    wide = left_a.shape[1] // units
-    slice_width = width // dp
-    blocks = max(1, 1024 // slice_width)
-    parts = wide // pad
-    left = pl.BlockSpec((total, wide), lambda u, j: (0, u))
-
-    def chunk(k):
-        return pl.BlockSpec((1, total, blocks * slice_width), lambda u, j: (k, 0, j))
-
-    return call(
-        functools.partial(units_body, keep, pad),
-        (units, dp // blocks),
-        [left, left, chunk(0), chunk(1)],
-        [pl.BlockSpec((blocks, 1, keep, slice_width), lambda u, j: (j, u, 0, 0))] * parts,
-        [jax.ShapeDtypeStruct((dp, units, keep, slice_width), BF)] * parts,
-        4 * total * units * wide * width,
-        (4 * total * width + 4 * total * units * wide + units * wide * width) * 2,
-    )(left_a, left_b, right, right)
 
 
 MESH = pl.DeviceIdType.MESH
@@ -1009,6 +837,324 @@
             collective_id=0, has_side_effects=True, vmem_limit_bytes=VMEM_LIMIT
         ),
     )(codes, misc, gains, cos_rows, sin_rows, *arrays, *units)
+
+
+def middle_body(
+    sizes,
+    hidden_ref,
+    codes_ref,
+    router_ref,
+    rows_ref,
+    grads_ref,
+    gateup_ref,
+    down_ref,
+    output_ref,
+    terms_out,
+    probs_out,
+    grad_own,
+    grad_sib,
+    grad_far,
+    gate_total,
+    up_total,
+    down_total,
+    gate_in,
+    wide_w,
+    down_w,
+    xs,
+    ys,
+    pair,
+    act,
+    outs,
+    backs,
+    near_in,
+    back_in,
+    far_in,
+    z_in,
+    stage,
+    weights,
+    routed,
+    probs,
+    terms,
+    terms_in,
+    send,
+    recv,
+    here,
+):
+    dp, depth, experts, top_count, keep = sizes
+    me, z = lax.axis_index("dp"), lax.axis_index("tensor")
+    y = me // 4
+    rows, width = output_ref.shape
+    seq_len = rows * depth
+    total = 2 * seq_len
+    units, wide, _ = wide_w.shape
+    half = wide // 2
+    slice_width = width // dp
+    sibling, beside, over = peer_of(me, 1), peer_of(me, 2), peer_of(me, 4)
+    c = Copies(send, recv, here)
+
+    greet(me, z, dp, depth)
+
+    def load(source, chunk, target):
+        copies = [
+            c.local(source.at[2 * chunk + s], target.at[pl.ds(s * seq_len, seq_len)])
+            for s in range(2)
+        ]
+        for copy in copies:
+            copy.start()
+        return copies
+
+    def wait(copies):
+        for copy in copies:
+            copy.wait()
+
+    loads = load(rows_ref, 1, xs)
+    first = [(c.local(gateup_ref.at[u], wide_w.at[u]), c.local(down_ref.at[u], down_w.at[u])) for u in range(units)]
+    first[0][0].start()
+    first[0][1].start()
+    loads += load(grads_ref, 1, ys)
+    for u in range(1, units):
+        first[u][0].start()
+        first[u][1].start()
+
+    block = seq_len // 2
+    lanes = weights.shape[1]
+
+    def gate_weights(chunk):
+        def step(i, carry):
+            at = pl.ds(pl.multiple_of(i * block, block), block)
+            logits = dot(xs[at, :], router_ref[...], 1, 1)
+            lane = lax.broadcasted_iota(jnp.int32, logits.shape, 1)
+            chosen = jnp.where(lane < experts, logits, -1e30)
+            raised = jnp.exp(chosen - jnp.max(chosen, axis=1, keepdims=True))
+            soft = raised / jnp.sum(raised, axis=1, keepdims=True)
+            probs[at, :] = jnp.where(lane < experts, soft, jax.nn.sigmoid(logits))
+            return carry
+
+        lax.fori_loop(0, total // block, step, 0)
+        for s in range(2):
+            codes = codes_ref[2 * chunk + s]
+            row = lax.broadcasted_iota(jnp.int32, codes.shape, 0)
+            named = row == experts
+            for k in range(top_count):
+                named = jnp.logical_or(named, codes[k : k + 1] == row)
+            named = jnp.logical_and(named, row <= experts).astype(F32).astype(BF)
+            place = (codes.shape[0], lanes)
+            same = lax.broadcasted_iota(jnp.int32, place, 0) == lax.broadcasted_iota(
+                jnp.int32, place, 1
+            )
+            routed[s * seq_len : (s + 1) * seq_len] = dot(named, same.astype(F32).astype(BF), 0, 0)
+        weights[...] = probs[...] * routed[...]
+
+    def activate(chunk):
+        for u in range(units):
+            if chunk == 1:
+                wait(first[u])
+            if u == 0:
+                gate_weights(chunk)
+            place = me % 4 * (units - 1) + u if u < units - 1 else experts
+
+            def step(i, carry, u=u, place=place):
+                at = pl.ds(pl.multiple_of(i * block, block), block)
+                mine = lax.broadcasted_iota(jnp.int32, (block, lanes), 1) == place
+                weight = jnp.sum(jnp.where(mine, weights[at, :], 0.0), axis=1, keepdims=True)
+                both = dot(xs[at, :], wide_w[u], 1, 1)
+                cot = dot(ys[at, :], down_w[u], 1, 1)
+                gate_act, gate_slope = silu_parts(both[:, :half])
+                value = gate_act * both[:, half:]
+                inner = jnp.sum(value * cot, axis=1, keepdims=True)
+                inner = jnp.where(mine, inner * routed[at, :], 0.0)
+                terms[chunk, at, :] = inner if u == 0 else terms[chunk, at, :] + inner
+                cot = cot * weight
+                act[chunk, at, u * half : (u + 1) * half] = (value * weight).astype(BF)
+                a = u * wide
+                pair[chunk, at, a : a + half] = (cot * both[:, half:] * gate_slope).astype(BF)
+                pair[chunk, at, a + half : a + wide] = (cot * gate_act).astype(BF)
+                return carry
+
+            lax.fori_loop(0, total // block, step, 0)
+
+    cols = 512
+
+    def back(left, chunk, s, weight, target):
+        at = slice(s * seq_len, (s + 1) * seq_len)
+        for j in range(width // cols):
+            part = weight[:, :, j * cols : (j + 1) * cols]
+            part = part.reshape(-1, cols)
+            target[:, j * cols : (j + 1) * cols] = dot(left[chunk, at, :], part).astype(BF)
+
+    def add_into(target, other):
+        def step(i, carry):
+            at = pl.ds(pl.multiple_of(i * rows, rows), rows)
+            target[at, :] = (target[at, :].astype(F32) + other[at, :].astype(F32)).astype(BF)
+            return carry
+
+        lax.fori_loop(0, depth, step, 0)
+
+    wait(loads)
+    activate(1)
+    loads = load(rows_ref, 0, xs) + load(grads_ref, 0, ys)
+    terms_near = c.remote(terms.at[1, pl.ds(seq_len, seq_len)], terms_in, dp=sibling)
+    terms_near.start()
+    back(act, 1, 1, down_w, outs.at[1])
+    out_near = c.remote(outs.at[1], near_in, dp=sibling)
+    out_near.start()
+    back(act, 1, 0, down_w, outs.at[0])
+    terms_near.wait()
+    terms[1, :seq_len] = terms[1, :seq_len] + terms_in[...]
+    terms_across = c.remote(terms.at[1, pl.ds(0, seq_len)], terms_out.at[2], dp=beside)
+    terms_across.start()
+    out_near.wait()
+    add_into(outs.at[0], near_in)
+    out_across = c.remote(outs.at[0], far_in, dp=beside)
+    out_across.start()
+    back(pair, 1, 1, wide_w, outs.at[1])
+    grad_near = c.remote(outs.at[1], back_in, dp=sibling)
+    grad_near.start()
+    back(pair, 1, 0, wide_w, backs)
+    grad_near.wait()
+    add_into(backs, back_in)
+    grad_across = c.remote(backs, grad_far, dp=beside)
+    grad_across.start()
+
+    wait(loads)
+    activate(0)
+    probs_out[...] = probs[pl.ds(pl.multiple_of(z * rows, rows), rows), :]
+    loads = load(rows_ref, 1, ys)
+    terms_out[0] = terms[0, :seq_len]
+    terms_last = c.remote(terms.at[0, pl.ds(seq_len, seq_len)], terms_out.at[1], dp=sibling)
+    terms_last.start()
+    back(act, 0, 1, down_w, outs.at[1])
+    out_last = c.remote(outs.at[1], near_in, dp=sibling)
+    out_last.start()
+    back(act, 0, 0, down_w, back_in)
+
+    staged, moved = [None, None], []
+    blocks = stage.shape[2]
+
+    def outer(left, parts, targets, u, j, slot):
+        at = slice(j * blocks * slice_width, (j + 1) * blocks * slice_width)
+        n = parts * half
+        value = dot(left[0, :, u * n : (u + 1) * n], xs[:, at], 0, 0)
+        value = (value + dot(left[1, :, u * n : (u + 1) * n], ys[:, at], 0, 0)).astype(BF)
+        if staged[slot] is not None:
+            wait(staged[slot])
+        copies = []
+        for k, target in enumerate(targets):
+            for b in range(blocks):
+                stage[slot, k, b] = value[
+                    k * half : k * half + keep, b * slice_width : (b + 1) * slice_width
+                ]
+            copies.append(c.local(stage.at[slot, k], target.at[pl.ds(j * blocks, blocks), u]))
+            copies[-1].start()
+        staged[slot] = copies
+
+    wait(loads)
+    steps = dp // blocks
+    scatter = []
+    over_copies = []
+    for u in range(units):
+        for j in range(steps):
+            outer(pair, 2, (gate_total, up_total), u, j, j % 2)
+        if u == 0:
+            out_last.wait()
+            out_across.wait()
+            for r in list(range(1, depth)) + [0]:
+                at = pl.ds(pl.multiple_of((z + r) % depth * rows, rows), rows)
+                part = back_in[at, :].astype(F32) + near_in[at, :].astype(F32)
+                part = part + far_in[at, :].astype(F32)
+                if r:
+                    back_in[at, :] = part.astype(BF)
+                    copy = c.remote(back_in.at[at], z_in.at[r - 1], tensor=(z + r) % depth)
+                    copy.start()
+                    scatter.append(copy)
+                else:
+                    near_in[at, :] = part.astype(BF)
+        for slot in range(2):
+            wait(staged[slot])
+            staged[slot] = None
+        source = gate_total.at[pl.ds((1 - y) * 4, 4), u]
+        over_copies.append(c.remote(source, gate_in.at[:, u], dp=over))
+        over_copies[-1].start()
+    loads = load(grads_ref, 0, xs) + load(grads_ref, 1, ys)
+
+    back(pair, 0, 1, wide_w, outs.at[1])
+    grad_last = c.remote(outs.at[1], grad_sib, dp=sibling)
+    grad_last.start()
+    back(pair, 0, 0, wide_w, outs.at[0])
+    grad_here = c.local(outs.at[0], grad_own)
+    grad_here.start()
+    wait(loads)
+    for u in range(units):
+        for j in range(steps):
+            outer(act, 1, (down_total,), u, j, j % 2)
+    for copy in scatter:
+        copy.wait_recv()
+    value = near_in[pl.ds(pl.multiple_of(z * rows, rows), rows), :].astype(F32)
+    value = value + hidden_ref[...]
+    for r in range(1, depth):
+        value = value + z_in[r - 1].astype(F32)
+    output_ref[...] = value.astype(BF)
+    for slot in range(2):
+        wait(staged[slot])
+    for copy in scatter:
+        copy.wait_send()
+    wait([grad_here, grad_last, terms_last, terms_across, grad_across] + over_copies)
+
+
+def middle_call(dp, depth, experts, top_count, hidden_units, hidden, codes, router, arrays):
+    rows, width = hidden.shape
+    seq_len = rows * depth
+    norm, grads, gateup, down = arrays
+    units, wide, _ = gateup.shape
+    half = wide // 2
+    slice_width = width // dp
+    blocks = max(1, 1024 // slice_width)
+    vmem, hbm = pl.BlockSpec(memory_space=pltpu.VMEM), pl.BlockSpec(memory_space=pl.ANY)
+    shape = jax.ShapeDtypeStruct
+    total = shape((dp, units, hidden_units, slice_width), BF)
+    return pl.pallas_call(
+        functools.partial(middle_body, (dp, depth, experts, top_count, hidden_units)),
+        in_specs=[vmem] * 3 + [hbm] * 4,
+        out_specs=[vmem] * 3 + [hbm] * 7,
+        out_shape=[
+            shape((rows, width), BF),
+            shape((3, seq_len, 128), F32),
+            shape((rows, 128), F32),
+            shape((seq_len, width), BF),
+            shape((seq_len, width), BF),
+            shape((seq_len, width), BF),
+            total,
+            total,
+            total,
+            shape((4, units, hidden_units, slice_width), BF),
+        ],
+        scratch_shapes=[
+            pltpu.VMEM((units, wide, width), BF),
+            pltpu.VMEM((units, half, width), BF),
+            pltpu.VMEM((2 * seq_len, width), BF),
+            pltpu.VMEM((2 * seq_len, width), BF),
+            pltpu.VMEM((2, 2 * seq_len, units * wide), BF),
+            pltpu.VMEM((2, 2 * seq_len, units * half), BF),
+            pltpu.VMEM((2, seq_len, width), BF),
+            pltpu.VMEM((seq_len, width), BF),
+            pltpu.VMEM((seq_len, width), BF),
+            pltpu.VMEM((seq_len, width), BF),
+            pltpu.VMEM((seq_len, width), BF),
+            pltpu.VMEM((depth - 1, rows, width), BF),
+            pltpu.VMEM((2, 2, blocks, hidden_units, slice_width), BF),
+            pltpu.VMEM((2 * seq_len, 128), F32),
+            pltpu.VMEM((2 * seq_len, 128), F32),
+            pltpu.VMEM((2 * seq_len, 128), F32),
+            pltpu.VMEM((2, 2 * seq_len, 128), F32),
+            pltpu.VMEM((seq_len, 128), F32),
+            pltpu.SemaphoreType.DMA((32,)),
+            pltpu.SemaphoreType.DMA((32,)),
+            pltpu.SemaphoreType.DMA((64,)),
+        ],
+        compiler_params=pltpu.CompilerParams(
+            collective_id=2, has_side_effects=True, vmem_limit_bytes=63 * 2**20
+        ),
+    )(hidden, codes, router, norm, grads, gateup, down)
 
 
 def backward_body(
@@ -1969,8 +2115,6 @@
     local_rows = tokens.shape[0]
     width = tokens.shape[1]
     experts, slice_width, hidden_units = expert_gate.shape
-    top_count = routes.shape[1]
-    capacity = 5 * seq_len * top_count // (4 * experts)
     heads_local = qkv_bias.shape[1]
     head_width = w_query.shape[1] // heads_local
     pair_heads = heads_local // 2
@@ -1978,13 +2122,7 @@
     mine_experts = experts // 4
     hidden_pad = -(-hidden_units // 128) * 128
 
-    me = lax.axis_index("dp")
     zi = lax.axis_index("tensor")
-    core, xi = me % 2, (me // 2) % 2
-    group = me % 4
-    def swap(array, bit):
-        return lax.ppermute(array, "dp", [(i, i ^ bit) for i in range(dp)])
-
     codes = jnp.concatenate([routes.T, slot_order.T, picture_ids[None]], axis=0)
     codes = jnp.pad(codes, ((0, 16 - codes.shape[0]), (0, 0)))
     bias_cores = qkv_bias.reshape(3, 2, -1).swapaxes(0, 1).reshape(2, -1)
@@ -2032,63 +2170,35 @@
     )
     gateup_all = gateup_all.reshape(mine_experts + 1, 2 * hidden_pad, width)
     down_all = down_all.reshape(mine_experts + 1, hidden_pad, width)
-    group_ids = group.astype(jnp.int32).reshape(1)
-
-    def feed(chunk, group_in):
-        return act_call(
-            experts,
-            top_count,
-            chunk,
-            group_in,
-            codes_all,
-            norm_all,
-            grads_all,
-            router_rows,
-            gateup_all,
-            down_all,
-        )
-
-    def across(own, sibling):
-        total = own.astype(F32) + swap(sibling, 1).astype(F32)
-        return total.astype(own.dtype)
-
-    units = mine_experts + 1
-    pair_b, act_b, terms_b, _ = feed(1, group_ids)
-    out_b = back_call(act_b, down_all)
-    grad_b = back_call(after(pair_b, out_b[0]), gateup_all)
-    out_far = across(*out_b)
-    pair_a, act_a, terms_a, probs_out = feed(0, after(group_ids, out_far, grad_b[0]))
-    grad_far = across(*grad_b)
-    terms_far = swap(across(terms_b[0], terms_b[1]), 2)
-    out_a = back_call(after(act_a, grad_far, terms_far), down_all)
-    gate_total, up_total = units_call(
-        hidden_units, hidden_pad, dp, units, after(pair_a, out_a[0]), pair_b, norm_all
-    )
-    gate_sent = lax.dynamic_slice_in_dim(gate_total, (1 - me // 4) * 4, 4, 0)
-    gate_in = swap(gate_sent, 4)
-    out_sum = out_a[0].astype(F32) + swap(out_a[1], 1).astype(F32) + swap(out_far, 2).astype(F32)
-    grad_a = back_call(after(pair_a, gate_sent), gateup_all)
-    (down_total,) = units_call(
-        hidden_units, hidden_pad, dp, units, act_a, after(act_b, grad_a[0], out_sum), grads_all
-    )
-    output = hidden + lax.dynamic_slice_in_dim(out_sum, zi * local_rows, local_rows, 0)
-    for r in range(1, depth):
-        start = (zi + r) % depth * local_rows
-        sent = lax.dynamic_slice_in_dim(out_sum, start, local_rows, 0).astype(BF)
-        moved = lax.ppermute(sent, "tensor", [(i, (i + r) % depth) for i in range(depth)])
-        output = output + moved.astype(F32)
-    output = output.astype(BF)
-    grad_parts = (grad_a[0], swap(grad_a[1], 1), swap(grad_far, 2))
-    terms = jnp.stack([terms_a[0], swap(terms_a[1], 1), terms_far])
-    probs_mine = lax.dynamic_slice_in_dim(probs_out[0], zi * local_rows, local_rows, 0)
+    (
+        output,
+        terms,
+        probs_mine,
+        grad_own,
+        grad_sib,
+        grad_far,
+        gate_total,
+        up_total,
+        down_total,
+        gate_in,
+    ) = middle_call(
+        dp,
+        depth,
+        experts,
+        routes.shape[1],
+        hidden_units,
+        hidden,
+        codes_all,
+        router_rows,
+        (norm_all, grads_all, gateup_all, down_all),
+    )
     input_grad, gate_sum, up_sum, down_sum, attn_sum, misc_sum, gains_sum = backward_call(
         dp,
         depth,
         experts,
         head_width,
-        (after(terms, output), probs_mine, router_rows, gain_rows, cos_rows, sin_rows, hidden, out_grad),
-        grad_parts
-        + (gate_in, gate_total, up_total, down_total)
+        (terms, probs_mine, router_rows, gain_rows, cos_rows, sin_rows, hidden, out_grad),
+        (grad_own, grad_sib, grad_far, gate_in, gate_total, up_total, down_total)
         + (tok, attn_weights, qkv, probs_low, heads_out, norm_all),
     )
 

time: 634 us -> 567 us (0.89)
  waiting for transfers between devices: 29.4 us -> 0 us
  other arithmetic: 16.9 us -> 4.17 us
  starting transfers between devices: 8.75 us -> 0 us
  local copies, waits for them, and re-layouts: 19.7 us -> 12.8 us
    ppermute x13 -> x0, waiting for transfers between devices: 29.4 us -> none  [the longest x3 24.6 us: local_fused(): lax.ppermute(sent, 'tensor', [(i, (i + r) % depth) for i in range(depth)])]
    convert_element_type x3 -> x0, other arithmetic: 8.98 us -> none  [the longest x2 6.62 us: across(): return total.astype(own.dtype)]
    ppermute x13 -> x0, starting transfers between devices: 8.75 us -> none  [the longest x10 5.62 us: swap(): return lax.ppermute(array, 'dp', [(i, i ^ bit) for i in range(dp)])]
    pallas_call x8 -> x1, Pallas kernels: 148 us -> 142 us  [middle_call(): pl.pallas_call(functools.partial(middle_body, (dp, depth, experts, top_co...]
  transfers between devices with their start and end apart: 13 -> 0, of which waited for: 4 -> 0; matrix products, arithmetic and copies ran while one was open for 3% -> 0% of each run, Pallas kernels for 18% -> 0%
where the time goes in v7:
time: 567 us; the launch traced here: 562 us
  Pallas kernels  544 us (96%)
  local copies, waits for them, and re-layouts  12.8 us (2%)
    pallas_call x1, Pallas kernels, forward_call(): pl.pallas_call(functools.partial(forward_body, (dp, depth, experts, hidde...  219 us
    pallas_call x1, Pallas kernels, backward_call(): pl.pallas_call(functools.partial(backward_body, (dp, depth, experts, head...  173 us
    pallas_call x1, Pallas kernels, middle_call(): pl.pallas_call(functools.partial(middle_body, (dp, depth, experts, top_co...  142 us

profile of v7, /device:TPU:0, one launch (start us, length us, event | category | flops | bytes accessed | tf_op | source)
XLA Modules:
  0.0 562.0 jit_solution(10032565202424654904)
XLA Ops:
  0.6 0.0 copy-start
  0.7 0.7 convert_element_type.24
  1.4 0.8 reshape.129
  2.2 0.1 reshape.128
  2.3 0.3 dynamic_update_slice.3.gains_ref
  2.6 0.0 copy-start.4
  2.6 0.7 pad_convert_fusion
  3.3 0.2 scatter.14.misc_ref
  3.5 0.0 copy-start.3
  3.5 0.7 pad_add_fusion
  4.3 0.6 pad.12.codes_ref
  4.9 1.8 copy.39
  6.7 2.2 copy.40
  9.0 0.0 copy-done
  9.0 1.1 copy.41
  10.1 1.0 fusion.2
  11.1 0.0 copy-done.4
  11.1 1.0 pad_maximum_fusion
  12.1 0.0 copy-done.3
  12.1 218.6 %shard_map.289 = (f32[128,2048]{1,0:T(8,128)}, bf16[4,512,2048]{2,1,0:T(8,128)(2,1)}, bf16[4,512,2048]{2,1,0:T(8,128)(2,1)}, bf16[3,2,384,2048]{3,2,1,0:T(8,128)...) custom-call(s32[16,512]{1,0:T(8,128)} %pad.12.codes_ref, ...), custom_call_target="tpu_custom_call" | custom-call | tf_op jit(solution)/shard_map/pallas_call | solution.py:799
  230.7 141.5 %shard_map.290 = (bf16[128,2048]{1,0:T(8,128)(2,1)}, f32[3,512,128]{2,1,0:T(8,128)}, f32[128,128]{1,0:T(8,128)}, bf16[512,2048]{1,0:T(8,128)(2,1)}, bf16[512,204...) custom-call(f32[128,2048]{1,0:T(8,128)} %get-tuple-element.79.hidden, ...), custom_call_target="tpu_custom_call" | custom-call | tf_op jit(solution)/shard_map/pallas_call | solution.py:1115
  372.3 173.5 %shard_map.291 = (bf16[128,2048]{1,0:T(8,128)(2,1)}, bf16[4,3,352,256]{3,2,1,0:T(8,128)(2,1)}, bf16[4,3,352,256]{3,2,1,0:T(8,128)(2,1)}, bf16[4,3,352,256]{3,2,1...) custom-call(f32[3,512,128]{2,1,0:T(8,128)} %get-tuple-element.87.terms_ref, ...), custom_call_target="tpu_custom_call" | custom-call | tf_op jit(solution)/shard_map/pallas_call | solution.py:1557
  545.7 0.7 slice.49
  546.4 1.3 slice_bitcast_fusion
  547.8 0.7 slice.48
  548.5 0.6 constant_dynamic-slice_fusion
  549.1 0.1 reshape.126
  549.2 0.6 copy.42
  549.8 0.0 copy-start.1
  549.8 0.0 copy-start.2
  549.8 10.3 %shard_map.292 = (f32[8,352,256]{2,1,0:T(8,128)}, f32[8,352,256]{2,1,0:T(8,128)}, f32[8,352,256]{2,1,0:T(8,128)}, f32[256,1408]{1,0:T(8,128)}, f32[256,1408]{1,0...) custom-call(bf16[4,3,352,256]{3,2,1,0:T(8,128)(2,1)} %get-tuple-elem, ...), custom_call_target="tpu_custom_call" | custom-call | bytes 19464192 | tf_op jit(solution)/shard_map/pallas_call | solution.py:1645
  560.1 0.0 copy-done.1
  560.1 0.8 copy.49
  560.9 0.0 copy-done.2
  560.9 0.8 copy.50
  (3 shorter events, 0.0 us)
Async XLA Ops:
  0.6 8.3 %copy-start = (bf16[256,1408]{1,0:T(8,128)(2,1)S(1)}, bf16[256,1408]{1,0:T(8,128)(2,1)}, u32[]{:S(2)}) copy-start(bf16[256,1408]{1,0:T(8,128)(2,1)} %param.34) | copy-start | bytes 2162692
  2.6 8.5 %copy-start.4 = (f32[8,256]{1,0:T(8,128)}, f32[8,256]{1,0:T(8,128)S(1)}, u32[]{:S(2)}) copy-start(f32[8,256]{1,0:T(8,128)S(1)} %dynamic_update_slice.3.gains_ref) | copy-start | bytes 24580
  3.5 8.6 %copy-start.3 = (f32[16,256]{1,0:T(8,128)}, f32[16,256]{1,0:T(8,128)S(1)}, u32[]{:S(2)}) copy-start(f32[16,256]{1,0:T(8,128)S(1)} %scatter.14.misc_ref) | copy-start | bytes 49156
  549.8 10.4 %copy-start.1 = (bf16[128,2048]{1,0:T(8,128)(2,1)S(1)}, bf16[128,2048]{1,0:T(8,128)(2,1)}, u32[]{:S(2)}) copy-start(bf16[128,2048]{1,0:T(8,128)(2,1)} %get-tuple-element.139) | copy-start | bytes 1572868
  549.8 11.2 %copy-start.2 = (bf16[128,2048]{1,0:T(8,128)(2,1)S(1)}, bf16[128,2048]{1,0:T(8,128)(2,1)}, u32[]{:S(2)}) copy-start(bf16[128,2048]{1,0:T(8,128)(2,1)} %get-tuple-element.140) | copy-start | bytes 1572868

commit v8 on v7

--- a/solution.py
+++ b/solution.py
@@ -486,6 +486,7 @@
     for copy in core_copies:
         copy.start()
 
+    beside = peer_of(me, 2)
     own_tok.wait()
     tok_line = Line(c, tok.at[0], z, depth, rows)
     tok_line.begin()
@@ -541,6 +542,12 @@
     vo_copies = weight_copies(bits[:0:-1], 1)
     qk_copies[0].start()
     vo_copies[0].start()
+    grad_cut = width * 12 // 16
+    grad_left, grad_right = pl.ds(0, grad_cut), pl.ds(grad_cut, width - grad_cut)
+    far_grads = grads_ref.at[2, :, grad_right]
+    grad_beside = c.remote(outgrad_ref.at[:, grad_right], piece(far_grads, z), dp=beside)
+    grad_beside.start()
+    far_grad_line = Line(c, far_grads, z, depth, rows)
     for copy in pads + [copy for m in near for copy in m]:
         copy.start()
 
@@ -641,6 +648,8 @@
     norm_rows(0)
     project(0)
     line_step(grad_line, 1)
+    grad_beside.wait()
+    far_grad_line.begin()
     for copy in far[0]:
         copy.wait_recv()
     over[0].start()
@@ -685,6 +694,7 @@
     attend(1)
     if depth > 2:
         line_step(grad_line, 2)
+        line_step(far_grad_line, 1)
     project_out(1)
     part_pass = c.remote(part.at[1], part_in, dp=peer_of(me, 1))
     part_pass.start()
@@ -704,35 +714,27 @@
     ]
     for copy in saved:
         copy.start()
-    scatter = []
-    for r in list(range(1, depth)) + [0]:
-        at = pl.ds(pl.multiple_of((z + r) % depth * rows, rows), rows)
-        total = part[0, at, :].astype(F32) + part_in[at, :].astype(F32)
-        if r:
-            part[0, at, :] = total.astype(BF)
-            copy = c.remote(part.at[0, at], scatter_in.at[r - 1], tensor=(z + r) % depth)
-            copy.start()
-            scatter.append(copy)
-        else:
-            hidden_ref[...] = total + tok[0, at, :].astype(F32)
-
     for k in range(3, depth):
         line_step(grad_line, k)
-    x_grad = c.remote(grads_ref.at[0], grads_ref.at[2], dp=peer_of(me, 2))
+        line_step(far_grad_line, k - 1)
+    x_grad = c.remote(grads_ref.at[0, :, grad_left], grads_ref.at[2, :, grad_left], dp=beside)
     x_grad.start()
     own_pass = c.remote(grads_ref.at[0], grads_ref.at[1], dp=peer_of(me, 1))
     own_pass.start()
+    here_at = pl.ds(pl.multiple_of(z * rows, rows), rows)
+    hidden_ref[...] = part[0, here_at, :].astype(F32) + part_in[here_at, :].astype(F32)
+    hidden_ref[...] += tok[0, here_at, :].astype(F32)
+    for r in range(depth):
+        at = pl.ds(r * rows, rows)
+        part[0, at, :] = (part[0, at, :].astype(F32) + part_in[at, :].astype(F32)).astype(BF)
+    scatter = LineSum(c, part.at[0], scatter_in.at[0], scatter_in.at[1], z, depth, rows)
+    scatter.run()
     for k in (1, 2):
         for copy in far[k]:
             copy.wait_recv()
         over[k].start()
-
-    for copy in scatter:
-        copy.wait_recv()
+    scatter.collect(hidden_ref)
     total = hidden_ref[...]
-    for r in range(1, depth):
-        total = total + scatter_in[r - 1].astype(F32)
-    hidden_ref[...] = total
     scale = lax.rsqrt(jnp.mean(total * total, axis=-1, keepdims=True) + EPS)
     norm_mine[...] = (total * scale * gain_rows[1:2, :]).astype(BF)
     norm_here = c.local(norm_mine, piece(norm_ref.at[0], z))
@@ -740,30 +742,39 @@
     norm_here.wait()
     norm_line = Line(c, norm_ref.at[0], z, depth, rows)
     norm_line.begin()
-    beside = peer_of(me, 2)
+    cut = width * 10 // 16
+    left, right = pl.ds(0, cut), pl.ds(cut, width - cut)
     norm_own = c.remote(piece(norm_ref.at[0], z), piece(norm_ref.at[1], z), dp=sibling)
     norm_far = c.remote(piece(norm_ref.at[0], z), piece(norm_ref.at[2], z), dp=beside)
     norm_far.start()
     norm_own.start()
+    far_line = Line(c, norm_ref.at[2, :, right], z, depth, rows)
     norm_passed, far_passed = [], []
     pass_norm = pass_on(
         c, norm_ref.at[0], norm_ref.at[1], z, depth, rows, sibling, norm_passed
     )
-    pass_far = pass_on(c, norm_ref.at[0], norm_ref.at[2], z, depth, rows, beside, far_passed)
+    pass_far = pass_on(
+        c, norm_ref.at[0, :, left], norm_ref.at[2, :, left], z, depth, rows, beside, far_passed
+    )
 
     def pass_both(k, up):
         pass_far(k, up)
         pass_norm(k, up)
 
-    for k in range(1, depth):
+    line_step(norm_line, 1, pass_both)
+    norm_far.wait()
+    far_line.begin()
+    for k in range(2, depth):
         line_step(norm_line, k, pass_both)
-
+        line_step(far_line, k - 1)
+    line_step(far_line, depth - 1)
+
+    line_step(far_grad_line, depth - 1)
     x_grad.wait_recv()
     grad_pass = c.remote(grads_ref.at[2], grads_ref.at[3], dp=peer_of(me, 1))
     grad_pass.start()
     for copy in over_near + over:
         copy.wait()
-    norm_far.wait()
     for copy, there in far_passed:
         pl.when(there)(copy.wait)
     norm_pass = c.remote(norm_ref.at[2], norm_ref.at[3], dp=sibling)
@@ -774,11 +785,11 @@
     norm_pass.wait()
     own_pass.wait()
     grad_pass.wait()
-    for line in (tok_line, grad_line, norm_line):
+    for line in (tok_line, grad_line, far_grad_line, norm_line, far_line, scatter):
         line.finish()
     for copy in pads + saved:
         copy.wait()
-    for copy in gain_copies + misc_copies + gain_spread + qk_copies + vo_copies + scatter:
+    for copy in gain_copies + misc_copies + gain_spread + qk_copies + vo_copies:
         copy.wait_send()
     for copy in [part_pass, x_grad] + [y for m in far for y in m]:
         copy.wait_send()
@@ -826,7 +837,7 @@
             pltpu.VMEM((seq_len, width), BF),
             pltpu.VMEM((2, seq_len, width), BF),
             pltpu.VMEM((seq_len, width), BF),
-            pltpu.VMEM((depth - 1, rows, width), BF),
+            pltpu.VMEM((2, depth - 1, rows, width), BF),
             pltpu.VMEM((depth, dp) + gains.shape, F32),
             pltpu.VMEM((routed + 1, hidden_pad - hidden_units, width), BF),
             pltpu.SemaphoreType.DMA((160,)),
@@ -1155,6 +1166,98 @@
             collective_id=2, has_side_effects=True, vmem_limit_bytes=63 * 2**20
         ),
     )(hidden, codes, router, norm, grads, gateup, down)
+
+
+class LineSum:
+    def __init__(self, c, data, ups, downs, z, depth, rows):
+        self.data, self.ups, self.downs = data, ups, downs
+        self.z, self.depth, self.rows = z, depth, rows
+        self.up_copies = [
+            c.remote(self.piece(t), ups.at[t - 1], tensor=z + 1) for t in range(1, depth)
+        ]
+        self.down_copies = [
+            c.remote(self.piece(t), downs.at[t], tensor=z - 1) for t in range(depth - 1)
+        ]
+
+    def piece(self, t):
+        return self.data.at[pl.ds(t * self.rows, self.rows)]
+
+    def add(self, t, other):
+        at = pl.ds(t * self.rows, self.rows)
+        self.data[at, :] = (self.data[at, :].astype(F32) + other.astype(F32)).astype(BF)
+
+    def up(self, t):
+        copy = self.up_copies[t - 1]
+
+        @pl.when(self.z < t)
+        def _():
+            @pl.when(self.z > 0)
+            def _():
+                copy.wait_recv()
+                self.add(t, self.ups[t - 1])
+
+            copy.start()
+
+    def down(self, t):
+        copy = self.down_copies[t]
+
+        @pl.when(self.z > t)
+        def _():
+            @pl.when(self.z < self.depth - 1)
+            def _():
+                copy.wait_recv()
+                self.add(t, self.downs[t])
+
+            copy.start()
+
+    def begin(self):
+        top = self.depth - 1
+
+        @pl.when(self.z == 0)
+        def _():
+            for k in range(top):
+                self.up_copies[top - k - 1].start()
+
+        @pl.when(self.z == top)
+        def _():
+            for k in range(top):
+                self.down_copies[k].start()
+
+    def step(self, k):
+        top = self.depth - 1
+
+        @pl.when(jnp.logical_and(self.z > 0, self.z < self.depth // 2))
+        def _():
+            self.up(top - k)
+            self.down(k)
+
+        @pl.when(jnp.logical_and(self.z >= self.depth // 2, self.z < top))
+        def _():
+            self.down(k)
+            self.up(top - k)
+
+    def run(self):
+        self.begin()
+        for k in range(self.depth - 1):
+            self.step(k)
+
+    def collect(self, total_ref):
+        for t in range(self.depth):
+
+            @pl.when(self.z == t)
+            def _(t=t):
+                if t > 0:
+                    self.up_copies[t - 1].wait_recv()
+                    total_ref[...] += self.ups[t - 1].astype(F32)
+                if t < self.depth - 1:
+                    self.down_copies[t].wait_recv()
+                    total_ref[...] += self.downs[t].astype(F32)
+
+    def finish(self):
+        for t in range(1, self.depth):
+            pl.when(self.z < t)(self.up_copies[t - 1].wait_send)
+        for t in range(self.depth - 1):
+            pl.when(self.z > t)(self.down_copies[t].wait_send)
 
 
 def backward_body(
@@ -1262,23 +1365,22 @@
 
     for copy in loads:
         copy.wait()
-    scatter, small = [], []
-    for r in list(range(1, depth)) + [0]:
+    small = []
+    for r in range(depth):
         at = at_of((z + r) % depth)
         total = three[0, at, :].astype(F32) + three[1, at, :].astype(F32)
         total = total + three[2, at, :].astype(F32)
+        three[0, at, :] = total.astype(BF)
         extra = terms_ref[0, at, :] + terms_ref[1, at, :] + terms_ref[2, at, :]
+        terms_sum[at, :] = extra
         if r:
-            three[0, at, :] = total.astype(BF)
-            terms_sum[at, :] = extra
-            peer = (z + r) % depth
-            scatter.append(c.remote(three.at[0, at], scatter_in.at[0, r - 1], tensor=peer))
-            small.append(c.remote(terms_sum.at[at], terms_in.at[r - 1], tensor=peer))
-            scatter[-1].start()
-            small[-1].start()
+            copy = c.remote(terms_sum.at[at], terms_in.at[r - 1], tensor=(z + r) % depth)
+            copy.start()
+            small.append(copy)
         else:
             keep[0] = total
-            terms_sum[at, :] = extra
+    scatter = LineSum(c, three.at[0], scatter_in.at[0, 0], scatter_in.at[0, 1], z, depth, rows)
+    scatter.run()
 
     def add_over(m):
         own_loads[m].wait()
@@ -1304,15 +1406,13 @@
         return copies
 
     units = add_over(0)
-    for copy in scatter:
-        copy.wait_recv()
     for copy in small:
         copy.wait_recv()
     route = terms_sum[at_of(z), :]
+    for r in range(1, depth):
+        route = route + terms_in[r - 1]
+    scatter.collect(keep.at[0])
     grad = keep[0]
-    for r in range(1, depth):
-        grad = grad + scatter_in[0, r - 1].astype(F32)
-        route = route + terms_in[r - 1]
     probs_mine = probs_mine_ref[...]
     lane = lax.broadcasted_iota(jnp.int32, route.shape, 1)
     inner = jnp.sum(jnp.where(lane < experts, probs_mine * route, 0.0), axis=1, keepdims=True)
@@ -1341,8 +1441,6 @@
     back_own.start()
     passed = []
     pass_back = pass_on(c, back.at[0], back.at[1], z, depth, rows, sibling, passed)
-    for copy in scatter:
-        copy.wait_send()
     line_step(line, 1, pass_back)
 
     for copy in inputs:
@@ -1356,8 +1454,8 @@
         return carry
 
     lax.fori_loop(0, depth, scale_rows, 0)
+    units += add_over(1)
     line_step(line, 2, pass_back)
-    units += add_over(1)
     line_step(line, 3, pass_back)
     back_own.wait()
     for copy, there in passed:
@@ -1405,26 +1503,22 @@
             row = jnp.sum(total * unit_block, axis=0, keepdims=True)
             vectors[2 + s : 3 + s, slab(d)] = row
 
+    units += add_over(2)
     attention(1)
     first_grad(1)
     part_pass = c.remote(three.at[2], part_in, dp=sibling)
     part_pass.start()
-    units += add_over(2)
     attention(0)
     first_grad(0)
     part_pass.wait_recv()
-    first_scatter = []
-    for r in list(range(1, depth)) + [0]:
-        at = at_of((z + r) % depth)
-        total = three[1, at, :].astype(F32) + part_in[at, :].astype(F32)
-        if r:
-            three[1, at, :] = total.astype(BF)
-            peer = (z + r) % depth
-            copy = c.remote(three.at[1, at], scatter_in.at[1, r - 1], tensor=peer)
-            copy.start()
-            first_scatter.append(copy)
-        else:
-            keep[1] = total
+    keep[1] = three[1, at_of(z), :].astype(F32) + part_in[at_of(z), :].astype(F32)
+    for r in range(depth):
+        at = at_of(r)
+        three[1, at, :] = (three[1, at, :].astype(F32) + part_in[at, :].astype(F32)).astype(BF)
+    first_scatter = LineSum(
+        c, three.at[1], scatter_in.at[1, 0], scatter_in.at[1, 1], z, depth, rows
+    )
+    first_scatter.begin()
 
     for d in range(dp):
         total = jnp.zeros((slice_width, 3 * pair), F32)
@@ -1450,7 +1544,9 @@
     )
     qk_first.start()
     vo_first.start()
-
+    first_scatter.step(0)
+
+    scatter.finish()
     norm_load = c.local(norm_hbm.at[0], three.at[0])
     norm_load.start()
     norm_load.wait()
@@ -1481,6 +1577,8 @@
         misc_copies.append(c.remote(misc_part.at[to], misc_in.at[r - 1], dp=to))
         misc_copies[-1].start()
 
+    for k in range(1, depth - 1):
+        first_scatter.step(k)
     qk_first.wait()
     mine = index(pl.ds(y, 1), every, 0)
     total_a[mine] = (total_a[mine].astype(F32) + first_qk[...].astype(F32)).astype(BF)
@@ -1521,11 +1619,8 @@
             finals.append(c.remote(source, place, dp=sibling) if other else c.local(source, place))
             finals[-1].start()
 
-    for copy in first_scatter:
-        copy.wait_recv()
+    first_scatter.collect(keep.at[1])
     total = keep[1]
-    for r in range(1, depth):
-        total = total + scatter_in[1, r - 1].astype(F32)
     total = total * gain_rows[0:1, :]
     scale = scales[0, at_of(z), :]
     unit = tok[0, at_of(z), :].astype(F32) * scale
@@ -1540,7 +1635,8 @@
     for copy in finals + units:
         copy.wait()
     line.finish()
-    for copy in over[1:] + small + first_scatter + misc_copies + [part_pass]:
+    first_scatter.finish()
+    for copy in over[1:] + small + misc_copies + [part_pass]:
         copy.wait_send()
 
 
@@ -1571,7 +1667,7 @@
             pltpu.VMEM((4,) + units, BF),
             pltpu.VMEM((3, 4) + units, BF),
             pltpu.VMEM((3, seq_len, width), BF),
-            pltpu.VMEM((2, depth - 1, output_rows, width), BF),
+            pltpu.VMEM((2, 2, depth - 1, output_rows, width), BF),
             pltpu.VMEM((seq_len, 128), F32),
             pltpu.VMEM((depth - 1, output_rows, 128), F32),
             pltpu.VMEM((2, seq_len, width + 128), BF),

time: 567 us -> 543 us (0.958)
  Pallas kernels: 544 us -> 516 us
    pallas_call x1, Pallas kernels: 219 us -> 201 us  [forward_call(): pl.pallas_call(functools.partial(forward_body, (dp, depth, experts, hidde...]
    pallas_call x1, Pallas kernels: 173 us -> 164 us  [backward_call(): pl.pallas_call(functools.partial(backward_body, (dp, depth, experts, head...]
where the time goes in v8:
time: 543 us; the launch traced here: 534 us
  Pallas kernels  516 us (95%)
  local copies, waits for them, and re-layouts  12.8 us (2%)
    pallas_call x1, Pallas kernels, forward_call(): pl.pallas_call(functools.partial(forward_body, (dp, depth, experts, hidde...  201 us
    pallas_call x1, Pallas kernels, backward_call(): pl.pallas_call(functools.partial(backward_body, (dp, depth, experts, head...  164 us
    pallas_call x1, Pallas kernels, middle_call(): pl.pallas_call(functools.partial(middle_body, (dp, depth, experts, top_co...  141 us

profile of v8, /device:TPU:0, one launch (start us, length us, event | category | flops | bytes accessed | tf_op | source)
XLA Modules:
  0.0 534.1 jit_solution(11621857922892555238)
XLA Ops:
  0.6 0.0 copy-start
  0.7 0.7 convert_element_type.24
  1.4 0.8 reshape.129
  2.2 0.1 reshape.128
  2.3 0.3 dynamic_update_slice.3.gains_ref
  2.6 0.0 copy-start.4
  2.6 0.7 pad_convert_fusion
  3.3 0.2 scatter.14.misc_ref
  3.5 0.0 copy-start.3
  3.5 0.7 pad_add_fusion
  4.3 0.6 pad.12.codes_ref
  4.9 1.8 copy.39
  6.7 2.2 copy.40
  9.0 0.0 copy-done
  9.0 1.1 copy.41
  10.1 1.0 fusion.2
  11.1 0.0 copy-done.4
  11.1 1.0 pad_maximum_fusion
  12.1 0.0 copy-done.3
  12.1 201.0 %shard_map.289 = (f32[128,2048]{1,0:T(8,128)}, bf16[4,512,2048]{2,1,0:T(8,128)(2,1)}, bf16[4,512,2048]{2,1,0:T(8,128)(2,1)}, bf16[3,2,384,2048]{3,2,1,0:T(8,128)...) custom-call(s32[16,512]{1,0:T(8,128)} %pad.12.codes_ref, ...), custom_call_target="tpu_custom_call" | custom-call | tf_op jit(solution)/shard_map/pallas_call | solution.py:810
  213.1 140.9 %shard_map.290 = (bf16[128,2048]{1,0:T(8,128)(2,1)}, f32[3,512,128]{2,1,0:T(8,128)}, f32[128,128]{1,0:T(8,128)}, bf16[512,2048]{1,0:T(8,128)(2,1)}, bf16[512,204...) custom-call(f32[128,2048]{1,0:T(8,128)} %get-tuple-element.79.hidden, ...), custom_call_target="tpu_custom_call" | custom-call | tf_op jit(solution)/shard_map/pallas_call | solution.py:1126
  354.0 163.7 %shard_map.291 = (bf16[128,2048]{1,0:T(8,128)(2,1)}, bf16[4,3,352,256]{3,2,1,0:T(8,128)(2,1)}, bf16[4,3,352,256]{3,2,1,0:T(8,128)(2,1)}, bf16[4,3,352,256]{3,2,1...) custom-call(f32[3,512,128]{2,1,0:T(8,128)} %get-tuple-element.87.terms_ref, ...), custom_call_target="tpu_custom_call" | custom-call | tf_op jit(solution)/shard_map/pallas_call | solution.py:1653
  517.6 0.7 slice.49
  518.3 1.3 slice_bitcast_fusion
  519.7 0.7 slice.48
  520.4 0.6 constant_dynamic-slice_fusion
  521.0 0.1 reshape.126
  521.1 0.6 copy.42
  521.7 0.0 copy-start.1
  521.7 0.0 copy-start.2
  521.7 10.3 %shard_map.292 = (f32[8,352,256]{2,1,0:T(8,128)}, f32[8,352,256]{2,1,0:T(8,128)}, f32[8,352,256]{2,1,0:T(8,128)}, f32[256,1408]{1,0:T(8,128)}, f32[256,1408]{1,0...) custom-call(bf16[4,3,352,256]{3,2,1,0:T(8,128)(2,1)} %get-tuple-elem, ...), custom_call_target="tpu_custom_call" | custom-call | bytes 19464192 | tf_op jit(solution)/shard_map/pallas_call | solution.py:1741
  532.0 0.0 copy-done.1
  532.0 0.8 copy.49
  532.8 0.0 copy-done.2
  532.8 0.8 copy.50
  (3 shorter events, 0.0 us)
Async XLA Ops:
  0.6 8.3 %copy-start = (bf16[256,1408]{1,0:T(8,128)(2,1)S(1)}, bf16[256,1408]{1,0:T(8,128)(2,1)}, u32[]{:S(2)}) copy-start(bf16[256,1408]{1,0:T(8,128)(2,1)} %param.34) | copy-start | bytes 2162692
  2.6 8.5 %copy-start.4 = (f32[8,256]{1,0:T(8,128)}, f32[8,256]{1,0:T(8,128)S(1)}, u32[]{:S(2)}) copy-start(f32[8,256]{1,0:T(8,128)S(1)} %dynamic_update_slice.3.gains_ref) | copy-start | bytes 24580
  3.5 8.6 %copy-start.3 = (f32[16,256]{1,0:T(8,128)}, f32[16,256]{1,0:T(8,128)S(1)}, u32[]{:S(2)}) copy-start(f32[16,256]{1,0:T(8,128)S(1)} %scatter.14.misc_ref) | copy-start | bytes 49156
  521.7 10.4 %copy-start.1 = (bf16[128,2048]{1,0:T(8,128)(2,1)S(1)}, bf16[128,2048]{1,0:T(8,128)(2,1)}, u32[]{:S(2)}) copy-start(bf16[128,2048]{1,0:T(8,128)(2,1)} %get-tuple-element.139) | copy-start | bytes 1572868
  521.7 11.2 %copy-start.2 = (bf16[128,2048]{1,0:T(8,128)(2,1)S(1)}, bf16[128,2048]{1,0:T(8,128)(2,1)}, u32[]{:S(2)}) copy-start(bf16[128,2048]{1,0:T(8,128)(2,1)} %get-tuple-element.140) | copy-start | bytes 1572868

commit v9 on v8

--- a/solution.py
+++ b/solution.py
@@ -2,6 +2,7 @@
 
 import jax
 import jax.numpy as jnp
+import numpy as np
 from jax import lax
 from jax.experimental import pallas as pl
 from jax.experimental.pallas import tpu as pltpu
@@ -18,6 +19,12 @@
     inverse = THETA ** (-(2.0 * jnp.arange(half_width, dtype=F32)) / width)
     angles = jnp.arange(length, dtype=F32)[:, None] * inverse[None, :]
     return jnp.cos(angles), jnp.sin(angles)
+
+
+def rope_arrays(length, width):
+    inverse = THETA ** (-(2.0 * np.arange(width // 2)) / width)
+    angles = np.arange(length)[:, None] * inverse[None, :]
+    return np.cos(angles).astype(np.float32), np.sin(angles).astype(np.float32)
 
 
 def rotate(field_in, cos_part, sin_part):
@@ -433,6 +440,8 @@
     scatter_in,
     gains_all,
     zeros,
+    shared_raw,
+    shared_rows,
     send,
     recv,
     here,
@@ -470,8 +479,9 @@
 
     own_tok = c.local(tokens_ref, piece(tok.at[0], z))
     own_tok.start()
-    own_grad = c.local(outgrad_ref, piece(grads_ref.at[0], z))
-    own_grad.start()
+    grad_up = c.local(outgrad_ref, norm_mine)
+    grad_up.start()
+    own_grad = c.local(norm_mine, piece(grads_ref.at[0], z))
 
     def columns(k, n):
         return pl.ds(pl.multiple_of(k * n, n), n)
@@ -493,11 +503,14 @@
     tok_pass = [c.remote(tokens_ref, piece(tok.at[1], z), dp=peer_of(me, 1))]
     tok_pass[0].start()
 
+    shared_loads = [c.local(sg_ref, shared_raw.at[0]), c.local(su_ref, shared_raw.at[1])]
+    for copy in shared_loads:
+        copy.start()
     zeros[...] = jnp.zeros_like(zeros)
     pad = zeros.shape[1]
     pads = [c.local(zeros, down_ref.at[:, 0, pl.ds(hidden_units, pad)])]
     pads += [c.local(zeros, gateup_ref.at[:, k, pl.ds(hidden_units, pad)]) for k in range(2)]
-    matrices = ((ed_ref, sd_ref, down_ref, 0), (eg_ref, sg_ref, gateup_ref, 0), (eu_ref, su_ref, gateup_ref, 1))
+    matrices = ((ed_ref, sd_ref, down_ref, 0), (eg_ref, shared_rows.at[0], gateup_ref, 0), (eu_ref, shared_rows.at[1], gateup_ref, 1))
     slab = columns(me, slice_width)
 
     def group_copies(routed_src, shared_src, dst, k, r):
@@ -514,15 +527,15 @@
     near = [[copy for r in (0, 1) for copy in group_copies(*m, r)] for m in matrices]
     far = [[copy for r in (2, 3) for copy in group_copies(*m, r)] for m in matrices]
 
-    def over_copy(dst, k, far_chip):
+    def over_copy(dst, k):
         n = 2 * slice_width
-        chip = me // 2 + far_chip * (1 - 2 * x)
+        chip = me // 2 + 1 - 2 * x
         cols = pl.ds(pl.multiple_of(chip * n, n), n)
         place = dst.at[:, k, pl.ds(0, hidden_units), cols]
         return c.remote(place, place, dp=peer_of(me, 4))
 
-    over_near = [over_copy(m[2], m[3], 0) for m in matrices]
-    over = [over_copy(m[2], m[3], 1) for m in matrices]
+    over_near = [copy for m in matrices for r in (4, 5) for copy in group_copies(*m, r)]
+    over = [over_copy(m[2], m[3]) for m in matrices]
 
     for copy in core_copies:
         copy.wait()
@@ -548,6 +561,10 @@
     grad_beside = c.remote(outgrad_ref.at[:, grad_right], piece(far_grads, z), dp=beside)
     grad_beside.start()
     far_grad_line = Line(c, far_grads, z, depth, rows)
+    for k in range(2):
+        shared_loads[k].wait()
+        flipped = jnp.transpose(shared_raw[k].astype(F32)).astype(BF)
+        shared_rows[k] = flipped.reshape(shared_rows.shape[1:])
     for copy in pads + [copy for m in near for copy in m]:
         copy.start()
 
@@ -570,6 +587,8 @@
         qk_copies[k].start()
         vo_copies[k - 1].wait_recv()
         vo_copies[k].start()
+    grad_up.wait()
+    own_grad.start()
     own_grad.wait()
     grad_line = Line(c, grads_ref.at[0], z, depth, rows)
     for k in range(2, depth):
@@ -622,9 +641,7 @@
     for m in far:
         for copy in m:
             copy.start()
-    for m, copy in zip(near, over_near):
-        for part_copy in m:
-            part_copy.wait()
+    for copy in over_near:
         copy.start()
     pairs = pair // head
 
@@ -742,7 +759,7 @@
     norm_here.wait()
     norm_line = Line(c, norm_ref.at[0], z, depth, rows)
     norm_line.begin()
-    cut = width * 10 // 16
+    cut = width * 12 // 16
     left, right = pl.ds(0, cut), pl.ds(cut, width - cut)
     norm_own = c.remote(piece(norm_ref.at[0], z), piece(norm_ref.at[1], z), dp=sibling)
     norm_far = c.remote(piece(norm_ref.at[0], z), piece(norm_ref.at[2], z), dp=beside)
@@ -773,7 +790,7 @@
     x_grad.wait_recv()
     grad_pass = c.remote(grads_ref.at[2], grads_ref.at[3], dp=peer_of(me, 1))
     grad_pass.start()
-    for copy in over_near + over:
+    for copy in over_near + over + [copy for m in near for copy in m]:
         copy.wait()
     for copy, there in far_passed:
         pl.when(there)(copy.wait)
@@ -840,6 +857,8 @@
             pltpu.VMEM((2, depth - 1, rows, width), BF),
             pltpu.VMEM((depth, dp) + gains.shape, F32),
             pltpu.VMEM((routed + 1, hidden_pad - hidden_units, width), BF),
+            pltpu.VMEM((2, width // dp, 4 * hidden_units), BF),
+            pltpu.VMEM((2, 4, hidden_units, width // dp), BF),
             pltpu.SemaphoreType.DMA((160,)),
             pltpu.SemaphoreType.DMA((160,)),
             pltpu.SemaphoreType.DMA((40,)),
@@ -2231,9 +2250,9 @@
         norm_gains.astype(F32),
         (jnp.int32(0), zi * norm_gains.shape[1]),
     )
-    cos_part, sin_part = rope_tables(seq_len, head_width)
-    cos_rows = jnp.concatenate([cos_part, cos_part], axis=1)
-    sin_rows = jnp.concatenate([-sin_part, sin_part], axis=1)
+    cos_part, sin_part = rope_arrays(seq_len, head_width)
+    cos_rows = np.concatenate([cos_part, cos_part], axis=1)
+    sin_rows = np.concatenate([-sin_part, sin_part], axis=1)
     (
         hidden,
         norm_all,
@@ -2259,8 +2278,8 @@
             expert_gate.swapaxes(1, 2),
             expert_up.swapaxes(1, 2),
             expert_down,
-            shared_gate.T.reshape(4, hidden_units, slice_width),
-            shared_up.T.reshape(4, hidden_units, slice_width),
+            shared_gate,
+            shared_up,
             shared_down.reshape(4, hidden_units, slice_width),
         ),
     )

time: 543 us -> 535 us (0.985)
  no operation moved by 1% of the time
where the time goes in v9:
time: 535 us; the launch traced here: 526 us
  Pallas kernels  514 us (96%)
  local copies, waits for them, and re-layouts  9.45 us (2%)
    pallas_call x1, Pallas kernels, forward_call(): pl.pallas_call(functools.partial(forward_body, (dp, depth, experts, hidde...  199 us
    pallas_call x1, Pallas kernels, backward_call(): pl.pallas_call(functools.partial(backward_body, (dp, depth, experts, head...  163 us
    pallas_call x1, Pallas kernels, middle_call(): pl.pallas_call(functools.partial(middle_body, (dp, depth, experts, top_co...  141 us

profile of v9, /device:TPU:0, one launch (start us, length us, event | category | flops | bytes accessed | tf_op | source)
XLA Modules:
  0.0 526.4 jit_solution(6326146907751710521)
XLA Ops:
  0.7 0.7 convert_element_type.24
  1.3 0.8 reshape.114
  2.1 0.1 reshape.113
  2.2 0.3 dynamic_update_slice.3.gains_ref
  2.5 0.0 copy-start.3
  2.5 0.7 pad_convert_fusion
  3.2 0.2 scatter.14.misc_ref
  3.4 0.0 copy-start.2
  3.5 0.7 pad_add_fusion
  4.2 0.6 pad.12.codes_ref
  4.8 1.8 copy.39
  6.6 0.0 copy-done.3
  6.6 0.0 copy-done.2
  6.6 199.0 %shard_map.307 = (f32[128,2048]{1,0:T(8,128)}, bf16[4,512,2048]{2,1,0:T(8,128)(2,1)}, bf16[4,512,2048]{2,1,0:T(8,128)(2,1)}, bf16[3,2,384,2048]{3,2,1,0:T(8,128)...) custom-call(s32[16,512]{1,0:T(8,128)} %pad.12.codes_ref, ...), custom_call_target="tpu_custom_call" | custom-call | tf_op jit(solution)/shard_map/pallas_call | solution.py:827
  205.6 141.1 %shard_map.308 = (bf16[128,2048]{1,0:T(8,128)(2,1)}, f32[3,512,128]{2,1,0:T(8,128)}, f32[128,128]{1,0:T(8,128)}, bf16[512,2048]{1,0:T(8,128)(2,1)}, bf16[512,204...) custom-call(f32[128,2048]{1,0:T(8,128)} %get-tuple-element.79.hidden, ...), custom_call_target="tpu_custom_call" | custom-call | tf_op jit(solution)/shard_map/pallas_call | solution.py:1145
  346.8 163.1 %shard_map.309 = (bf16[128,2048]{1,0:T(8,128)(2,1)}, bf16[4,3,352,256]{3,2,1,0:T(8,128)(2,1)}, bf16[4,3,352,256]{3,2,1,0:T(8,128)(2,1)}, bf16[4,3,352,256]{3,2,1...) custom-call(f32[3,512,128]{2,1,0:T(8,128)} %get-tuple-element.87.terms_ref, ...), custom_call_target="tpu_custom_call" | custom-call | tf_op jit(solution)/shard_map/pallas_call | solution.py:1672
  509.9 0.7 slice.49
  510.6 1.3 slice_bitcast_fusion
  511.9 0.7 slice.48
  512.6 0.6 constant_dynamic-slice_fusion
  513.3 0.1 reshape.111
  513.4 0.6 copy.40
  514.0 0.0 copy-start
  514.0 0.0 copy-start.1
  514.0 10.3 %shard_map.310 = (f32[8,352,256]{2,1,0:T(8,128)}, f32[8,352,256]{2,1,0:T(8,128)}, f32[8,352,256]{2,1,0:T(8,128)}, f32[256,1408]{1,0:T(8,128)}, f32[256,1408]{1,0...) custom-call(bf16[4,3,352,256]{3,2,1,0:T(8,128)(2,1)} %get-tuple-elem, ...), custom_call_target="tpu_custom_call" | custom-call | bytes 19464192 | tf_op jit(solution)/shard_map/pallas_call | solution.py:1760
  524.3 0.0 copy-done
  524.3 0.8 copy.47
  525.1 0.0 copy-done.1
  525.1 0.8 copy.48
  (2 shorter events, 0.0 us)
Async XLA Ops:
  2.5 4.1 copy-start.3
  3.4 3.2 copy-start.2
  514.0 10.4 %copy-start = (bf16[128,2048]{1,0:T(8,128)(2,1)S(1)}, bf16[128,2048]{1,0:T(8,128)(2,1)}, u32[]{:S(2)}) copy-start(bf16[128,2048]{1,0:T(8,128)(2,1)} %get-tuple-element.134) | copy-start | bytes 1572868
  514.0 11.2 %copy-start.1 = (bf16[128,2048]{1,0:T(8,128)(2,1)S(1)}, bf16[128,2048]{1,0:T(8,128)(2,1)}, u32[]{:S(2)}) copy-start(bf16[128,2048]{1,0:T(8,128)(2,1)} %get-tuple-element.135) | copy-start | bytes 1572868

commit v10 on v9

--- a/solution.py
+++ b/solution.py
@@ -1718,14 +1718,14 @@
 
 
 def finish_body(
-    gate_ref, up_ref, down_ref, attn_ref, eg_ref, eu_ref, ed_ref, sg_ref, su_ref, sd_ref,
-    q_ref, k_ref, v_ref, o_ref, sg_rows, su_rows
+    gate_ref, up_ref, down_ref, attn_ref, misc_ref, eg_ref, eu_ref, ed_ref, sg_ref, su_ref, sd_ref,
+    q_ref, k_ref, v_ref, o_ref, router_ref, sg_rows, su_rows
 ):
-    group, groups = pl.program_id(0), pl.num_programs(0)
+    group = pl.program_id(0)
     many, rows, _ = eg_ref.shape
     for source, routed, shared in (
-        (gate_ref, eg_ref, sg_rows.at[group]),
-        (up_ref, eu_ref, su_rows.at[group]),
+        (gate_ref, eg_ref, sg_rows.at[pl.ds(pl.multiple_of(group * rows, 8), rows)]),
+        (up_ref, eu_ref, su_rows.at[pl.ds(pl.multiple_of(group * rows, 8), rows)]),
         (down_ref, ed_ref, sd_ref),
     ):
         for unit in range(many):
@@ -1734,6 +1734,7 @@
 
     @pl.when(group == 0)
     def _():
+        router_ref[...] = misc_ref[: router_ref.shape[0]]
         pair = attn_ref.shape[2] // 4
         for c in range(2):
             at = slice(c * pair, (c + 1) * pair)
@@ -1741,13 +1742,16 @@
                 out_ref[:, at] = attn_ref[c, :, kind * pair : (kind + 1) * pair].astype(F32)
             o_ref[at, :] = jnp.transpose(attn_ref[c, :, 3 * pair :].astype(F32))
 
-    @pl.when(group == groups - 1)
-    def _():
-        for source, out_ref in ((sg_rows, sg_ref), (su_rows, su_ref)):
-            out_ref[...] = jnp.transpose(source[...].reshape(groups * rows, -1))
-
-
-def finish_call(gate, up, down, attn):
+    for g in range(sg_rows.shape[0] // rows):
+
+        @pl.when(group == g)
+        def _(g=g):
+            at = slice(g * rows // 128 * 128, (g + 1) * rows // 128 * 128)
+            for source, out_ref in ((sg_rows, sg_ref), (su_rows, su_ref)):
+                out_ref[:, at] = jnp.transpose(source[at])
+
+
+def finish_call(columns, gate, up, down, attn, misc):
     groups, units, rows, slice_width = gate.shape
     many, pair = units - 1, attn.shape[2] // 4
     shape = jax.ShapeDtypeStruct
@@ -1760,21 +1764,21 @@
     return call(
         finish_body,
         (groups,),
-        [source] * 3 + [whole(*attn.shape)],
+        [source] * 3 + [whole(*attn.shape), whole(*misc.shape)],
         [routed] * 3
         + [whole(slice_width, groups * rows)] * 2
         + [pl.BlockSpec((rows, slice_width), lambda g: (g, 0))]
         + [whole(slice_width, 2 * pair)] * 3
-        + [whole(2 * pair, slice_width)],
+        + [whole(2 * pair, slice_width), whole(columns, slice_width)],
         [shape((groups * many, rows, slice_width), F32)] * 3
         + [shape((slice_width, groups * rows), F32)] * 2
         + [shape((groups * rows, slice_width), F32)]
         + [shape((slice_width, 2 * pair), F32)] * 3
-        + [shape((2 * pair, slice_width), F32)],
+        + [shape((2 * pair, slice_width), F32), shape((columns, slice_width), F32)],
         0,
         groups * units * rows * slice_width * 18,
-        [pltpu.VMEM((groups, rows, slice_width), F32)] * 2,
-    )(gate, up, down, attn)
+        [pltpu.VMEM((groups * rows, slice_width), F32)] * 2,
+    )(gate, up, down, attn, misc)
 
 
 def local_plain(
@@ -2317,8 +2321,8 @@
         + (tok, attn_weights, qkv, probs_low, heads_out, norm_all),
     )
 
-    egate_sum, eup_sum, edown_sum, sgate_sum, sup_sum, sdown_sum, *attn_sums = finish_call(
-        gate_sum, up_sum, down_sum, attn_sum
+    egate_sum, eup_sum, edown_sum, sgate_sum, sup_sum, sdown_sum, *attn_sums, router_sum = finish_call(
+        experts + 1, gate_sum, up_sum, down_sum, attn_sum, misc_sum
     )
     bias_sums = misc_sum[experts + 1 : experts + 3, :bias_width].reshape(2, 3, pair_heads, -1)
     bias_sums = bias_sums.swapaxes(0, 1).reshape(3, heads_local, -1)
@@ -2330,7 +2334,7 @@
         gain_sums,
         *attn_sums,
         bias_sums,
-        misc_sum[: experts + 1].T,
+        router_sum.T,
         sgate_sum,
         sup_sum,
         sdown_sum,

time: 535 us -> 533 us (level)
  no operation moved by 1% of the time
where the time goes in v10:
time: 533 us; the launch traced here: 524 us
  Pallas kernels  513 us (96%)
  local copies, waits for them, and re-layouts  8.13 us (2%)
    pallas_call x1, Pallas kernels, forward_call(): pl.pallas_call(functools.partial(forward_body, (dp, depth, experts, hidde...  199 us
    pallas_call x1, Pallas kernels, backward_call(): pl.pallas_call(functools.partial(backward_body, (dp, depth, experts, head...  163 us
    pallas_call x1, Pallas kernels, middle_call(): pl.pallas_call(functools.partial(middle_body, (dp, depth, experts, top_co...  141 us

profile of v10, /device:TPU:0, one launch (start us, length us, event | category | flops | bytes accessed | tf_op | source)
XLA Modules:
  0.0 524.4 jit_solution(706331613087056784)
XLA Ops:
  0.6 0.7 convert_element_type.24
  1.3 0.8 reshape.114
  2.1 0.1 reshape.113
  2.2 0.3 dynamic_update_slice.3.gains_ref
  2.5 0.0 copy-start.3
  2.5 0.7 pad_convert_fusion
  3.2 0.2 scatter.14.misc_ref
  3.4 0.0 copy-start.2
  3.5 0.7 pad_add_fusion
  4.2 0.6 pad.12.codes_ref
  4.8 1.8 copy.39
  6.6 0.0 copy-done.3
  6.6 0.0 copy-done.2
  6.6 199.0 %shard_map.307 = (f32[128,2048]{1,0:T(8,128)}, bf16[4,512,2048]{2,1,0:T(8,128)(2,1)}, bf16[4,512,2048]{2,1,0:T(8,128)(2,1)}, bf16[3,2,384,2048]{3,2,1,0:T(8,128)...) custom-call(s32[16,512]{1,0:T(8,128)} %pad.12.codes_ref, ...), custom_call_target="tpu_custom_call" | custom-call | tf_op jit(solution)/shard_map/pallas_call | solution.py:827
  205.6 141.1 %shard_map.308 = (bf16[128,2048]{1,0:T(8,128)(2,1)}, f32[3,512,128]{2,1,0:T(8,128)}, f32[128,128]{1,0:T(8,128)}, bf16[512,2048]{1,0:T(8,128)(2,1)}, bf16[512,204...) custom-call(f32[128,2048]{1,0:T(8,128)} %get-tuple-element.80.hidden, ...), custom_call_target="tpu_custom_call" | custom-call | tf_op jit(solution)/shard_map/pallas_call | solution.py:1145
  346.8 163.1 %shard_map.309 = (bf16[128,2048]{1,0:T(8,128)(2,1)}, bf16[4,3,352,256]{3,2,1,0:T(8,128)(2,1)}, bf16[4,3,352,256]{3,2,1,0:T(8,128)(2,1)}, bf16[4,3,352,256]{3,2,1...) custom-call(f32[3,512,128]{2,1,0:T(8,128)} %get-tuple-element.88.terms_ref, ...), custom_call_target="tpu_custom_call" | custom-call | tf_op jit(solution)/shard_map/pallas_call | solution.py:1672
  509.9 0.7 slice.46
  510.6 0.7 slice.45
  511.3 0.6 constant_dynamic-slice_fusion
  511.9 0.1 reshape.111
  512.0 0.6 copy.40
  512.6 0.0 copy-start
  512.6 0.0 copy-start.1
  512.6 9.7 %shard_map.310 = (f32[8,352,256]{2,1,0:T(8,128)}, f32[8,352,256]{2,1,0:T(8,128)}, f32[8,352,256]{2,1,0:T(8,128)}, f32[256,1408]{1,0:T(8,128)}, f32[256,1408]{1,0...) custom-call(bf16[4,3,352,256]{3,2,1,0:T(8,128)(2,1)} %get-tuple-elem, ...), custom_call_target="tpu_custom_call" | custom-call | bytes 19464192 | tf_op jit(solution)/shard_map/pallas_call | solution.py:1764
  522.4 0.0 copy-done
  522.4 0.8 copy.47
  523.2 0.0 copy-done.1
  523.2 0.8 copy.48
  (2 shorter events, 0.0 us)
Async XLA Ops:
  2.5 4.1 copy-start.3
  3.4 3.2 copy-start.2
  512.6 9.7 %copy-start = (bf16[128,2048]{1,0:T(8,128)(2,1)S(1)}, bf16[128,2048]{1,0:T(8,128)(2,1)}, u32[]{:S(2)}) copy-start(bf16[128,2048]{1,0:T(8,128)(2,1)} %get-tuple-element.136) | copy-start | bytes 1572868
  512.6 10.5 %copy-start.1 = (bf16[128,2048]{1,0:T(8,128)(2,1)S(1)}, bf16[128,2048]{1,0:T(8,128)(2,1)}, u32[]{:S(2)}) copy-start(bf16[128,2048]{1,0:T(8,128)(2,1)} %get-tuple-element.137) | copy-start | bytes 1572868
